TPU v7x, 128 devices: a whole 4x4x4 slice. The times are simulated.
128 devices in a mesh: leaf: 8 (over z, core), row: 16 (over x, y).
Axes of the slice: x: 4, y: 4, z: 4, core: 2. Of those that a mesh axis runs over, the one named last changes fastest.
Arguments:
- points: float32 [65536, 64], P(('leaf', 'row')), may hold values from -6 to 6
- samples: float32 [65536, 512], P(('leaf', 'row')), may hold values from -6 to 6
- test_matrix: float32 [65536, 512], P(('leaf', 'row')), may hold values from -0.0625 to 0.0625
- near_mask: int32 [8, 2], P('leaf'), may hold values from 0 to 1, as said below
- leaf_pivots: int32 [8, 256], P('leaf'), may hold values from 0 to 8191, as said below
- mid_pivots: int32 [4, 256], replicated, may hold values from 0 to 511, as said below
- top_pivots: int32 [2, 256], replicated, may hold values from 0 to 511, as said below
Outputs:
- leaf_basis: float32 [65536, 256], P(('leaf', 'row'))
- mid_basis: float32 [2048, 256], P(('leaf', 'row'))
- top_basis: float32 [1024, 256], P(('leaf', 'row'))
Inputs may be any that keep to these rules, and one draw needn't show every extreme that they name: Siblings are always near: near_mask[c, 1] is 1 for even c and near_mask[c, 0] is 1 for odd c; the other entry of each row is 0 or 1. `leaf_pivots`: each row holds 256 distinct values, among them 0 and 8191. `mid_pivots`: each row holds 256 distinct values, among them 0 and 511. `top_pivots`: each row holds 256 distinct values, among them 0 and 511.
All inputs are finite; a program needn't handle non-finite values.
Results may differ from a plain program's by a relative error of at most 0.0003.
Values sent between devices are 32-bit elements; how exact they have to be, the bound alone decides.
No kernel may reach another device: no remote copies, remote signals or barrier semaphores. Data moves between devices by JAX's collectives and lax.ppermute only.
A program may use at most 256 MiB of HBM per device.

v0:
```python
import jax
import jax.numpy as jnp
from jax import lax
from jax.sharding import PartitionSpec as P

DIM = 64
RANK = 256


HIGHEST = lax.Precision.HIGHEST


def partner_2(value, axis, stride):
    mask = 2**stride
    pairs = [(source, source ^ mask) for source in range(lax.axis_size(axis))]
    return lax.ppermute(value, axis, pairs)


def from_behind(block, axis, distance):
    devices = range(lax.axis_size(axis))
    route = [(i - distance, i) for i in devices if i - distance in devices]
    return lax.ppermute(block, axis, route)


def kernel(source, target):
    source_sq = jnp.sum(source * source, axis=1)
    target_sq = jnp.sum(target * target, axis=1)
    inner_prod = jnp.dot(source, target.T, precision=HIGHEST)
    return jnp.exp(-(source_sq[:, None] + target_sq[None, :] - 2.0 * inner_prod) / DIM)


def contract_rows(first_mat, second_mat):
    return lax.dot_general(first_mat, second_mat, (((0,), (0,)), ((), ())), precision=HIGHEST)


def solve_coeffs(picked):
    gram_matrix = jnp.dot(picked, picked.T, precision=HIGHEST)
    ridge_shift = jnp.trace(gram_matrix) / RANK + 1e-06
    gram_matrix = gram_matrix + ridge_shift * jnp.eye(RANK, dtype=jnp.float32)
    factor = jnp.linalg.cholesky(gram_matrix)
    return jax.scipy.linalg.cho_solve((factor, True), picked)


def combine(first_node, second_node, pivots):
    coupling = kernel(first_node[0], second_node[0])
    upper_half = first_node[1] - jnp.dot(coupling, second_node[2], precision=HIGHEST)
    lower_half = second_node[1] - contract_rows(coupling, first_node[2])
    stacked = jnp.concatenate([upper_half, lower_half], axis=0)
    skel_stack = jnp.concatenate([first_node[0], second_node[0]], axis=0)
    proj_stack = jnp.concatenate([first_node[2], second_node[2]], axis=0)
    picked = jnp.take(stacked, pivots, axis=0)
    coeffs = solve_coeffs(picked)
    basis_rows = jnp.dot(stacked, coeffs.T, precision=HIGHEST)
    projection = jnp.dot(coeffs, contract_rows(stacked, proj_stack), precision=HIGHEST)
    return (basis_rows, (jnp.take(skel_stack, pivots, axis=0), picked, projection))


def merge_level(tree_node, pivot_table, level_bit, leaf_index):
    partner = partner_2((tree_node[0], tree_node[1], tree_node[2]), "leaf", level_bit)
    is_lower = leaf_index >> level_bit & 1 == 0
    first_node = tuple(
        (
            jnp.where(is_lower, own_part, peer_part)
            for own_part, peer_part in zip(tree_node, partner)
        )
    )
    second_node = tuple(
        (
            jnp.where(is_lower, peer_part, own_part)
            for own_part, peer_part in zip(tree_node, partner)
        )
    )
    pivot_row = lax.dynamic_index_in_dim(
        pivot_table, leaf_index >> level_bit + 1, 0, keepdims=False
    )
    return combine(first_node, second_node, pivot_row)


def body(points, samples, test_matrix, near_mask, leaf_pivots, mid_pivots, top_pivots):
    local_rows = points.shape[0]
    leaf_index = lax.axis_index("leaf")
    row_index = lax.axis_index("row")
    row_count = lax.axis_size("row")
    weight_before = near_mask[0, 0].astype(jnp.float32)
    weight_after = near_mask[0, 1].astype(jnp.float32)

    def tile_fold(shard_piece):
        return jnp.dot(kernel(points, shard_piece[0]), shard_piece[1], precision=HIGHEST)

    before_pts, before_test = from_behind((points, test_matrix), "leaf", 1)
    after_pts, after_test = from_behind((points, test_matrix), "leaf", -1)

    def near_tile(tile_pts, tile_test):
        return tile_fold(
            (
                lax.all_gather(tile_pts, "row", axis=0, tiled=True),
                lax.all_gather(tile_test, "row", axis=0, tiled=True),
            )
        )

    near_field = near_tile(points, test_matrix)
    near_field = near_field + weight_before * near_tile(before_pts, before_test)
    near_field = near_field + weight_after * near_tile(after_pts, after_test)
    residual = samples - near_field
    pivots = leaf_pivots[0]
    positions = row_index * local_rows + jnp.arange(local_rows, dtype=jnp.int32)
    selector = (pivots[:, None] == positions[None, :]).astype(jnp.float32)
    picked, skeleton, moments = lax.psum(
        (
            jnp.dot(selector, residual, precision=HIGHEST),
            jnp.dot(selector, points, precision=HIGHEST),
            contract_rows(residual, test_matrix),
        ),
        "row",
    )
    coeffs = solve_coeffs(picked)
    leaf_basis = jnp.dot(residual, coeffs.T, precision=HIGHEST)
    projection = jnp.dot(coeffs, moments, precision=HIGHEST)
    tree_node = (skeleton, picked, projection)
    mid_full, tree_node = merge_level(tree_node, mid_pivots, 0, leaf_index)
    top_full, tree_node = merge_level(tree_node, top_pivots, 1, leaf_index)
    mid_share = RANK // row_count
    top_share = RANK // (2 * row_count)
    mid_start = (leaf_index & 1) * RANK + row_index * mid_share
    mid_basis = lax.dynamic_slice_in_dim(mid_full, mid_start, mid_share, 0)
    top_start = (
        (leaf_index >> 1 & 1) * RANK + (leaf_index & 1) * (RANK // 2) + row_index * top_share
    )
    top_basis = lax.dynamic_slice_in_dim(top_full, top_start, top_share, 0)
    return (leaf_basis, mid_basis, top_basis)


def solution(mesh):
    return jax.shard_map(
        body,
        mesh=mesh,
        in_specs=(
            P(("leaf", "row"), None),
            P(("leaf", "row"), None),
            P(("leaf", "row"), None),
            P("leaf", None),
            P("leaf", None),
            P(),
            P(),
        ),
        out_specs=(P(("leaf", "row"), None), P(("leaf", "row"), None), P(("leaf", "row"), None)),
        check_vma=False,
    )
```

profile of v0, /device:TPU:1, one launch (start us, length us, event | category | flops | bytes accessed | tf_op | source)
XLA Modules:
  0.0 860.8 jit_solution(8180343994644696453)
XLA Ops:
  8.0 4.9 collective-permute-start
  12.9 2.2 collective-permute-done
  15.9 1.9 collective-permute-start.2
  17.8 5.2 collective-permute-done.2
  24.3 1.9 collective-permute-start.1
  26.2 12.0 %collective-permute-done.1 = f32[512,512]{1,0:T(8,128)S(1)} collective-permute-done((f32[512,512]{1,0:T(8,128)}, f32[512,512]{1,0:T(8,128)S(1)}, u32[]{:S(2)}, u32[]{:S(2)}) %collective-permute-start.1) | collective-permute-done | bytes 1048608 | tf_op jit(solution)/shard_map/ppermute | solution.py:22
  39.3 1.9 collective-permute-start.3
  41.2 15.4 %collective-permute-done.3 = f32[512,512]{1,0:T(8,128)S(1)} collective-permute-done((f32[512,512]{1,0:T(8,128)}, f32[512,512]{1,0:T(8,128)S(1)}, u32[]{:S(2)}, u32[]{:S(2)}) %collective-permute-start.3) | collective-permute-done | bytes 1048608 | tf_op jit(solution)/shard_map/ppermute | solution.py:22
  61.3 2.0 fusion.52
  63.3 1.8 multiply_reduce_fusion.2
  65.1 17.0 %fusion.145 = f32[512,8192]{1,0:T(8,128)} fusion(f32[512,64]{0,1:T(8,128)} %param.12, f32[8192,64]{0,1:T(8,128)} %all-gather.7.cloned.1.call-done), kind=kOutput, calls=%fused_computation.236 | convolution fusion | flops 3221225472 | bytes 19005440 | tf_op jit(solution)/shard_map/dot_general | solution.py:28
  82.0 22.4 %all-gather.11.cloned.1.call-done = f32[8192,64]{0,1:T(8,128)} async-done(((f32[512,64]{0,1:T(8,128)}), f32[8192,64]{0,1:T(8,128)}) %all-gather.11.cloned.1.call-update) | async-done | bytes 2097168 | tf_op jit(solution)/shard_map/all_gather | solution.py:96
  104.4 1.8 multiply_reduce_fusion.1
  106.2 44.6 %all-gather.15.cloned.1.call-done = f32[8192,64]{0,1:T(8,128)} async-done(((f32[512,64]{0,1:T(8,128)}), f32[8192,64]{0,1:T(8,128)}) %all-gather.15.cloned.1.call-update) | async-done | bytes 2097168 | tf_op jit(solution)/shard_map/all_gather | solution.py:96
  150.8 1.9 multiply_reduce_fusion
  152.8 17.0 %fusion.146 = f32[512,8192]{1,0:T(8,128)} fusion(f32[512,64]{0,1:T(8,128)S(1)} %copy-done.3, f32[8192,64]{0,1:T(8,128)} %all-gather.11.cloned.1.call-done), kind=kOutput, calls=%fused_computation.237 | convolution fusion | flops 3221225472 | bytes 19005440 | tf_op jit(solution)/shard_map/dot_general | solution.py:28
  169.8 15.8 %fusion.147 = f32[512,8192]{1,0:T(8,128)} fusion(f32[512,64]{0,1:T(8,128)S(1)} %copy-done.3, f32[8192,64]{0,1:T(8,128)S(1)} %copy-done.2), kind=kOutput, calls=%fused_computation.238 | convolution fusion | flops 3221225472 | bytes 19005440 | tf_op jit(solution)/shard_map/dot_general | solution.py:28
  185.6 78.7 %all-gather.9.cloned.1.call-done = f32[8192,512]{1,0:T(8,128)} async-done(((f32[512,512]{1,0:T(8,128)}), f32[8192,512]{1,0:T(8,128)}) %all-gather.9.cloned.1.call-update) | async-done | bytes 16777232 | tf_op jit(solution)/shard_map/all_gather | solution.py:97
  264.2 34.5 %fusion.14 = f32[512,512]{1,0:T(8,128)} fusion(f32[8192,512]{1,0:T(8,128)} %all-gather.9.cloned.1.call-done, f32[512,8192]{1,0:T(8,128)} %fusion.145, f32[8192]{0:T(1024)S(1)} %multiply_reduce_fusion.2, f32[512]{0:T(512)S(1)} %multiply_reduce_fusion.5), kind=kOutput, calls=%fused_computation.23 | convolution fusion | flops 25790775296 | bytes 34637824 | tf_op jit(solution)/shard_map/dot_general | solution.py:88
  298.8 78.4 %all-gather.13.cloned.1.call-done = f32[8192,512]{1,0:T(8,128)} async-done(((f32[512,512]{1,0:T(8,128)}), f32[8192,512]{1,0:T(8,128)}) %all-gather.13.cloned.1.call-update) | async-done | bytes 16777232 | tf_op jit(solution)/shard_map/all_gather | solution.py:97
  377.2 34.1 %fusion.45 = f32[512,512]{1,0:T(8,128)S(1)} fusion(f32[512,512]{1,0:T(8,128)} %fusion.14, f32[8192,512]{1,0:T(8,128)} %all-gather.13.cloned.1.call-done, f32[512,8192]{1,0:T(8,128)} %fusion.146, f32[8192]{0:T(1024)S(1)} %multiply_reduce_fusion.1, f32[512]{0:T(512)S(1)} %multiply_reduce_fusion.5, f32[]{:T(128)} %bitcast), kind=kOutput, calls=%fused_computation.49 | convolution fusion | flops 25791299584 | bytes 35686404 | tf_op jit(solution)/shard_map/dot_general | solution.py:88
  411.3 78.8 %all-gather.17.cloned.1.call-done = f32[8192,512]{1,0:T(8,128)} async-done(((f32[512,512]{1,0:T(8,128)}), f32[8192,512]{1,0:T(8,128)}) %all-gather.17.cloned.1.call-update) | async-done | bytes 16777232 | tf_op jit(solution)/shard_map/all_gather | solution.py:97
  490.1 34.0 %fusion.42 = f32[512,512]{1,0:T(8,128)S(1)} fusion(f32[512,512]{1,0:T(8,128)S(1)} %copy-done.12, f32[512,512]{1,0:T(8,128)S(1)} %fusion.45, f32[8192,512]{1,0:T(8,128)} %all-gather.17.cloned.1.call-done, f32[512,8192]{1,0:T(8,128)} %fusion.147, f32[8192]{0:T(1024)S(1)} %multiply_reduce_fusion, f32[512]{0:T(512)S(1)} %multiply_reduce_fusion.5, f32[]{:T(128)} %bitcast.1), kind=kOutput, calls=%fused_computation.48 | convolution fusion | flops 25791561728 | bytes 36734980 | tf_op jit(solution)/shard_map/dot_general | solution.py:88
  525.7 2.9 fusion.148
  531.2 84.4 %all-reduce.4.cloned.1.call-done = (f32[256,512]{1,0:T(8,128)}, f32[512,512]{1,0:T(8,128)}, f32[256,64]{0,1:T(8,128)}) async-done(((f32[256,512]{1,0:T(8,128)}, f32[512,512]{1,0:T(8,128)}, f32[256,64]{0,1:T(8,128)}), (f32[256,512]{1,0:T(8,128)}, f32[512,512]{1,0:T(8,128)}, f32[256,64]{0,1:T(8,128)})) %all-reduce.4.cloned.1.call-update) | async-done | bytes 1638416 | tf_op jit(solution)/shard_map/psum | solution.py:108
  615.6 2.5 select_reduce_fusion.2
  618.1 2.2 collective-permute-start.4
  621.6 11.7 %cholesky.172 = f32[128,128]{1,0:T(8,128)S(1)} custom-call(f32[128,128]{1,0:T(8,128)S(1)} %cholesky.270), custom_call_target="Cholesky" | custom-call | tf_op jit(solution)/shard_map/jit(cholesky)/cholesky | solution.py:40
  633.3 9.8 %custom-call.17 = f32[1,128,128]{1,2,0:T(8,128)S(1)} custom-call(f32[1,128,128]{2,1,0:T(8,128)S(1)} %get-tuple-element.85), custom_call_target="InvertDiagBlocksLowerTriangular" | custom-call | tf_op jit(solution)/shard_map/jit(cholesky)/cholesky | solution.py:40
  643.6 11.7 %cholesky.189 = f32[128,128]{1,0:T(8,128)S(1)} custom-call(f32[128,128]{1,0:T(8,128)S(1)} %convolution_subtract_fusion.8), custom_call_target="Cholesky" | custom-call | tf_op jit(solution)/shard_map/jit(cholesky)/cholesky | solution.py:40
  657.5 4.2 while.6
  661.6 19.7 %custom-call.18 = f32[2,128,128]{1,2,0:T(8,128)S(1)} custom-call(f32[2,128,128]{2,1,0:T(8,128)S(1)} %get-tuple-element.26), custom_call_target="InvertDiagBlocksLowerTriangular" | custom-call | tf_op jit(solution)/shard_map/jit(_cho_solve)/triangular_solve | solution.py:41
  685.6 1.8 fusion.67
  687.5 2.3 fusion.66
  695.6 2.9 fusion.48
  702.5 11.7 %cholesky.206 = f32[128,128]{1,0:T(8,128)S(1)} custom-call(f32[128,128]{1,0:T(8,128)S(1)} %cholesky.273), custom_call_target="Cholesky" | custom-call | tf_op jit(solution)/shard_map/jit(cholesky)/cholesky | solution.py:40
  714.2 9.8 %custom-call.19 = f32[1,128,128]{1,2,0:T(8,128)S(1)} custom-call(f32[1,128,128]{2,1,0:T(8,128)S(1)} %get-tuple-element.81), custom_call_target="InvertDiagBlocksLowerTriangular" | custom-call | tf_op jit(solution)/shard_map/jit(cholesky)/cholesky | solution.py:40
  724.5 11.7 %cholesky.223 = f32[128,128]{1,0:T(8,128)S(1)} custom-call(f32[128,128]{1,0:T(8,128)S(1)} %convolution_subtract_fusion.7), custom_call_target="Cholesky" | custom-call | tf_op jit(solution)/shard_map/jit(cholesky)/cholesky | solution.py:40
  738.9 5.3 while.7
  744.2 19.7 %custom-call.20 = f32[2,128,128]{1,2,0:T(8,128)S(1)} custom-call(f32[2,128,128]{2,1,0:T(8,128)S(1)} %get-tuple-element.27), custom_call_target="InvertDiagBlocksLowerTriangular" | custom-call | tf_op jit(solution)/shard_map/jit(_cho_solve)/triangular_solve | solution.py:41
  769.0 2.3 fusion.64
  771.3 1.5 collective-permute-start.9
  775.1 9.3 %collective-permute-done.9 = f32[256,512]{1,0:T(8,128)S(1)} collective-permute-done((f32[256,512]{1,0:T(8,128)S(1)}, f32[256,512]{1,0:T(8,128)S(1)}, u32[]{:S(2)}, u32[]{:S(2)}) %collective-permute-start.9) | collective-permute-done | bytes 524320 | tf_op jit(solution)/shard_map/ppermute | solution.py:16
  789.3 11.7 %cholesky.240 = f32[128,128]{1,0:T(8,128)S(1)} custom-call(f32[128,128]{1,0:T(8,128)S(1)} %cholesky.276), custom_call_target="Cholesky" | custom-call | tf_op jit(solution)/shard_map/jit(cholesky)/cholesky | solution.py:40
  801.1 9.8 %custom-call.21 = f32[1,128,128]{1,2,0:T(8,128)S(1)} custom-call(f32[1,128,128]{2,1,0:T(8,128)S(1)} %get-tuple-element.77), custom_call_target="InvertDiagBlocksLowerTriangular" | custom-call | tf_op jit(solution)/shard_map/jit(cholesky)/cholesky | solution.py:40
  811.4 11.9 %cholesky.257 = f32[128,128]{1,0:T(8,128)S(1)} custom-call(f32[128,128]{1,0:T(8,128)S(1)} %convolution_subtract_fusion.6), custom_call_target="Cholesky" | custom-call | tf_op jit(solution)/shard_map/jit(cholesky)/cholesky | solution.py:40
  826.0 4.0 while.8
  830.0 19.7 %custom-call.22 = f32[2,128,128]{1,2,0:T(8,128)S(1)} custom-call(f32[2,128,128]{2,1,0:T(8,128)S(1)} %get-tuple-element.28), custom_call_target="InvertDiagBlocksLowerTriangular" | custom-call | tf_op jit(solution)/shard_map/jit(_cho_solve)/triangular_solve | solution.py:41
  (167 shorter events, 58.7 us)
Async XLA Ops:
  7.2 521.5 %copy-start = (s32[2,256]{1,0:T(2,128)S(1)}, s32[2,256]{1,0:T(2,128)}, u32[]{:S(2)}) copy-start(s32[2,256]{1,0:T(2,128)} %param.18) | copy-start | bytes 6148
  7.2 145.6 %copy-start.3 = (f32[512,64]{0,1:T(8,128)S(1)}, f32[512,64]{0,1:T(8,128)}, u32[]{:S(2)}) copy-start(f32[512,64]{0,1:T(8,128)} %param.12) | copy-start | bytes 393220
  7.2 56.1 %all-gather.7.cloned.1.call-start = ((), (), s32[]{:S(2)}) async-start(), calls=%async_computation | async-start | bytes 2228224 | tf_op jit(solution)/shard_map/all_gather | solution.py:96
  7.9 96.5 %all-gather.11.cloned.1.call-start = ((), (), s32[]{:S(2)}) async-start(), calls=%async_computation.2 | async-start | bytes 2228224 | tf_op jit(solution)/shard_map/all_gather | solution.py:96
  8.0 7.2 collective-permute-start
  15.2 0.7 copy-start.8
  15.8 135.0 %all-gather.15.cloned.1.call-start = ((), (), s32[]{:S(2)}) async-start(), calls=%async_computation.4 | async-start | bytes 2228224 | tf_op jit(solution)/shard_map/all_gather | solution.py:96
  15.9 7.1 collective-permute-start.2
  23.0 0.6 copy-start.9
  23.7 240.6 %all-gather.9.cloned.1.call-start = ((), (), s32[]{:S(2)}) async-start(), calls=%async_computation.1 | async-start | bytes 17825792 | tf_op jit(solution)/shard_map/all_gather | solution.py:97
  24.2 352.9 %all-gather.13.cloned.1.call-start = ((), (), s32[]{:S(2)}) async-start(), calls=%async_computation.3 | async-start | bytes 17825792 | tf_op jit(solution)/shard_map/all_gather | solution.py:97
  24.3 14.0 %collective-permute-start.1 = (f32[512,512]{1,0:T(8,128)}, f32[512,512]{1,0:T(8,128)S(1)}, u32[]{:S(2)}, u32[]{:S(2)}) collective-permute-start(f32[512,512]{1,0:T(8,128)} %param.14), channel_id=1, source_target_pairs={{0,16},{16,32},{32,48},{48,64},{64,80},{80,96},{96,112},{1,17},{17... | collective-permute-start | bytes 3145736 | tf_op jit(solution)/shard_map/ppermute | solution.py:22
  38.3 1.0 copy-start.5
  39.2 450.9 %all-gather.17.cloned.1.call-start = ((), (), s32[]{:S(2)}) async-start(), calls=%async_computation.5 | async-start | bytes 17825792 | tf_op jit(solution)/shard_map/all_gather | solution.py:97
  39.3 17.4 %collective-permute-start.3 = (f32[512,512]{1,0:T(8,128)}, f32[512,512]{1,0:T(8,128)S(1)}, u32[]{:S(2)}, u32[]{:S(2)}) collective-permute-start(f32[512,512]{1,0:T(8,128)} %param.14), channel_id=1, source_target_pairs={{16,0},{32,16},{48,32},{64,48},{80,64},{96,80},{112,96},{17,1},{33... | collective-permute-start | bytes 3145736 | tf_op jit(solution)/shard_map/ppermute | solution.py:22
  56.7 1.0 copy-start.6
  57.7 558.0 %all-reduce.4.cloned.1.call-start = ((), (), s32[]{:S(2)}) async-start(), calls=%async_computation.6 | async-start | bytes 3276800 | tf_op jit(solution)/shard_map/psum | solution.py:108
  150.8 18.9 %copy-start.2 = (f32[8192,64]{0,1:T(8,128)S(1)}, f32[8192,64]{0,1:T(8,128)}, u32[]{:S(2)}) copy-start(f32[8192,64]{0,1:T(8,128)} %all-gather.15.cloned.1.call-done) | copy-start | bytes 6291460
  377.2 112.9 %copy-start.12 = (f32[512,512]{1,0:T(8,128)S(1)}, f32[512,512]{1,0:T(8,128)}, u32[]{:S(2)}) copy-start(f32[512,512]{1,0:T(8,128)} %param.13) | copy-start | bytes 3145732
  490.1 34.1 %copy-start.10 = (s32[1,256]{1,0:T(1,128)S(1)}, s32[1,256]{1,0:T(1,128)}, u32[]{:S(2)}) copy-start(s32[1,256]{1,0:T(1,128)} %param.16) | copy-start | bytes 3076
  490.1 35.6 %copy-start.4 = (f32[512,512]{1,0:T(8,128)S(1)}, f32[512,512]{1,0:T(8,128)}, u32[]{:S(2)}) copy-start(f32[512,512]{1,0:T(8,128)} %param.14) | copy-start | bytes 3145732
  615.6 78.5 %copy-start.1 = (f32[256,512]{1,0:T(8,128)S(1)}, f32[256,512]{1,0:T(8,128)}, u32[]{:S(2)}) copy-start(f32[256,512]{1,0:T(8,128)} %get-tuple-element.55) | copy-start | bytes 1572868
  618.1 76.0 %collective-permute-start.4 = (f32[256,512]{1,0:T(8,128)}, f32[256,512]{1,0:T(8,128)S(1)}, u32[]{:S(2)}, u32[]{:S(2)}) collective-permute-start(f32[256,512]{1,0:T(8,128)} %get-tuple-element.55), channel_id=1, source_target_pairs={{0,16},{16,0},{32,48},{48,32},{64,80},{80,64},{96,112},{112,96},{1... | collective-permute-start | bytes 1572872 | tf_op jit(solution)/shard_map/ppermute | solution.py:16
  620.3 70.0 %collective-permute-start.5 = (f32[256,64]{0,1:T(8,128)}, f32[256,64]{0,1:T(8,128)S(1)}, u32[]{:S(2)}, u32[]{:S(2)}) collective-permute-start(f32[256,64]{0,1:T(8,128)} %get-tuple-element.57), channel_id=1, source_target_pairs={{0,16},{16,0},{32,48},{48,32},{64,80},{80,64},{96,112},{112,96},{1... | collective-permute-start | bytes 196616 | tf_op jit(solution)/shard_map/ppermute | solution.py:16
  661.6 30.5 %copy-start.13 = (s32[2,2]{1,0:T(2,128)}, s32[2,2]{1,0:T(2,128)S(1)}, u32[]{:S(2)}) copy-start(s32[2,2]{1,0:T(2,128)S(1)} %get-tuple-element.297) | copy-start | bytes 52
  689.7 4.2 collective-permute-start.6
  692.2 80.6 %collective-permute-start.8 = (f32[256,64]{1,0:T(8,128)S(1)}, f32[256,64]{1,0:T(8,128)S(1)}, u32[]{:S(2)}, u32[]{:S(2)}) collective-permute-start(f32[256,64]{1,0:T(8,128)S(1)} %broadcast_select_fusion.4), channel_id=1, source_target_pairs={{0,32},{16,48},{32,0},{48,16},{64,96},{80,112},{96,64},{112,80},{1... | collective-permute-start | bytes 196616 | tf_op jit(solution)/shard_map/ppermute | solution.py:16
  698.5 88.5 %copy-start.11 = (pred[256]{0:T(512)(128)(4,1)S(1)}, pred[256]{0:T(512)(128)(4,1)}, u32[]{:S(2)}) copy-start(pred[256]{0:T(512)(128)(4,1)} %get-tuple-element.100) | copy-start | bytes 772
  701.0 83.4 %collective-permute-start.7 = (f32[256,512]{1,0:T(8,128)S(1)}, f32[256,512]{1,0:T(8,128)S(1)}, u32[]{:S(2)}, u32[]{:S(2)}) collective-permute-start(f32[256,512]{1,0:T(8,128)S(1)} %broadcast_select_fusion.1), channel_id=1, source_target_pairs={{0,32},{16,48},{32,0},{48,16},{64,96},{80,112},{96,64},{112,80},{1... | collective-permute-start | bytes 1572872 | tf_op jit(solution)/shard_map/ppermute | solution.py:16
  744.2 81.8 %copy-start.14 = (s32[2,2]{1,0:T(2,128)S(1)}, s32[2,2]{1,0:T(2,128)}, u32[]{:S(2)}) copy-start(s32[2,2]{1,0:T(2,128)} %get-tuple-element.298) | copy-start | bytes 52
  763.9 0.6 copy-start.7
  771.3 13.1 %collective-permute-start.9 = (f32[256,512]{1,0:T(8,128)S(1)}, f32[256,512]{1,0:T(8,128)S(1)}, u32[]{:S(2)}, u32[]{:S(2)}) collective-permute-start(f32[256,512]{1,0:T(8,128)S(1)} %fusion.64), channel_id=1, source_target_pairs={{0,32},{16,48},{32,0},{48,16},{64,96},{80,112},{96,64},{112,80},{1... | collective-permute-start | bytes 1572872 | tf_op jit(solution)/shard_map/ppermute | solution.py:16
Sparse Core Ops, SparseCore 0:
  10.2 47.1 all-gather.6
  60.2 44.1 all-gather.10
  106.6 44.1 all-gather.14
  152.8 111.3 all-gather.8
  266.2 110.8 all-gather.12
  379.2 110.8 all-gather.16
  528.8 86.7 all-reduce.3
where the time goes:
time: 870 us; the launch traced here: 861 us
  waiting for transfers between devices  433 us (50%)
  matrix products  192 us (22%)
  other arithmetic  173 us (20%)
  local copies, waits for them, and re-layouts  22.7 us (3%)
  between operations  22.3 us (3%)
  starting transfers between devices  17.6 us (2%)
    all_gather x3, waiting for transfers between devices, near_tile(): lax.all_gather(tile_test, 'row', axis=0, tiled=True)  236 us
    another operation x20, other arithmetic, solve_coeffs(): factor = jnp.linalg.cholesky(gram_matrix)  103 us
    dot_general x3, matrix products, tile_fold(): jnp.dot(kernel(points, shard_piece[0]), shard_piece[1], precision=HIGHEST)  103 us
    psum x1, waiting for transfers between devices, body(): lax.psum((jnp.dot(selector, residual, precision=HIGHEST), jnp.dot(selecto...  84.4 us
    all_gather x3, waiting for transfers between devices, near_tile(): lax.all_gather(tile_pts, 'row', axis=0, tiled=True)  67 us
    another operation x7, other arithmetic, solve_coeffs(): return jax.scipy.linalg.cho_solve((factor, True), picked)  59.1 us
    dot_general x5, matrix products, kernel(): inner_prod = jnp.dot(source, target.T, precision=HIGHEST)  50.6 us
    ppermute x4, waiting for transfers between devices, from_behind(): return lax.ppermute(block, axis, route)  34.9 us
  transfers between devices with their start and end apart: 17, of which 11 were waited for; matrix products, arithmetic and copies ran while one was open for 32% of the time, Pallas kernels for 0%

commit v1 on v0

v1 whole, which is shorter than its diff:
```python
import functools
import math

import jax
import jax.numpy as jnp
from jax import lax
from jax.experimental import pallas as pl
from jax.experimental.pallas import tpu as pltpu
from jax.sharding import PartitionSpec as P

DIM = 64
RANK = 256
SAMP = 512
BLK = 512
HALF = SAMP // 2
SIDE = 4
SCALE = math.log2(math.e) / DIM
HIGHEST = lax.Precision.HIGHEST
F32, BF16 = jnp.float32, jnp.bfloat16
VMEM = pltpu.VMEM


def along_x(k):
    return [(4 * x + y, 4 * ((x + k) % 4) + y) for x in range(4) for y in range(4)]


def along_y(k):
    return [(4 * x + y, 4 * x + (y + k) % 4) for x in range(4) for y in range(4)]


SIBLING = [(i, i ^ 1) for i in range(8)]
OUTER = [(1, 2), (2, 1), (3, 4), (4, 3), (5, 6), (6, 5)]
COUSIN = [(i, i ^ 2) for i in range(8)]


NN = (((1,), (0,)), ((), ()))
NT = (((1,), (1,)), ((), ()))


def mm(a, b, dims=NN):
    return lax.dot_general(a, b, dims, preferred_element_type=F32)


def split2(a):
    hi = a.astype(BF16)
    return hi, (a - hi.astype(F32)).astype(BF16)


def split3(a):
    hi = a.astype(BF16)
    rest = a - hi.astype(F32)
    mid = rest.astype(BF16)
    return hi, mid, (rest - mid.astype(F32)).astype(BF16)


def dot3(a, b, dims=NN):
    ah, al = split2(a)
    bh, bl = split2(b)
    return mm(ah, bh, dims) + (mm(ah, bl, dims) + mm(al, bh, dims))


def dot6(a, b, dims=NN):
    ah, am, al = split3(a)
    bh, bm, bl = split3(b)
    return mm(ah, bh, dims) + (
        (mm(ah, bm, dims) + mm(am, bh, dims))
        + (mm(am, bm, dims) + (mm(ah, bl, dims) + mm(al, bh, dims)))
    )


def pick(one_hot, a):
    h, m, l = split3(a)
    return (mm(one_hot, h) + mm(one_hot, m)) + mm(one_hot, l)


SHIFTS = (1, 3, 2)
LINE_X = (0, 1, 2, 3)
LINE_Y = (0, 4, 5, 6)
BLOCKS = 2 * SIDE - 1


def norm_rows(xt, first):
    rows = lax.broadcasted_iota(jnp.int32, (DIM, BLK), 0)
    sq = jnp.sum(xt * xt, axis=0, keepdims=True) * (-SCALE)
    h, m, l = (v.astype(F32) for v in split3(sq))
    one = jnp.ones_like(sq)
    aux = jnp.zeros((DIM, BLK), F32)
    for n, part in enumerate((h, m, l, one, one, one) if first else (one, one, one, h, m, l)):
        aux = jnp.where(rows == n, part, aux)
    return aux


def feature_kernel(points_ref, feat_ref):
    for i in range(BLOCKS):
        xt = points_ref[i * DIM:(i + 1) * DIM, :]
        scaled = xt * (2.0 * SCALE)
        hi = scaled.astype(BF16).astype(F32)
        feat = jnp.concatenate([hi, hi, scaled - hi, norm_rows(xt, True)], axis=0)
        feat_ref[i] = feat.T.astype(BF16)


def features(points_all):
    return pl.pallas_call(
        feature_kernel,
        out_shape=jax.ShapeDtypeStruct((BLOCKS, BLK, 4 * DIM), BF16),
        in_specs=[pl.BlockSpec(memory_space=VMEM)],
        out_specs=pl.BlockSpec(memory_space=VMEM),
        compiler_params=pltpu.CompilerParams(vmem_limit_bytes=32 * 2**20),
        cost_estimate=pl.CostEstimate(flops=10**9, bytes_accessed=3 * 2**20, transcendentals=0),
        name="features",
    )(points_all)


def near_kernel(plan, n_points, n_tests, weight_ref, feat_ref, *refs):
    refs = list(refs)
    points = [refs.pop(0) for _ in range(n_points)]
    tests = [refs.pop(0) for _ in range(n_tests)]
    before = [[refs.pop(0) for _ in g[0]] if g[2] else None for g in plan]
    outs = [[refs.pop(0) for _ in g[0]] for g in plan]
    buf_a, buf_b, *scratch = refs
    for n, (targets, sources, chained) in enumerate(plan):
        feat_t, feat_s, split_t, acc = scratch[4 * n:4 * n + 4]
        for i, target in enumerate(targets):
            feat_t[i] = feat_ref[target]
            acc[i] = before[n][i][...] if chained else jnp.zeros((BLK, HALF), F32)
        for b, (array, block, weighted, where, part, half) in enumerate(sources):
            xt = points[array][block * DIM:(block + 1) * DIM, :]
            hi, lo = split2(xt)
            feat_s[b, 0:DIM, :] = hi
            feat_s[b, DIM:2 * DIM, :] = lo
            feat_s[b, 2 * DIM:3 * DIM, :] = hi
            feat_s[b, 3 * DIM:, :] = norm_rows(xt, False).astype(BF16)
            test = tests[where][part * BLK:(part + 1) * BLK, half * HALF:(half + 1) * HALF]
            if weighted:
                test = test * weight_ref[0, 0]
            hi, lo = split2(test)
            split_t[b, 0:BLK, :] = hi
            split_t[b, BLK:2 * BLK, :] = hi
            split_t[b, 2 * BLK:, :] = lo
        count = len(sources)
        total = len(targets) * count

        def entries(t, buf):
            k = jnp.exp2(mm(feat_t[t // count], feat_s[t % count]))
            hi = k.astype(BF16)
            buf[:, 0:BLK] = hi
            buf[:, BLK:] = (k - hi.astype(F32)).astype(BF16)

        def fold(t, buf):
            b = t % count
            acc[t // count] += mm(buf[...], split_t[b, 0:2 * BLK, :]) + mm(
                buf[:, 0:BLK], split_t[b, 2 * BLK:, :]
            )

        entries(0, buf_a)

        @pl.loop(0, total // 2)
        def _(u):
            t = 2 * u
            entries(t + 1, buf_b)
            fold(t, buf_a)
            entries(jnp.minimum(t + 2, total - 1), buf_a)
            fold(t + 1, buf_b)

        if total % 2:
            fold(total - 1, buf_a)
        for i in range(len(targets)):
            outs[n][i][...] = acc[i]


def near(name, groups, tests, *, weight, feats, points):
    plan = [(t, src, acc is not None) for t, src, acc in groups]
    args = [weight, feats, *points, *tests]
    for _, _, acc in groups:
        args += acc or []
    n_out = sum(len(g[0]) for g in groups)
    work = sum(len(g[0]) * len(g[1]) for g in groups) * BLK * BLK
    scratch = [VMEM((BLK, 2 * BLK), BF16), VMEM((BLK, 2 * BLK), BF16)]
    for t, src, _ in groups:
        scratch += [
            VMEM((len(t), BLK, 4 * DIM), BF16),
            VMEM((len(src), 4 * DIM, BLK), BF16),
            VMEM((len(src), 3 * BLK, HALF), BF16),
            VMEM((len(t), BLK, HALF), F32),
        ]
    out = pl.pallas_call(
        functools.partial(near_kernel, plan, len(points), len(tests)),
        out_shape=[jax.ShapeDtypeStruct((BLK, HALF), F32)] * n_out,
        in_specs=[pl.BlockSpec(memory_space=pltpu.SMEM)]
        + [pl.BlockSpec(memory_space=VMEM)] * (len(args) - 1),
        out_specs=[pl.BlockSpec(memory_space=VMEM)] * n_out,
        scratch_shapes=scratch,
        compiler_params=pltpu.CompilerParams(vmem_limit_bytes=50 * 2**20),
        cost_estimate=pl.CostEstimate(
            flops=2 * work * (4 * DIM + 3 * HALF),
            bytes_accessed=4 * len(args) * BLK * HALF,
            transcendentals=work,
        ),
        name=name,
    )(*args)
    sums = []
    for t, _, _ in groups:
        sums.append(list(out[:len(t)]))
        out = out[len(t):]
    return sums


EXT = SAMP + 128


def resid_kernel(start_ref, piv_ref, samp_ref, points_ref, *refs):
    part_a, part_b = refs[:SIDE], refs[SIDE:2 * SIDE]
    resid_ref, picked_ref = refs[2 * SIDE:]
    near_a = (part_a[0][...] + part_a[1][...]) + (part_a[2][...] + part_a[3][...])
    near_b = (part_b[0][...] + part_b[1][...]) + (part_b[2][...] + part_b[3][...])
    resid_ref[:, :HALF] = samp_ref[:, :HALF] - near_a
    resid_ref[:, HALF:] = samp_ref[:, HALF:] - near_b
    column = lax.broadcasted_iota(jnp.int32, (RANK, BLK), 1) + start_ref[0, 0]
    one_hot = jnp.where(piv_ref[...] == column, 1.0, 0.0).astype(BF16)
    picked_ref[:, :SAMP] = pick(one_hot, resid_ref[...])
    skel = sum(mm(one_hot, part, NT) for part in split3(points_ref[...]))
    picked_ref[:, SAMP:] = jnp.concatenate([skel, jnp.zeros((RANK, EXT - SAMP - DIM), F32)], axis=1)


def vmem_call(kernel, outs, n_smem, n_vmem, scratch=(), name=None, flops=0):
    return pl.pallas_call(
        kernel,
        out_shape=[jax.ShapeDtypeStruct(s, F32) for s in outs],
        in_specs=[pl.BlockSpec(memory_space=pltpu.SMEM)] * n_smem
        + [pl.BlockSpec(memory_space=VMEM)] * n_vmem,
        out_specs=[pl.BlockSpec(memory_space=VMEM)] * len(outs),
        scratch_shapes=list(scratch),
        compiler_params=pltpu.CompilerParams(vmem_limit_bytes=48 * 2**20),
        cost_estimate=pl.CostEstimate(flops=flops, bytes_accessed=4 * 2**20, transcendentals=0),
        name=name,
    )


SOLVE_SCRATCH = [VMEM((RANK, RANK), F32), VMEM((RANK, RANK), F32)]


def inverse_gram(picked, err_ref, inv_ref):
    gram = dot6(picked, picked, NT)
    eye = (
        lax.broadcasted_iota(jnp.int32, (RANK, RANK), 0)
        == lax.broadcasted_iota(jnp.int32, (RANK, RANK), 1)
    ).astype(F32)
    shift = jnp.sum(gram * eye) / RANK + 1e-06
    gram = gram + shift * eye
    bound = jnp.max(jnp.sum(jnp.abs(gram), axis=0, keepdims=True))
    alpha = 2.0 / (jnp.full((1, 1), 1.0, F32) * (bound + shift))
    err_ref[...] = eye - alpha * gram
    inv_ref[...] = alpha * eye

    def step(state):
        n, _ = state
        err = err_ref[...]
        eh, el = split2(err)
        ih, il = split2(inv_ref[...])
        inv_ref[...] += mm(ih, eh) + (mm(ih, el) + mm(il, eh))
        sq = mm(eh, eh) + (mm(eh, el) + mm(el, eh))
        err_ref[...] = sq
        return n + 1, jnp.sum(sq * sq)

    lax.while_loop(lambda st: (st[0] < 24) & (st[1] > 1e-6), step, (jnp.int32(0), jnp.float32(1e9)))
    for _ in range(2):
        inv = inv_ref[...]
        inv_ref[...] = inv + dot3(inv, eye - dot6(gram, inv))
    return inv_ref[...]


def leaf_kernel(resid_ref, test_ref, picked_ref, basis_ref, proj_ref, err_ref, inv_ref):
    picked = picked_ref[:, :SAMP]
    coeffs = dot3(inverse_gram(picked, err_ref, inv_ref), picked)
    resid = resid_ref[...]
    basis_ref[...] = dot3(resid, coeffs, NT)
    proj_ref[...] = dot3(dot3(coeffs, resid, NT), test_ref[...])


def coupling(a, b):
    def norm3(v):
        return split3(v * v)

    ones = jnp.ones((RANK, DIM), BF16)
    inner = dot6(a, b, NT)
    na = sum(mm(p, ones, NT) for p in norm3(a))
    nb = sum(mm(ones, p, NT) for p in norm3(b))
    return jnp.exp2(-SCALE * (na + nb - 2.0 * inner))


def merge_kernel(top, share, info_ref, piv_ref, *refs):
    if top:
        pick_own, proj_own, first, other, share_ref, stack_ref, err_ref, inv_ref = refs
        core0 = info_ref[0, 2] == 0
        peer_pick = jnp.where(core0, first[...], other[...])
        peer_proj = jnp.where(core0, other[:, :SAMP], first[:, :SAMP])
    else:
        (pick_own, proj_own, pick_peer, proj_peer) = refs[:4]
        (share_ref, picked_ref, proj_ref, send_ref, stack_ref, err_ref, inv_ref) = refs[4:]
        peer_pick, peer_proj = pick_peer[...], proj_peer[...]
    lower = info_ref[0, 0] == 0

    def order(own, peer):
        return jnp.where(lower, own, peer), jnp.where(lower, peer, own)

    pick_a, pick_b = order(pick_own[...], peer_pick)
    proj_a, proj_b = order(proj_own[...], peer_proj)
    skel_a, skel_b = pick_a[:, SAMP:SAMP + DIM], pick_b[:, SAMP:SAMP + DIM]
    stack_ref[0:RANK, :SAMP] = pick_a[:, :SAMP] - dot3(coupling(skel_a, skel_b), proj_b)
    stack_ref[RANK:, :SAMP] = pick_b[:, :SAMP] - dot3(coupling(skel_b, skel_a), proj_a)
    stack_ref[0:RANK, SAMP:] = pick_a[:, SAMP:]
    stack_ref[RANK:, SAMP:] = pick_b[:, SAMP:]
    one_hot = jnp.where(
        piv_ref[...] == lax.broadcasted_iota(jnp.int32, (RANK, 2 * RANK), 1), 1.0, 0.0
    ).astype(BF16)
    picked_all = pick(one_hot, stack_ref[...])
    picked = picked_all[:, :SAMP]
    coeffs = dot3(inverse_gram(picked, err_ref, inv_ref), picked)
    rows = stack_ref[pl.ds(pl.multiple_of(info_ref[0, 1], 8), share), :SAMP]
    share_ref[...] = dot3(rows, coeffs, NT)
    if not top:
        picked_ref[...] = picked_all
        basis_t = dot3(coeffs, stack_ref[:, :SAMP], NT)
        proj = dot3(basis_t[:, :RANK], proj_a) + dot3(basis_t[:, RANK:], proj_b)
        proj_ref[...] = proj
        send_ref[:, :SAMP] = jnp.where(lower, picked, proj)
        send_ref[:, SAMP:] = picked_all[:, SAMP:]


def merge(top, share, info, pivots, *node):
    outs = [(share, RANK)] if top else [(share, RANK), (RANK, EXT), (RANK, SAMP), (RANK, EXT)]
    return vmem_call(
        functools.partial(merge_kernel, top, share),
        outs, 1, 5,
        [VMEM((2 * RANK, EXT), F32), *SOLVE_SCRATCH],
        name="merge_top" if top else "merge_mid",
        flops=3 * 10**9,
    )(info, pivots.reshape(RANK, 1), *node)


def sum_row(part):
    share = part.shape[0] // 16
    parts = lax.all_to_all(part.reshape(16, share, -1), "row", 0, 0)
    mine = jnp.sum(parts, axis=0)
    every = lax.all_to_all(jnp.broadcast_to(mine[None], (16, share, mine.shape[1])), "row", 0, 0)
    return every.reshape(part.shape)


def body(points, samples, test_matrix, near_mask, leaf_pivots, mid_pivots, top_pivots):
    leaf = lax.axis_index("leaf")
    row = lax.axis_index("row")
    core = leaf & 1
    xt = points.T
    x_line = [lax.ppermute(xt, "row", along_x(k)) for k in SHIFTS]
    y_line = [lax.ppermute(xt, "row", along_y(k)) for k in SHIFTS]
    pts = jnp.concatenate([xt, *x_line, *y_line], axis=0)
    pts_sib = lax.ppermute(pts, "leaf", SIBLING)
    pts_out = lax.ppermute(pts, "leaf", OUTER)
    points_all = [pts, pts_sib, pts_out]

    weight = jnp.where(core == 0, near_mask[0, 0], near_mask[0, 1]).astype(F32).reshape(1, 1)
    feats = features(pts)
    run = functools.partial(near, weight=weight, feats=feats, points=points_all)

    test_sib = lax.ppermute(test_matrix, "leaf", SIBLING)
    test_out = lax.ppermute(test_matrix, "leaf", OUTER)
    test_a, test_b = test_matrix[:, :HALF], test_matrix[:, HALF:]
    far = {("a", k): lax.ppermute(test_a, "row", along_x(k)) for k in (2, 1, 3)}
    far.update({("b", k): lax.ppermute(test_b, "row", along_y(k)) for k in (2, 1)})

    part_a, part_b = run("near_local", [
        (LINE_Y, [(n, 0, n == 2, n, 0, 0) for n in range(3)], None),
        (LINE_X, [(n, 0, n == 2, n, 0, 1) for n in range(3)], None),
    ], [test_matrix, test_sib, test_out])

    late, far, part_a, part_b = lax.optimization_barrier((test_b, far, part_a, part_b))
    far["b", 3] = lax.ppermute(late, "row", along_y(3))
    line_a = [jnp.concatenate([far["a", k] for k in SHIFTS], axis=0)]
    line_b = [jnp.concatenate([far["b", k] for k in SHIFTS], axis=0)]
    for line in (line_a, line_b):
        line.append(lax.ppermute(line[0], "leaf", SIBLING))
        line.append(lax.ppermute(line[0], "leaf", OUTER))

    def sources(line, arrays, first=0):
        return [(n, line[p + 1], n == 2, first + n - arrays[0], p, 0) for n in arrays for p in range(3)]

    (far_a,) = run("near_a", [(LINE_Y[1:], sources(LINE_X, (0, 1)), part_a[1:])], line_a[:2])
    (far_b,) = run("near_b", [(LINE_X[1:], sources(LINE_Y, (0, 1)), part_b[1:])], line_b[:2])
    (far_a,) = run("near_outer_a", [(LINE_Y[1:], sources(LINE_X, (2,)), far_a)], line_a[2:])
    got_a = [lax.ppermute(v, "row", along_y(-k)) for v, k in zip(far_a, SHIFTS)]
    (far_b,) = run("near_outer_b", [(LINE_X[1:], sources(LINE_Y, (2,)), far_b)], line_b[2:])
    got_b = [lax.ppermute(v, "row", along_x(-k)) for v, k in zip(far_b, SHIFTS)]
    own_a, own_b = run("near_own", [
        ((0,), sources(LINE_X, (0, 1, 2)), part_a[:1]),
        ((0,), sources(LINE_Y, (0, 1, 2), 3), part_b[:1]),
    ], line_a + line_b)

    pivots = leaf_pivots[0]
    resid, picked = vmem_call(
        resid_kernel, [(BLK, SAMP), (RANK, EXT)], 1, 3 + 2 * SIDE, name="residual", flops=10**9
    )((row * BLK).reshape(1, 1), pivots.reshape(RANK, 1), samples, xt, *own_a, *got_a, *own_b, *got_b)
    picked = sum_row(picked)
    picked_sib = lax.ppermute(picked, "leaf", SIBLING)
    leaf_basis, proj = vmem_call(
        leaf_kernel, [(BLK, RANK), (RANK, SAMP)], 0, 3, SOLVE_SCRATCH, name="leaf", flops=3 * 10**9
    )(resid, test_matrix, picked)
    proj = sum_row(proj)
    proj_sib = lax.ppermute(proj, "leaf", SIBLING)

    def info(lower, first):
        return jnp.stack([lower, first, core]).astype(jnp.int32).reshape(1, 3)

    mid_row = lax.dynamic_index_in_dim(mid_pivots, leaf >> 1, 0, keepdims=False)
    top_row = lax.dynamic_index_in_dim(top_pivots, leaf >> 2, 0, keepdims=False)
    mid_share, top_share = RANK // 16, RANK // 32
    mid_basis, picked, proj, send = merge(
        False, mid_share, info(core, core * RANK + row * mid_share), mid_row,
        picked, proj, picked_sib, proj_sib,
    )
    first = lax.ppermute(send, "leaf", COUSIN)
    other = lax.ppermute(first, "leaf", SIBLING)
    second = leaf >> 1 & 1
    (top_basis,) = merge(
        True, top_share, info(second, second * RANK + core * (RANK // 2) + row * top_share), top_row,
        picked, proj, first, other,
    )
    return (leaf_basis, mid_basis, top_basis)


def solution(mesh):
    split = P(("leaf", "row"), None)
    return jax.shard_map(
        body,
        mesh=mesh,
        in_specs=(split, split, split, P("leaf", None), P("leaf", None), P(), P()),
        out_specs=(split, split, split),
        check_vma=False,
    )
```

time: 870 us -> 320 us (0.37)
  waiting for transfers between devices: 433 us -> 52.2 us
  matrix products: 192 us -> 0 us
  other arithmetic: 173 us -> 0.23 us
  Pallas kernels: 0 us -> 133 us
  starting transfers between devices: 17.6 us -> 65.4 us
  blocking collectives: 0 us -> 44.6 us
  between operations: 22.3 us -> 2.74 us
    all_gather x6 -> x0, waiting for transfers between devices: 303 us -> none  [the longest x3 236 us: near_tile(): lax.all_gather(tile_test, 'row', axis=0, tiled=True)]
    dot_general x24 -> x0, matrix products: 179 us -> none  [the longest x3 103 us: tile_fold(): jnp.dot(kernel(points, shard_piece[0]), shard_piece[1], precision=HIGHEST)]
    another operation x27 -> x0, other arithmetic: 162 us -> none  [the longest x20 103 us: solve_coeffs(): factor = jnp.linalg.cholesky(gram_matrix)]
    pallas_call x0 -> x11, Pallas kernels: none -> 133 us  [the longest x6 97.1 us: near(): pl.pallas_call(functools.partial(near_kernel, plan, len(points), len(test...]
    psum x1 -> x0, waiting for transfers between devices: 84.4 us -> none  [body(): lax.psum((jnp.dot(selector, residual, precision=HIGHEST), jnp.dot(selecto...]
    all_to_all x0 -> x3, blocking collectives: none -> 44.6 us  [the longest x2 28.3 us: sum_row(): parts = lax.all_to_all(part.reshape(16, share, -1), 'row', 0, 0)]
    ppermute x10 -> x30, starting transfers between devices: 17.3 us -> 61.1 us  [the longest x3 12.5 us: body(): got_b = [lax.ppermute(v, 'row', along_x(-k)) for v, k in zip(far_b, SHIFTS)]]
    another operation x28 -> x1, local copies, waits for them, and re-layouts: 13.2 us -> 0.13 us  [body(): pivots.reshape(RANK, 1)]
  transfers between devices with their start and end apart: 17 -> 31, of which waited for: 11 -> 8; matrix products, arithmetic and copies ran while one was open for 32% -> 2% of each run, Pallas kernels for 0% -> 31%
where the time goes in v1:
time: 320 us; the launch traced here: 315 us
  Pallas kernels  133 us (42%)
  starting transfers between devices  65.4 us (20%)
  waiting for transfers between devices  52.2 us (16%)
  blocking collectives  44.6 us (14%)
  local copies, waits for them, and re-layouts  16.5 us (5%)
    pallas_call x6, Pallas kernels, near(): pl.pallas_call(functools.partial(near_kernel, plan, len(points), len(test...  97.1 us
    all_to_all x2, blocking collectives, sum_row(): parts = lax.all_to_all(part.reshape(16, share, -1), 'row', 0, 0)  28.3 us
    pallas_call x2, Pallas kernels, merge(): vmem_call(functools.partial(merge_kernel, top, share), outs, 1, 5, [VMEM(...  24.7 us
    all_to_all x1, blocking collectives, sum_row(): lax.all_to_all(jnp.broadcast_to(mine[None], (16, share, mine.shape[1])),...  16.3 us
    ppermute x1, waiting for transfers between devices, body(): pts_out = lax.ppermute(pts, 'leaf', OUTER)  15.8 us
    ppermute x1, waiting for transfers between devices, body(): first = lax.ppermute(send, 'leaf', COUSIN)  14.5 us
    ppermute x3, starting transfers between devices, body(): got_b = [lax.ppermute(v, 'row', along_x(-k)) for v, k in zip(far_b, SHIFTS)]  12.5 us
    unnamed x62, local copies, waits for them, and re-layouts  11.8 us
  transfers between devices with their start and end apart: 31, of which 8 were waited for; matrix products, arithmetic and copies ran while one was open for 2% of the time, Pallas kernels for 31%

profile of v1, /device:TPU:1, one launch (start us, length us, event | category | flops | bytes accessed | tf_op | source)
XLA Modules:
  0.0 315.1 jit_solution(13845672956619599389)
XLA Ops:
  0.7 3.8 %collective-permute-start.5 = (f32[64,512]{1,0:T(8,128)}, f32[64,512]{1,0:T(8,128)S(1)}, u32[]{:S(2)}, u32[]{:S(2)}) collective-permute-start(f32[64,512]{1,0:T(8,128)} %bitcast.27), channel_id=1, source_target_pairs={{0,2},{1,3},{2,0},{3,1},{4,6},{5,7},{6,4},{7,5},{8,10},{9,11},{10,... | collective-permute-start | bytes 393224 | tf_op jit(solution)/shard_map/ppermute | solution.py:355
  5.9 2.5 collective-permute-start.1
  8.4 1.0 constant_dynamic-update-slice_fusion.6
  9.4 4.3 %collective-permute-done = f32[64,512]{1,0:T(8,128)S(1)} collective-permute-done((f32[64,512]{1,0:T(8,128)}, f32[64,512]{1,0:T(8,128)S(1)}, u32[]{:S(2)}, u32[]{:S(2)}) %collective-permute-start) | collective-permute-done | bytes 131104 | tf_op jit(solution)/shard_map/ppermute | solution.py:354
  13.7 3.0 collective-permute-start.13
  16.7 2.5 collective-permute-done.2
  19.2 7.5 %collective-permute-start.14 = (f32[512,512]{1,0:T(8,128)}, f32[512,512]{1,0:T(8,128)}, u32[]{:S(2)}, u32[]{:S(2)}) collective-permute-start(f32[512,512]{1,0:T(8,128)} %test_ref.1), channel_id=1, source_target_pairs={{16,32},{32,16},{48,64},{64,48},{80,96},{96,80},{17,33},{33,17},{4... | collective-permute-start | bytes 3145736 | tf_op jit(solution)/shard_map/ppermute | solution.py:366
  26.8 1.9 collective-permute-start.7
  28.9 1.0 fusion
  32.5 1.2 copy-done.8
  33.7 15.8 %collective-permute-done.7.refs_2_ = f32[448,512]{1,0:T(8,128)} collective-permute-done((f32[448,512]{1,0:T(8,128)S(1)}, f32[448,512]{1,0:T(8,128)}, u32[]{:S(2)}, u32[]{:S(2)}) %collective-permute-start.7) | collective-permute-done | bytes 917536 | tf_op jit(solution)/shard_map/ppermute | solution.py:358
  50.2 2.1 collective-permute-start.11
  52.3 22.9 %near_local.1 = (f32[512,256]{1,0:T(8,128)S(1)}, f32[512,256]{1,0:T(8,128)S(1)}, f32[512,256]{1,0:T(8,128)S(1)}, f32[512,256]{1,0:T(8,128)S(1)}, f32[512,256]{1,...) custom-call(f32[1,1]{1,0:T(1,128)} %bitcast.5.weight_ref, ...), custom_call_target="tpu_custom_call" | custom-call | flops 12884901888 | bytes 4194304 | tf_op jit(solution)/shard_map/near_local/pallas_call | solution.py:186
  76.0 1.0 constant_dynamic-update-slice_fusion.9
  77.0 1.9 constant_dynamic-update-slice_fusion.8
  80.5 5.4 %collective-permute-start.16 = (f32[1536,256]{1,0:T(8,128)}, f32[1536,256]{1,0:T(8,128)}, u32[]{:S(2)}, u32[]{:S(2)}) collective-permute-start(f32[1536,256]{1,0:T(8,128)} %constant_dynamic-update-slice_fusion.7.refs_3_), channel_id=1, source_target_pairs={{16,32},{32,16},{48,64},{64,48},{80,96},{96,80},{17,33},{33,17},{4... | collective-permute-start | bytes 4718600 | tf_op jit(solution)/shard_map/ppermute | solution.py:382
  86.7 6.5 %collective-permute-done.17 = f32[512,256]{1,0:T(8,128)S(1)} collective-permute-done((f32[512,256]{1,0:T(8,128)}, f32[512,256]{1,0:T(8,128)S(1)}, u32[]{:S(2)}, u32[]{:S(2)}) %collective-permute-start.17) | collective-permute-done | bytes 524320 | tf_op jit(solution)/shard_map/ppermute | solution.py:377
  94.9 1.2 collective-permute-start.18
  96.3 4.6 %collective-permute-start.19 = (f32[1536,256]{1,0:T(8,128)}, f32[1536,256]{1,0:T(8,128)S(1)}, u32[]{:S(2)}, u32[]{:S(2)}) collective-permute-start(f32[1536,256]{1,0:T(8,128)} %constant_dynamic-update-slice_fusion.10.refs_6_.refs_3_), channel_id=1, source_target_pairs={{16,32},{32,16},{48,64},{64,48},{80,96},{96,80},{17,33},{33,17},{4... | collective-permute-start | bytes 4718600 | tf_op jit(solution)/shard_map/ppermute | solution.py:382
  100.9 1.0 copy-done.21
  101.9 17.1 %near_a.1 = (f32[512,256]{1,0:T(8,128)S(1)}, f32[512,256]{1,0:T(8,128)S(1)}, f32[512,256]{1,0:T(8,128)S(1)}) custom-call(f32[1,1]{1,0:T(1,128)} %bitcast.5.weight_ref, bf16[7,512,256]{2,1,0:T(8,128)(2,1)} %copy-done.8, f32[448,512]{1,0:T(8,128)S(1)} %copy-done.5, f32[448,512]{1,0:T(8,128)} %copy-done.6, f32[448,512]{1,0:T(8,128)} %collective-permute-done.7.refs_2_, ...), custom_call_target="tpu_custom_call" | custom-call | flops 9663676416 | bytes 5242880 | tf_op jit(solution)/shard_map/near_a/pallas_call | solution.py:186
  119.1 9.8 %near_outer_a.1 = (f32[512,256]{1,0:T(8,128)S(1)}, f32[512,256]{1,0:T(8,128)S(1)}, f32[512,256]{1,0:T(8,128)S(1)}) custom-call(f32[1,1]{1,0:T(1,128)} %bitcast.5.weight_ref, bf16[7,512,256]{2,1,0:T(8,128)(2,1)} %copy-done.8, f32[448,512]{1,0:T(8,128)S(1)} %copy-done.5, f32[448,512]{1,0:T(8,128)} %copy-done.6, f32[448,512]{1,0:T(8,128)} %collective-permute-done.7.refs_2_, ...), custom_call_target="tpu_custom_call" | custom-call | flops 4831838208 | bytes 4718592 | tf_op jit(solution)/shard_map/near_outer_a/pallas_call | solution.py:186
  128.9 2.6 collective-permute-start.20
  131.6 1.3 collective-permute-start.22
  132.8 17.2 %near_b.1 = (f32[512,256]{1,0:T(8,128)S(1)}, f32[512,256]{1,0:T(8,128)S(1)}, f32[512,256]{1,0:T(8,128)S(1)}) custom-call(f32[1,1]{1,0:T(1,128)} %bitcast.5.weight_ref, bf16[7,512,256]{2,1,0:T(8,128)(2,1)} %copy-done.8, f32[448,512]{1,0:T(8,128)S(1)} %copy-done.5, f32[448,512]{1,0:T(8,128)} %copy-done.6, f32[448,512]{1,0:T(8,128)} %collective-permute-done.7.refs_2_, ...), custom_call_target="tpu_custom_call" | custom-call | flops 9663676416 | bytes 5242880 | tf_op jit(solution)/shard_map/near_b/pallas_call | solution.py:186
  150.0 1.2 copy-done.25
  151.3 9.8 %near_outer_b.1 = (f32[512,256]{1,0:T(8,128)S(1)}, f32[512,256]{1,0:T(8,128)S(1)}, f32[512,256]{1,0:T(8,128)S(1)}) custom-call(f32[1,1]{1,0:T(1,128)} %bitcast.5.weight_ref, bf16[7,512,256]{2,1,0:T(8,128)(2,1)} %copy-done.8, f32[448,512]{1,0:T(8,128)S(1)} %copy-done.5, f32[448,512]{1,0:T(8,128)} %copy-done.6, f32[448,512]{1,0:T(8,128)} %collective-permute-done.7.refs_2_, ...), custom_call_target="tpu_custom_call" | custom-call | flops 4831838208 | bytes 4718592 | tf_op jit(solution)/shard_map/near_outer_b/pallas_call | solution.py:186
  161.1 1.7 collective-permute-start.23
  163.0 10.5 %collective-permute-start.25 = (f32[512,256]{1,0:T(8,128)S(1)}, f32[512,256]{1,0:T(8,128)S(1)}, u32[]{:S(2)}, u32[]{:S(2)}) collective-permute-start(f32[512,256]{1,0:T(8,128)S(1)} %get-tuple-element.82), channel_id=1, source_target_pairs={{0,8},{1,9},{2,10},{3,11},{4,12},{5,13},{6,14},{7,15},{8,0},{9,1},... | collective-permute-start | bytes 1572872 | tf_op jit(solution)/shard_map/ppermute | solution.py:392
  173.6 20.4 %near_own.1 = (f32[512,256]{1,0:T(8,128)S(1)}, f32[512,256]{1,0:T(8,128)S(1)}) custom-call(f32[1,1]{1,0:T(1,128)} %bitcast.5.weight_ref, bf16[7,512,256]{2,1,0:T(8,128)(2,1)} %copy-done.8, f32[448,512]{1,0:T(8,128)S(1)} %copy-done.5, f32[448,512]{1,0:T(8,128)S(1)} %copy-done.7, f32[448,512]{1,0:T(8,128)} %collective-permute-done.7.refs_2_, ...), custom_call_target="tpu_custom_call" | custom-call | flops 9663676416 | bytes 6815744 | tf_op jit(solution)/shard_map/near_own/pallas_call | solution.py:186
  194.1 2.3 residual.1
  196.3 16.3 %all_to_all.20 = f32[16,16,640]{2,1,0:T(8,128)S(1)} all-to-all(f32[16,16,640]{2,1,0:T(8,128)S(1)} %bitcast.26), channel_id=1, replica_groups=mesh['leaf'=8,'row'=16] {'row'}, dimensions={0} | all-to-all | bytes 1310720 | tf_op jit(solution)/shard_map/all_to_all | solution.py:343
  212.7 16.3 %all_to_all.21 = f32[16,16,640]{2,1,0:T(8,128)S(1)} all-to-all(f32[16,16,640]{2,1,0:T(8,128)S(1)} %broadcast_in_dim.4), channel_id=1, replica_groups=mesh['leaf'=8,'row'=16] {'row'}, dimensions={0} | all-to-all | bytes 1310720 | tf_op jit(solution)/shard_map/all_to_all | solution.py:345
  229.1 8.7 %leaf.1 = (f32[512,256]{1,0:T(8,128)}, f32[256,512]{1,0:T(8,128)S(1)}) custom-call(f32[512,512]{1,0:T(8,128)S(1)} %get-tuple-element.83.resid_ref, f32[512,512]{1,0:T(8,128)S(1)} %copy-done.2, f32[256,640]{1,0:T(8,128)S(1)} %bitcast.23), custom_call_target="tpu_custom_call" | custom-call | flops 3000000000 | bytes 4194304 | tf_op jit(solution)/shard_map/leaf/pallas_call | solution.py:404
  237.7 12.0 %all_to_all.22 = f32[16,16,512]{2,1,0:T(8,128)S(1)} all-to-all(f32[16,16,512]{2,1,0:T(8,128)S(1)} %bitcast.36), channel_id=1, replica_groups=mesh['leaf'=8,'row'=16] {'row'}, dimensions={0} | all-to-all | bytes 1048576 | tf_op jit(solution)/shard_map/all_to_all | solution.py:343
  249.7 0.9 broadcast_in_dim.5
  250.6 4.3 %all-to-all-start.3 = ((f32[16,16,512]{2,1,0:T(8,128)}), f32[16,16,512]{2,1,0:T(8,128)S(1)}, u32[]{:S(2)}, u32[]{:S(2)}) async-start(f32[16,16,512]{2,1,0:T(8,128)} %broadcast_in_dim.5), calls=%async_computation.3 | async-start | bytes 1048576 | tf_op jit(solution)/shard_map/all_to_all | solution.py:345
  255.0 3.0 collective-permute-start.26
  258.0 5.9 %all-to-all-done.3 = f32[16,16,512]{2,1,0:T(8,128)S(1)} async-done(((f32[16,16,512]{2,1,0:T(8,128)}), f32[16,16,512]{2,1,0:T(8,128)S(1)}, u32[]{:S(2)}, u32[]{:S(2)}) %all-to-all-start.3) | async-done | bytes 524320 | tf_op jit(solution)/shard_map/all_to_all | solution.py:345
  263.9 4.1 %collective-permute-start.27 = (f32[256,512]{1,0:T(8,128)S(1)}, f32[256,512]{1,0:T(8,128)S(1)}, u32[]{:S(2)}, u32[]{:S(2)}) collective-permute-start(f32[256,512]{1,0:T(8,128)S(1)} %bitcast.34), channel_id=1, source_target_pairs={{0,16},{16,0},{32,48},{48,32},{64,80},{80,64},{96,112},{112,96},{1... | collective-permute-start | bytes 1572872 | tf_op jit(solution)/shard_map/ppermute | solution.py:408
  268.2 1.3 collective-permute-done.27.refs_3_
  269.5 12.5 %merge_mid.1 = (f32[16,256]{1,0:T(8,128)}, f32[256,640]{1,0:T(8,128)S(1)}, f32[256,512]{1,0:T(8,128)S(1)}, f32[256,640]{1,0:T(8,128)S(1)}) custom-call(s32[1,3]{1,0:T(1,128)S(1)} %add_bitcast_fusion.info_ref, s32[256,1]{1,0:T(8,128)S(1)} %copy.11.piv_ref, f32[256,640]{1,0:T(8,128)S(1)} %bitcast.25, f32[256,512]{1,0:T(8,128)S(1)} %bitcast.35, ...), custom_call_target="tpu_custom_call" | custom-call | flops 3000000000 | bytes 4194304 | tf_op jit(solution)/shard_map/merge_mid/pallas_call | solution.py:332
  282.8 1.4 collective-permute-start.28
  284.2 14.5 %collective-permute-done.28.refs_2_ = f32[256,640]{1,0:T(8,128)S(1)} collective-permute-done((f32[256,640]{1,0:T(8,128)S(1)}, f32[256,640]{1,0:T(8,128)S(1)}, u32[]{:S(2)}, u32[]{:S(2)}) %collective-permute-start.28) | collective-permute-done | bytes 655392 | tf_op jit(solution)/shard_map/ppermute | solution.py:420
  298.7 1.2 collective-permute-start.29
  300.2 1.5 collective-permute-done.29.refs_3_
  301.7 1.0 copy-done.10
  302.7 12.2 %merge_top.1 = f32[8,256]{1,0:T(8,128)} custom-call(s32[1,3]{1,0:T(1,128)S(1)} %add_bitcast_fusion.1.info_ref, s32[256,1]{1,0:T(8,128)S(1)} %copy.12.piv_ref, f32[256,640]{1,0:T(8,128)S(1)} %get-tuple-element.88.refs_0_, f32[256,512]{1,0:T(8,128)S(1)} %copy-done.10, f32[256,640]{1,0:T(8,128)S(1)} %collective-permute-done.28.refs_2_, ...), custom_call_target="tpu_custom_call" | custom-call | flops 3000000000 | bytes 4194304 | tf_op jit(solution)/shard_map/merge_top/pallas_call | solution.py:332
  (106 shorter events, 10.2 us)
Async XLA Ops:
  0.6 267.3 %copy-start = (s32[4,256]{1,0:T(4,128)S(1)}, s32[4,256]{1,0:T(4,128)}, u32[]{:S(2)}) copy-start(s32[4,256]{1,0:T(4,128)} %param.12) | copy-start | bytes 12292
  0.6 28.2 %copy-start.1 = (f32[512,512]{1,0:T(8,128)S(1)}, f32[512,512]{1,0:T(8,128)}, u32[]{:S(2)}) copy-start(f32[512,512]{1,0:T(8,128)} %test_ref.1) | copy-start | bytes 3145732
  0.7 26.1 %collective-permute-start.5 = (f32[64,512]{1,0:T(8,128)}, f32[64,512]{1,0:T(8,128)S(1)}, u32[]{:S(2)}, u32[]{:S(2)}) collective-permute-start(f32[64,512]{1,0:T(8,128)} %bitcast.27), channel_id=1, source_target_pairs={{0,2},{1,3},{2,0},{3,1},{4,6},{5,7},{6,4},{7,5},{8,10},{9,11},{10,... | collective-permute-start | bytes 393224 | tf_op jit(solution)/shard_map/ppermute | solution.py:355
  4.5 22.3 %collective-permute-start.4 = (f32[64,512]{1,0:T(8,128)}, f32[64,512]{1,0:T(8,128)S(1)}, u32[]{:S(2)}, u32[]{:S(2)}) collective-permute-start(f32[64,512]{1,0:T(8,128)} %bitcast.28), channel_id=1, source_target_pairs={{0,3},{1,0},{2,1},{3,2},{4,7},{5,4},{6,5},{7,6},{8,11},{9,8},{10,9... | collective-permute-start | bytes 393224 | tf_op jit(solution)/shard_map/ppermute | solution.py:355
  5.3 21.5 %collective-permute-start.3 = (f32[64,512]{1,0:T(8,128)}, f32[64,512]{1,0:T(8,128)S(1)}, u32[]{:S(2)}, u32[]{:S(2)}) collective-permute-start(f32[64,512]{1,0:T(8,128)} %bitcast.29), channel_id=1, source_target_pairs={{0,1},{1,2},{2,3},{3,0},{4,5},{5,6},{6,7},{7,4},{8,9},{9,10},{10,1... | collective-permute-start | bytes 393224 | tf_op jit(solution)/shard_map/ppermute | solution.py:355
  5.9 7.7 %collective-permute-start.1 = (f32[64,512]{1,0:T(8,128)}, f32[64,512]{1,0:T(8,128)S(1)}, u32[]{:S(2)}, u32[]{:S(2)}) collective-permute-start(f32[64,512]{1,0:T(8,128)} %bitcast.30), channel_id=1, source_target_pairs={{0,12},{1,13},{2,14},{3,15},{4,0},{5,1},{6,2},{7,3},{8,4},{9,5},{1... | collective-permute-start | bytes 393224 | tf_op jit(solution)/shard_map/ppermute | solution.py:354
  8.4 5.2 %collective-permute-start = (f32[64,512]{1,0:T(8,128)}, f32[64,512]{1,0:T(8,128)S(1)}, u32[]{:S(2)}, u32[]{:S(2)}) collective-permute-start(f32[64,512]{1,0:T(8,128)} %bitcast.31), channel_id=1, source_target_pairs={{0,4},{1,5},{2,6},{3,7},{4,8},{5,9},{6,10},{7,11},{8,12},{9,13},{1... | collective-permute-start | bytes 393224 | tf_op jit(solution)/shard_map/ppermute | solution.py:354
  13.7 5.5 %collective-permute-start.2 = (f32[64,512]{1,0:T(8,128)}, f32[64,512]{1,0:T(8,128)S(1)}, u32[]{:S(2)}, u32[]{:S(2)}) collective-permute-start(f32[64,512]{1,0:T(8,128)} %bitcast.32), channel_id=1, source_target_pairs={{0,8},{1,9},{2,10},{3,11},{4,12},{5,13},{6,14},{7,15},{8,0},{9,1},... | collective-permute-start | bytes 393224 | tf_op jit(solution)/shard_map/ppermute | solution.py:354
  13.7 35.9 %collective-permute-start.13 = (f32[512,512]{1,0:T(8,128)}, f32[512,512]{1,0:T(8,128)}, u32[]{:S(2)}, u32[]{:S(2)}) collective-permute-start(f32[512,512]{1,0:T(8,128)} %test_ref.1), channel_id=1, source_target_pairs={{0,16},{16,0},{32,48},{48,32},{64,80},{80,64},{96,112},{112,96},{1... | collective-permute-start | bytes 3145736 | tf_op jit(solution)/shard_map/ppermute | solution.py:365
  16.7 13.2 %copy-start.22 = (s32[1,2]{1,0:T(1,128)S(1)}, s32[1,2]{1,0:T(1,128)}, u32[]{:S(2)}) copy-start(s32[1,2]{1,0:T(1,128)} %param.10) | copy-start | bytes 28
  19.2 31.0 %collective-permute-start.14 = (f32[512,512]{1,0:T(8,128)}, f32[512,512]{1,0:T(8,128)}, u32[]{:S(2)}, u32[]{:S(2)}) collective-permute-start(f32[512,512]{1,0:T(8,128)} %test_ref.1), channel_id=1, source_target_pairs={{16,32},{32,16},{48,64},{64,48},{80,96},{96,80},{17,33},{33,17},{4... | collective-permute-start | bytes 3145736 | tf_op jit(solution)/shard_map/ppermute | solution.py:366
  26.8 5.7 %copy-start.4 = (f32[448,512]{1,0:T(8,128)}, f32[448,512]{1,0:T(8,128)S(1)}, u32[]{:S(2)}) copy-start(f32[448,512]{1,0:T(8,128)S(1)} %constant_dynamic-update-slice_fusion.points_ref.refs_0_) | copy-start | bytes 2752516
  26.8 22.7 %collective-permute-start.7 = (f32[448,512]{1,0:T(8,128)S(1)}, f32[448,512]{1,0:T(8,128)}, u32[]{:S(2)}, u32[]{:S(2)}) collective-permute-start(f32[448,512]{1,0:T(8,128)S(1)} %constant_dynamic-update-slice_fusion.points_ref.refs_0_), channel_id=1, source_target_pairs={{16,32},{32,16},{48,64},{64,48},{80,96},{96,80},{17,33},{33,17},{4... | collective-permute-start | bytes 2752520 | tf_op jit(solution)/shard_map/ppermute | solution.py:358
  28.8 20.8 %collective-permute-start.6 = (f32[448,512]{1,0:T(8,128)S(1)}, f32[448,512]{1,0:T(8,128)S(1)}, u32[]{:S(2)}, u32[]{:S(2)}) collective-permute-start(f32[448,512]{1,0:T(8,128)S(1)} %constant_dynamic-update-slice_fusion.points_ref.refs_0_), channel_id=1, source_target_pairs={{0,16},{16,0},{32,48},{48,32},{64,80},{80,64},{96,112},{112,96},{1... | collective-permute-start | bytes 2752520 | tf_op jit(solution)/shard_map/ppermute | solution.py:357
  29.9 46.0 %collective-permute-start.10 = (f32[512,256]{1,0:T(8,128)}, f32[512,256]{1,0:T(8,128)}, u32[]{:S(2)}, u32[]{:S(2)}) collective-permute-start(f32[512,256]{1,0:T(8,128)} %get-tuple-element.91), channel_id=1, source_target_pairs={{0,12},{1,13},{2,14},{3,15},{4,0},{5,1},{6,2},{7,3},{8,4},{9,5},{1... | collective-permute-start | bytes 1572872 | tf_op jit(solution)/shard_map/ppermute | solution.py:368
  49.5 26.5 %collective-permute-start.9 = (f32[512,256]{1,0:T(8,128)}, f32[512,256]{1,0:T(8,128)S(1)}, u32[]{:S(2)}, u32[]{:S(2)}) collective-permute-start(f32[512,256]{1,0:T(8,128)} %get-tuple-element.91), channel_id=1, source_target_pairs={{0,8},{1,9},{2,10},{3,11},{4,12},{5,13},{6,14},{7,15},{8,0},{9,1},... | collective-permute-start | bytes 1572872 | tf_op jit(solution)/shard_map/ppermute | solution.py:368
  49.5 26.4 %collective-permute-start.8 = (f32[512,256]{1,0:T(8,128)}, f32[512,256]{1,0:T(8,128)S(1)}, u32[]{:S(2)}, u32[]{:S(2)}) collective-permute-start(f32[512,256]{1,0:T(8,128)} %get-tuple-element.91), channel_id=1, source_target_pairs={{0,4},{1,5},{2,6},{3,7},{4,8},{5,9},{6,10},{7,11},{8,12},{9,13},{1... | collective-permute-start | bytes 1572872 | tf_op jit(solution)/shard_map/ppermute | solution.py:368
  49.6 26.4 %collective-permute-start.12 = (f32[512,256]{1,0:T(8,128)}, f32[512,256]{1,0:T(8,128)S(1)}, u32[]{:S(2)}, u32[]{:S(2)}) collective-permute-start(f32[512,256]{1,0:T(8,128)} %get-tuple-element.59), channel_id=1, source_target_pairs={{0,2},{1,3},{2,0},{3,1},{4,6},{5,7},{6,4},{7,5},{8,10},{9,11},{10,... | collective-permute-start | bytes 1572872 | tf_op jit(solution)/shard_map/ppermute | solution.py:369
  50.2 25.9 %collective-permute-start.11 = (f32[512,256]{1,0:T(8,128)}, f32[512,256]{1,0:T(8,128)S(1)}, u32[]{:S(2)}, u32[]{:S(2)}) collective-permute-start(f32[512,256]{1,0:T(8,128)} %get-tuple-element.59), channel_id=1, source_target_pairs={{0,1},{1,2},{2,3},{3,0},{4,5},{5,6},{6,7},{7,4},{8,9},{9,10},{10,1... | collective-permute-start | bytes 1572872 | tf_op jit(solution)/shard_map/ppermute | solution.py:369
  76.0 3.8 %copy-start.16 = (f32[512,256]{1,0:T(8,128)}, f32[512,256]{1,0:T(8,128)S(1)}, u32[]{:S(2)}) copy-start(f32[512,256]{1,0:T(8,128)S(1)} %get-tuple-element.64.refs_5_) | copy-start | bytes 1572868
  76.0 3.8 %copy-start.18 = (f32[512,256]{1,0:T(8,128)}, f32[512,256]{1,0:T(8,128)S(1)}, u32[]{:S(2)}) copy-start(f32[512,256]{1,0:T(8,128)S(1)} %get-tuple-element.65.refs_6_) | copy-start | bytes 1572868
  79.7 16.4 %copy-start.23 = (s32[1,256]{1,0:T(1,128)S(1)}, s32[1,256]{1,0:T(1,128)}, u32[]{:S(2)}) copy-start(s32[1,256]{1,0:T(1,128)} %param.11) | copy-start | bytes 3076
  79.7 21.1 %copy-start.5 = (f32[448,512]{1,0:T(8,128)S(1)}, f32[448,512]{1,0:T(8,128)}, u32[]{:S(2)}) copy-start(f32[448,512]{1,0:T(8,128)} %copy-done.4) | copy-start | bytes 2752516
  79.8 21.1 %collective-permute-start.15 = (f32[1536,256]{1,0:T(8,128)}, f32[1536,256]{1,0:T(8,128)}, u32[]{:S(2)}, u32[]{:S(2)}) collective-permute-start(f32[1536,256]{1,0:T(8,128)} %constant_dynamic-update-slice_fusion.7.refs_3_), channel_id=1, source_target_pairs={{0,16},{16,0},{32,48},{48,32},{64,80},{80,64},{96,112},{112,96},{1... | collective-permute-start | bytes 4718600 | tf_op jit(solution)/shard_map/ppermute | solution.py:381
  79.8 21.0 %copy-start.17 = (f32[512,256]{1,0:T(8,128)S(1)}, f32[512,256]{1,0:T(8,128)}, u32[]{:S(2)}) copy-start(f32[512,256]{1,0:T(8,128)} %copy-done.16) | copy-start | bytes 1572868
  79.9 21.0 %copy-start.19 = (f32[512,256]{1,0:T(8,128)S(1)}, f32[512,256]{1,0:T(8,128)}, u32[]{:S(2)}) copy-start(f32[512,256]{1,0:T(8,128)} %copy-done.18) | copy-start | bytes 1572868
  79.9 13.4 %collective-permute-start.17 = (f32[512,256]{1,0:T(8,128)}, f32[512,256]{1,0:T(8,128)S(1)}, u32[]{:S(2)}, u32[]{:S(2)}) collective-permute-start(f32[512,256]{1,0:T(8,128)} %get-tuple-element.59), channel_id=1, source_target_pairs={{0,3},{1,0},{2,1},{3,2},{4,7},{5,4},{6,5},{7,6},{8,11},{9,8},{10,9... | collective-permute-start | bytes 1572872 | tf_op jit(solution)/shard_map/ppermute | solution.py:377
  80.5 38.6 %collective-permute-start.16 = (f32[1536,256]{1,0:T(8,128)}, f32[1536,256]{1,0:T(8,128)}, u32[]{:S(2)}, u32[]{:S(2)}) collective-permute-start(f32[1536,256]{1,0:T(8,128)} %constant_dynamic-update-slice_fusion.7.refs_3_), channel_id=1, source_target_pairs={{16,32},{32,16},{48,64},{64,48},{80,96},{96,80},{17,33},{33,17},{4... | collective-permute-start | bytes 4718600 | tf_op jit(solution)/shard_map/ppermute | solution.py:382
  94.9 37.9 %collective-permute-start.18 = (f32[1536,256]{1,0:T(8,128)}, f32[1536,256]{1,0:T(8,128)}, u32[]{:S(2)}, u32[]{:S(2)}) collective-permute-start(f32[1536,256]{1,0:T(8,128)} %constant_dynamic-update-slice_fusion.10.refs_6_.refs_3_), channel_id=1, source_target_pairs={{0,16},{16,0},{32,48},{48,32},{64,80},{80,64},{96,112},{112,96},{1... | collective-permute-start | bytes 4718600 | tf_op jit(solution)/shard_map/ppermute | solution.py:381
  96.3 53.7 %collective-permute-start.19 = (f32[1536,256]{1,0:T(8,128)}, f32[1536,256]{1,0:T(8,128)S(1)}, u32[]{:S(2)}, u32[]{:S(2)}) collective-permute-start(f32[1536,256]{1,0:T(8,128)} %constant_dynamic-update-slice_fusion.10.refs_6_.refs_3_), channel_id=1, source_target_pairs={{16,32},{32,16},{48,64},{64,48},{80,96},{96,80},{17,33},{33,17},{4... | collective-permute-start | bytes 4718600 | tf_op jit(solution)/shard_map/ppermute | solution.py:382
  119.1 13.8 %copy-start.12 = (f32[512,256]{1,0:T(8,128)S(1)}, f32[512,256]{1,0:T(8,128)}, u32[]{:S(2)}) copy-start(f32[512,256]{1,0:T(8,128)} %copy-done.11) | copy-start | bytes 1572868
  119.1 13.8 %copy-start.14 = (f32[512,256]{1,0:T(8,128)S(1)}, f32[512,256]{1,0:T(8,128)}, u32[]{:S(2)}) copy-start(f32[512,256]{1,0:T(8,128)} %copy-done.13) | copy-start | bytes 1572868
  119.1 13.7 %copy-start.15 = (f32[512,256]{1,0:T(8,128)S(1)}, f32[512,256]{1,0:T(8,128)}, u32[]{:S(2)}) copy-start(f32[512,256]{1,0:T(8,128)} %get-tuple-element.76.refs_7_) | copy-start | bytes 1572868
  128.9 34.1 %collective-permute-start.20 = (f32[512,256]{1,0:T(8,128)S(1)}, f32[512,256]{1,0:T(8,128)S(1)}, u32[]{:S(2)}, u32[]{:S(2)}) collective-permute-start(f32[512,256]{1,0:T(8,128)S(1)} %get-tuple-element.70), channel_id=1, source_target_pairs={{0,3},{1,0},{2,1},{3,2},{4,7},{5,4},{6,5},{7,6},{8,11},{9,8},{10,9... | collective-permute-start | bytes 1572872 | tf_op jit(solution)/shard_map/ppermute | solution.py:390
  131.6 62.4 %collective-permute-start.21 = (f32[512,256]{1,0:T(8,128)S(1)}, f32[512,256]{1,0:T(8,128)S(1)}, u32[]{:S(2)}, u32[]{:S(2)}) collective-permute-start(f32[512,256]{1,0:T(8,128)S(1)} %get-tuple-element.71), channel_id=1, source_target_pairs={{0,1},{1,2},{2,3},{3,0},{4,5},{5,6},{6,7},{7,4},{8,9},{9,10},{10,1... | collective-permute-start | bytes 1572872 | tf_op jit(solution)/shard_map/ppermute | solution.py:390
  131.6 62.4 %collective-permute-start.22 = (f32[512,256]{1,0:T(8,128)S(1)}, f32[512,256]{1,0:T(8,128)S(1)}, u32[]{:S(2)}, u32[]{:S(2)}) collective-permute-start(f32[512,256]{1,0:T(8,128)S(1)} %get-tuple-element.72), channel_id=1, source_target_pairs={{0,2},{1,3},{2,0},{3,1},{4,6},{5,7},{6,4},{7,5},{8,10},{9,11},{10,... | collective-permute-start | bytes 1572872 | tf_op jit(solution)/shard_map/ppermute | solution.py:390
  151.3 22.3 %copy-start.7 = (f32[448,512]{1,0:T(8,128)S(1)}, f32[448,512]{1,0:T(8,128)}, u32[]{:S(2)}) copy-start(f32[448,512]{1,0:T(8,128)} %copy-done.6) | copy-start | bytes 2752516
  161.1 33.0 %collective-permute-start.23 = (f32[512,256]{1,0:T(8,128)S(1)}, f32[512,256]{1,0:T(8,128)S(1)}, u32[]{:S(2)}, u32[]{:S(2)}) collective-permute-start(f32[512,256]{1,0:T(8,128)S(1)} %get-tuple-element.80), channel_id=1, source_target_pairs={{0,12},{1,13},{2,14},{3,15},{4,0},{5,1},{6,2},{7,3},{8,4},{9,5},{1... | collective-permute-start | bytes 1572872 | tf_op jit(solution)/shard_map/ppermute | solution.py:392
  162.8 31.2 %collective-permute-start.24 = (f32[512,256]{1,0:T(8,128)S(1)}, f32[512,256]{1,0:T(8,128)S(1)}, u32[]{:S(2)}, u32[]{:S(2)}) collective-permute-start(f32[512,256]{1,0:T(8,128)S(1)} %get-tuple-element.81), channel_id=1, source_target_pairs={{0,4},{1,5},{2,6},{3,7},{4,8},{5,9},{6,10},{7,11},{8,12},{9,13},{1... | collective-permute-start | bytes 1572872 | tf_op jit(solution)/shard_map/ppermute | solution.py:392
  163.0 31.0 %copy-start.3 = (f32[512,64]{0,1:T(8,128)S(1)}, f32[512,64]{0,1:T(8,128)}, u32[]{:S(2)}) copy-start(f32[512,64]{0,1:T(8,128)} %param.7) | copy-start | bytes 393220
  163.0 31.0 %collective-permute-start.25 = (f32[512,256]{1,0:T(8,128)S(1)}, f32[512,256]{1,0:T(8,128)S(1)}, u32[]{:S(2)}, u32[]{:S(2)}) collective-permute-start(f32[512,256]{1,0:T(8,128)S(1)} %get-tuple-element.82), channel_id=1, source_target_pairs={{0,8},{1,9},{2,10},{3,11},{4,12},{5,13},{6,14},{7,15},{8,0},{9,1},... | collective-permute-start | bytes 1572872 | tf_op jit(solution)/shard_map/ppermute | solution.py:392
  212.6 16.4 %copy-start.2 = (f32[512,512]{1,0:T(8,128)S(1)}, f32[512,512]{1,0:T(8,128)}, u32[]{:S(2)}) copy-start(f32[512,512]{1,0:T(8,128)} %test_ref.1) | copy-start | bytes 3145732
  250.6 13.3 %all-to-all-start.3 = ((f32[16,16,512]{2,1,0:T(8,128)}), f32[16,16,512]{2,1,0:T(8,128)S(1)}, u32[]{:S(2)}, u32[]{:S(2)}) async-start(f32[16,16,512]{2,1,0:T(8,128)} %broadcast_in_dim.5), calls=%async_computation.3 | async-start | bytes 1048576 | tf_op jit(solution)/shard_map/all_to_all | solution.py:345
  255.0 13.2 %collective-permute-start.26 = (f32[256,640]{1,0:T(8,128)S(1)}, f32[256,640]{1,0:T(8,128)S(1)}, u32[]{:S(2)}, u32[]{:S(2)}) collective-permute-start(f32[256,640]{1,0:T(8,128)S(1)} %bitcast.24), channel_id=1, source_target_pairs={{0,16},{16,0},{32,48},{48,32},{64,80},{80,64},{96,112},{112,96},{1... | collective-permute-start | bytes 1966088 | tf_op jit(solution)/shard_map/ppermute | solution.py:403
  263.9 5.6 %collective-permute-start.27 = (f32[256,512]{1,0:T(8,128)S(1)}, f32[256,512]{1,0:T(8,128)S(1)}, u32[]{:S(2)}, u32[]{:S(2)}) collective-permute-start(f32[256,512]{1,0:T(8,128)S(1)} %bitcast.34), channel_id=1, source_target_pairs={{0,16},{16,0},{32,48},{48,32},{64,80},{80,64},{96,112},{112,96},{1... | collective-permute-start | bytes 1572872 | tf_op jit(solution)/shard_map/ppermute | solution.py:408
  268.2 31.8 %copy-start.24 = (s32[2,256]{1,0:T(2,128)S(1)}, s32[2,256]{1,0:T(2,128)}, u32[]{:S(2)}) copy-start(s32[2,256]{1,0:T(2,128)} %param.13) | copy-start | bytes 6148
  282.8 15.9 %collective-permute-start.28 = (f32[256,640]{1,0:T(8,128)S(1)}, f32[256,640]{1,0:T(8,128)S(1)}, u32[]{:S(2)}, u32[]{:S(2)}) collective-permute-start(f32[256,640]{1,0:T(8,128)S(1)} %get-tuple-element.90), channel_id=1, source_target_pairs={{0,32},{16,48},{32,0},{48,16},{64,96},{80,112},{96,64},{112,80},{1... | collective-permute-start | bytes 1966088 | tf_op jit(solution)/shard_map/ppermute | solution.py:420
  298.7 2.9 collective-permute-start.29
  (9 other events, 15.7 us)

commit v2 on v1

v2 whole, which is shorter than its diff:
```python
import functools
import math

import jax
import jax.numpy as jnp
from jax import lax
from jax.experimental import pallas as pl
from jax.experimental.pallas import tpu as pltpu
from jax.sharding import PartitionSpec as P

DIM = 64
RANK = 256
SAMP = 512
BLK = 512
SIDE = 4
SCALE = math.log2(math.e) / DIM
HIGHEST = lax.Precision.HIGHEST
F32, BF16 = jnp.float32, jnp.bfloat16
VMEM = pltpu.VMEM


def along_x(k):
    return [(4 * x + y, 4 * ((x + k) % 4) + y) for x in range(4) for y in range(4)]


def along_y(k):
    return [(4 * x + y, 4 * x + (y + k) % 4) for x in range(4) for y in range(4)]


SIBLING = [(i, i ^ 1) for i in range(8)]
OUTER = [(1, 2), (2, 1), (3, 4), (4, 3), (5, 6), (6, 5)]
COUSIN = [(i, i ^ 2) for i in range(8)]


NN = (((1,), (0,)), ((), ()))
NT = (((1,), (1,)), ((), ()))


def mm(a, b, dims=NN):
    return lax.dot_general(a, b, dims, preferred_element_type=F32)


def split2(a):
    hi = a.astype(BF16)
    return hi, (a - hi.astype(F32)).astype(BF16)


def split3(a):
    hi = a.astype(BF16)
    rest = a - hi.astype(F32)
    mid = rest.astype(BF16)
    return hi, mid, (rest - mid.astype(F32)).astype(BF16)


def dot3(a, b, dims=NN):
    ah, al = split2(a)
    bh, bl = split2(b)
    return mm(ah, bh, dims) + (mm(ah, bl, dims) + mm(al, bh, dims))


def dot6(a, b, dims=NN):
    ah, am, al = split3(a)
    bh, bm, bl = split3(b)
    return mm(ah, bh, dims) + (
        (mm(ah, bm, dims) + mm(am, bh, dims))
        + (mm(am, bm, dims) + (mm(ah, bl, dims) + mm(al, bh, dims)))
    )


def pick(one_hot, a):
    h, m, l = split3(a)
    return (mm(one_hot, h) + mm(one_hot, m)) + mm(one_hot, l)


SHIFTS = (1, 3, 2)
MSG0, MSG1, MSG2 = BLK + DIM, 2 * (BLK + DIM), BLK + DIM
PLACES = ((0, 0, BLK), (1, 0, 2 * BLK), (1, BLK, 2 * BLK + DIM), (2, 0, BLK))
COUNT = 3 * SIDE


def norm_rows(xt, first):
    rows = lax.broadcasted_iota(jnp.int32, (DIM, BLK), 0)
    sq = jnp.sum(xt * xt, axis=0, keepdims=True) * (-SCALE)
    h, m, l = (v.astype(F32) for v in split3(sq))
    one = jnp.ones_like(sq)
    aux = jnp.zeros((DIM, BLK), F32)
    for n, part in enumerate((h, m, l, one, one, one) if first else (one, one, one, h, m, l)):
        aux = jnp.where(rows == n, part, aux)
    return aux


def left_features(xt):
    scaled = xt * (2.0 * SCALE)
    hi = scaled.astype(BF16).astype(F32)
    feat = jnp.concatenate([hi, hi, scaled - hi, norm_rows(xt, True)], axis=0)
    return feat.T.astype(BF16)


def right_features(xt, ref):
    hi, lo = split2(xt)
    ref[0:DIM, :] = hi
    ref[DIM:2 * DIM, :] = lo
    ref[2 * DIM:3 * DIM, :] = hi
    ref[3 * DIM:, :] = norm_rows(xt, False).astype(BF16)


def pivot_kernel(
    info_ref, weight_ref, piv_ref, all_ref, samp_ref, own_ref, sib_ref, out_ref,
    feat_ref, part_ref, skel_ref, right_ref
):
    row = info_ref[0, 0]
    x, y = row >> 2, row & 3
    for i, k in enumerate((0,) + SHIFTS):
        feat_ref[i] = left_features(all_ref[x << 2 | (y + SIDE - k & 3)])
    column = lax.broadcasted_iota(jnp.int32, (RANK, BLK), 1)
    piv = piv_ref[...]

    def rows_of(r):
        return jnp.where(piv == column + r * BLK, 1.0, 0.0).astype(BF16)

    got = jnp.zeros((RANK, 3 * DIM), F32)
    for r in range(16):
        got += mm(rows_of(r), jnp.concatenate(split3(all_ref[r]), axis=0), NT)
    skel = (got[:, :DIM] + got[:, DIM:2 * DIM]) + got[:, 2 * DIM:]
    skel_ref[...] = jnp.concatenate([skel, jnp.zeros((RANK, DIM), F32)], axis=1)
    scaled = skel * (2.0 * SCALE)
    hi = scaled.astype(BF16).astype(F32)
    lane = lax.broadcasted_iota(jnp.int32, (RANK, DIM), 1)
    sq = jnp.sum(skel * skel, axis=1, keepdims=True) * (-SCALE)
    aux = jnp.where(lane < 6, 1.0, 0.0)
    for n, part in enumerate(split3(sq)):
        aux = jnp.where(lane == n, part.astype(F32), aux)
    feat = jnp.concatenate([hi, hi, scaled - hi, aux], axis=1).astype(BF16)
    total = pick(rows_of(row), samp_ref[...])
    for n, ref in enumerate((own_ref, sib_ref, out_ref)):
        right_features(ref[BLK:, :], right_ref)
        kern = jnp.exp2(mm(feat, right_ref[...]))
        if n == 2:
            kern = kern * weight_ref[0, 0]
        total -= dot3(kern, ref[0:BLK, :])
    part_ref[...] = total


def weights_kernel(weight_ref, coeffs_ref, *refs):
    msgs = [refs[3 * n:3 * n + 3] for n in range(3)]
    prod_ref, right_ref = refs[9:]
    ch, cl = split2(coeffs_ref[...])
    for n in range(3):
        for p, (m, first, point) in enumerate(PLACES):
            ref, at = msgs[n][m], n * SIDE + p
            right_features(ref[point:point + DIM, :], right_ref.at[at])
            test = ref[first:first + BLK, :]
            if n == 2:
                test = test * weight_ref[0, 0]
            th, tl = split2(test)
            hi, lo = split2(mm(th, ch, NT) + (mm(th, cl, NT) + mm(tl, ch, NT)))
            prod_ref[at, 0:BLK, :] = hi
            prod_ref[at, BLK:, :] = lo


def near_kernel(targets, feat_ref, prod_ref, right_ref, *refs):
    outs, (acc, buf_a, buf_b) = refs[:len(targets)], refs[len(targets):]
    acc[...] = jnp.zeros_like(acc)
    total = len(targets) * COUNT

    def left(t):
        i = t // COUNT
        return feat_ref[targets[0] + i * (targets[-1] - targets[0])]

    def entries(t, buf):
        k = jnp.exp2(mm(left(t), right_ref[t % COUNT]))
        hi = k.astype(BF16)
        buf[:, BLK:] = hi
        buf[:, 0:BLK] = (k - hi.astype(F32)).astype(BF16)

    def fold(t, buf):
        b = t % COUNT
        acc[t // COUNT] += mm(buf[...], prod_ref[b]) + mm(buf[:, BLK:], prod_ref[b, 0:BLK, :])

    entries(0, buf_a)

    @pl.loop(0, total // 2)
    def _(u):
        t = 2 * u
        entries(t + 1, buf_b)
        fold(t, buf_a)
        entries(jnp.minimum(t + 2, total - 1), buf_a)
        fold(t + 1, buf_b)

    for i in range(len(targets)):
        outs[i][...] = acc[i]


def call(kernel, outs, n_smem, n_vmem, scratch=(), name=None, flops=0, trans=0):
    return pl.pallas_call(
        kernel,
        out_shape=[jax.ShapeDtypeStruct(s, t) for s, t in outs],
        in_specs=[pl.BlockSpec(memory_space=pltpu.SMEM)] * n_smem
        + [pl.BlockSpec(memory_space=VMEM)] * n_vmem,
        out_specs=[pl.BlockSpec(memory_space=VMEM)] * len(outs),
        scratch_shapes=list(scratch),
        compiler_params=pltpu.CompilerParams(vmem_limit_bytes=50 * 2**20),
        cost_estimate=pl.CostEstimate(flops=flops, bytes_accessed=4 * 2**20, transcendentals=trans),
        name=name,
    )


def near(targets, feats, prods, rights):
    return call(
        functools.partial(near_kernel, targets),
        [((BLK, RANK), F32)] * len(targets), 0, 3,
        [VMEM((len(targets), BLK, RANK), F32), VMEM((BLK, 2 * BLK), BF16), VMEM((BLK, 2 * BLK), BF16)],
        name="near", flops=10**6, trans=0,
    )(feats, prods, rights)


SOLVE_SCRATCH = [VMEM((RANK, RANK), F32), VMEM((RANK, RANK), F32)]


def inverse_gram(picked, err_ref, inv_ref):
    gram = dot6(picked, picked, NT)
    eye = (
        lax.broadcasted_iota(jnp.int32, (RANK, RANK), 0)
        == lax.broadcasted_iota(jnp.int32, (RANK, RANK), 1)
    ).astype(F32)
    shift = jnp.sum(gram * eye) / RANK + 1e-06
    gram = gram + shift * eye
    bound = jnp.max(jnp.sum(jnp.abs(gram), axis=0, keepdims=True))
    alpha = 2.0 / (jnp.full((1, 1), 1.0, F32) * (bound + shift))
    err_ref[...] = eye - alpha * gram
    inv_ref[...] = alpha * eye

    def step(state):
        n, _ = state
        err = err_ref[...]
        eh, el = split2(err)
        ih, il = split2(inv_ref[...])
        inv_ref[...] += mm(ih, eh) + (mm(ih, el) + mm(il, eh))
        sq = mm(eh, eh) + (mm(eh, el) + mm(el, eh))
        err_ref[...] = sq
        return n + 1, jnp.sum(sq * sq)

    lax.while_loop(lambda st: (st[0] < 24) & (st[1] > 1e-6), step, (jnp.int32(0), jnp.float32(1e9)))
    for _ in range(2):
        inv = inv_ref[...]
        inv_ref[...] = inv + dot3(inv, eye - dot6(gram, inv))
    return inv_ref[...]


def solve_kernel(picked_ref, coeffs_ref, err_ref, inv_ref):
    picked = picked_ref[...]
    coeffs_ref[...] = dot3(inverse_gram(picked, err_ref, inv_ref), picked)


def basis_kernel(samp_ref, test_ref, coeffs_ref, *refs):
    parts, (basis_ref, proj_ref) = refs[:SIDE], refs[SIDE:]
    near_field = (parts[0][...] + parts[1][...]) + (parts[2][...] + parts[3][...])
    basis = dot3(samp_ref[...], coeffs_ref[...], NT) - near_field
    basis_ref[...] = basis
    proj_ref[...] = dot3(basis.T, test_ref[...])


def coupling(a, b):
    def norm3(v):
        return split3(v * v)

    ones = jnp.ones((RANK, DIM), BF16)
    inner = dot6(a, b, NT)
    na = sum(mm(p, ones, NT) for p in norm3(a))
    nb = sum(mm(ones, p, NT) for p in norm3(b))
    return jnp.exp2(-SCALE * (na + nb - 2.0 * inner))


EXT = SAMP + 2 * DIM


def merge_kernel(top, share, info_ref, piv_ref, *refs):
    if top:
        pick_ref, skel_ref, proj_own, first, other, share_ref, stack_ref, err_ref, inv_ref = refs
        core0 = info_ref[0, 2] == 0
        peer_pick = jnp.where(core0, first[:, :SAMP], other[:, :SAMP])
        peer_proj = jnp.where(core0, other[:, :SAMP], first[:, :SAMP])
        peer_skel = first[:, SAMP:]
    else:
        (pick_ref, skel_ref, proj_own, pick_peer, skel_peer, proj_peer) = refs[:6]
        (share_ref, picked_ref, skel_out, proj_ref, send_ref, stack_ref, err_ref, inv_ref) = refs[6:]
        peer_pick, peer_proj, peer_skel = pick_peer[...], proj_peer[...], skel_peer[...]
    lower = info_ref[0, 0] == 0

    def order(own, peer):
        return jnp.where(lower, own, peer), jnp.where(lower, peer, own)

    pick_a, pick_b = order(pick_ref[...], peer_pick)
    proj_a, proj_b = order(proj_own[...], peer_proj)
    skel_a, skel_b = order(skel_ref[...], peer_skel)
    stack_ref[0:RANK, :SAMP] = pick_a - dot3(coupling(skel_a[:, :DIM], skel_b[:, :DIM]), proj_b)
    stack_ref[RANK:, :SAMP] = pick_b - dot3(coupling(skel_b[:, :DIM], skel_a[:, :DIM]), proj_a)
    stack_ref[0:RANK, SAMP:] = skel_a
    stack_ref[RANK:, SAMP:] = skel_b
    one_hot = jnp.where(
        piv_ref[...] == lax.broadcasted_iota(jnp.int32, (RANK, 2 * RANK), 1), 1.0, 0.0
    ).astype(BF16)
    picked_all = pick(one_hot, stack_ref[...])
    picked = picked_all[:, :SAMP]
    coeffs = dot3(inverse_gram(picked, err_ref, inv_ref), picked)
    rows = stack_ref[pl.ds(pl.multiple_of(info_ref[0, 1], 8), share), :SAMP]
    share_ref[...] = dot3(rows, coeffs, NT)
    if not top:
        picked_ref[...] = picked
        skel_out[...] = picked_all[:, SAMP:]
        basis_t = dot3(coeffs, stack_ref[:, :SAMP], NT)
        proj = dot3(basis_t[:, :RANK], proj_a) + dot3(basis_t[:, RANK:], proj_b)
        proj_ref[...] = proj
        send_ref[:, :SAMP] = jnp.where(lower, picked, proj)
        send_ref[:, SAMP:] = picked_all[:, SAMP:]


def merge(top, share, info, pivots, *node):
    outs = [(share, RANK)]
    if not top:
        outs += [(RANK, SAMP), (RANK, 2 * DIM), (RANK, SAMP), (RANK, EXT)]
    return call(
        functools.partial(merge_kernel, top, share),
        [(o, F32) for o in outs], 1, 1 + len(node),
        [VMEM((2 * RANK, EXT), F32), *SOLVE_SCRATCH],
        name="merge_top" if top else "merge_mid",
        flops=3 * 10**9,
    )(info, pivots.reshape(RANK, 1), *node)


def every_row(part):
    return lax.all_to_all(jnp.broadcast_to(part[None], (16, *part.shape)), "row", 0, 0)


def sum_row(part, between=None):
    share = part.shape[0] // 16
    parts = lax.all_to_all(part.reshape(16, share, -1), "row", 0, 0)
    mine = jnp.sum(parts, axis=0)
    if between is not None:
        mine, between = lax.optimization_barrier((mine, between))
    return every_row(mine).reshape(part.shape), between


def body(points, samples, test_matrix, near_mask, leaf_pivots, mid_pivots, top_pivots):
    leaf = lax.axis_index("leaf")
    row = lax.axis_index("row")
    core, x, y = leaf & 1, row >> 2, row & 3
    xt = points.T
    pivots = leaf_pivots[0].reshape(RANK, 1)
    weight = jnp.where(core == 0, near_mask[0, 0], near_mask[0, 1]).astype(F32).reshape(1, 1)

    def relay(message):
        return [message, lax.ppermute(message, "leaf", SIBLING), lax.ppermute(message, "leaf", OUTER)]

    message_0 = relay(jnp.concatenate([test_matrix, xt], axis=0))
    test_1 = lax.ppermute(test_matrix, "row", along_x(1))
    test_3 = lax.ppermute(test_matrix, "row", along_x(3))
    points_all = every_row(xt)

    def points_from(k):
        return lax.dynamic_index_in_dim(points_all, (x + SIDE - k & 3) << 2 | y, 0, keepdims=False)

    feats, part, skel = call(
        pivot_kernel,
        [((SIDE, BLK, 4 * DIM), BF16), ((RANK, SAMP), F32), ((RANK, 2 * DIM), F32)], 2, 6,
        [VMEM((4 * DIM, BLK), BF16)], name="pivot", flops=3 * 10**9,
    )(row.reshape(1, 1), weight, pivots, points_all, samples, *message_0)
    late, part, test_1, test_3 = lax.optimization_barrier((test_matrix, part, test_1, test_3))
    test_2 = lax.ppermute(late, "row", along_x(2))
    message_1 = jnp.concatenate([test_1, test_3, points_from(1), points_from(3)], axis=0)
    message_1, part = lax.optimization_barrier((message_1, part))
    message_1 = relay(message_1)
    message_2 = jnp.concatenate([test_2, points_from(2)], axis=0)
    picked, message_2 = sum_row(part, message_2)
    message_2 = relay(message_2)
    (coeffs,) = call(
        solve_kernel, [((RANK, SAMP), F32)], 0, 1, SOLVE_SCRATCH, name="solve", flops=3 * 10**9
    )(picked)
    picked_sib = lax.ppermute(picked, "leaf", SIBLING)
    skel_sib = lax.ppermute(skel, "leaf", SIBLING)

    messages = [m[n] for n in range(3) for m in (message_0, message_1, message_2)]
    prods, rights = call(
        weights_kernel,
        [((COUNT, 2 * BLK, RANK), BF16), ((COUNT, 4 * DIM, BLK), BF16)], 1, 10,
        name="weights", flops=6 * 10**9,
    )(weight, coeffs, *messages)
    (sum_2,) = near((3,), feats, prods, rights)
    sum_2 = lax.ppermute(sum_2, "row", along_y(-2))
    sum_1, sum_3 = near((1, 2), feats, prods, rights)
    sum_1 = lax.ppermute(sum_1, "row", along_y(-1))
    sum_3 = lax.ppermute(sum_3, "row", along_y(-3))
    (sum_0,) = near((0,), feats, prods, rights)
    leaf_basis, proj = call(
        basis_kernel, [((BLK, RANK), F32), ((RANK, SAMP), F32)], 0, 3 + SIDE, name="basis", flops=10**9
    )(samples, test_matrix, coeffs, sum_0, sum_1, sum_2, sum_3)
    proj, _ = sum_row(proj)
    proj_sib = lax.ppermute(proj, "leaf", SIBLING)

    def info(lower, first):
        return jnp.stack([lower, first, core]).astype(jnp.int32).reshape(1, 3)

    mid_row = lax.dynamic_index_in_dim(mid_pivots, leaf >> 1, 0, keepdims=False)
    top_row = lax.dynamic_index_in_dim(top_pivots, leaf >> 2, 0, keepdims=False)
    mid_share, top_share = RANK // 16, RANK // 32
    mid_basis, picked, skel, proj, send = merge(
        False, mid_share, info(core, core * RANK + row * mid_share), mid_row,
        picked, skel, proj, picked_sib, skel_sib, proj_sib,
    )
    first = lax.ppermute(send, "leaf", COUSIN)
    other = lax.ppermute(first, "leaf", SIBLING)
    second = leaf >> 1 & 1
    (top_basis,) = merge(
        True, top_share, info(second, second * RANK + core * (RANK // 2) + row * top_share), top_row,
        picked, skel, proj, first, other,
    )
    return (leaf_basis, mid_basis, top_basis)


def solution(mesh):
    split = P(("leaf", "row"), None)
    return jax.shard_map(
        body,
        mesh=mesh,
        in_specs=(split, split, split, P("leaf", None), P("leaf", None), P(), P()),
        out_specs=(split, split, split),
        check_vma=False,
    )
```

time: 320 us -> 279 us (0.87); the launches traced: 315 us -> 278 us
  Pallas kernels: 133 us -> 102 us
  starting transfers between devices: 65.4 us -> 44.4 us
  waiting for transfers between devices: 52.2 us -> 63.8 us
  local copies, waits for them, and re-layouts: 16.5 us -> 8.72 us
  blocking collectives: 44.6 us -> 50.6 us
  other arithmetic: 0.23 us -> 6.11 us
    pallas_call x11 -> x9, Pallas kernels: 133 us -> 102 us  [the longest x3 45.8 us: near(): call(functools.partial(near_kernel, targets), [((BLK, RANK), F32)] * len(...]
    ppermute x26 -> x13, starting transfers between devices: 51.4 us -> 22.7 us  [the longest x3 10.4 us: relay(): lax.ppermute(message, 'leaf', OUTER)]
    all_to_all x2, blocking collectives: 28.3 us -> 37.1 us  [sum_row(): parts = lax.all_to_all(part.reshape(16, share, -1), 'row', 0, 0)]
    unnamed x62 -> x20, local copies, waits for them, and re-layouts: 11.8 us -> 3.25 us
    all_to_all x1 -> x2, waiting for transfers between devices: 5.9 us -> 14.4 us  [every_row(): lax.all_to_all(jnp.broadcast_to(part[None], (16, *part.shape)), 'row', 0, 0)]
    all_to_all x1 -> x2, starting transfers between devices: 4.33 us -> 11.5 us  [every_row(): lax.all_to_all(jnp.broadcast_to(part[None], (16, *part.shape)), 'row', 0, 0)]
    concatenate x0 -> x3, other arithmetic: none -> 5.89 us  [the longest x1 3.16 us: body(): jnp.concatenate([test_1, test_3, points_from(1), points_from(3)], axis=0)]
    ppermute x26 -> x13, waiting for transfers between devices: 29.1 us -> 32.9 us  [the longest x1 13 us: body(): test_1 = lax.ppermute(test_matrix, 'row', along_x(1))]
  transfers between devices with their start and end apart: 31 -> 19, of which waited for: 8 -> 8; matrix products, arithmetic and copies ran while one was open for 2% -> 3% of each run, Pallas kernels for 31% -> 10%
where the time goes in v2:
time: 279 us; the launch traced here: 278 us
  Pallas kernels  102 us (37%)
  waiting for transfers between devices  63.8 us (23%)
  blocking collectives  50.6 us (18%)
  starting transfers between devices  44.4 us (16%)
  local copies, waits for them, and re-layouts  8.72 us (3%)
  other arithmetic  6.11 us (2%)
    pallas_call x3, Pallas kernels, near(): call(functools.partial(near_kernel, targets), [((BLK, RANK), F32)] * len(...  45.8 us
    all_to_all x2, blocking collectives, sum_row(): parts = lax.all_to_all(part.reshape(16, share, -1), 'row', 0, 0)  37.1 us
    pallas_call x2, Pallas kernels, merge(): call(functools.partial(merge_kernel, top, share), [(o, F32) for o in outs...  25.5 us
    ppermute x1, waiting for transfers between devices, body(): first = lax.ppermute(send, 'leaf', COUSIN)  15 us
    all_to_all x2, waiting for transfers between devices, every_row(): lax.all_to_all(jnp.broadcast_to(part[None], (16, *part.shape)), 'row', 0, 0)  14.4 us
    all_to_all x1, blocking collectives, every_row(): lax.all_to_all(jnp.broadcast_to(part[None], (16, *part.shape)), 'row', 0, 0)  13.5 us
    pallas_call x1, Pallas kernels, body(): call(weights_kernel, [((COUNT, 2 * BLK, RANK), BF16), ((COUNT, 4 * DIM, B...  13.5 us
    ppermute x1, waiting for transfers between devices, body(): test_1 = lax.ppermute(test_matrix, 'row', along_x(1))  13 us
  transfers between devices with their start and end apart: 19, of which 8 were waited for; matrix products, arithmetic and copies ran while one was open for 3% of the time, Pallas kernels for 10%

profile of v2, /device:TPU:1, one launch (start us, length us, event | category | flops | bytes accessed | tf_op | source)
XLA Modules:
  0.0 278.4 jit_solution(13205297658699634110)
XLA Ops:
  0.6 2.5 broadcast_in_dim.6
  3.1 7.8 %all-to-all-start = ((f32[16,64,512]{2,1,0:T(8,128)}), f32[16,64,512]{2,1,0:T(8,128)}, u32[]{:S(2)}, u32[]{:S(2)}) async-start(f32[16,64,512]{2,1,0:T(8,128)} %broadcast_in_dim.6), calls=%async_computation | async-start | bytes 4194304 | tf_op jit(solution)/shard_map/all_to_all | solution.py:332
  11.0 1.4 pad_maximum_fusion.1.own_ref.refs_0_
  12.4 1.0 collective-permute-start
  13.4 3.4 %collective-permute-start.1 = (f32[576,512]{1,0:T(8,128)S(1)}, f32[576,512]{1,0:T(8,128)}, u32[]{:S(2)}, u32[]{:S(2)}) collective-permute-start(f32[576,512]{1,0:T(8,128)S(1)} %pad_maximum_fusion.1.own_ref.refs_0_), channel_id=1, source_target_pairs={{16,32},{32,16},{48,64},{64,48},{80,96},{96,80},{17,33},{33,17},{4... | collective-permute-start | bytes 3538952 | tf_op jit(solution)/shard_map/ppermute | solution.py:353
  16.9 1.7 collective-permute-start.2
  18.5 1.3 collective-permute-start.3
  19.8 0.6 fusion.2
  21.9 9.4 %collective-permute-done.1.out_ref.refs_6_ = f32[576,512]{1,0:T(8,128)} collective-permute-done((f32[576,512]{1,0:T(8,128)S(1)}, f32[576,512]{1,0:T(8,128)}, u32[]{:S(2)}, u32[]{:S(2)}) %collective-permute-start.1) | collective-permute-done | bytes 1179680 | tf_op jit(solution)/shard_map/ppermute | solution.py:353
  31.3 7.2 %all-to-all-done.all_ref = f32[16,64,512]{2,1,0:T(8,128)} async-done(((f32[16,64,512]{2,1,0:T(8,128)}), f32[16,64,512]{2,1,0:T(8,128)}, u32[]{:S(2)}, u32[]{:S(2)}) %all-to-all-start) | async-done | bytes 2097184 | tf_op jit(solution)/shard_map/all_to_all | solution.py:332
  38.6 6.9 %pivot.1 = (bf16[4,512,256]{2,1,0:T(8,128)(2,1)S(1)}, f32[256,512]{1,0:T(8,128)S(1)}, f32[256,128]{1,0:T(8,128)S(1)}) custom-call(s32[1,1]{1,0:T(1,128)} %bitcast.info_ref, f32[1,1]{1,0:T(1,128)} %bitcast.3.weight_ref, s32[256,1]{1,0:T(8,128)S(1)} %copy.10.piv_ref, f32[16,64,512]{2,1,0:T(8,128)} %all-to-all-done.all_ref, f32[512,512]{1,0:T(8,128)S(1)} %copy-done.1, ...), custom_call_target="tpu_custom_call" | custom-call | flops 3000000000 | bytes 4194304 | tf_op jit(solution)/shard_map/pivot/pallas_call | solution.py:363
  45.5 13.0 %collective-permute-done.2 = f32[512,512]{1,0:T(8,128)} collective-permute-done((f32[512,512]{1,0:T(8,128)}, f32[512,512]{1,0:T(8,128)}, u32[]{:S(2)}, u32[]{:S(2)}) %collective-permute-start.2) | collective-permute-done | bytes 1048608 | tf_op jit(solution)/shard_map/ppermute | solution.py:356
  58.5 2.1 collective-permute-start.4
  60.6 1.1 dynamic-slice_bitcast_fusion
  61.7 3.2 %pad_maximum_fusion.refs_1_ = f32[1152,512]{1,0:T(8,128)} fusion(f32[64,512]{1,0:T(8,128)S(1)} %get-tuple-element.48, f32[64,512]{1,0:T(8,128)S(1)} %get-tuple-element.49, f32[512,512]{1,0:T(8,128)} %collective-permute-done.3, f32[512,512]{1,0:T(8,128)} %collective-permute-done.2), kind=kLoop, calls=%fused_computation | loop fusion | flops 1769472 | bytes 4718592 | tf_op jit(solution)/shard_map/concatenate | solution.py:370
  64.8 2.1 collective-permute-start.5
  66.9 3.4 %collective-permute-start.7 = (f32[1152,512]{1,0:T(8,128)}, f32[1152,512]{1,0:T(8,128)}, u32[]{:S(2)}, u32[]{:S(2)}) collective-permute-start(f32[1152,512]{1,0:T(8,128)} %pad_maximum_fusion.refs_1_), channel_id=1, source_target_pairs={{16,32},{32,16},{48,64},{64,48},{80,96},{96,80},{17,33},{33,17},{4... | collective-permute-start | bytes 7077896 | tf_op jit(solution)/shard_map/ppermute | solution.py:353
  70.4 23.0 %all_to_all.25 = f32[16,16,512]{2,1,0:T(8,128)S(1)} all-to-all(f32[16,16,512]{2,1,0:T(8,128)S(1)} %bitcast.33), channel_id=1, replica_groups=mesh['leaf'=8,'row'=16] {'row'}, dimensions={0} | all-to-all | bytes 1048576 | tf_op jit(solution)/shard_map/all_to_all | solution.py:337
  93.4 1.3 pad_maximum_fusion.2.refs_2_
  94.7 0.5 collective-permute-start.6
  95.2 3.5 %collective-permute-start.8 = (f32[576,512]{1,0:T(8,128)S(1)}, f32[576,512]{1,0:T(8,128)S(1)}, u32[]{:S(2)}, u32[]{:S(2)}) collective-permute-start(f32[576,512]{1,0:T(8,128)S(1)} %pad_maximum_fusion.2.refs_2_), channel_id=1, source_target_pairs={{16,32},{32,16},{48,64},{64,48},{80,96},{96,80},{17,33},{33,17},{4... | collective-permute-start | bytes 3538952 | tf_op jit(solution)/shard_map/ppermute | solution.py:353
  98.8 13.5 %all_to_all.26 = f32[16,16,512]{2,1,0:T(8,128)S(1)} all-to-all(f32[16,16,512]{2,1,0:T(8,128)S(1)} %broadcast_in_dim.7), channel_id=1, replica_groups=mesh['leaf'=8,'row'=16] {'row'}, dimensions={0} | all-to-all | bytes 1048576 | tf_op jit(solution)/shard_map/all_to_all | solution.py:332
  112.3 7.4 %solve.1.coeffs_ref = f32[256,512]{1,0:T(8,128)S(1)} custom-call(f32[256,512]{1,0:T(8,128)S(1)} %bitcast.28), custom_call_target="tpu_custom_call" | custom-call | flops 3000000000 | bytes 4194304 | tf_op jit(solution)/shard_map/solve/pallas_call | solution.py:376
  119.7 1.0 copy-done.8
  120.7 0.4 copy-done.9
  121.1 13.5 %weights.1 = (bf16[12,1024,256]{2,1,0:T(8,128)(2,1)}, bf16[12,256,512]{2,1,0:T(8,128)(2,1)}) custom-call(f32[1,1]{1,0:T(1,128)} %bitcast.3.weight_ref, f32[256,512]{1,0:T(8,128)S(1)} %solve.1.coeffs_ref, f32[576,512]{1,0:T(8,128)S(1)} %pad_maximum_fusion.1.own_ref.refs_0_, f32[1152,512]{1,0:T(8,128)} %pad_maximum_fusion.refs_1_, ...), custom_call_target="tpu_custom_call" | custom-call | flops 6000000000 | bytes 4194304 | tf_op jit(solution)/shard_map/weights/pallas_call | solution.py:383
  134.6 12.4 %near.5 = f32[512,256]{1,0:T(8,128)S(1)} custom-call(bf16[4,512,256]{2,1,0:T(8,128)(2,1)S(1)} %get-tuple-element.32.feat_ref, bf16[12,1024,256]{2,1,0:T(8,128)(2,1)} %get-tuple-element.35.prod_ref, bf16[12,256,512]{2,1,0:T(8,128)(2,1)} %get-tuple-element.36.right_ref), custom_call_target="tpu_custom_call" | custom-call | flops 1000000 | bytes 4194304 | tf_op jit(solution)/shard_map/near/pallas_call | solution.py:209
  146.9 21.0 %near.4 = (f32[512,256]{1,0:T(8,128)S(1)}, f32[512,256]{1,0:T(8,128)S(1)}) custom-call(bf16[4,512,256]{2,1,0:T(8,128)(2,1)S(1)} %get-tuple-element.32.feat_ref, bf16[12,1024,256]{2,1,0:T(8,128)(2,1)} %get-tuple-element.35.prod_ref, bf16[12,256,512]{2,1,0:T(8,128)(2,1)} %get-tuple-element.36.right_ref), custom_call_target="tpu_custom_call" | custom-call | flops 1000000 | bytes 4194304 | tf_op jit(solution)/shard_map/near/pallas_call | solution.py:209
  168.0 0.9 collective-permute-start.10
  168.9 2.7 collective-permute-start.9
  171.6 12.4 %near.3.refs_0_ = f32[512,256]{1,0:T(8,128)S(1)} custom-call(bf16[4,512,256]{2,1,0:T(8,128)(2,1)S(1)} %get-tuple-element.32.feat_ref, bf16[12,1024,256]{2,1,0:T(8,128)(2,1)} %get-tuple-element.35.prod_ref, bf16[12,256,512]{2,1,0:T(8,128)(2,1)} %get-tuple-element.36.right_ref), custom_call_target="tpu_custom_call" | custom-call | flops 1000000 | bytes 4194304 | tf_op jit(solution)/shard_map/near/pallas_call | solution.py:209
  184.0 9.0 %collective-permute-done.11.refs_3_ = f32[512,256]{1,0:T(8,128)S(1)} collective-permute-done((f32[512,256]{1,0:T(8,128)S(1)}, f32[512,256]{1,0:T(8,128)S(1)}, u32[]{:S(2)}, u32[]{:S(2)}) %collective-permute-start.11) | collective-permute-done | bytes 524320 | tf_op jit(solution)/shard_map/ppermute | solution.py:392
  193.0 3.4 %basis.1 = (f32[512,256]{1,0:T(8,128)}, f32[256,512]{1,0:T(8,128)S(1)}) custom-call(f32[512,512]{1,0:T(8,128)} %samp_ref.3, f32[512,512]{1,0:T(8,128)} %test_ref.1, f32[256,512]{1,0:T(8,128)S(1)} %solve.1.coeffs_ref, f32[512,256]{1,0:T(8,128)S(1)} %near.3.refs_0_, f32[512,256]{1,0:T(8,128)S(1)} %collective-permute-done.9.refs_1_, ...), custom_call_target="tpu_custom_call" | custom-call | flops 1000000000 | bytes 4194304 | tf_op jit(solution)/shard_map/basis/pallas_call | solution.py:394
  196.4 14.1 %all_to_all.27 = f32[16,16,512]{2,1,0:T(8,128)S(1)} all-to-all(f32[16,16,512]{2,1,0:T(8,128)S(1)} %bitcast.34), channel_id=1, replica_groups=mesh['leaf'=8,'row'=16] {'row'}, dimensions={0} | all-to-all | bytes 1048576 | tf_op jit(solution)/shard_map/all_to_all | solution.py:337
  210.6 0.9 broadcast_in_dim.8
  211.4 3.7 %all-to-all-start.4 = ((f32[16,16,512]{2,1,0:T(8,128)}), f32[16,16,512]{2,1,0:T(8,128)S(1)}, u32[]{:S(2)}, u32[]{:S(2)}) async-start(f32[16,16,512]{2,1,0:T(8,128)} %broadcast_in_dim.8), calls=%async_computation.4 | async-start | bytes 1048576 | tf_op jit(solution)/shard_map/all_to_all | solution.py:332
  215.2 2.0 collective-permute-start.12
  217.2 7.2 %all-to-all-done.4 = f32[16,16,512]{2,1,0:T(8,128)S(1)} async-done(((f32[16,16,512]{2,1,0:T(8,128)}), f32[16,16,512]{2,1,0:T(8,128)S(1)}, u32[]{:S(2)}, u32[]{:S(2)}) %all-to-all-start.4) | async-done | bytes 524320 | tf_op jit(solution)/shard_map/all_to_all | solution.py:332
  224.4 3.2 %collective-permute-start.14 = (f32[256,512]{1,0:T(8,128)S(1)}, f32[256,512]{1,0:T(8,128)S(1)}, u32[]{:S(2)}, u32[]{:S(2)}) collective-permute-start(f32[256,512]{1,0:T(8,128)S(1)} %bitcast.31), channel_id=1, source_target_pairs={{0,16},{16,0},{32,48},{48,32},{64,80},{80,64},{96,112},{112,96},{1... | collective-permute-start | bytes 1572872 | tf_op jit(solution)/shard_map/ppermute | solution.py:398
  227.8 1.5 collective-permute-done.13.refs_4_
  229.3 13.3 %merge_mid.1 = (f32[16,256]{1,0:T(8,128)}, f32[256,512]{1,0:T(8,128)S(1)}, f32[256,128]{1,0:T(8,128)S(1)}, f32[256,512]{1,0:T(8,128)S(1)}, f32[256,640]{1,0:T(8,128)}) custom-call(s32[1,3]{1,0:T(1,128)S(1)} %add_bitcast_fusion.info_ref, s32[256,1]{1,0:T(8,128)S(1)} %copy.11.piv_ref, f32[256,512]{1,0:T(8,128)S(1)} %bitcast.30, ...), custom_call_target="tpu_custom_call" | custom-call | flops 3000000000 | bytes 4194304 | tf_op jit(solution)/shard_map/merge_mid/pallas_call | solution.py:322
  242.6 0.8 copy-done.2
  243.4 4.1 %collective-permute-start.15 = (f32[256,640]{1,0:T(8,128)}, f32[256,640]{1,0:T(8,128)S(1)}, u32[]{:S(2)}, u32[]{:S(2)}) collective-permute-start(f32[256,640]{1,0:T(8,128)} %get-tuple-element.46), channel_id=1, source_target_pairs={{0,32},{16,48},{32,0},{48,16},{64,96},{80,112},{96,64},{112,80},{1... | collective-permute-start | bytes 1966088 | tf_op jit(solution)/shard_map/ppermute | solution.py:410
  247.5 15.0 %collective-permute-done.15.refs_3_ = f32[256,640]{1,0:T(8,128)S(1)} collective-permute-done((f32[256,640]{1,0:T(8,128)}, f32[256,640]{1,0:T(8,128)S(1)}, u32[]{:S(2)}, u32[]{:S(2)}) %collective-permute-start.15) | collective-permute-done | bytes 655392 | tf_op jit(solution)/shard_map/ppermute | solution.py:410
  262.5 0.9 collective-permute-start.16
  263.7 1.5 collective-permute-done.16.refs_4_
  265.2 1.0 copy-done.3
  266.2 12.2 %merge_top.1 = f32[8,256]{1,0:T(8,128)} custom-call(s32[1,3]{1,0:T(1,128)S(1)} %add_bitcast_fusion.1.info_ref, s32[256,1]{1,0:T(8,128)S(1)} %copy.12.piv_ref, f32[256,512]{1,0:T(8,128)S(1)} %get-tuple-element.43.refs_0_, f32[256,128]{1,0:T(8,128)S(1)} %get-tuple-element.44.refs_1_, f32[256,512]{1,0:T(8,128)S(1)} %copy-done.3, ...), custom_call_target="tpu_custom_call" | custom-call | flops 3000000000 | bytes 4194304 | tf_op jit(solution)/shard_map/merge_top/pallas_call | solution.py:322
  (39 shorter events, 0.8 us)
Async XLA Ops:
  0.6 227.0 %copy-start = (s32[4,256]{1,0:T(4,128)S(1)}, s32[4,256]{1,0:T(4,128)}, u32[]{:S(2)}) copy-start(s32[4,256]{1,0:T(4,128)} %param.12) | copy-start | bytes 12292
  3.1 7.8 %copy-start.4 = (f32[512,64]{0,1:T(8,128)S(1)}, f32[512,64]{0,1:T(8,128)}, u32[]{:S(2)}) copy-start(f32[512,64]{0,1:T(8,128)} %param.7) | copy-start | bytes 393220
  3.1 35.4 %all-to-all-start = ((f32[16,64,512]{2,1,0:T(8,128)}), f32[16,64,512]{2,1,0:T(8,128)}, u32[]{:S(2)}, u32[]{:S(2)}) async-start(f32[16,64,512]{2,1,0:T(8,128)} %broadcast_in_dim.6), calls=%async_computation | async-start | bytes 4194304 | tf_op jit(solution)/shard_map/all_to_all | solution.py:332
  10.9 8.9 %copy-start.5 = (s32[1,2]{1,0:T(1,128)S(1)}, s32[1,2]{1,0:T(1,128)}, u32[]{:S(2)}) copy-start(s32[1,2]{1,0:T(1,128)} %param.10) | copy-start | bytes 28
  10.9 10.8 %copy-start.6 = (s32[1,256]{1,0:T(1,128)S(1)}, s32[1,256]{1,0:T(1,128)}, u32[]{:S(2)}) copy-start(s32[1,256]{1,0:T(1,128)} %param.11) | copy-start | bytes 3076
  11.0 27.6 %copy-start.1 = (f32[512,512]{1,0:T(8,128)S(1)}, f32[512,512]{1,0:T(8,128)}, u32[]{:S(2)}) copy-start(f32[512,512]{1,0:T(8,128)} %samp_ref.3) | copy-start | bytes 3145732
  12.4 9.5 %collective-permute-start = (f32[576,512]{1,0:T(8,128)S(1)}, f32[576,512]{1,0:T(8,128)}, u32[]{:S(2)}, u32[]{:S(2)}) collective-permute-start(f32[576,512]{1,0:T(8,128)S(1)} %pad_maximum_fusion.1.own_ref.refs_0_), channel_id=1, source_target_pairs={{0,16},{16,0},{32,48},{48,32},{64,80},{80,64},{96,112},{112,96},{1... | collective-permute-start | bytes 3538952 | tf_op jit(solution)/shard_map/ppermute | solution.py:353
  13.4 17.9 %collective-permute-start.1 = (f32[576,512]{1,0:T(8,128)S(1)}, f32[576,512]{1,0:T(8,128)}, u32[]{:S(2)}, u32[]{:S(2)}) collective-permute-start(f32[576,512]{1,0:T(8,128)S(1)} %pad_maximum_fusion.1.own_ref.refs_0_), channel_id=1, source_target_pairs={{16,32},{32,16},{48,64},{64,48},{80,96},{96,80},{17,33},{33,17},{4... | collective-permute-start | bytes 3538952 | tf_op jit(solution)/shard_map/ppermute | solution.py:353
  16.9 41.6 %collective-permute-start.2 = (f32[512,512]{1,0:T(8,128)}, f32[512,512]{1,0:T(8,128)}, u32[]{:S(2)}, u32[]{:S(2)}) collective-permute-start(f32[512,512]{1,0:T(8,128)} %test_ref.1), channel_id=1, source_target_pairs={{0,4},{1,5},{2,6},{3,7},{4,8},{5,9},{6,10},{7,11},{8,12},{9,13},{1... | collective-permute-start | bytes 3145736 | tf_op jit(solution)/shard_map/ppermute | solution.py:356
  18.5 40.0 %collective-permute-start.3 = (f32[512,512]{1,0:T(8,128)}, f32[512,512]{1,0:T(8,128)}, u32[]{:S(2)}, u32[]{:S(2)}) collective-permute-start(f32[512,512]{1,0:T(8,128)} %test_ref.1), channel_id=1, source_target_pairs={{0,12},{1,13},{2,14},{3,15},{4,0},{5,1},{6,2},{7,3},{8,4},{9,5},{1... | collective-permute-start | bytes 3145736 | tf_op jit(solution)/shard_map/ppermute | solution.py:357
  58.5 34.9 %collective-permute-start.4 = (f32[512,512]{1,0:T(8,128)}, f32[512,512]{1,0:T(8,128)}, u32[]{:S(2)}, u32[]{:S(2)}) collective-permute-start(f32[512,512]{1,0:T(8,128)} %test_ref.1), channel_id=1, source_target_pairs={{0,8},{1,9},{2,10},{3,11},{4,12},{5,13},{6,14},{7,15},{8,0},{9,1},... | collective-permute-start | bytes 3145736 | tf_op jit(solution)/shard_map/ppermute | solution.py:369
  64.8 54.9 %collective-permute-start.5 = (f32[1152,512]{1,0:T(8,128)}, f32[1152,512]{1,0:T(8,128)}, u32[]{:S(2)}, u32[]{:S(2)}) collective-permute-start(f32[1152,512]{1,0:T(8,128)} %pad_maximum_fusion.refs_1_), channel_id=1, source_target_pairs={{0,16},{16,0},{32,48},{48,32},{64,80},{80,64},{96,112},{112,96},{1... | collective-permute-start | bytes 7077896 | tf_op jit(solution)/shard_map/ppermute | solution.py:353
  66.9 52.8 %collective-permute-start.7 = (f32[1152,512]{1,0:T(8,128)}, f32[1152,512]{1,0:T(8,128)}, u32[]{:S(2)}, u32[]{:S(2)}) collective-permute-start(f32[1152,512]{1,0:T(8,128)} %pad_maximum_fusion.refs_1_), channel_id=1, source_target_pairs={{16,32},{32,16},{48,64},{64,48},{80,96},{96,80},{17,33},{33,17},{4... | collective-permute-start | bytes 7077896 | tf_op jit(solution)/shard_map/ppermute | solution.py:353
  94.7 25.0 %collective-permute-start.6 = (f32[576,512]{1,0:T(8,128)S(1)}, f32[576,512]{1,0:T(8,128)S(1)}, u32[]{:S(2)}, u32[]{:S(2)}) collective-permute-start(f32[576,512]{1,0:T(8,128)S(1)} %pad_maximum_fusion.2.refs_2_), channel_id=1, source_target_pairs={{0,16},{16,0},{32,48},{48,32},{64,80},{80,64},{96,112},{112,96},{1... | collective-permute-start | bytes 3538952 | tf_op jit(solution)/shard_map/ppermute | solution.py:353
  95.2 24.5 %collective-permute-start.8 = (f32[576,512]{1,0:T(8,128)S(1)}, f32[576,512]{1,0:T(8,128)S(1)}, u32[]{:S(2)}, u32[]{:S(2)}) collective-permute-start(f32[576,512]{1,0:T(8,128)S(1)} %pad_maximum_fusion.2.refs_2_), channel_id=1, source_target_pairs={{16,32},{32,16},{48,64},{64,48},{80,96},{96,80},{17,33},{33,17},{4... | collective-permute-start | bytes 3538952 | tf_op jit(solution)/shard_map/ppermute | solution.py:353
  119.7 1.0 copy-start.8
  119.7 1.4 copy-start.9
  168.0 16.0 %collective-permute-start.10 = (f32[512,256]{1,0:T(8,128)S(1)}, f32[512,256]{1,0:T(8,128)S(1)}, u32[]{:S(2)}, u32[]{:S(2)}) collective-permute-start(f32[512,256]{1,0:T(8,128)S(1)} %near.5), channel_id=1, source_target_pairs={{0,2},{1,3},{2,0},{3,1},{4,6},{5,7},{6,4},{7,5},{8,10},{9,11},{10,... | collective-permute-start | bytes 1572872 | tf_op jit(solution)/shard_map/ppermute | solution.py:389
  168.9 24.1 %collective-permute-start.11 = (f32[512,256]{1,0:T(8,128)S(1)}, f32[512,256]{1,0:T(8,128)S(1)}, u32[]{:S(2)}, u32[]{:S(2)}) collective-permute-start(f32[512,256]{1,0:T(8,128)S(1)} %get-tuple-element.38), channel_id=1, source_target_pairs={{0,1},{1,2},{2,3},{3,0},{4,5},{5,6},{6,7},{7,4},{8,9},{9,10},{10,1... | collective-permute-start | bytes 1572872 | tf_op jit(solution)/shard_map/ppermute | solution.py:392
  168.9 24.1 %collective-permute-start.9 = (f32[512,256]{1,0:T(8,128)S(1)}, f32[512,256]{1,0:T(8,128)S(1)}, u32[]{:S(2)}, u32[]{:S(2)}) collective-permute-start(f32[512,256]{1,0:T(8,128)S(1)} %get-tuple-element.37), channel_id=1, source_target_pairs={{0,3},{1,0},{2,1},{3,2},{4,7},{5,4},{6,5},{7,6},{8,11},{9,8},{10,9... | collective-permute-start | bytes 1572872 | tf_op jit(solution)/shard_map/ppermute | solution.py:391
  211.4 13.0 %all-to-all-start.4 = ((f32[16,16,512]{2,1,0:T(8,128)}), f32[16,16,512]{2,1,0:T(8,128)S(1)}, u32[]{:S(2)}, u32[]{:S(2)}) async-start(f32[16,16,512]{2,1,0:T(8,128)} %broadcast_in_dim.8), calls=%async_computation.4 | async-start | bytes 1048576 | tf_op jit(solution)/shard_map/all_to_all | solution.py:332
  215.2 14.2 %collective-permute-start.12 = (f32[256,512]{1,0:T(8,128)S(1)}, f32[256,512]{1,0:T(8,128)S(1)}, u32[]{:S(2)}, u32[]{:S(2)}) collective-permute-start(f32[256,512]{1,0:T(8,128)S(1)} %bitcast.29), channel_id=1, source_target_pairs={{0,16},{16,0},{32,48},{48,32},{64,80},{80,64},{96,112},{112,96},{1... | collective-permute-start | bytes 1572872 | tf_op jit(solution)/shard_map/ppermute | solution.py:379
  224.4 4.9 %collective-permute-start.14 = (f32[256,512]{1,0:T(8,128)S(1)}, f32[256,512]{1,0:T(8,128)S(1)}, u32[]{:S(2)}, u32[]{:S(2)}) collective-permute-start(f32[256,512]{1,0:T(8,128)S(1)} %bitcast.31), channel_id=1, source_target_pairs={{0,16},{16,0},{32,48},{48,32},{64,80},{80,64},{96,112},{112,96},{1... | collective-permute-start | bytes 1572872 | tf_op jit(solution)/shard_map/ppermute | solution.py:398
  227.6 1.7 collective-permute-start.13
  227.8 35.6 %copy-start.7 = (s32[2,256]{1,0:T(2,128)S(1)}, s32[2,256]{1,0:T(2,128)}, u32[]{:S(2)}) copy-start(s32[2,256]{1,0:T(2,128)} %param.13) | copy-start | bytes 6148
  242.6 0.8 copy-start.2
  243.4 19.1 %collective-permute-start.15 = (f32[256,640]{1,0:T(8,128)}, f32[256,640]{1,0:T(8,128)S(1)}, u32[]{:S(2)}, u32[]{:S(2)}) collective-permute-start(f32[256,640]{1,0:T(8,128)} %get-tuple-element.46), channel_id=1, source_target_pairs={{0,32},{16,48},{32,0},{48,16},{64,96},{80,112},{96,64},{112,80},{1... | collective-permute-start | bytes 1966088 | tf_op jit(solution)/shard_map/ppermute | solution.py:410
  262.5 2.6 collective-permute-start.16
  265.2 1.0 copy-start.3

commit v3 on v2

v3 whole, which is shorter than its diff:
```python
import functools
import math

import jax
import jax.numpy as jnp
from jax import lax
from jax.experimental import pallas as pl
from jax.experimental.pallas import tpu as pltpu
from jax.sharding import PartitionSpec as P

DIM = 64
RANK = 256
SAMP = 512
BLK = 512
SIDE = 4
SCALE = math.log2(math.e) / DIM
HIGHEST = lax.Precision.HIGHEST
F32, BF16 = jnp.float32, jnp.bfloat16
VMEM = pltpu.VMEM


def along_x(k):
    return [(4 * x + y, 4 * ((x + k) % 4) + y) for x in range(4) for y in range(4)]


def along_y(k):
    return [(4 * x + y, 4 * x + (y + k) % 4) for x in range(4) for y in range(4)]


SIBLING = [(i, i ^ 1) for i in range(8)]
OUTER = [(1, 2), (2, 1), (3, 4), (4, 3), (5, 6), (6, 5)]
COUSIN = [(i, i ^ 2) for i in range(8)]


NN = (((1,), (0,)), ((), ()))
NT = (((1,), (1,)), ((), ()))


def mm(a, b, dims=NN):
    return lax.dot_general(a, b, dims, preferred_element_type=F32)


def split2(a):
    hi = a.astype(BF16)
    return hi, (a - hi.astype(F32)).astype(BF16)


def split3(a):
    hi = a.astype(BF16)
    rest = a - hi.astype(F32)
    mid = rest.astype(BF16)
    return hi, mid, (rest - mid.astype(F32)).astype(BF16)


def dot3(a, b, dims=NN):
    ah, al = split2(a)
    bh, bl = split2(b)
    return mm(ah, bh, dims) + (mm(ah, bl, dims) + mm(al, bh, dims))


def dot6(a, b, dims=NN):
    ah, am, al = split3(a)
    bh, bm, bl = split3(b)
    return mm(ah, bh, dims) + (
        (mm(ah, bm, dims) + mm(am, bh, dims))
        + (mm(am, bm, dims) + (mm(ah, bl, dims) + mm(al, bh, dims)))
    )


def pick(one_hot, a):
    h, m, l = split3(a)
    return (mm(one_hot, h) + mm(one_hot, m)) + mm(one_hot, l)


SHIFTS = (1, 3, 2)
COUNT = 3 * SIDE


def norm_rows(xt, first):
    rows = lax.broadcasted_iota(jnp.int32, (DIM, BLK), 0)
    sq = jnp.sum(xt * xt, axis=0, keepdims=True) * (-SCALE)
    h, m, l = (v.astype(F32) for v in split3(sq))
    one = jnp.ones_like(sq)
    aux = jnp.zeros((DIM, BLK), F32)
    for n, part in enumerate((h, m, l, one, one, one) if first else (one, one, one, h, m, l)):
        aux = jnp.where(rows == n, part, aux)
    return aux


def left_features(xt):
    scaled = xt * (2.0 * SCALE)
    hi = scaled.astype(BF16).astype(F32)
    feat = jnp.concatenate([hi, hi, scaled - hi, norm_rows(xt, True)], axis=0)
    return feat.T.astype(BF16)


def right_features(xt, ref):
    hi, lo = split2(xt)
    ref[0:DIM, :] = hi
    ref[DIM:2 * DIM, :] = lo
    ref[2 * DIM:3 * DIM, :] = hi
    ref[3 * DIM:, :] = norm_rows(xt, False).astype(BF16)


def rows_of(start, piv_ref):
    column = lax.broadcasted_iota(jnp.int32, (RANK, BLK), 1)
    return jnp.where(piv_ref[...] == column + start, 1.0, 0.0).astype(BF16)


def skel_kernel(start_ref, piv_ref, points_ref, skel_ref):
    one_hot = rows_of(start_ref[0, 0], piv_ref)
    skel = sum(mm(one_hot, part, NT) for part in split3(points_ref[...]))
    skel_ref[...] = jnp.concatenate([skel, jnp.zeros((RANK, DIM), F32)], axis=1)


def feature_kernel(p0, p1, p2, p3, feat_ref):
    for i, ref in enumerate((p0, p1, p2, p3)):
        feat_ref[i] = left_features(ref[...])


def pivot_kernel(
    start_ref, weight_ref, piv_ref, skel_ref, samp_ref, own_ref, sib_ref, out_ref, part_ref, right_ref
):
    skel = skel_ref[:, :DIM]
    scaled = skel * (2.0 * SCALE)
    hi = scaled.astype(BF16).astype(F32)
    lane = lax.broadcasted_iota(jnp.int32, (RANK, DIM), 1)
    sq = jnp.sum(skel * skel, axis=1, keepdims=True) * (-SCALE)
    aux = jnp.where(lane < 6, 1.0, 0.0)
    for n, part in enumerate(split3(sq)):
        aux = jnp.where(lane == n, part.astype(F32), aux)
    feat = jnp.concatenate([hi, hi, scaled - hi, aux], axis=1).astype(BF16)
    total = pick(rows_of(start_ref[0, 0], piv_ref), samp_ref[...])
    for n, ref in enumerate((own_ref, sib_ref, out_ref)):
        right_features(ref[BLK:, :], right_ref)
        kern = jnp.exp2(mm(feat, right_ref[...]))
        if n == 2:
            kern = kern * weight_ref[0, 0]
        total -= dot3(kern, ref[0:BLK, :])
    part_ref[...] = total


def far_kernel(targets, weight_ref, coeffs_ref, feat_ref, *refs):
    msgs, refs = refs[:COUNT], refs[COUNT:]
    outs, (prod_ref, right_ref), scratch = refs[:len(targets)], refs[len(targets):-3], refs[-3:]
    ch, cl = split2(coeffs_ref[...])
    for at, ref in enumerate(msgs):
        right_features(ref[BLK:, :], right_ref.at[at])
        test = ref[0:BLK, :]
        if at >= 2 * SIDE:
            test = test * weight_ref[0, 0]
        th, tl = split2(test)
        hi, lo = split2(mm(th, ch, NT) + (mm(th, cl, NT) + mm(tl, ch, NT)))
        prod_ref[at, 0:BLK, :] = hi
        prod_ref[at, BLK:, :] = lo
    near_kernel(targets, feat_ref, prod_ref, right_ref, *outs, *scratch)


def near_kernel(targets, feat_ref, prod_ref, right_ref, *refs):
    outs, (acc, buf_a, buf_b) = refs[:len(targets)], refs[len(targets):]
    acc[...] = jnp.zeros_like(acc)
    total = len(targets) * COUNT

    def left(t):
        return feat_ref[targets[0] + t // COUNT]

    def entries(t, buf):
        k = jnp.exp2(mm(left(t), right_ref[t % COUNT]))
        hi = k.astype(BF16)
        buf[:, BLK:] = hi
        buf[:, 0:BLK] = (k - hi.astype(F32)).astype(BF16)

    def fold(t, buf):
        b = t % COUNT
        acc[t // COUNT] += mm(buf[...], prod_ref[b]) + mm(buf[:, BLK:], prod_ref[b, 0:BLK, :])

    entries(0, buf_a)

    @pl.loop(0, total // 2)
    def _(u):
        t = 2 * u
        entries(t + 1, buf_b)
        fold(t, buf_a)
        entries(jnp.minimum(t + 2, total - 1), buf_a)
        fold(t + 1, buf_b)

    for i in range(len(targets)):
        outs[i][...] = acc[i]


def call(kernel, outs, n_smem, n_vmem, scratch=(), name=None, flops=0, trans=0):
    return pl.pallas_call(
        kernel,
        out_shape=[jax.ShapeDtypeStruct(s, t) for s, t in outs],
        in_specs=[pl.BlockSpec(memory_space=pltpu.SMEM)] * n_smem
        + [pl.BlockSpec(memory_space=VMEM)] * n_vmem,
        out_specs=[pl.BlockSpec(memory_space=VMEM)] * len(outs),
        scratch_shapes=list(scratch),
        compiler_params=pltpu.CompilerParams(vmem_limit_bytes=50 * 2**20),
        cost_estimate=pl.CostEstimate(flops=flops, bytes_accessed=4 * 2**20, transcendentals=trans),
        name=name,
    )


def near_scratch(targets):
    return [VMEM((len(targets), BLK, RANK), F32), VMEM((BLK, 2 * BLK), BF16), VMEM((BLK, 2 * BLK), BF16)]


SOLVE_SCRATCH = [VMEM((RANK, RANK), F32), VMEM((RANK, RANK), F32)]


def inverse_gram(picked, err_ref, inv_ref):
    gram = dot6(picked, picked, NT)
    eye = (
        lax.broadcasted_iota(jnp.int32, (RANK, RANK), 0)
        == lax.broadcasted_iota(jnp.int32, (RANK, RANK), 1)
    ).astype(F32)
    shift = jnp.sum(gram * eye) / RANK + 1e-06
    gram = gram + shift * eye
    bound = jnp.max(jnp.sum(jnp.abs(gram), axis=0, keepdims=True))
    alpha = 2.0 / (jnp.full((1, 1), 1.0, F32) * (bound + shift))
    err_ref[...] = eye - alpha * gram
    inv_ref[...] = alpha * eye

    def step(state):
        n, _ = state
        err = err_ref[...]
        eh, el = split2(err)
        ih, il = split2(inv_ref[...])
        inv_ref[...] += mm(ih, eh) + (mm(ih, el) + mm(il, eh))
        sq = mm(eh, eh) + (mm(eh, el) + mm(el, eh))
        err_ref[...] = sq
        return n + 1, jnp.sum(sq * sq)

    lax.while_loop(lambda st: (st[0] < 24) & (st[1] > 1e-6), step, (jnp.int32(0), jnp.float32(1e9)))

    def correct(state):
        inv = inv_ref[...]
        err = eye - dot6(gram, inv)
        inv_ref[...] = inv + dot3(inv, err)
        return state[0] + 1, jnp.sum(err * err)

    lax.while_loop(lambda st: (st[0] < 4) & (st[1] > 1e-5), correct, (jnp.int32(0), jnp.float32(1e9)))
    return inv_ref[...]


def solve_kernel(picked_ref, coeffs_ref, err_ref, inv_ref):
    picked = picked_ref[...]
    coeffs_ref[...] = dot3(inverse_gram(picked, err_ref, inv_ref), picked)


def basis_kernel(samp_ref, test_ref, coeffs_ref, *refs):
    parts, (basis_ref, proj_ref) = refs[:SIDE], refs[SIDE:]
    near_field = (parts[0][...] + parts[1][...]) + (parts[2][...] + parts[3][...])
    basis = dot3(samp_ref[...], coeffs_ref[...], NT) - near_field
    basis_ref[...] = basis
    proj_ref[...] = dot3(basis.T, test_ref[...])


def coupling(a, b):
    def norm3(v):
        return split3(v * v)

    ones = jnp.ones((RANK, DIM), BF16)
    inner = dot6(a, b, NT)
    na = sum(mm(p, ones, NT) for p in norm3(a))
    nb = sum(mm(ones, p, NT) for p in norm3(b))
    return jnp.exp2(-SCALE * (na + nb - 2.0 * inner))


EXT = SAMP + 2 * DIM
HALF = RANK // 2


def stack_node(lower, pick_own, skel_own, proj_own, pick_peer, skel_peer, proj_peer, stack_ref):
    def order(own, peer):
        return jnp.where(lower, own, peer), jnp.where(lower, peer, own)

    pick_a, pick_b = order(pick_own, pick_peer)
    proj_a, proj_b = order(proj_own, proj_peer)
    skel_a, skel_b = order(skel_own, skel_peer)
    stack_ref[0:RANK, :SAMP] = pick_a - dot3(coupling(skel_a[:, :DIM], skel_b[:, :DIM]), proj_b)
    stack_ref[RANK:, :SAMP] = pick_b - dot3(coupling(skel_b[:, :DIM], skel_a[:, :DIM]), proj_a)
    stack_ref[0:RANK, SAMP:] = skel_a
    stack_ref[RANK:, SAMP:] = skel_b


def picked_of(piv_ref, stack_ref):
    column = lax.broadcasted_iota(jnp.int32, (RANK, 2 * RANK), 1)
    one_hot = jnp.where(piv_ref[...] == column, 1.0, 0.0).astype(BF16)
    return pick(one_hot, stack_ref[...])


def half_of(lower, full):
    return jnp.where(lower, full[:HALF], full[HALF:])


def stack_kernel(
    info_ref, piv_ref, pick_own, skel_own, proj_own, pick_peer, skel_peer, proj_peer,
    stack_ref, picked_ref, skel_ref, send_ref
):
    lower = info_ref[0, 0] == 0
    stack_node(
        lower, pick_own[...], skel_own[...], proj_own[...],
        pick_peer[...], skel_peer[...], proj_peer[...], stack_ref,
    )
    picked = picked_of(piv_ref, stack_ref)
    picked_ref[...] = picked[:, :SAMP]
    skel_ref[...] = picked[:, SAMP:]
    send_ref[...] = half_of(lower, picked)


def mid_kernel(
    share, info_ref, stack_ref, picked_ref, proj_own, proj_peer, share_ref, proj_ref, send_ref, err_ref, inv_ref
):
    lower = info_ref[0, 0] == 0
    picked = picked_ref[...]
    coeffs = dot3(inverse_gram(picked, err_ref, inv_ref), picked)
    basis_t = dot3(coeffs, stack_ref[:, :SAMP], NT)
    left, right = basis_t[:, :RANK], basis_t[:, RANK:]
    proj = dot3(jnp.where(lower, left, right), proj_own[...]) + dot3(
        jnp.where(lower, right, left), proj_peer[...]
    )
    proj_ref[...] = proj
    send_ref[...] = half_of(lower, proj)
    rows = stack_ref[pl.ds(pl.multiple_of(info_ref[0, 1], 8), share), :SAMP]
    share_ref[...] = dot3(rows, coeffs, NT)


def top_kernel(
    share, info_ref, piv_ref, pick_own, skel_own, proj_own, pick_1, pick_2, proj_1, proj_2,
    share_ref, stack_ref, err_ref, inv_ref
):
    core0 = info_ref[0, 2] == 0

    def whole(first, second):
        f, o = first[...], second[...]
        return jnp.concatenate([jnp.where(core0, f, o), jnp.where(core0, o, f)], axis=0)

    peer = whole(pick_1, pick_2)
    stack_node(
        info_ref[0, 0] == 0, pick_own[...], skel_own[...], proj_own[...],
        peer[:, :SAMP], peer[:, SAMP:], whole(proj_1, proj_2), stack_ref,
    )
    picked = picked_of(piv_ref, stack_ref)[:, :SAMP]
    coeffs = dot3(inverse_gram(picked, err_ref, inv_ref), picked)
    rows = stack_ref[pl.ds(pl.multiple_of(info_ref[0, 1], 8), share), :SAMP]
    share_ref[...] = dot3(rows, coeffs, NT)


def after(first, *then):
    return lax.optimization_barrier((first, *then))


def sum_row(part, *then):
    share = part.shape[0] // 16
    parts = lax.all_to_all(part.reshape(16, share, -1), "row", 0, 0)
    mine, *then = after(jnp.sum(parts, axis=0), *then)
    every = lax.all_to_all(jnp.broadcast_to(mine[None], (16, *mine.shape)), "row", 0, 0)
    return (every.reshape(part.shape), *then)


def body(points, samples, test_matrix, near_mask, leaf_pivots, mid_pivots, top_pivots):
    leaf = lax.axis_index("leaf")
    row = lax.axis_index("row")
    core = leaf & 1
    start = (row * BLK).reshape(1, 1)
    xt = points.T
    pivots = leaf_pivots[0].reshape(RANK, 1)
    weight = jnp.where(core == 0, near_mask[0, 0], near_mask[0, 1]).astype(F32).reshape(1, 1)

    (skel,) = call(skel_kernel, [((RANK, 2 * DIM), F32)], 1, 2, name="skel")(start, pivots, xt)
    skel, message, xt = after(skel, jnp.concatenate([test_matrix, xt], axis=0), xt)
    own = [message, lax.ppermute(message, "row", along_x(1)), lax.ppermute(message, "row", along_x(3))]
    sib = [lax.ppermute(message, "leaf", SIBLING)]
    outer = [lax.ppermute(message, "leaf", OUTER)]
    skel, message = sum_row(skel, message)
    own.append(lax.ppermute(message, "row", along_x(2)))
    (part,) = call(
        pivot_kernel, [((RANK, SAMP), F32)], 2, 6, [VMEM((4 * DIM, BLK), BF16)], name="pivot", flops=2 * 10**9
    )(start, weight, pivots, skel, samples, own[0], sib[0], outer[0])
    part, xt, own[1], own[2] = after(part, xt, own[1], own[2])
    (feats,) = call(feature_kernel, [((SIDE, BLK, 4 * DIM), BF16)], 0, 4, name="features")(
        xt, *[lax.ppermute(xt, "row", along_y(k)) for k in SHIFTS]
    )
    picked, own[3] = sum_row(part, own[3])
    sib += [lax.ppermute(m, "leaf", SIBLING) for m in own[1:]]
    outer += [lax.ppermute(m, "leaf", OUTER) for m in own[1:]]
    (coeffs,) = call(
        solve_kernel, [((RANK, SAMP), F32)], 0, 1, SOLVE_SCRATCH, name="solve", flops=3 * 10**9
    )(picked)
    picked_sib = lax.ppermute(picked, "leaf", SIBLING)
    skel_sib = lax.ppermute(skel, "leaf", SIBLING)

    block = ((BLK, RANK), F32)
    sum_1, sum_3, sum_2, prods, rights = call(
        functools.partial(far_kernel, (1, 2, 3)),
        [block] * 3 + [((COUNT, 2 * BLK, RANK), BF16), ((COUNT, 4 * DIM, BLK), BF16)], 1, 2 + COUNT,
        near_scratch((1, 2, 3)), name="near_far", flops=30 * 10**9,
    )(weight, coeffs, feats, *own, *sib, *outer)
    sum_2 = lax.ppermute(sum_2, "row", along_y(-2))
    sum_1 = lax.ppermute(sum_1, "row", along_y(-1))
    sum_3 = lax.ppermute(sum_3, "row", along_y(-3))
    (sum_0,) = call(
        functools.partial(near_kernel, (0,)), [block], 0, 3, near_scratch((0,)), name="near_own", flops=10**9
    )(feats, prods, rights)
    leaf_basis, proj = call(
        basis_kernel, [block, ((RANK, SAMP), F32)], 0, 3 + SIDE, name="basis", flops=10**9
    )(samples, test_matrix, coeffs, sum_0, sum_1, sum_2, sum_3)
    (proj,) = sum_row(proj)
    proj_sib = lax.ppermute(proj, "leaf", SIBLING)

    def info(lower, first):
        return jnp.stack([lower, first, core]).astype(jnp.int32).reshape(1, 3)

    def row_of(table, node):
        return lax.dynamic_index_in_dim(table, node, 0, keepdims=False).reshape(RANK, 1)

    node = ((RANK, SAMP), F32)
    mid_share, top_share = RANK // 16, RANK // 32
    mid_info = info(core, core * RANK + row * mid_share)
    stack, picked, skel, send = call(
        stack_kernel, [((2 * RANK, EXT), F32), node, ((RANK, 2 * DIM), F32), ((HALF, EXT), F32)], 1, 7,
        name="mid_stack", flops=10**9,
    )(mid_info, row_of(mid_pivots, leaf >> 1), picked, skel, proj, picked_sib, skel_sib, proj_sib)
    pick_1 = lax.ppermute(send, "leaf", COUSIN)
    pick_2 = lax.ppermute(pick_1, "leaf", SIBLING)
    mid_basis, proj, send = call(
        functools.partial(mid_kernel, mid_share),
        [((mid_share, RANK), F32), node, ((HALF, SAMP), F32)], 1, 4, SOLVE_SCRATCH,
        name="mid_solve", flops=3 * 10**9,
    )(mid_info, stack, picked, proj, proj_sib)
    proj_1 = lax.ppermute(send, "leaf", COUSIN)
    proj_2 = lax.ppermute(proj_1, "leaf", SIBLING)
    second = leaf >> 1 & 1
    (top_basis,) = call(
        functools.partial(top_kernel, top_share), [((top_share, RANK), F32)], 1, 8,
        [VMEM((2 * RANK, EXT), F32), *SOLVE_SCRATCH], name="top", flops=3 * 10**9,
    )(
        info(second, second * RANK + core * (RANK // 2) + row * top_share), row_of(top_pivots, leaf >> 2),
        picked, skel, proj, pick_1, pick_2, proj_1, proj_2,
    )
    return (leaf_basis, mid_basis, top_basis)


def solution(mesh):
    split = P(("leaf", "row"), None)
    return jax.shard_map(
        body,
        mesh=mesh,
        in_specs=(split, split, split, P("leaf", None), P("leaf", None), P(), P()),
        out_specs=(split, split, split),
        check_vma=False,
    )
```

time: 279 us -> 257 us (0.921)
  starting transfers between devices: 44.4 us -> 56 us
  Pallas kernels: 102 us -> 90.5 us
  blocking collectives: 50.6 us -> 42.9 us
  waiting for transfers between devices: 63.8 us -> 57.5 us
  other arithmetic: 6.11 us -> 1.65 us
  local copies, waits for them, and re-layouts: 8.72 us -> 5.38 us
    ppermute x11 -> x18, waiting for transfers between devices: 38.9 us -> 8.13 us  [the longest x1 6.51 us: body(): proj_1 = lax.ppermute(send, 'leaf', COUSIN)]
    all_to_all x2 -> x4, waiting for transfers between devices: 14.4 us -> 35.4 us  [the longest x3 20 us: sum_row(): lax.all_to_all(jnp.broadcast_to(mine[None], (16, *mine.shape)), 'row', 0, 0)]
    all_to_all x1 -> x0, blocking collectives: 13.5 us -> none  [every_row(): lax.all_to_all(jnp.broadcast_to(part[None], (16, *part.shape)), 'row', 0, 0)]
    pallas_call x8 -> x9, Pallas kernels: 95.1 us -> 84.4 us  [the longest x1 38.8 us: body(): call(functools.partial(far_kernel, (1, 2, 3)), [block] * 3 + [((COUNT, 2...]
    ppermute x11 -> x18, starting transfers between devices: 24.1 us -> 32.6 us  [the longest x3 11.7 us: body(): outer += [lax.ppermute(m, 'leaf', OUTER) for m in own[1:]]]
    all_to_all x2, blocking collectives: 37.1 us -> 42.9 us  [sum_row(): parts = lax.all_to_all(part.reshape(16, share, -1), 'row', 0, 0)]
    all_to_all x2 -> x4, starting transfers between devices: 11.5 us -> 16.1 us  [the longest x3 12.5 us: sum_row(): lax.all_to_all(jnp.broadcast_to(mine[None], (16, *mine.shape)), 'row', 0, 0)]
    concatenate x3 -> x1, other arithmetic: 5.89 us -> 1.41 us  [body(): jnp.concatenate([test_matrix, xt], axis=0)]
  transfers between devices with their start and end apart: 19 -> 28, of which waited for: 8 -> 10; matrix products, arithmetic and copies ran while one was open for 3% -> 1% of each run, Pallas kernels for 10% -> 13%
where the time goes in v3:
time: 257 us; the launch traced here: 256 us
  Pallas kernels  90.5 us (35%)
  waiting for transfers between devices  57.5 us (22%)
  starting transfers between devices  56 us (22%)
  blocking collectives  42.9 us (17%)
  local copies, waits for them, and re-layouts  5.38 us (2%)
    all_to_all x2, blocking collectives, sum_row(): parts = lax.all_to_all(part.reshape(16, share, -1), 'row', 0, 0)  42.9 us
    pallas_call x1, Pallas kernels, body(): call(functools.partial(far_kernel, (1, 2, 3)), [block] * 3 + [((COUNT, 2...  38.8 us
    all_to_all x3, waiting for transfers between devices, sum_row(): lax.all_to_all(jnp.broadcast_to(mine[None], (16, *mine.shape)), 'row', 0, 0)  20 us
    all_to_all x1, waiting for transfers between devices, sum_row(): parts = lax.all_to_all(part.reshape(16, share, -1), 'row', 0, 0)  15.4 us
    all_to_all x3, starting transfers between devices, sum_row(): lax.all_to_all(jnp.broadcast_to(mine[None], (16, *mine.shape)), 'row', 0, 0)  12.5 us
    pallas_call x1, Pallas kernels, body(): call(functools.partial(near_kernel, (0,)), [block], 0, 3, near_scratch((0...  12.5 us
    ppermute x3, starting transfers between devices, body(): outer += [lax.ppermute(m, 'leaf', OUTER) for m in own[1:]]  11.7 us
    ppermute x1, waiting for transfers between devices, body(): sum_3 = lax.ppermute(sum_3, 'row', along_y(-3))  11.3 us
  transfers between devices with their start and end apart: 28, of which 10 were waited for; matrix products, arithmetic and copies ran while one was open for 1% of the time, Pallas kernels for 13%

profile of v3, /device:TPU:1, one launch (start us, length us, event | category | flops | bytes accessed | tf_op | source)
XLA Modules:
  0.0 256.2 jit_solution(13427051638265191908)
XLA Ops:
  0.7 0.8 copy.11.piv_ref
  1.5 1.4 pad_maximum_fusion.own_ref.refs_0_
  3.4 1.5 collective-permute-start
  4.9 3.7 %collective-permute-start.1 = (f32[576,512]{1,0:T(8,128)S(1)}, f32[576,512]{1,0:T(8,128)}, u32[]{:S(2)}, u32[]{:S(2)}) collective-permute-start(f32[576,512]{1,0:T(8,128)S(1)} %pad_maximum_fusion.own_ref.refs_0_), channel_id=1, source_target_pairs={{16,32},{32,16},{48,64},{64,48},{80,96},{96,80},{17,33},{33,17},{4... | collective-permute-start | bytes 3538952 | tf_op jit(solution)/shard_map/ppermute | solution.py:376
  8.5 1.3 collective-permute-start.2
  9.8 1.5 collective-permute-start.3
  11.3 29.5 %all_to_all.30 = f32[16,16,128]{2,1,0:T(8,128)S(1)} all-to-all(f32[16,16,128]{2,1,0:T(8,128)S(1)} %bitcast.37), channel_id=1, replica_groups=mesh['leaf'=8,'row'=16] {'row'}, dimensions={0} | all-to-all | bytes 262144 | tf_op jit(solution)/shard_map/all_to_all | solution.py:357
  40.8 0.7 broadcast_in_dim.6
  41.5 4.4 %all-to-all-start.1 = ((f32[16,16,128]{2,1,0:T(8,128)}), f32[16,16,128]{2,1,0:T(8,128)S(1)}, u32[]{:S(2)}, u32[]{:S(2)}) async-start(f32[16,16,128]{2,1,0:T(8,128)} %broadcast_in_dim.6), calls=%async_computation.1 | async-start | bytes 262144 | tf_op jit(solution)/shard_map/all_to_all | solution.py:359
  47.8 2.9 %collective-permute-start.4 = (f32[576,512]{1,0:T(8,128)S(1)}, f32[576,512]{1,0:T(8,128)}, u32[]{:S(2)}, u32[]{:S(2)}) collective-permute-start(f32[576,512]{1,0:T(8,128)S(1)} %pad_maximum_fusion.own_ref.refs_0_), channel_id=1, source_target_pairs={{0,8},{1,9},{2,10},{3,11},{4,12},{5,13},{6,14},{7,15},{8,0},{9,1},... | collective-permute-start | bytes 3538952 | tf_op jit(solution)/shard_map/ppermute | solution.py:378
  50.7 2.4 all-to-all-done.1
  53.1 4.9 %pivot.1 = f32[256,512]{1,0:T(8,128)} custom-call(s32[1,1]{1,0:T(1,128)} %bitcast.start_ref, f32[1,1]{1,0:T(1,128)} %bitcast.3.weight_ref, s32[256,1]{1,0:T(8,128)S(1)} %copy.11.piv_ref, f32[256,128]{1,0:T(8,128)S(1)} %bitcast.38, f32[512,512]{1,0:T(8,128)S(1)} %copy-done.3, f32[576,512]{1,0:T(8,128)S(1)} %pad_maximum_fusion.own_ref.refs_0_, ...), custom_call_target="tpu_custom_call" | custom-call | flops 2000000000 | bytes 4194304 | tf_op jit(solution)/shard_map/pivot/pallas_call | solution.py:379
  58.0 4.7 %collective-permute-start.11 = (f32[576,512]{1,0:T(8,128)}, f32[576,512]{1,0:T(8,128)}, u32[]{:S(2)}, u32[]{:S(2)}) collective-permute-start(f32[576,512]{1,0:T(8,128)} %collective-permute-done.2.refs_1_), channel_id=1, source_target_pairs={{16,32},{32,16},{48,64},{64,48},{80,96},{96,80},{17,33},{33,17},{4... | collective-permute-start | bytes 3538952 | tf_op jit(solution)/shard_map/ppermute | solution.py:388
  62.7 3.6 %all-to-all-start.2 = ((f32[16,16,512]{2,1,0:T(8,128)}), f32[16,16,512]{2,1,0:T(8,128)S(1)}, u32[]{:S(2)}, u32[]{:S(2)}) async-start(f32[16,16,512]{2,1,0:T(8,128)} %bitcast.8), calls=%async_computation.2 | async-start | bytes 1048576 | tf_op jit(solution)/shard_map/all_to_all | solution.py:357
  66.3 1.2 collective-permute-start.5
  67.6 1.5 collective-permute-start.6
  69.1 1.5 collective-permute-start.7
  70.5 15.4 %all-to-all-done.2 = f32[16,16,512]{2,1,0:T(8,128)S(1)} async-done(((f32[16,16,512]{2,1,0:T(8,128)}), f32[16,16,512]{2,1,0:T(8,128)S(1)}, u32[]{:S(2)}, u32[]{:S(2)}) %all-to-all-start.2) | async-done | bytes 524320 | tf_op jit(solution)/shard_map/all_to_all | solution.py:357
  85.9 0.7 collective-permute-start.8
  86.6 3.5 %collective-permute-start.12 = (f32[576,512]{1,0:T(8,128)}, f32[576,512]{1,0:T(8,128)}, u32[]{:S(2)}, u32[]{:S(2)}) collective-permute-start(f32[576,512]{1,0:T(8,128)} %collective-permute-done.3.refs_2_), channel_id=1, source_target_pairs={{16,32},{32,16},{48,64},{64,48},{80,96},{96,80},{17,33},{33,17},{4... | collective-permute-start | bytes 3538952 | tf_op jit(solution)/shard_map/ppermute | solution.py:388
  90.7 3.4 %collective-permute-start.13 = (f32[576,512]{1,0:T(8,128)}, f32[576,512]{1,0:T(8,128)}, u32[]{:S(2)}, u32[]{:S(2)}) collective-permute-start(f32[576,512]{1,0:T(8,128)} %collective-permute-done.4.refs_3_), channel_id=1, source_target_pairs={{16,32},{32,16},{48,64},{64,48},{80,96},{96,80},{17,33},{33,17},{4... | collective-permute-start | bytes 3538952 | tf_op jit(solution)/shard_map/ppermute | solution.py:388
  94.2 0.9 broadcast_in_dim.7
  95.0 4.4 %all-to-all-start.3 = ((f32[16,16,512]{2,1,0:T(8,128)}), f32[16,16,512]{2,1,0:T(8,128)S(1)}, u32[]{:S(2)}, u32[]{:S(2)}) async-start(f32[16,16,512]{2,1,0:T(8,128)} %broadcast_in_dim.7), calls=%async_computation.3 | async-start | bytes 1048576 | tf_op jit(solution)/shard_map/all_to_all | solution.py:359
  99.8 10.5 %all-to-all-done.3 = f32[16,16,512]{2,1,0:T(8,128)S(1)} async-done(((f32[16,16,512]{2,1,0:T(8,128)}), f32[16,16,512]{2,1,0:T(8,128)S(1)}, u32[]{:S(2)}, u32[]{:S(2)}) %all-to-all-start.3) | async-done | bytes 524320 | tf_op jit(solution)/shard_map/all_to_all | solution.py:359
  110.3 6.1 %solve.1.coeffs_ref = f32[256,512]{1,0:T(8,128)S(1)} custom-call(f32[256,512]{1,0:T(8,128)S(1)} %bitcast.30), custom_call_target="tpu_custom_call" | custom-call | flops 3000000000 | bytes 4194304 | tf_op jit(solution)/shard_map/solve/pallas_call | solution.py:389
  116.4 0.7 collective-permute-done.13.refs_11_
  117.1 38.8 %near_far.1 = (f32[512,256]{1,0:T(8,128)S(1)}, f32[512,256]{1,0:T(8,128)S(1)}, f32[512,256]{1,0:T(8,128)S(1)}, bf16[12,1024,256]{2,1,0:T(8,128)(2,1)}, bf16[12,256,512]{2,1,0:T(8,128)(2,1)}) custom-call(f32[1,1]{1,0:T(1,128)} %bitcast.3.weight_ref, f32[256,512]{1,0:T(8,128)S(1)} %solve.1.coeffs_ref, bf16[4,512,256]{2,1,0:T(8,128)(2,1)S(1)} %features.1.feat_ref, ...), custom_call_target="tpu_custom_call" | custom-call | flops 30000001024 | bytes 4194304 | tf_op jit(solution)/shard_map/near_far/pallas_call | solution.py:396
  156.3 1.6 collective-permute-start.15
  157.9 12.5 %near_own.1.refs_0_ = f32[512,256]{1,0:T(8,128)S(1)} custom-call(bf16[4,512,256]{2,1,0:T(8,128)(2,1)S(1)} %features.1.feat_ref, bf16[12,1024,256]{2,1,0:T(8,128)(2,1)} %get-tuple-element.39.prod_ref, bf16[12,256,512]{2,1,0:T(8,128)(2,1)} %get-tuple-element.40.right_ref), custom_call_target="tpu_custom_call" | custom-call | flops 1000000000 | bytes 4194304 | tf_op jit(solution)/shard_map/near_own/pallas_call | solution.py:404
  170.5 1.2 collective-permute-done.15.refs_2_
  171.6 11.3 %collective-permute-done.16.refs_3_ = f32[512,256]{1,0:T(8,128)S(1)} collective-permute-done((f32[512,256]{1,0:T(8,128)S(1)}, f32[512,256]{1,0:T(8,128)S(1)}, u32[]{:S(2)}, u32[]{:S(2)}) %collective-permute-start.16) | collective-permute-done | bytes 524320 | tf_op jit(solution)/shard_map/ppermute | solution.py:403
  182.9 3.4 %basis.1 = (f32[512,256]{1,0:T(8,128)}, f32[256,512]{1,0:T(8,128)S(1)}) custom-call(f32[512,512]{1,0:T(8,128)} %samp_ref.3, f32[512,512]{1,0:T(8,128)} %test_ref.1, f32[256,512]{1,0:T(8,128)S(1)} %solve.1.coeffs_ref, f32[512,256]{1,0:T(8,128)S(1)} %near_own.1.refs_0_, f32[512,256]{1,0:T(8,128)S(1)} %collective-permute-done.14.refs_1_, ...), custom_call_target="tpu_custom_call" | custom-call | flops 1000000000 | bytes 4194304 | tf_op jit(solution)/shard_map/basis/pallas_call | solution.py:407
  186.4 13.4 %all_to_all.31 = f32[16,16,512]{2,1,0:T(8,128)S(1)} all-to-all(f32[16,16,512]{2,1,0:T(8,128)S(1)} %bitcast.36), channel_id=1, replica_groups=mesh['leaf'=8,'row'=16] {'row'}, dimensions={0} | all-to-all | bytes 1048576 | tf_op jit(solution)/shard_map/all_to_all | solution.py:357
  199.8 0.8 broadcast_in_dim.8
  200.7 3.7 %all-to-all-start.5 = ((f32[16,16,512]{2,1,0:T(8,128)}), f32[16,16,512]{2,1,0:T(8,128)S(1)}, u32[]{:S(2)}, u32[]{:S(2)}) async-start(f32[16,16,512]{2,1,0:T(8,128)} %broadcast_in_dim.8), calls=%async_computation.5 | async-start | bytes 1048576 | tf_op jit(solution)/shard_map/all_to_all | solution.py:359
  204.4 2.0 collective-permute-start.17
  206.4 7.2 %all-to-all-done.5 = f32[16,16,512]{2,1,0:T(8,128)S(1)} async-done(((f32[16,16,512]{2,1,0:T(8,128)}), f32[16,16,512]{2,1,0:T(8,128)S(1)}, u32[]{:S(2)}, u32[]{:S(2)}) %all-to-all-start.5) | async-done | bytes 524320 | tf_op jit(solution)/shard_map/all_to_all | solution.py:359
  213.6 3.2 %collective-permute-start.19 = (f32[256,512]{1,0:T(8,128)S(1)}, f32[256,512]{1,0:T(8,128)S(1)}, u32[]{:S(2)}, u32[]{:S(2)}) collective-permute-start(f32[256,512]{1,0:T(8,128)S(1)} %bitcast.33), channel_id=1, source_target_pairs={{0,16},{16,0},{32,48},{48,32},{64,80},{80,64},{96,112},{112,96},{1... | collective-permute-start | bytes 1572872 | tf_op jit(solution)/shard_map/ppermute | solution.py:411
  217.1 1.5 collective-permute-done.18.skel_peer
  218.6 3.9 %mid_stack.1 = (f32[512,640]{1,0:T(8,128)}, f32[256,512]{1,0:T(8,128)S(1)}, f32[256,128]{1,0:T(8,128)S(1)}, f32[128,640]{1,0:T(8,128)S(1)}) custom-call(s32[1,3]{1,0:T(1,128)S(1)} %add_bitcast_fusion.info_ref, s32[256,1]{1,0:T(8,128)S(1)} %copy.12.piv_ref, f32[256,512]{1,0:T(8,128)S(1)} %bitcast.32, f32[256,128]{1,0:T(8,128)S(1)} %bitcast.40, ...), custom_call_target="tpu_custom_call" | custom-call | flops 1000000000 | bytes 4194304 | tf_op jit(solution)/shard_map/mid_stack/pallas_call | solution.py:422
  222.5 2.4 collective-permute-start.20
  224.9 1.3 copy-done.4
  226.2 9.0 %mid_solve.1 = (f32[16,256]{1,0:T(8,128)}, f32[256,512]{1,0:T(8,128)S(1)}, f32[128,512]{1,0:T(8,128)S(1)}) custom-call(s32[1,3]{1,0:T(1,128)S(1)} %add_bitcast_fusion.info_ref, f32[512,640]{1,0:T(8,128)S(1)} %copy-done.4, f32[256,512]{1,0:T(8,128)S(1)} %get-tuple-element.47.picked_ref.pick_own, f32[256,512]{1,0:T(8,128)S(1)} %bitcast.35, ...), custom_call_target="tpu_custom_call" | custom-call | flops 3000000000 | bytes 4194304 | tf_op jit(solution)/shard_map/mid_solve/pallas_call | solution.py:428
  235.3 0.7 collective-permute-start.21
  235.9 6.5 %collective-permute-done.22.proj_1 = f32[128,512]{1,0:T(8,128)S(1)} collective-permute-done((f32[128,512]{1,0:T(8,128)S(1)}, f32[128,512]{1,0:T(8,128)S(1)}, u32[]{:S(2)}, u32[]{:S(2)}) %collective-permute-start.22) | collective-permute-done | bytes 262176 | tf_op jit(solution)/shard_map/ppermute | solution.py:433
  242.4 1.5 collective-permute-start.23
  244.2 0.9 collective-permute-done.23.proj_2
  245.2 11.1 %top.1 = f32[8,256]{1,0:T(8,128)} custom-call(s32[1,3]{1,0:T(1,128)S(1)} %add_bitcast_fusion.1.info_ref, s32[256,1]{1,0:T(8,128)S(1)} %copy.13.piv_ref, f32[256,512]{1,0:T(8,128)S(1)} %get-tuple-element.47.picked_ref.pick_own, f32[256,128]{1,0:T(8,128)S(1)} %get-tuple-element.49.skel_own, f32[256,512]{1,0:T(8,128)S(1)} %get-tuple-element.50.proj_own, ...), custom_call_target="tpu_custom_call" | custom-call | flops 3000000000 | bytes 4194304 | tf_op jit(solution)/shard_map/top/pallas_call | solution.py:436
  (49 shorter events, 3.0 us)
Async XLA Ops:
  0.6 216.2 %copy-start = (s32[4,256]{1,0:T(4,128)S(1)}, s32[4,256]{1,0:T(4,128)}, u32[]{:S(2)}) copy-start(s32[4,256]{1,0:T(4,128)} %param.12) | copy-start | bytes 12292
  1.5 1.5 copy-start.1
  2.9 55.1 %copy-start.2 = (f32[576,512]{1,0:T(8,128)}, f32[576,512]{1,0:T(8,128)S(1)}, u32[]{:S(2)}) copy-start(f32[576,512]{1,0:T(8,128)S(1)} %pad_maximum_fusion.own_ref.refs_0_) | copy-start | bytes 3538948
  2.9 43.0 %copy-start.5 = (s32[1,2]{1,0:T(1,128)S(1)}, s32[1,2]{1,0:T(1,128)}, u32[]{:S(2)}) copy-start(s32[1,2]{1,0:T(1,128)} %param.10) | copy-start | bytes 28
  2.9 50.2 %copy-start.3 = (f32[512,512]{1,0:T(8,128)S(1)}, f32[512,512]{1,0:T(8,128)}, u32[]{:S(2)}) copy-start(f32[512,512]{1,0:T(8,128)} %samp_ref.3) | copy-start | bytes 3145732
  3.4 49.7 %collective-permute-start = (f32[576,512]{1,0:T(8,128)S(1)}, f32[576,512]{1,0:T(8,128)}, u32[]{:S(2)}, u32[]{:S(2)}) collective-permute-start(f32[576,512]{1,0:T(8,128)S(1)} %pad_maximum_fusion.own_ref.refs_0_), channel_id=1, source_target_pairs={{0,16},{16,0},{32,48},{48,32},{64,80},{80,64},{96,112},{112,96},{1... | collective-permute-start | bytes 3538952 | tf_op jit(solution)/shard_map/ppermute | solution.py:375
  4.9 48.2 %collective-permute-start.1 = (f32[576,512]{1,0:T(8,128)S(1)}, f32[576,512]{1,0:T(8,128)}, u32[]{:S(2)}, u32[]{:S(2)}) collective-permute-start(f32[576,512]{1,0:T(8,128)S(1)} %pad_maximum_fusion.own_ref.refs_0_), channel_id=1, source_target_pairs={{16,32},{32,16},{48,64},{64,48},{80,96},{96,80},{17,33},{33,17},{4... | collective-permute-start | bytes 3538952 | tf_op jit(solution)/shard_map/ppermute | solution.py:376
  8.5 49.4 %collective-permute-start.2 = (f32[576,512]{1,0:T(8,128)S(1)}, f32[576,512]{1,0:T(8,128)}, u32[]{:S(2)}, u32[]{:S(2)}) collective-permute-start(f32[576,512]{1,0:T(8,128)S(1)} %pad_maximum_fusion.own_ref.refs_0_), channel_id=1, source_target_pairs={{0,4},{1,5},{2,6},{3,7},{4,8},{5,9},{6,10},{7,11},{8,12},{9,13},{1... | collective-permute-start | bytes 3538952 | tf_op jit(solution)/shard_map/ppermute | solution.py:374
  9.8 48.2 %collective-permute-start.3 = (f32[576,512]{1,0:T(8,128)S(1)}, f32[576,512]{1,0:T(8,128)}, u32[]{:S(2)}, u32[]{:S(2)}) collective-permute-start(f32[576,512]{1,0:T(8,128)S(1)} %pad_maximum_fusion.own_ref.refs_0_), channel_id=1, source_target_pairs={{0,12},{1,13},{2,14},{3,15},{4,0},{5,1},{6,2},{7,3},{8,4},{9,5},{1... | collective-permute-start | bytes 3538952 | tf_op jit(solution)/shard_map/ppermute | solution.py:374
  41.5 11.6 %all-to-all-start.1 = ((f32[16,16,128]{2,1,0:T(8,128)}), f32[16,16,128]{2,1,0:T(8,128)S(1)}, u32[]{:S(2)}, u32[]{:S(2)}) async-start(f32[16,16,128]{2,1,0:T(8,128)} %broadcast_in_dim.6), calls=%async_computation.1 | async-start | bytes 262144 | tf_op jit(solution)/shard_map/all_to_all | solution.py:359
  47.8 38.2 %collective-permute-start.4 = (f32[576,512]{1,0:T(8,128)S(1)}, f32[576,512]{1,0:T(8,128)}, u32[]{:S(2)}, u32[]{:S(2)}) collective-permute-start(f32[576,512]{1,0:T(8,128)S(1)} %pad_maximum_fusion.own_ref.refs_0_), channel_id=1, source_target_pairs={{0,8},{1,9},{2,10},{3,11},{4,12},{5,13},{6,14},{7,15},{8,0},{9,1},... | collective-permute-start | bytes 3538952 | tf_op jit(solution)/shard_map/ppermute | solution.py:378
  58.0 32.7 %collective-permute-start.11 = (f32[576,512]{1,0:T(8,128)}, f32[576,512]{1,0:T(8,128)}, u32[]{:S(2)}, u32[]{:S(2)}) collective-permute-start(f32[576,512]{1,0:T(8,128)} %collective-permute-done.2.refs_1_), channel_id=1, source_target_pairs={{16,32},{32,16},{48,64},{64,48},{80,96},{96,80},{17,33},{33,17},{4... | collective-permute-start | bytes 3538952 | tf_op jit(solution)/shard_map/ppermute | solution.py:388
  62.7 23.2 %all-to-all-start.2 = ((f32[16,16,512]{2,1,0:T(8,128)}), f32[16,16,512]{2,1,0:T(8,128)S(1)}, u32[]{:S(2)}, u32[]{:S(2)}) async-start(f32[16,16,512]{2,1,0:T(8,128)} %bitcast.8), calls=%async_computation.2 | async-start | bytes 1048576 | tf_op jit(solution)/shard_map/all_to_all | solution.py:357
  66.3 20.3 %collective-permute-start.5 = (f32[64,512]{1,0:T(8,128)S(1)}, f32[64,512]{1,0:T(8,128)S(1)}, u32[]{:S(2)}, u32[]{:S(2)}) collective-permute-start(f32[64,512]{1,0:T(8,128)S(1)} %bitcast.26), channel_id=1, source_target_pairs={{0,1},{1,2},{2,3},{3,0},{4,5},{5,6},{6,7},{7,4},{8,9},{9,10},{10,1... | collective-permute-start | bytes 393224 | tf_op jit(solution)/shard_map/ppermute | solution.py:384
  67.6 22.5 %collective-permute-start.6 = (f32[64,512]{1,0:T(8,128)S(1)}, f32[64,512]{1,0:T(8,128)S(1)}, u32[]{:S(2)}, u32[]{:S(2)}) collective-permute-start(f32[64,512]{1,0:T(8,128)S(1)} %bitcast.27), channel_id=1, source_target_pairs={{0,3},{1,0},{2,1},{3,2},{4,7},{5,4},{6,5},{7,6},{8,11},{9,8},{10,9... | collective-permute-start | bytes 393224 | tf_op jit(solution)/shard_map/ppermute | solution.py:384
  69.1 21.2 %collective-permute-start.7 = (f32[64,512]{1,0:T(8,128)S(1)}, f32[64,512]{1,0:T(8,128)S(1)}, u32[]{:S(2)}, u32[]{:S(2)}) collective-permute-start(f32[64,512]{1,0:T(8,128)S(1)} %bitcast.28), channel_id=1, source_target_pairs={{0,2},{1,3},{2,0},{3,1},{4,6},{5,7},{6,4},{7,5},{8,10},{9,11},{10,... | collective-permute-start | bytes 393224 | tf_op jit(solution)/shard_map/ppermute | solution.py:384
  85.9 30.4 %collective-permute-start.8 = (f32[576,512]{1,0:T(8,128)}, f32[576,512]{1,0:T(8,128)}, u32[]{:S(2)}, u32[]{:S(2)}) collective-permute-start(f32[576,512]{1,0:T(8,128)} %collective-permute-done.2.refs_1_), channel_id=1, source_target_pairs={{0,16},{16,0},{32,48},{48,32},{64,80},{80,64},{96,112},{112,96},{1... | collective-permute-start | bytes 3538952 | tf_op jit(solution)/shard_map/ppermute | solution.py:387
  86.6 29.8 %collective-permute-start.12 = (f32[576,512]{1,0:T(8,128)}, f32[576,512]{1,0:T(8,128)}, u32[]{:S(2)}, u32[]{:S(2)}) collective-permute-start(f32[576,512]{1,0:T(8,128)} %collective-permute-done.3.refs_2_), channel_id=1, source_target_pairs={{16,32},{32,16},{48,64},{64,48},{80,96},{96,80},{17,33},{33,17},{4... | collective-permute-start | bytes 3538952 | tf_op jit(solution)/shard_map/ppermute | solution.py:388
  90.1 26.3 %collective-permute-start.9 = (f32[576,512]{1,0:T(8,128)}, f32[576,512]{1,0:T(8,128)}, u32[]{:S(2)}, u32[]{:S(2)}) collective-permute-start(f32[576,512]{1,0:T(8,128)} %collective-permute-done.3.refs_2_), channel_id=1, source_target_pairs={{0,16},{16,0},{32,48},{48,32},{64,80},{80,64},{96,112},{112,96},{1... | collective-permute-start | bytes 3538952 | tf_op jit(solution)/shard_map/ppermute | solution.py:387
  90.2 26.2 %collective-permute-start.10 = (f32[576,512]{1,0:T(8,128)}, f32[576,512]{1,0:T(8,128)}, u32[]{:S(2)}, u32[]{:S(2)}) collective-permute-start(f32[576,512]{1,0:T(8,128)} %collective-permute-done.4.refs_3_), channel_id=1, source_target_pairs={{0,16},{16,0},{32,48},{48,32},{64,80},{80,64},{96,112},{112,96},{1... | collective-permute-start | bytes 3538952 | tf_op jit(solution)/shard_map/ppermute | solution.py:387
  90.7 26.4 %collective-permute-start.13 = (f32[576,512]{1,0:T(8,128)}, f32[576,512]{1,0:T(8,128)}, u32[]{:S(2)}, u32[]{:S(2)}) collective-permute-start(f32[576,512]{1,0:T(8,128)} %collective-permute-done.4.refs_3_), channel_id=1, source_target_pairs={{16,32},{32,16},{48,64},{64,48},{80,96},{96,80},{17,33},{33,17},{4... | collective-permute-start | bytes 3538952 | tf_op jit(solution)/shard_map/ppermute | solution.py:388
  95.0 15.3 %all-to-all-start.3 = ((f32[16,16,512]{2,1,0:T(8,128)}), f32[16,16,512]{2,1,0:T(8,128)S(1)}, u32[]{:S(2)}, u32[]{:S(2)}) async-start(f32[16,16,512]{2,1,0:T(8,128)} %broadcast_in_dim.7), calls=%async_computation.3 | async-start | bytes 1048576 | tf_op jit(solution)/shard_map/all_to_all | solution.py:359
  155.9 14.6 %collective-permute-start.14 = (f32[512,256]{1,0:T(8,128)S(1)}, f32[512,256]{1,0:T(8,128)S(1)}, u32[]{:S(2)}, u32[]{:S(2)}) collective-permute-start(f32[512,256]{1,0:T(8,128)S(1)} %get-tuple-element.41), channel_id=1, source_target_pairs={{0,3},{1,0},{2,1},{3,2},{4,7},{5,4},{6,5},{7,6},{8,11},{9,8},{10,9... | collective-permute-start | bytes 1572872 | tf_op jit(solution)/shard_map/ppermute | solution.py:402
  156.3 15.3 %collective-permute-start.15 = (f32[512,256]{1,0:T(8,128)S(1)}, f32[512,256]{1,0:T(8,128)S(1)}, u32[]{:S(2)}, u32[]{:S(2)}) collective-permute-start(f32[512,256]{1,0:T(8,128)S(1)} %get-tuple-element.42), channel_id=1, source_target_pairs={{0,2},{1,3},{2,0},{3,1},{4,6},{5,7},{6,4},{7,5},{8,10},{9,11},{10,... | collective-permute-start | bytes 1572872 | tf_op jit(solution)/shard_map/ppermute | solution.py:401
  157.9 25.0 %collective-permute-start.16 = (f32[512,256]{1,0:T(8,128)S(1)}, f32[512,256]{1,0:T(8,128)S(1)}, u32[]{:S(2)}, u32[]{:S(2)}) collective-permute-start(f32[512,256]{1,0:T(8,128)S(1)} %get-tuple-element.43), channel_id=1, source_target_pairs={{0,1},{1,2},{2,3},{3,0},{4,5},{5,6},{6,7},{7,4},{8,9},{9,10},{10,1... | collective-permute-start | bytes 1572872 | tf_op jit(solution)/shard_map/ppermute | solution.py:403
  200.7 13.0 %all-to-all-start.5 = ((f32[16,16,512]{2,1,0:T(8,128)}), f32[16,16,512]{2,1,0:T(8,128)S(1)}, u32[]{:S(2)}, u32[]{:S(2)}) async-start(f32[16,16,512]{2,1,0:T(8,128)} %broadcast_in_dim.8), calls=%async_computation.5 | async-start | bytes 1048576 | tf_op jit(solution)/shard_map/all_to_all | solution.py:359
  204.4 14.2 %collective-permute-start.17 = (f32[256,512]{1,0:T(8,128)S(1)}, f32[256,512]{1,0:T(8,128)S(1)}, u32[]{:S(2)}, u32[]{:S(2)}) collective-permute-start(f32[256,512]{1,0:T(8,128)S(1)} %bitcast.31), channel_id=1, source_target_pairs={{0,16},{16,0},{32,48},{48,32},{64,80},{80,64},{96,112},{112,96},{1... | collective-permute-start | bytes 1572872 | tf_op jit(solution)/shard_map/ppermute | solution.py:392
  213.6 4.9 %collective-permute-start.19 = (f32[256,512]{1,0:T(8,128)S(1)}, f32[256,512]{1,0:T(8,128)S(1)}, u32[]{:S(2)}, u32[]{:S(2)}) collective-permute-start(f32[256,512]{1,0:T(8,128)S(1)} %bitcast.33), channel_id=1, source_target_pairs={{0,16},{16,0},{32,48},{48,32},{64,80},{80,64},{96,112},{112,96},{1... | collective-permute-start | bytes 1572872 | tf_op jit(solution)/shard_map/ppermute | solution.py:411
  216.9 1.7 collective-permute-start.18
  222.5 12.8 %collective-permute-start.20 = (f32[128,640]{1,0:T(8,128)S(1)}, f32[128,640]{1,0:T(8,128)S(1)}, u32[]{:S(2)}, u32[]{:S(2)}) collective-permute-start(f32[128,640]{1,0:T(8,128)S(1)} %get-tuple-element.51), channel_id=1, source_target_pairs={{0,32},{16,48},{32,0},{48,16},{64,96},{80,112},{96,64},{112,80},{1... | collective-permute-start | bytes 983048 | tf_op jit(solution)/shard_map/ppermute | solution.py:426
  224.9 1.3 copy-start.4
  226.2 17.8 %copy-start.6 = (s32[2,256]{1,0:T(2,128)S(1)}, s32[2,256]{1,0:T(2,128)}, u32[]{:S(2)}) copy-start(s32[2,256]{1,0:T(2,128)} %param.13) | copy-start | bytes 6148
  235.3 7.2 %collective-permute-start.22 = (f32[128,512]{1,0:T(8,128)S(1)}, f32[128,512]{1,0:T(8,128)S(1)}, u32[]{:S(2)}, u32[]{:S(2)}) collective-permute-start(f32[128,512]{1,0:T(8,128)S(1)} %get-tuple-element.52), channel_id=1, source_target_pairs={{0,32},{16,48},{32,0},{48,16},{64,96},{80,112},{96,64},{112,80},{1... | collective-permute-start | bytes 786440 | tf_op jit(solution)/shard_map/ppermute | solution.py:433
  235.3 9.9 %collective-permute-start.21 = (f32[128,640]{1,0:T(8,128)S(1)}, f32[128,640]{1,0:T(8,128)S(1)}, u32[]{:S(2)}, u32[]{:S(2)}) collective-permute-start(f32[128,640]{1,0:T(8,128)S(1)} %collective-permute-done.20.pick_1), channel_id=1, source_target_pairs={{0,16},{16,0},{32,48},{48,32},{64,80},{80,64},{96,112},{112,96},{1... | collective-permute-start | bytes 983048 | tf_op jit(solution)/shard_map/ppermute | solution.py:427
  242.4 2.7 %collective-permute-start.23 = (f32[128,512]{1,0:T(8,128)S(1)}, f32[128,512]{1,0:T(8,128)S(1)}, u32[]{:S(2)}, u32[]{:S(2)}) collective-permute-start(f32[128,512]{1,0:T(8,128)S(1)} %collective-permute-done.22.proj_1), channel_id=1, source_target_pairs={{0,16},{16,0},{32,48},{48,32},{64,80},{80,64},{96,112},{112,96},{1... | collective-permute-start | bytes 786440 | tf_op jit(solution)/shard_map/ppermute | solution.py:434

commit v4 on v3

--- a/solution.py
+++ b/solution.py
@@ -19,12 +19,8 @@
 VMEM = pltpu.VMEM
 
 
-def along_x(k):
-    return [(4 * x + y, 4 * ((x + k) % 4) + y) for x in range(4) for y in range(4)]
-
-
-def along_y(k):
-    return [(4 * x + y, 4 * x + (y + k) % 4) for x in range(4) for y in range(4)]
+def shift(dx, dy):
+    return [(4 * x + y, 4 * ((x + dx) % 4) + (y + dy) % 4) for x in range(4) for y in range(4)]
 
 
 SIBLING = [(i, i ^ 1) for i in range(8)]
@@ -72,7 +68,8 @@
     return (mm(one_hot, h) + mm(one_hot, m)) + mm(one_hot, l)
 
 
-SHIFTS = (1, 3, 2)
+SOURCE = ((-1, 0), (0, -1), (1, 1))
+TARGET = ((2, 0), (0, 2), (2, 2))
 COUNT = 3 * SIDE
 
 
@@ -157,8 +154,10 @@
 
 
 def near_kernel(targets, feat_ref, prod_ref, right_ref, *refs):
-    outs, (acc, buf_a, buf_b) = refs[:len(targets)], refs[len(targets):]
+    before, outs, (acc, buf_a, buf_b) = refs[:-3 - len(targets)], refs[-3 - len(targets):-3], refs[-3:]
     acc[...] = jnp.zeros_like(acc)
+    for ref in before:
+        acc[0] += ref[...]
     total = len(targets) * COUNT
 
     def left(t):
@@ -250,8 +249,8 @@
 
 
 def basis_kernel(samp_ref, test_ref, coeffs_ref, *refs):
-    parts, (basis_ref, proj_ref) = refs[:SIDE], refs[SIDE:]
-    near_field = (parts[0][...] + parts[1][...]) + (parts[2][...] + parts[3][...])
+    parts, (basis_ref, proj_ref) = refs[:3], refs[3:]
+    near_field = parts[0][...] + (parts[1][...] + parts[2][...])
     basis = dot3(samp_ref[...], coeffs_ref[...], NT) - near_field
     basis_ref[...] = basis
     proj_ref[...] = dot3(basis.T, test_ref[...])
@@ -370,22 +369,22 @@
     weight = jnp.where(core == 0, near_mask[0, 0], near_mask[0, 1]).astype(F32).reshape(1, 1)
 
     (skel,) = call(skel_kernel, [((RANK, 2 * DIM), F32)], 1, 2, name="skel")(start, pivots, xt)
-    skel, message, xt = after(skel, jnp.concatenate([test_matrix, xt], axis=0), xt)
-    own = [message, lax.ppermute(message, "row", along_x(1)), lax.ppermute(message, "row", along_x(3))]
+    skel, message = after(skel, jnp.concatenate([test_matrix, xt], axis=0))
+    own = [message]
     sib = [lax.ppermute(message, "leaf", SIBLING)]
     outer = [lax.ppermute(message, "leaf", OUTER)]
     skel, message = sum_row(skel, message)
-    own.append(lax.ppermute(message, "row", along_x(2)))
+    own += [lax.ppermute(message, "row", shift(*by)) for by in SOURCE]
     (part,) = call(
         pivot_kernel, [((RANK, SAMP), F32)], 2, 6, [VMEM((4 * DIM, BLK), BF16)], name="pivot", flops=2 * 10**9
     )(start, weight, pivots, skel, samples, own[0], sib[0], outer[0])
-    part, xt, own[1], own[2] = after(part, xt, own[1], own[2])
-    (feats,) = call(feature_kernel, [((SIDE, BLK, 4 * DIM), BF16)], 0, 4, name="features")(
-        xt, *[lax.ppermute(xt, "row", along_y(k)) for k in SHIFTS]
-    )
-    picked, own[3] = sum_row(part, own[3])
+    part, *own[1:] = after(part, *own[1:])
     sib += [lax.ppermute(m, "leaf", SIBLING) for m in own[1:]]
     outer += [lax.ppermute(m, "leaf", OUTER) for m in own[1:]]
+    picked, xt = sum_row(part, xt)
+    (feats,) = call(feature_kernel, [((SIDE, BLK, 4 * DIM), BF16)], 0, 4, name="features")(
+        xt, *[lax.ppermute(xt, "row", shift(*by)) for by in TARGET]
+    )
     (coeffs,) = call(
         solve_kernel, [((RANK, SAMP), F32)], 0, 1, SOLVE_SCRATCH, name="solve", flops=3 * 10**9
     )(picked)
@@ -393,20 +392,23 @@
     skel_sib = lax.ppermute(skel, "leaf", SIBLING)
 
     block = ((BLK, RANK), F32)
-    sum_1, sum_3, sum_2, prods, rights = call(
-        functools.partial(far_kernel, (1, 2, 3)),
-        [block] * 3 + [((COUNT, 2 * BLK, RANK), BF16), ((COUNT, 4 * DIM, BLK), BF16)], 1, 2 + COUNT,
-        near_scratch((1, 2, 3)), name="near_far", flops=30 * 10**9,
+    sum_3, prods, rights = call(
+        functools.partial(far_kernel, (3,)),
+        [block] + [((COUNT, 2 * BLK, RANK), BF16), ((COUNT, 4 * DIM, BLK), BF16)], 1, 2 + COUNT,
+        near_scratch((3,)), name="near_3", flops=10**10,
     )(weight, coeffs, feats, *own, *sib, *outer)
-    sum_2 = lax.ppermute(sum_2, "row", along_y(-2))
-    sum_1 = lax.ppermute(sum_1, "row", along_y(-1))
-    sum_3 = lax.ppermute(sum_3, "row", along_y(-3))
+    got_3 = lax.ppermute(sum_3, "row", shift(*TARGET[2]))
+    sum_1, sum_2 = call(
+        functools.partial(near_kernel, (1, 2)), [block] * 2, 0, 3, near_scratch((1, 2)), name="near_12", flops=2 * 10**10,
+    )(feats, prods, rights)
+    got_1 = lax.ppermute(sum_1, "row", shift(*TARGET[0]))
+    got_2 = lax.ppermute(sum_2, "row", shift(*TARGET[1]))
     (sum_0,) = call(
-        functools.partial(near_kernel, (0,)), [block], 0, 3, near_scratch((0,)), name="near_own", flops=10**9
-    )(feats, prods, rights)
+        functools.partial(near_kernel, (0,)), [block], 0, 4, near_scratch((0,)), name="near_0", flops=10**10
+    )(feats, prods, rights, got_3)
     leaf_basis, proj = call(
-        basis_kernel, [block, ((RANK, SAMP), F32)], 0, 3 + SIDE, name="basis", flops=10**9
-    )(samples, test_matrix, coeffs, sum_0, sum_1, sum_2, sum_3)
+        basis_kernel, [block, ((RANK, SAMP), F32)], 0, 6, name="basis", flops=10**9
+    )(samples, test_matrix, coeffs, sum_0, got_1, got_2)
     (proj,) = sum_row(proj)
     proj_sib = lax.ppermute(proj, "leaf", SIBLING)
 

time: 257 us -> 261 us (1.016)
  Pallas kernels: 90.5 us -> 95 us
  blocking collectives: 42.9 us -> 39.1 us
    all_to_all x3, waiting for transfers between devices: 20 us -> 40.5 us  [sum_row(): lax.all_to_all(jnp.broadcast_to(mine[None], (16, *mine.shape)), 'row', 0, 0)]
    all_to_all x1 -> x0, waiting for transfers between devices: 15.4 us -> none  [sum_row(): parts = lax.all_to_all(part.reshape(16, share, -1), 'row', 0, 0)]
    ppermute x9, waiting for transfers between devices: 12.5 us -> 0.02 us  [the longest x3 0.01 us: body(): lax.ppermute(xt, 'row', shift(*by))]
    ppermute x3, waiting for transfers between devices: 0.67 us -> 10.4 us  [body(): outer += [lax.ppermute(m, 'leaf', OUTER) for m in own[1:]]]
    all_to_all x2 -> x3, blocking collectives: 42.9 us -> 39.1 us  [sum_row(): parts = lax.all_to_all(part.reshape(16, share, -1), 'row', 0, 0)]
    ppermute x1, starting transfers between devices: 2.4 us -> 6.16 us  [body(): pick_1 = lax.ppermute(send, 'leaf', COUSIN)]
    pallas_call x3 -> x4, Pallas kernels: 54.7 us -> 58.5 us  [the longest x1 21.8 us: body(): call(functools.partial(far_kernel, (3,)), [block] + [((COUNT, 2 * BLK, RA...]
    all_to_all x1 -> x0, starting transfers between devices: 3.59 us -> none  [sum_row(): parts = lax.all_to_all(part.reshape(16, share, -1), 'row', 0, 0)]
  transfers between devices with their start and end apart: 28 -> 27, of which waited for: 10 -> 7; matrix products, arithmetic and copies ran while one was open for 1% -> 1% of each run, Pallas kernels for 13% -> 21%
where the time goes in v4:
time: 261 us; the launch traced here: 260 us
  Pallas kernels  95 us (36%)
  waiting for transfers between devices  59.7 us (23%)
  starting transfers between devices  55.4 us (21%)
  blocking collectives  39.1 us (15%)
  local copies, waits for them, and re-layouts  7.2 us (3%)
    all_to_all x3, waiting for transfers between devices, sum_row(): lax.all_to_all(jnp.broadcast_to(mine[None], (16, *mine.shape)), 'row', 0, 0)  40.5 us
    all_to_all x3, blocking collectives, sum_row(): parts = lax.all_to_all(part.reshape(16, share, -1), 'row', 0, 0)  39.1 us
    pallas_call x1, Pallas kernels, body(): call(functools.partial(far_kernel, (3,)), [block] + [((COUNT, 2 * BLK, RA...  21.8 us
    pallas_call x1, Pallas kernels, body(): call(functools.partial(near_kernel, (1, 2)), [block] * 2, 0, 3, near_scra...  21 us
    all_to_all x3, starting transfers between devices, sum_row(): lax.all_to_all(jnp.broadcast_to(mine[None], (16, *mine.shape)), 'row', 0, 0)  13.2 us
    pallas_call x1, Pallas kernels, body(): call(functools.partial(near_kernel, (0,)), [block], 0, 4, near_scratch((0...  12.6 us
    ppermute x3, starting transfers between devices, body(): outer += [lax.ppermute(m, 'leaf', OUTER) for m in own[1:]]  12.2 us
    pallas_call x1, Pallas kernels, body(): call(functools.partial(top_kernel, top_share), [((top_share, RANK), F32)]...  11.1 us
  transfers between devices with their start and end apart: 27, of which 7 were waited for; matrix products, arithmetic and copies ran while one was open for 1% of the time, Pallas kernels for 21%

profile of v4, /device:TPU:1, one launch (start us, length us, event | category | flops | bytes accessed | tf_op | source)
XLA Modules:
  0.0 260.3 jit_solution(16291455952920529076)
XLA Ops:
  0.7 0.8 copy.11.piv_ref
  1.5 1.4 pad_maximum_fusion.own_ref.refs_0_
  3.3 1.5 collective-permute-start
  4.8 3.5 %collective-permute-start.1 = (f32[576,512]{1,0:T(8,128)S(1)}, f32[576,512]{1,0:T(8,128)}, u32[]{:S(2)}, u32[]{:S(2)}) collective-permute-start(f32[576,512]{1,0:T(8,128)S(1)} %pad_maximum_fusion.own_ref.refs_0_), channel_id=1, source_target_pairs={{16,32},{32,16},{48,64},{64,48},{80,96},{96,80},{17,33},{33,17},{4... | collective-permute-start | bytes 3538952 | tf_op jit(solution)/shard_map/ppermute | solution.py:375
  8.4 13.2 %all_to_all.30 = f32[16,16,128]{2,1,0:T(8,128)S(1)} all-to-all(f32[16,16,128]{2,1,0:T(8,128)S(1)} %bitcast.35), channel_id=1, replica_groups=mesh['leaf'=8,'row'=16] {'row'}, dimensions={0} | all-to-all | bytes 262144 | tf_op jit(solution)/shard_map/all_to_all | solution.py:356
  21.7 1.0 collective-permute-start.2
  22.6 0.8 collective-permute-start.3
  23.4 1.0 collective-permute-start.4
  24.4 0.7 broadcast_in_dim.6
  25.0 5.2 %all-to-all-start.1 = ((f32[16,16,128]{2,1,0:T(8,128)}), f32[16,16,128]{2,1,0:T(8,128)S(1)}, u32[]{:S(2)}, u32[]{:S(2)}) async-start(f32[16,16,128]{2,1,0:T(8,128)} %broadcast_in_dim.6), calls=%async_computation.1 | async-start | bytes 262144 | tf_op jit(solution)/shard_map/all_to_all | solution.py:358
  32.1 23.4 %all-to-all-done.1 = f32[16,16,128]{2,1,0:T(8,128)S(1)} async-done(((f32[16,16,128]{2,1,0:T(8,128)}), f32[16,16,128]{2,1,0:T(8,128)S(1)}, u32[]{:S(2)}, u32[]{:S(2)}) %all-to-all-start.1) | async-done | bytes 131104 | tf_op jit(solution)/shard_map/all_to_all | solution.py:358
  55.6 4.1 %pivot.1 = f32[256,512]{1,0:T(8,128)S(1)} custom-call(s32[1,1]{1,0:T(1,128)} %bitcast.start_ref, f32[1,1]{1,0:T(1,128)} %bitcast.3.weight_ref, s32[256,1]{1,0:T(8,128)S(1)} %copy.11.piv_ref, f32[256,128]{1,0:T(8,128)S(1)} %bitcast.36, f32[512,512]{1,0:T(8,128)S(1)} %copy-done.2, f32[576,512]{1,0:T(8,128)S(1)} %pad_maximum_fusion.own_ref.refs_0_, ...), custom_call_target="tpu_custom_call" | custom-call | flops 2000000000 | bytes 4194304 | tf_op jit(solution)/shard_map/pivot/pallas_call | solution.py:378
  59.7 1.2 collective-permute-start.10
  60.9 13.9 %all_to_all.31 = f32[16,16,512]{2,1,0:T(8,128)S(1)} all-to-all(f32[16,16,512]{2,1,0:T(8,128)S(1)} %bitcast.33), channel_id=1, replica_groups=mesh['leaf'=8,'row'=16] {'row'}, dimensions={0} | all-to-all | bytes 1048576 | tf_op jit(solution)/shard_map/all_to_all | solution.py:356
  74.8 1.6 collective-permute-start.5
  76.4 1.8 collective-permute-start.6
  78.1 2.4 collective-permute-start.7
  80.5 6.7 %collective-permute-start.13 = (f32[576,512]{1,0:T(8,128)}, f32[576,512]{1,0:T(8,128)}, u32[]{:S(2)}, u32[]{:S(2)}) collective-permute-start(f32[576,512]{1,0:T(8,128)} %collective-permute-done.4.refs_3_), channel_id=1, source_target_pairs={{16,32},{32,16},{48,64},{64,48},{80,96},{96,80},{17,33},{33,17},{4... | collective-permute-start | bytes 3538952 | tf_op jit(solution)/shard_map/ppermute | solution.py:383
  87.2 1.9 collective-permute-start.11
  89.2 3.6 %collective-permute-start.12 = (f32[576,512]{1,0:T(8,128)}, f32[576,512]{1,0:T(8,128)}, u32[]{:S(2)}, u32[]{:S(2)}) collective-permute-start(f32[576,512]{1,0:T(8,128)} %collective-permute-done.3.refs_2_), channel_id=1, source_target_pairs={{16,32},{32,16},{48,64},{64,48},{80,96},{96,80},{17,33},{33,17},{4... | collective-permute-start | bytes 3538952 | tf_op jit(solution)/shard_map/ppermute | solution.py:383
  93.5 0.9 broadcast_in_dim.7
  94.3 4.4 %all-to-all-start.3 = ((f32[16,16,512]{2,1,0:T(8,128)}), f32[16,16,512]{2,1,0:T(8,128)}, u32[]{:S(2)}, u32[]{:S(2)}) async-start(f32[16,16,512]{2,1,0:T(8,128)} %broadcast_in_dim.7), calls=%async_computation.3 | async-start | bytes 1048576 | tf_op jit(solution)/shard_map/all_to_all | solution.py:358
  98.8 0.9 copy-done.4
  99.7 0.9 copy-done.6
  101.0 8.2 %all-to-all-done.3 = f32[16,16,512]{2,1,0:T(8,128)} async-done(((f32[16,16,512]{2,1,0:T(8,128)}), f32[16,16,512]{2,1,0:T(8,128)}, u32[]{:S(2)}, u32[]{:S(2)}) %all-to-all-start.3) | async-done | bytes 524320 | tf_op jit(solution)/shard_map/all_to_all | solution.py:358
  109.2 7.1 %solve.1.coeffs_ref = f32[256,512]{1,0:T(8,128)S(1)} custom-call(f32[256,512]{1,0:T(8,128)} %bitcast.9.picked_ref.pick_own), custom_call_target="tpu_custom_call" | custom-call | flops 3000000000 | bytes 4194304 | tf_op jit(solution)/shard_map/solve/pallas_call | solution.py:388
  116.3 10.4 %collective-permute-done.12.refs_10_ = f32[576,512]{1,0:T(8,128)} collective-permute-done((f32[576,512]{1,0:T(8,128)}, f32[576,512]{1,0:T(8,128)}, u32[]{:S(2)}, u32[]{:S(2)}) %collective-permute-start.12) | collective-permute-done | bytes 1179680 | tf_op jit(solution)/shard_map/ppermute | solution.py:383
  126.7 21.8 %near_3.1 = (f32[512,256]{1,0:T(8,128)S(1)}, bf16[12,1024,256]{2,1,0:T(8,128)(2,1)}, bf16[12,256,512]{2,1,0:T(8,128)(2,1)}) custom-call(f32[1,1]{1,0:T(1,128)} %bitcast.3.weight_ref, f32[256,512]{1,0:T(8,128)S(1)} %solve.1.coeffs_ref, bf16[4,512,256]{2,1,0:T(8,128)(2,1)S(1)} %features.1.feat_ref, f32[576,512]{1,0:T(8,128)S(1)} %pad_maximum_fusion.own_ref.refs_0_, ...), custom_call_target="tpu_custom_call" | custom-call | flops 10000000000 | bytes 4194304 | tf_op jit(solution)/shard_map/near_3/pallas_call | solution.py:395
  148.5 1.8 collective-permute-start.14
  150.3 21.0 %near_12.1 = (f32[512,256]{1,0:T(8,128)S(1)}, f32[512,256]{1,0:T(8,128)S(1)}) custom-call(bf16[4,512,256]{2,1,0:T(8,128)(2,1)S(1)} %features.1.feat_ref, bf16[12,1024,256]{2,1,0:T(8,128)(2,1)} %get-tuple-element.37.prod_ref, bf16[12,256,512]{2,1,0:T(8,128)(2,1)} %get-tuple-element.38.right_ref), custom_call_target="tpu_custom_call" | custom-call | flops 20000000000 | bytes 4194304 | tf_op jit(solution)/shard_map/near_12/pallas_call | solution.py:401
  171.3 1.8 collective-permute-start.15
  173.1 2.2 collective-permute-start.16
  175.3 12.6 %near_0.1.refs_0_ = f32[512,256]{1,0:T(8,128)S(1)} custom-call(bf16[4,512,256]{2,1,0:T(8,128)(2,1)S(1)} %features.1.feat_ref, bf16[12,1024,256]{2,1,0:T(8,128)(2,1)} %get-tuple-element.37.prod_ref, bf16[12,256,512]{2,1,0:T(8,128)(2,1)} %get-tuple-element.38.right_ref, f32[512,256]{1,0:T(8,128)S(1)} %collective-permute-done.14.refs_0_), custom_call_target="tpu_custom_call" | custom-call | flops 10000000000 | bytes 4194304 | tf_op jit(solution)/shard_map/near_0/pallas_call | solution.py:406
  187.8 3.1 %basis.1 = (f32[512,256]{1,0:T(8,128)}, f32[256,512]{1,0:T(8,128)S(1)}) custom-call(f32[512,512]{1,0:T(8,128)S(1)} %copy-done.2, f32[512,512]{1,0:T(8,128)} %test_ref.1, f32[256,512]{1,0:T(8,128)S(1)} %solve.1.coeffs_ref, f32[512,256]{1,0:T(8,128)S(1)} %near_0.1.refs_0_, f32[512,256]{1,0:T(8,128)S(1)} %collective-permute-done.15.refs_1_, ...), custom_call_target="tpu_custom_call" | custom-call | flops 1000000000 | bytes 4194304 | tf_op jit(solution)/shard_map/basis/pallas_call | solution.py:409
  191.0 11.9 %all_to_all.32 = f32[16,16,512]{2,1,0:T(8,128)S(1)} all-to-all(f32[16,16,512]{2,1,0:T(8,128)S(1)} %bitcast.34), channel_id=1, replica_groups=mesh['leaf'=8,'row'=16] {'row'}, dimensions={0} | all-to-all | bytes 1048576 | tf_op jit(solution)/shard_map/all_to_all | solution.py:356
  203.0 0.9 broadcast_in_dim.8
  203.8 3.6 %all-to-all-start.5 = ((f32[16,16,512]{2,1,0:T(8,128)}), f32[16,16,512]{2,1,0:T(8,128)S(1)}, u32[]{:S(2)}, u32[]{:S(2)}) async-start(f32[16,16,512]{2,1,0:T(8,128)} %broadcast_in_dim.8), calls=%async_computation.5 | async-start | bytes 1048576 | tf_op jit(solution)/shard_map/all_to_all | solution.py:358
  207.5 8.8 %all-to-all-done.5 = f32[16,16,512]{2,1,0:T(8,128)S(1)} async-done(((f32[16,16,512]{2,1,0:T(8,128)}), f32[16,16,512]{2,1,0:T(8,128)S(1)}, u32[]{:S(2)}, u32[]{:S(2)}) %all-to-all-start.5) | async-done | bytes 524320 | tf_op jit(solution)/shard_map/all_to_all | solution.py:358
  217.1 1.3 collective-permute-done.18.skel_peer
  218.4 4.4 %mid_stack.1 = (f32[512,640]{1,0:T(8,128)}, f32[256,512]{1,0:T(8,128)S(1)}, f32[256,128]{1,0:T(8,128)S(1)}, f32[128,640]{1,0:T(8,128)S(1)}) custom-call(s32[1,3]{1,0:T(1,128)S(1)} %add_bitcast_fusion.info_ref, s32[256,1]{1,0:T(8,128)S(1)} %copy.12.piv_ref, f32[256,512]{1,0:T(8,128)} %bitcast.9.picked_ref.pick_own, f32[256,128]{1,0:T(8,128)S(1)} %bitcast.38, ...), custom_call_target="tpu_custom_call" | custom-call | flops 1000000000 | bytes 4194304 | tf_op jit(solution)/shard_map/mid_stack/pallas_call | solution.py:424
  222.9 6.2 %collective-permute-start.20 = (f32[128,640]{1,0:T(8,128)S(1)}, f32[128,640]{1,0:T(8,128)S(1)}, u32[]{:S(2)}, u32[]{:S(2)}) collective-permute-start(f32[128,640]{1,0:T(8,128)S(1)} %get-tuple-element.49), channel_id=1, source_target_pairs={{0,32},{16,48},{32,0},{48,16},{64,96},{80,112},{96,64},{112,80},{1... | collective-permute-start | bytes 983048 | tf_op jit(solution)/shard_map/ppermute | solution.py:428
  229.0 1.3 copy-done.9
  230.3 9.0 %mid_solve.1 = (f32[16,256]{1,0:T(8,128)}, f32[256,512]{1,0:T(8,128)S(1)}, f32[128,512]{1,0:T(8,128)S(1)}) custom-call(s32[1,3]{1,0:T(1,128)S(1)} %add_bitcast_fusion.info_ref, f32[512,640]{1,0:T(8,128)S(1)} %copy-done.9, f32[256,512]{1,0:T(8,128)S(1)} %get-tuple-element.45.picked_ref.pick_own, f32[256,512]{1,0:T(8,128)S(1)} %bitcast.32, ...), custom_call_target="tpu_custom_call" | custom-call | flops 3000000000 | bytes 4194304 | tf_op jit(solution)/shard_map/mid_solve/pallas_call | solution.py:430
  239.4 0.7 collective-permute-start.21
  240.0 6.5 %collective-permute-done.22.proj_1 = f32[128,512]{1,0:T(8,128)S(1)} collective-permute-done((f32[128,512]{1,0:T(8,128)S(1)}, f32[128,512]{1,0:T(8,128)S(1)}, u32[]{:S(2)}, u32[]{:S(2)}) %collective-permute-start.22) | collective-permute-done | bytes 262176 | tf_op jit(solution)/shard_map/ppermute | solution.py:435
  246.6 1.5 collective-permute-start.23
  248.3 0.9 collective-permute-done.23.proj_2
  249.3 11.1 %top.1 = f32[8,256]{1,0:T(8,128)} custom-call(s32[1,3]{1,0:T(1,128)S(1)} %add_bitcast_fusion.1.info_ref, s32[256,1]{1,0:T(8,128)S(1)} %copy.13.piv_ref, f32[256,512]{1,0:T(8,128)S(1)} %get-tuple-element.45.picked_ref.pick_own, f32[256,128]{1,0:T(8,128)S(1)} %get-tuple-element.47.skel_own, f32[256,512]{1,0:T(8,128)S(1)} %get-tuple-element.48.proj_own, ...), custom_call_target="tpu_custom_call" | custom-call | flops 3000000000 | bytes 4194304 | tf_op jit(solution)/shard_map/top/pallas_call | solution.py:438
  (59 shorter events, 3.2 us)
Async XLA Ops:
  0.6 216.2 %copy-start = (s32[4,256]{1,0:T(4,128)S(1)}, s32[4,256]{1,0:T(4,128)}, u32[]{:S(2)}) copy-start(s32[4,256]{1,0:T(4,128)} %param.12) | copy-start | bytes 12292
  1.5 1.4 copy-start.1
  2.9 27.4 %copy-start.10 = (s32[1,2]{1,0:T(1,128)S(1)}, s32[1,2]{1,0:T(1,128)}, u32[]{:S(2)}) copy-start(s32[1,2]{1,0:T(1,128)} %param.10) | copy-start | bytes 28
  2.9 52.7 %copy-start.2 = (f32[512,512]{1,0:T(8,128)S(1)}, f32[512,512]{1,0:T(8,128)}, u32[]{:S(2)}) copy-start(f32[512,512]{1,0:T(8,128)} %samp_ref.3) | copy-start | bytes 3145732
  3.3 52.2 %collective-permute-start = (f32[576,512]{1,0:T(8,128)S(1)}, f32[576,512]{1,0:T(8,128)}, u32[]{:S(2)}, u32[]{:S(2)}) collective-permute-start(f32[576,512]{1,0:T(8,128)S(1)} %pad_maximum_fusion.own_ref.refs_0_), channel_id=1, source_target_pairs={{0,16},{16,0},{32,48},{48,32},{64,80},{80,64},{96,112},{112,96},{1... | collective-permute-start | bytes 3538952 | tf_op jit(solution)/shard_map/ppermute | solution.py:374
  4.8 50.7 %collective-permute-start.1 = (f32[576,512]{1,0:T(8,128)S(1)}, f32[576,512]{1,0:T(8,128)}, u32[]{:S(2)}, u32[]{:S(2)}) collective-permute-start(f32[576,512]{1,0:T(8,128)S(1)} %pad_maximum_fusion.own_ref.refs_0_), channel_id=1, source_target_pairs={{16,32},{32,16},{48,64},{64,48},{80,96},{96,80},{17,33},{33,17},{4... | collective-permute-start | bytes 3538952 | tf_op jit(solution)/shard_map/ppermute | solution.py:375
  21.7 38.1 %collective-permute-start.2 = (f32[576,512]{1,0:T(8,128)S(1)}, f32[576,512]{1,0:T(8,128)}, u32[]{:S(2)}, u32[]{:S(2)}) collective-permute-start(f32[576,512]{1,0:T(8,128)S(1)} %pad_maximum_fusion.own_ref.refs_0_), channel_id=1, source_target_pairs={{0,12},{1,13},{2,14},{3,15},{4,0},{5,1},{6,2},{7,3},{8,4},{9,5},{1... | collective-permute-start | bytes 3538952 | tf_op jit(solution)/shard_map/ppermute | solution.py:377
  22.6 37.1 %collective-permute-start.3 = (f32[576,512]{1,0:T(8,128)S(1)}, f32[576,512]{1,0:T(8,128)}, u32[]{:S(2)}, u32[]{:S(2)}) collective-permute-start(f32[576,512]{1,0:T(8,128)S(1)} %pad_maximum_fusion.own_ref.refs_0_), channel_id=1, source_target_pairs={{0,3},{1,0},{2,1},{3,2},{4,7},{5,4},{6,5},{7,6},{8,11},{9,8},{10,9... | collective-permute-start | bytes 3538952 | tf_op jit(solution)/shard_map/ppermute | solution.py:377
  23.4 36.3 %collective-permute-start.4 = (f32[576,512]{1,0:T(8,128)S(1)}, f32[576,512]{1,0:T(8,128)}, u32[]{:S(2)}, u32[]{:S(2)}) collective-permute-start(f32[576,512]{1,0:T(8,128)S(1)} %pad_maximum_fusion.own_ref.refs_0_), channel_id=1, source_target_pairs={{0,5},{1,6},{2,7},{3,4},{4,9},{5,10},{6,11},{7,8},{8,13},{9,14},{1... | collective-permute-start | bytes 3538952 | tf_op jit(solution)/shard_map/ppermute | solution.py:377
  25.0 30.5 %all-to-all-start.1 = ((f32[16,16,128]{2,1,0:T(8,128)}), f32[16,16,128]{2,1,0:T(8,128)S(1)}, u32[]{:S(2)}, u32[]{:S(2)}) async-start(f32[16,16,128]{2,1,0:T(8,128)} %broadcast_in_dim.6), calls=%async_computation.1 | async-start | bytes 262144 | tf_op jit(solution)/shard_map/all_to_all | solution.py:358
  55.6 4.1 %copy-start.7 = (f32[16,16,128]{2,1,0:T(8,128)}, f32[16,16,128]{2,1,0:T(8,128)S(1)}, u32[]{:S(2)}) copy-start(f32[16,16,128]{2,1,0:T(8,128)S(1)} %all-to-all-done.1) | copy-start | bytes 393220
  59.7 33.2 %collective-permute-start.10 = (f32[576,512]{1,0:T(8,128)}, f32[576,512]{1,0:T(8,128)}, u32[]{:S(2)}, u32[]{:S(2)}) collective-permute-start(f32[576,512]{1,0:T(8,128)} %collective-permute-done.4.refs_3_), channel_id=1, source_target_pairs={{0,16},{16,0},{32,48},{48,32},{64,80},{80,64},{96,112},{112,96},{1... | collective-permute-start | bytes 3538952 | tf_op jit(solution)/shard_map/ppermute | solution.py:382
  74.8 12.4 %collective-permute-start.5 = (f32[64,512]{1,0:T(8,128)S(1)}, f32[64,512]{1,0:T(8,128)S(1)}, u32[]{:S(2)}, u32[]{:S(2)}) collective-permute-start(f32[64,512]{1,0:T(8,128)S(1)} %bitcast.26), channel_id=1, source_target_pairs={{0,8},{1,9},{2,10},{3,11},{4,12},{5,13},{6,14},{7,15},{8,0},{9,1},... | collective-permute-start | bytes 393224 | tf_op jit(solution)/shard_map/ppermute | solution.py:386
  76.4 12.8 %collective-permute-start.6 = (f32[64,512]{1,0:T(8,128)S(1)}, f32[64,512]{1,0:T(8,128)S(1)}, u32[]{:S(2)}, u32[]{:S(2)}) collective-permute-start(f32[64,512]{1,0:T(8,128)S(1)} %bitcast.27), channel_id=1, source_target_pairs={{0,2},{1,3},{2,0},{3,1},{4,6},{5,7},{6,4},{7,5},{8,10},{9,11},{10,... | collective-permute-start | bytes 393224 | tf_op jit(solution)/shard_map/ppermute | solution.py:386
  78.1 14.7 %collective-permute-start.7 = (f32[64,512]{1,0:T(8,128)S(1)}, f32[64,512]{1,0:T(8,128)S(1)}, u32[]{:S(2)}, u32[]{:S(2)}) collective-permute-start(f32[64,512]{1,0:T(8,128)S(1)} %bitcast.28), channel_id=1, source_target_pairs={{0,10},{1,11},{2,8},{3,9},{4,14},{5,15},{6,12},{7,13},{8,2},{9,3},... | collective-permute-start | bytes 393224 | tf_op jit(solution)/shard_map/ppermute | solution.py:386
  80.5 46.2 %collective-permute-start.13 = (f32[576,512]{1,0:T(8,128)}, f32[576,512]{1,0:T(8,128)}, u32[]{:S(2)}, u32[]{:S(2)}) collective-permute-start(f32[576,512]{1,0:T(8,128)} %collective-permute-done.4.refs_3_), channel_id=1, source_target_pairs={{16,32},{32,16},{48,64},{64,48},{80,96},{96,80},{17,33},{33,17},{4... | collective-permute-start | bytes 3538952 | tf_op jit(solution)/shard_map/ppermute | solution.py:383
  87.2 29.0 %collective-permute-start.11 = (f32[576,512]{1,0:T(8,128)}, f32[576,512]{1,0:T(8,128)}, u32[]{:S(2)}, u32[]{:S(2)}) collective-permute-start(f32[576,512]{1,0:T(8,128)} %collective-permute-done.2.refs_1_), channel_id=1, source_target_pairs={{16,32},{32,16},{48,64},{64,48},{80,96},{96,80},{17,33},{33,17},{4... | collective-permute-start | bytes 3538952 | tf_op jit(solution)/shard_map/ppermute | solution.py:383
  89.2 5.1 %copy-start.3 = (f32[64,512]{1,0:T(8,128)}, f32[64,512]{1,0:T(8,128)S(1)}, u32[]{:S(2)}) copy-start(f32[64,512]{1,0:T(8,128)S(1)} %collective-permute-done.6.p2) | copy-start | bytes 393220
  89.2 37.5 %collective-permute-start.12 = (f32[576,512]{1,0:T(8,128)}, f32[576,512]{1,0:T(8,128)}, u32[]{:S(2)}, u32[]{:S(2)}) collective-permute-start(f32[576,512]{1,0:T(8,128)} %collective-permute-done.3.refs_2_), channel_id=1, source_target_pairs={{16,32},{32,16},{48,64},{64,48},{80,96},{96,80},{17,33},{33,17},{4... | collective-permute-start | bytes 3538952 | tf_op jit(solution)/shard_map/ppermute | solution.py:383
  92.9 1.5 copy-start.5
  92.9 33.8 %collective-permute-start.8 = (f32[576,512]{1,0:T(8,128)}, f32[576,512]{1,0:T(8,128)}, u32[]{:S(2)}, u32[]{:S(2)}) collective-permute-start(f32[576,512]{1,0:T(8,128)} %collective-permute-done.2.refs_1_), channel_id=1, source_target_pairs={{0,16},{16,0},{32,48},{48,32},{64,80},{80,64},{96,112},{112,96},{1... | collective-permute-start | bytes 3538952 | tf_op jit(solution)/shard_map/ppermute | solution.py:382
  93.0 33.7 %collective-permute-start.9 = (f32[576,512]{1,0:T(8,128)}, f32[576,512]{1,0:T(8,128)}, u32[]{:S(2)}, u32[]{:S(2)}) collective-permute-start(f32[576,512]{1,0:T(8,128)} %collective-permute-done.3.refs_2_), channel_id=1, source_target_pairs={{0,16},{16,0},{32,48},{48,32},{64,80},{80,64},{96,112},{112,96},{1... | collective-permute-start | bytes 3538952 | tf_op jit(solution)/shard_map/ppermute | solution.py:382
  94.3 14.9 %all-to-all-start.3 = ((f32[16,16,512]{2,1,0:T(8,128)}), f32[16,16,512]{2,1,0:T(8,128)}, u32[]{:S(2)}, u32[]{:S(2)}) async-start(f32[16,16,512]{2,1,0:T(8,128)} %broadcast_in_dim.7), calls=%async_computation.3 | async-start | bytes 1048576 | tf_op jit(solution)/shard_map/all_to_all | solution.py:358
  98.7 0.9 copy-start.4
  99.7 0.9 copy-start.6
  148.5 26.8 %collective-permute-start.14 = (f32[512,256]{1,0:T(8,128)S(1)}, f32[512,256]{1,0:T(8,128)S(1)}, u32[]{:S(2)}, u32[]{:S(2)}) collective-permute-start(f32[512,256]{1,0:T(8,128)S(1)} %get-tuple-element.39), channel_id=1, source_target_pairs={{0,10},{1,11},{2,8},{3,9},{4,14},{5,15},{6,12},{7,13},{8,2},{9,3},... | collective-permute-start | bytes 1572872 | tf_op jit(solution)/shard_map/ppermute | solution.py:400
  171.3 16.5 %collective-permute-start.15 = (f32[512,256]{1,0:T(8,128)S(1)}, f32[512,256]{1,0:T(8,128)S(1)}, u32[]{:S(2)}, u32[]{:S(2)}) collective-permute-start(f32[512,256]{1,0:T(8,128)S(1)} %get-tuple-element.40), channel_id=1, source_target_pairs={{0,8},{1,9},{2,10},{3,11},{4,12},{5,13},{6,14},{7,15},{8,0},{9,1},... | collective-permute-start | bytes 1572872 | tf_op jit(solution)/shard_map/ppermute | solution.py:404
  173.1 14.7 %collective-permute-start.16 = (f32[512,256]{1,0:T(8,128)S(1)}, f32[512,256]{1,0:T(8,128)S(1)}, u32[]{:S(2)}, u32[]{:S(2)}) collective-permute-start(f32[512,256]{1,0:T(8,128)S(1)} %get-tuple-element.41), channel_id=1, source_target_pairs={{0,2},{1,3},{2,0},{3,1},{4,6},{5,7},{6,4},{7,5},{8,10},{9,11},{10,... | collective-permute-start | bytes 1572872 | tf_op jit(solution)/shard_map/ppermute | solution.py:405
  202.9 13.4 %copy-start.8 = (f32[16,16,128]{2,1,0:T(8,128)S(1)}, f32[16,16,128]{2,1,0:T(8,128)}, u32[]{:S(2)}) copy-start(f32[16,16,128]{2,1,0:T(8,128)} %copy-done.7) | copy-start | bytes 393220
  203.8 12.5 %all-to-all-start.5 = ((f32[16,16,512]{2,1,0:T(8,128)}), f32[16,16,512]{2,1,0:T(8,128)S(1)}, u32[]{:S(2)}, u32[]{:S(2)}) async-start(f32[16,16,512]{2,1,0:T(8,128)} %broadcast_in_dim.8), calls=%async_computation.5 | async-start | bytes 1048576 | tf_op jit(solution)/shard_map/all_to_all | solution.py:358
  207.4 11.0 %collective-permute-start.17 = (f32[256,512]{1,0:T(8,128)}, f32[256,512]{1,0:T(8,128)S(1)}, u32[]{:S(2)}, u32[]{:S(2)}) collective-permute-start(f32[256,512]{1,0:T(8,128)} %bitcast.9.picked_ref.pick_own), channel_id=1, source_target_pairs={{0,16},{16,0},{32,48},{48,32},{64,80},{80,64},{96,112},{112,96},{1... | collective-permute-start | bytes 1572872 | tf_op jit(solution)/shard_map/ppermute | solution.py:391
  216.3 2.1 collective-permute-start.19
  216.3 2.1 collective-permute-start.18
  222.9 16.5 %collective-permute-start.20 = (f32[128,640]{1,0:T(8,128)S(1)}, f32[128,640]{1,0:T(8,128)S(1)}, u32[]{:S(2)}, u32[]{:S(2)}) collective-permute-start(f32[128,640]{1,0:T(8,128)S(1)} %get-tuple-element.49), channel_id=1, source_target_pairs={{0,32},{16,48},{32,0},{48,16},{64,96},{80,112},{96,64},{112,80},{1... | collective-permute-start | bytes 983048 | tf_op jit(solution)/shard_map/ppermute | solution.py:428
  229.0 1.3 copy-start.9
  230.3 17.8 %copy-start.11 = (s32[2,256]{1,0:T(2,128)S(1)}, s32[2,256]{1,0:T(2,128)}, u32[]{:S(2)}) copy-start(s32[2,256]{1,0:T(2,128)} %param.13) | copy-start | bytes 6148
  239.4 7.2 %collective-permute-start.22 = (f32[128,512]{1,0:T(8,128)S(1)}, f32[128,512]{1,0:T(8,128)S(1)}, u32[]{:S(2)}, u32[]{:S(2)}) collective-permute-start(f32[128,512]{1,0:T(8,128)S(1)} %get-tuple-element.50), channel_id=1, source_target_pairs={{0,32},{16,48},{32,0},{48,16},{64,96},{80,112},{96,64},{112,80},{1... | collective-permute-start | bytes 786440 | tf_op jit(solution)/shard_map/ppermute | solution.py:435
  239.4 9.9 %collective-permute-start.21 = (f32[128,640]{1,0:T(8,128)S(1)}, f32[128,640]{1,0:T(8,128)S(1)}, u32[]{:S(2)}, u32[]{:S(2)}) collective-permute-start(f32[128,640]{1,0:T(8,128)S(1)} %collective-permute-done.20.pick_1), channel_id=1, source_target_pairs={{0,16},{16,0},{32,48},{48,32},{64,80},{80,64},{96,112},{112,96},{1... | collective-permute-start | bytes 983048 | tf_op jit(solution)/shard_map/ppermute | solution.py:429
  246.6 2.7 %collective-permute-start.23 = (f32[128,512]{1,0:T(8,128)S(1)}, f32[128,512]{1,0:T(8,128)S(1)}, u32[]{:S(2)}, u32[]{:S(2)}) collective-permute-start(f32[128,512]{1,0:T(8,128)S(1)} %collective-permute-done.22.proj_1), channel_id=1, source_target_pairs={{0,16},{16,0},{32,48},{48,32},{64,80},{80,64},{96,112},{112,96},{1... | collective-permute-start | bytes 786440 | tf_op jit(solution)/shard_map/ppermute | solution.py:436

commit v5 on v4

--- a/solution.py
+++ b/solution.py
@@ -138,12 +138,14 @@
 
 
 def far_kernel(targets, weight_ref, coeffs_ref, feat_ref, *refs):
-    msgs, refs = refs[:COUNT], refs[COUNT:]
+    msgs, refs = refs[:6], refs[6:]
     outs, (prod_ref, right_ref), scratch = refs[:len(targets)], refs[len(targets):-3], refs[-3:]
     ch, cl = split2(coeffs_ref[...])
-    for at, ref in enumerate(msgs):
-        right_features(ref[BLK:, :], right_ref.at[at])
-        test = ref[0:BLK, :]
+    for at in range(COUNT):
+        n, place = divmod(at, SIDE)
+        ref, first = (msgs[2 * n + 1], (place - 1) * (BLK + DIM)) if place else (msgs[2 * n], 0)
+        right_features(ref[first + BLK:first + BLK + DIM, :], right_ref.at[at])
+        test = ref[first:first + BLK, :]
         if at >= 2 * SIDE:
             test = test * weight_ref[0, 0]
         th, tl = split2(test)
@@ -196,7 +198,7 @@
         out_specs=[pl.BlockSpec(memory_space=VMEM)] * len(outs),
         scratch_shapes=list(scratch),
         compiler_params=pltpu.CompilerParams(vmem_limit_bytes=50 * 2**20),
-        cost_estimate=pl.CostEstimate(flops=flops, bytes_accessed=4 * 2**20, transcendentals=trans),
+        cost_estimate=pl.CostEstimate(flops=flops, bytes_accessed=2**16, transcendentals=trans),
         name=name,
     )
 
@@ -373,20 +375,20 @@
     own = [message]
     sib = [lax.ppermute(message, "leaf", SIBLING)]
     outer = [lax.ppermute(message, "leaf", OUTER)]
-    skel, message = sum_row(skel, message)
     own += [lax.ppermute(message, "row", shift(*by)) for by in SOURCE]
+    skel, sib[0], outer[0], *own[1:] = sum_row(skel, sib[0], outer[0], *own[1:])
     (part,) = call(
-        pivot_kernel, [((RANK, SAMP), F32)], 2, 6, [VMEM((4 * DIM, BLK), BF16)], name="pivot", flops=2 * 10**9
+        pivot_kernel, [((RANK, SAMP), F32)], 2, 6, [VMEM((4 * DIM, BLK), BF16)], name="pivot"
     )(start, weight, pivots, skel, samples, own[0], sib[0], outer[0])
-    part, *own[1:] = after(part, *own[1:])
-    sib += [lax.ppermute(m, "leaf", SIBLING) for m in own[1:]]
-    outer += [lax.ppermute(m, "leaf", OUTER) for m in own[1:]]
+    own[1:] = [jnp.concatenate(own[1:], axis=0)]
+    sib.append(lax.ppermute(own[1], "leaf", SIBLING))
+    outer.append(lax.ppermute(own[1], "leaf", OUTER))
     picked, xt = sum_row(part, xt)
     (feats,) = call(feature_kernel, [((SIDE, BLK, 4 * DIM), BF16)], 0, 4, name="features")(
         xt, *[lax.ppermute(xt, "row", shift(*by)) for by in TARGET]
     )
     (coeffs,) = call(
-        solve_kernel, [((RANK, SAMP), F32)], 0, 1, SOLVE_SCRATCH, name="solve", flops=3 * 10**9
+        solve_kernel, [((RANK, SAMP), F32)], 0, 1, SOLVE_SCRATCH, name="solve"
     )(picked)
     picked_sib = lax.ppermute(picked, "leaf", SIBLING)
     skel_sib = lax.ppermute(skel, "leaf", SIBLING)
@@ -394,13 +396,14 @@
     block = ((BLK, RANK), F32)
     sum_3, prods, rights = call(
         functools.partial(far_kernel, (3,)),
-        [block] + [((COUNT, 2 * BLK, RANK), BF16), ((COUNT, 4 * DIM, BLK), BF16)], 1, 2 + COUNT,
+        [block] + [((COUNT, 2 * BLK, RANK), BF16), ((COUNT, 4 * DIM, BLK), BF16)], 1, 8,
         near_scratch((3,)), name="near_3", flops=10**10,
     )(weight, coeffs, feats, *own, *sib, *outer)
     got_3 = lax.ppermute(sum_3, "row", shift(*TARGET[2]))
     sum_1, sum_2 = call(
         functools.partial(near_kernel, (1, 2)), [block] * 2, 0, 3, near_scratch((1, 2)), name="near_12", flops=2 * 10**10,
     )(feats, prods, rights)
+    got_3, picked_sib, skel_sib = after(got_3, picked_sib, skel_sib)
     got_1 = lax.ppermute(sum_1, "row", shift(*TARGET[0]))
     got_2 = lax.ppermute(sum_2, "row", shift(*TARGET[1]))
     (sum_0,) = call(

time: 261 us -> 252 us (0.966)
  waiting for transfers between devices: 59.7 us -> 19.9 us
  blocking collectives: 39.1 us -> 70.7 us
  starting transfers between devices: 55.4 us -> 48.9 us
  local copies, waits for them, and re-layouts: 7.2 us -> 13.7 us
    all_to_all x3 -> x2, waiting for transfers between devices: 40.5 us -> 4.74 us  [sum_row(): lax.all_to_all(jnp.broadcast_to(mine[None], (16, *mine.shape)), 'row', 0, 0)]
    all_to_all x3, blocking collectives: 39.1 us -> 58.1 us  [sum_row(): parts = lax.all_to_all(part.reshape(16, share, -1), 'row', 0, 0)]
    all_to_all x0 -> x1, blocking collectives: none -> 12.6 us  [sum_row(): lax.all_to_all(jnp.broadcast_to(mine[None], (16, *mine.shape)), 'row', 0, 0)]
    ppermute x6 -> x2, waiting for transfers between devices: 10.4 us -> 0.01 us  [the longest x1 0.01 us: body(): sib.append(lax.ppermute(own[1], 'leaf', SIBLING))]
    ppermute x6 -> x2, starting transfers between devices: 14 us -> 4.41 us  [the longest x1 4.4 us: body(): outer.append(lax.ppermute(own[1], 'leaf', OUTER))]
    ppermute x3, waiting for transfers between devices: 0.01 us -> 6.42 us  [body(): lax.ppermute(xt, 'row', shift(*by))]
    all_to_all x3 -> x2, starting transfers between devices: 13.2 us -> 7.97 us  [sum_row(): lax.all_to_all(jnp.broadcast_to(mine[None], (16, *mine.shape)), 'row', 0, 0)]
    unnamed x24 -> x22, local copies, waits for them, and re-layouts: 3.16 us -> 8.05 us
  transfers between devices with their start and end apart: 27 -> 22, of which waited for: 7 -> 6; matrix products, arithmetic and copies ran while one was open for 1% -> 1% of each run, Pallas kernels for 21% -> 30%
where the time goes in v5:
time: 252 us; the launch traced here: 251 us
  Pallas kernels  93.6 us (37%)
  blocking collectives  70.7 us (28%)
  starting transfers between devices  48.9 us (19%)
  waiting for transfers between devices  19.9 us (8%)
  local copies, waits for them, and re-layouts  13.7 us (5%)
    all_to_all x3, blocking collectives, sum_row(): parts = lax.all_to_all(part.reshape(16, share, -1), 'row', 0, 0)  58.1 us
    pallas_call x1, Pallas kernels, body(): call(functools.partial(far_kernel, (3,)), [block] + [((COUNT, 2 * BLK, RA...  21.8 us
    pallas_call x1, Pallas kernels, body(): call(functools.partial(near_kernel, (1, 2)), [block] * 2, 0, 3, near_scra...  20.8 us
    all_to_all x1, blocking collectives, sum_row(): lax.all_to_all(jnp.broadcast_to(mine[None], (16, *mine.shape)), 'row', 0, 0)  12.6 us
    pallas_call x1, Pallas kernels, body(): call(functools.partial(near_kernel, (0,)), [block], 0, 4, near_scratch((0...  12.5 us
    pallas_call x1, Pallas kernels, body(): call(functools.partial(top_kernel, top_share), [((top_share, RANK), F32)]...  11.1 us
    pallas_call x1, Pallas kernels, body(): call(functools.partial(mid_kernel, mid_share), [((mid_share, RANK), F32),...  9.05 us
    unnamed x22, local copies, waits for them, and re-layouts  8.05 us
  transfers between devices with their start and end apart: 22, of which 6 were waited for; matrix products, arithmetic and copies ran while one was open for 1% of the time, Pallas kernels for 30%

profile of v5, /device:TPU:1, one launch (start us, length us, event | category | flops | bytes accessed | tf_op | source)
XLA Modules:
  0.0 250.6 jit_solution(18182545560474136170)
XLA Ops:
  0.7 0.8 copy.11.piv_ref
  1.5 1.4 pad_maximum_fusion.own_ref.refs_0_
  2.9 0.9 copy-done.2
  4.2 1.5 collective-permute-start
  5.7 3.5 %collective-permute-start.1 = (f32[576,512]{1,0:T(8,128)S(1)}, f32[576,512]{1,0:T(8,128)}, u32[]{:S(2)}, u32[]{:S(2)}) collective-permute-start(f32[576,512]{1,0:T(8,128)S(1)} %pad_maximum_fusion.own_ref.refs_0_), channel_id=1, source_target_pairs={{16,32},{32,16},{48,64},{64,48},{80,96},{96,80},{17,33},{33,17},{4... | collective-permute-start | bytes 3538952 | tf_op jit(solution)/shard_map/ppermute | solution.py:377
  9.2 2.5 %collective-permute-start.2 = (f32[576,512]{1,0:T(8,128)S(1)}, f32[576,512]{1,0:T(8,128)S(1)}, u32[]{:S(2)}, u32[]{:S(2)}) collective-permute-start(f32[576,512]{1,0:T(8,128)S(1)} %pad_maximum_fusion.own_ref.refs_0_), channel_id=1, source_target_pairs={{0,12},{1,13},{2,14},{3,15},{4,0},{5,1},{6,2},{7,3},{8,4},{9,5},{1... | collective-permute-start | bytes 3538952 | tf_op jit(solution)/shard_map/ppermute | solution.py:378
  11.8 2.7 %collective-permute-start.3 = (f32[576,512]{1,0:T(8,128)S(1)}, f32[576,512]{1,0:T(8,128)}, u32[]{:S(2)}, u32[]{:S(2)}) collective-permute-start(f32[576,512]{1,0:T(8,128)S(1)} %pad_maximum_fusion.own_ref.refs_0_), channel_id=1, source_target_pairs={{0,3},{1,0},{2,1},{3,2},{4,7},{5,4},{6,5},{7,6},{8,11},{9,8},{10,9... | collective-permute-start | bytes 3538952 | tf_op jit(solution)/shard_map/ppermute | solution.py:378
  14.5 31.9 %all_to_all.30 = f32[16,16,128]{2,1,0:T(8,128)S(1)} all-to-all(f32[16,16,128]{2,1,0:T(8,128)S(1)} %bitcast.41), channel_id=1, replica_groups=mesh['leaf'=8,'row'=16] {'row'}, dimensions={0} | all-to-all | bytes 262144 | tf_op jit(solution)/shard_map/all_to_all | solution.py:358
  46.5 1.1 constant_dynamic-update-slice_fusion.2
  47.6 2.5 constant_dynamic-update-slice_fusion.1
  50.1 2.4 constant_dynamic-update-slice_fusion.refs_1_
  52.5 4.4 %collective-permute-start.9 = (f32[1728,512]{1,0:T(8,128)}, f32[1728,512]{1,0:T(8,128)}, u32[]{:S(2)}, u32[]{:S(2)}) collective-permute-start(f32[1728,512]{1,0:T(8,128)} %constant_dynamic-update-slice_fusion.refs_1_), channel_id=1, source_target_pairs={{16,32},{32,16},{48,64},{64,48},{80,96},{96,80},{17,33},{33,17},{4... | collective-permute-start | bytes 10616840 | tf_op jit(solution)/shard_map/ppermute | solution.py:385
  56.9 0.7 broadcast_in_dim.6
  57.6 3.5 %all-to-all-start.1 = ((f32[16,16,128]{2,1,0:T(8,128)}), f32[16,16,128]{2,1,0:T(8,128)S(1)}, u32[]{:S(2)}, u32[]{:S(2)}) async-start(f32[16,16,128]{2,1,0:T(8,128)} %broadcast_in_dim.6), calls=%async_computation.1 | async-start | bytes 262144 | tf_op jit(solution)/shard_map/all_to_all | solution.py:360
  63.0 4.7 %all-to-all-done.1 = f32[16,16,128]{2,1,0:T(8,128)S(1)} async-done(((f32[16,16,128]{2,1,0:T(8,128)}), f32[16,16,128]{2,1,0:T(8,128)S(1)}, u32[]{:S(2)}, u32[]{:S(2)}) %all-to-all-start.1) | async-done | bytes 131104 | tf_op jit(solution)/shard_map/all_to_all | solution.py:360
  67.7 4.1 %pivot.1 = f32[256,512]{1,0:T(8,128)S(1)} custom-call(s32[1,1]{1,0:T(1,128)} %bitcast.start_ref, f32[1,1]{1,0:T(1,128)} %bitcast.3.weight_ref, s32[256,1]{1,0:T(8,128)S(1)} %copy.11.piv_ref, f32[256,128]{1,0:T(8,128)S(1)} %bitcast.34, f32[512,512]{1,0:T(8,128)S(1)} %copy-done.1, f32[576,512]{1,0:T(8,128)S(1)} %pad_maximum_fusion.own_ref.refs_0_, ...), custom_call_target="tpu_custom_call" | custom-call | bytes 65536 | tf_op jit(solution)/shard_map/pivot/pallas_call | solution.py:380
  71.8 13.3 %all_to_all.31 = f32[16,16,512]{2,1,0:T(8,128)S(1)} all-to-all(f32[16,16,512]{2,1,0:T(8,128)S(1)} %bitcast.24), channel_id=1, replica_groups=mesh['leaf'=8,'row'=16] {'row'}, dimensions={0} | all-to-all | bytes 1048576 | tf_op jit(solution)/shard_map/all_to_all | solution.py:358
  85.2 0.9 broadcast_in_dim.7
  86.1 4.5 %all-to-all-start.3 = ((f32[16,16,512]{2,1,0:T(8,128)}), f32[16,16,512]{2,1,0:T(8,128)S(1)}, u32[]{:S(2)}, u32[]{:S(2)}) async-start(f32[16,16,512]{2,1,0:T(8,128)} %broadcast_in_dim.7), calls=%async_computation.3 | async-start | bytes 1048576 | tf_op jit(solution)/shard_map/all_to_all | solution.py:360
  90.6 2.9 %collective-permute-start.5 = (f32[64,512]{1,0:T(8,128)S(1)}, f32[64,512]{1,0:T(8,128)S(1)}, u32[]{:S(2)}, u32[]{:S(2)}) collective-permute-start(f32[64,512]{1,0:T(8,128)S(1)} %bitcast.30), channel_id=1, source_target_pairs={{0,8},{1,9},{2,10},{3,11},{4,12},{5,13},{6,14},{7,15},{8,0},{9,1},... | collective-permute-start | bytes 393224 | tf_op jit(solution)/shard_map/ppermute | solution.py:388
  93.5 2.7 %collective-permute-start.6 = (f32[64,512]{1,0:T(8,128)S(1)}, f32[64,512]{1,0:T(8,128)S(1)}, u32[]{:S(2)}, u32[]{:S(2)}) collective-permute-start(f32[64,512]{1,0:T(8,128)S(1)} %bitcast.31), channel_id=1, source_target_pairs={{0,2},{1,3},{2,0},{3,1},{4,6},{5,7},{6,4},{7,5},{8,10},{9,11},{10,... | collective-permute-start | bytes 393224 | tf_op jit(solution)/shard_map/ppermute | solution.py:388
  96.3 5.1 %collective-permute-done.5.p1 = f32[64,512]{1,0:T(8,128)S(1)} collective-permute-done((f32[64,512]{1,0:T(8,128)S(1)}, f32[64,512]{1,0:T(8,128)S(1)}, u32[]{:S(2)}, u32[]{:S(2)}) %collective-permute-start.5) | collective-permute-done | bytes 131104 | tf_op jit(solution)/shard_map/ppermute | solution.py:388
  101.4 3.6 %collective-permute-start.12 = (f32[256,128]{1,0:T(8,128)S(1)}, f32[256,128]{1,0:T(8,128)}, u32[]{:S(2)}, u32[]{:S(2)}) collective-permute-start(f32[256,128]{1,0:T(8,128)S(1)} %bitcast.35), channel_id=1, source_target_pairs={{0,16},{16,0},{32,48},{48,32},{64,80},{80,64},{96,112},{112,96},{1... | collective-permute-start | bytes 393224 | tf_op jit(solution)/shard_map/ppermute | solution.py:394
  105.1 1.3 collective-permute-done.7.p3
  106.8 1.0 copy-done.4
  107.8 6.1 %solve.1.coeffs_ref = f32[256,512]{1,0:T(8,128)S(1)} custom-call(f32[256,512]{1,0:T(8,128)S(1)} %bitcast.25), custom_call_target="tpu_custom_call" | custom-call | bytes 65536 | tf_op jit(solution)/shard_map/solve/pallas_call | solution.py:390
  113.8 2.8 %collective-permute-start.11 = (f32[256,512]{1,0:T(8,128)S(1)}, f32[256,512]{1,0:T(8,128)S(1)}, u32[]{:S(2)}, u32[]{:S(2)}) collective-permute-start(f32[256,512]{1,0:T(8,128)S(1)} %bitcast.26), channel_id=1, source_target_pairs={{0,16},{16,0},{32,48},{48,32},{64,80},{80,64},{96,112},{112,96},{1... | collective-permute-start | bytes 1572872 | tf_op jit(solution)/shard_map/ppermute | solution.py:393
  116.6 1.2 copy-done.5
  117.9 21.8 %near_3.1 = (f32[512,256]{1,0:T(8,128)S(1)}, bf16[12,1024,256]{2,1,0:T(8,128)(2,1)}, bf16[12,256,512]{2,1,0:T(8,128)(2,1)}) custom-call(f32[1,1]{1,0:T(1,128)} %bitcast.3.weight_ref, f32[256,512]{1,0:T(8,128)S(1)} %solve.1.coeffs_ref, bf16[4,512,256]{2,1,0:T(8,128)(2,1)S(1)} %copy-done.5, f32[576,512]{1,0:T(8,128)S(1)} %pad_maximum_fusion.own_ref.refs_0_, ...), custom_call_target="tpu_custom_call" | custom-call | flops 10000000000 | bytes 65536 | tf_op jit(solution)/shard_map/near_3/pallas_call | solution.py:397
  139.6 0.7 collective-permute-start.10
  140.4 20.8 %near_12.1 = (f32[512,256]{1,0:T(8,128)S(1)}, f32[512,256]{1,0:T(8,128)S(1)}) custom-call(bf16[4,512,256]{2,1,0:T(8,128)(2,1)S(1)} %copy-done.6, bf16[12,1024,256]{2,1,0:T(8,128)(2,1)} %get-tuple-element.40.prod_ref, bf16[12,256,512]{2,1,0:T(8,128)(2,1)} %get-tuple-element.41.right_ref), custom_call_target="tpu_custom_call" | custom-call | flops 20000000000 | bytes 65536 | tf_op jit(solution)/shard_map/near_12/pallas_call | solution.py:403
  161.2 2.3 collective-permute-start.13
  163.5 2.7 %collective-permute-start.14 = (f32[512,256]{1,0:T(8,128)S(1)}, f32[512,256]{1,0:T(8,128)S(1)}, u32[]{:S(2)}, u32[]{:S(2)}) collective-permute-start(f32[512,256]{1,0:T(8,128)S(1)} %get-tuple-element.45), channel_id=1, source_target_pairs={{0,2},{1,3},{2,0},{3,1},{4,6},{5,7},{6,4},{7,5},{8,10},{9,11},{10,... | collective-permute-start | bytes 1572872 | tf_op jit(solution)/shard_map/ppermute | solution.py:408
  166.2 12.5 %near_0.1.refs_0_ = f32[512,256]{1,0:T(8,128)S(1)} custom-call(bf16[4,512,256]{2,1,0:T(8,128)(2,1)S(1)} %copy-done.6, bf16[12,1024,256]{2,1,0:T(8,128)(2,1)} %get-tuple-element.40.prod_ref, bf16[12,256,512]{2,1,0:T(8,128)(2,1)} %get-tuple-element.41.right_ref, f32[512,256]{1,0:T(8,128)S(1)} %collective-permute-done.10.refs_0_), custom_call_target="tpu_custom_call" | custom-call | flops 10000000000 | bytes 65536 | tf_op jit(solution)/shard_map/near_0/pallas_call | solution.py:409
  178.7 3.1 %basis.1 = (f32[512,256]{1,0:T(8,128)}, f32[256,512]{1,0:T(8,128)S(1)}) custom-call(f32[512,512]{1,0:T(8,128)S(1)} %copy-done.1, f32[512,512]{1,0:T(8,128)} %test_ref.1, f32[256,512]{1,0:T(8,128)S(1)} %solve.1.coeffs_ref, f32[512,256]{1,0:T(8,128)S(1)} %near_0.1.refs_0_, f32[512,256]{1,0:T(8,128)S(1)} %collective-permute-done.13.refs_1_, ...), custom_call_target="tpu_custom_call" | custom-call | flops 1000000000 | bytes 65536 | tf_op jit(solution)/shard_map/basis/pallas_call | solution.py:412
  181.9 12.8 %all_to_all.32 = f32[16,16,512]{2,1,0:T(8,128)S(1)} all-to-all(f32[16,16,512]{2,1,0:T(8,128)S(1)} %bitcast.40), channel_id=1, replica_groups=mesh['leaf'=8,'row'=16] {'row'}, dimensions={0} | all-to-all | bytes 1048576 | tf_op jit(solution)/shard_map/all_to_all | solution.py:358
  194.8 12.6 %all_to_all.33 = f32[16,16,512]{2,1,0:T(8,128)S(1)} all-to-all(f32[16,16,512]{2,1,0:T(8,128)S(1)} %broadcast_in_dim.8), channel_id=1, replica_groups=mesh['leaf'=8,'row'=16] {'row'}, dimensions={0} | all-to-all | bytes 1048576 | tf_op jit(solution)/shard_map/all_to_all | solution.py:360
  207.4 4.1 %collective-permute-start.15 = (f32[256,512]{1,0:T(8,128)S(1)}, f32[256,512]{1,0:T(8,128)S(1)}, u32[]{:S(2)}, u32[]{:S(2)}) collective-permute-start(f32[256,512]{1,0:T(8,128)S(1)} %bitcast.37), channel_id=1, source_target_pairs={{0,16},{16,0},{32,48},{48,32},{64,80},{80,64},{96,112},{112,96},{1... | collective-permute-start | bytes 1572872 | tf_op jit(solution)/shard_map/ppermute | solution.py:416
  211.7 1.3 collective-permute-done.15.proj_peer
  213.0 4.3 %mid_stack.1 = (f32[512,640]{1,0:T(8,128)}, f32[256,512]{1,0:T(8,128)S(1)}, f32[256,128]{1,0:T(8,128)S(1)}, f32[128,640]{1,0:T(8,128)S(1)}) custom-call(s32[1,3]{1,0:T(1,128)S(1)} %add_bitcast_fusion.info_ref, s32[256,1]{1,0:T(8,128)S(1)} %copy.12.piv_ref, f32[256,512]{1,0:T(8,128)S(1)} %bitcast.27, f32[256,128]{1,0:T(8,128)S(1)} %bitcast.36, ...), custom_call_target="tpu_custom_call" | custom-call | flops 1000000000 | bytes 65536 | tf_op jit(solution)/shard_map/mid_stack/pallas_call | solution.py:427
  217.3 2.0 collective-permute-start.16
  219.3 1.3 copy-done.7
  220.6 9.0 %mid_solve.1 = (f32[16,256]{1,0:T(8,128)}, f32[256,512]{1,0:T(8,128)S(1)}, f32[128,512]{1,0:T(8,128)S(1)}) custom-call(s32[1,3]{1,0:T(1,128)S(1)} %add_bitcast_fusion.info_ref, f32[512,640]{1,0:T(8,128)S(1)} %copy-done.7, f32[256,512]{1,0:T(8,128)S(1)} %get-tuple-element.51.picked_ref.pick_own, f32[256,512]{1,0:T(8,128)S(1)} %bitcast.39, ...), custom_call_target="tpu_custom_call" | custom-call | flops 3000000000 | bytes 65536 | tf_op jit(solution)/shard_map/mid_solve/pallas_call | solution.py:433
  229.6 0.7 collective-permute-start.17
  230.3 6.5 %collective-permute-done.18.proj_1 = f32[128,512]{1,0:T(8,128)S(1)} collective-permute-done((f32[128,512]{1,0:T(8,128)S(1)}, f32[128,512]{1,0:T(8,128)S(1)}, u32[]{:S(2)}, u32[]{:S(2)}) %collective-permute-start.18) | collective-permute-done | bytes 262176 | tf_op jit(solution)/shard_map/ppermute | solution.py:438
  236.8 1.5 collective-permute-start.19
  238.6 0.9 collective-permute-done.19.proj_2
  239.5 11.1 %top.1 = f32[8,256]{1,0:T(8,128)} custom-call(s32[1,3]{1,0:T(1,128)S(1)} %add_bitcast_fusion.1.info_ref, s32[256,1]{1,0:T(8,128)S(1)} %copy.13.piv_ref, f32[256,512]{1,0:T(8,128)S(1)} %get-tuple-element.51.picked_ref.pick_own, f32[256,128]{1,0:T(8,128)S(1)} %get-tuple-element.53.skel_own, f32[256,512]{1,0:T(8,128)S(1)} %get-tuple-element.54.proj_own, ...), custom_call_target="tpu_custom_call" | custom-call | flops 3000000000 | bytes 65536 | tf_op jit(solution)/shard_map/top/pallas_call | solution.py:441
  (49 shorter events, 2.1 us)
Async XLA Ops:
  0.6 210.8 %copy-start = (s32[4,256]{1,0:T(4,128)S(1)}, s32[4,256]{1,0:T(4,128)}, u32[]{:S(2)}) copy-start(s32[4,256]{1,0:T(4,128)} %param.12) | copy-start | bytes 12292
  2.9 0.9 copy-start.2
  4.2 42.3 %collective-permute-start = (f32[576,512]{1,0:T(8,128)S(1)}, f32[576,512]{1,0:T(8,128)}, u32[]{:S(2)}, u32[]{:S(2)}) collective-permute-start(f32[576,512]{1,0:T(8,128)S(1)} %pad_maximum_fusion.own_ref.refs_0_), channel_id=1, source_target_pairs={{0,16},{16,0},{32,48},{48,32},{64,80},{80,64},{96,112},{112,96},{1... | collective-permute-start | bytes 3538952 | tf_op jit(solution)/shard_map/ppermute | solution.py:376
  5.7 40.8 %collective-permute-start.1 = (f32[576,512]{1,0:T(8,128)S(1)}, f32[576,512]{1,0:T(8,128)}, u32[]{:S(2)}, u32[]{:S(2)}) collective-permute-start(f32[576,512]{1,0:T(8,128)S(1)} %pad_maximum_fusion.own_ref.refs_0_), channel_id=1, source_target_pairs={{16,32},{32,16},{48,64},{64,48},{80,96},{96,80},{17,33},{33,17},{4... | collective-permute-start | bytes 3538952 | tf_op jit(solution)/shard_map/ppermute | solution.py:377
  9.2 37.3 %collective-permute-start.2 = (f32[576,512]{1,0:T(8,128)S(1)}, f32[576,512]{1,0:T(8,128)S(1)}, u32[]{:S(2)}, u32[]{:S(2)}) collective-permute-start(f32[576,512]{1,0:T(8,128)S(1)} %pad_maximum_fusion.own_ref.refs_0_), channel_id=1, source_target_pairs={{0,12},{1,13},{2,14},{3,15},{4,0},{5,1},{6,2},{7,3},{8,4},{9,5},{1... | collective-permute-start | bytes 3538952 | tf_op jit(solution)/shard_map/ppermute | solution.py:378
  11.8 34.7 %collective-permute-start.3 = (f32[576,512]{1,0:T(8,128)S(1)}, f32[576,512]{1,0:T(8,128)}, u32[]{:S(2)}, u32[]{:S(2)}) collective-permute-start(f32[576,512]{1,0:T(8,128)S(1)} %pad_maximum_fusion.own_ref.refs_0_), channel_id=1, source_target_pairs={{0,3},{1,0},{2,1},{3,2},{4,7},{5,4},{6,5},{7,6},{8,11},{9,8},{10,9... | collective-permute-start | bytes 3538952 | tf_op jit(solution)/shard_map/ppermute | solution.py:378
  14.5 32.0 %collective-permute-start.4 = (f32[576,512]{1,0:T(8,128)S(1)}, f32[576,512]{1,0:T(8,128)}, u32[]{:S(2)}, u32[]{:S(2)}) collective-permute-start(f32[576,512]{1,0:T(8,128)S(1)} %pad_maximum_fusion.own_ref.refs_0_), channel_id=1, source_target_pairs={{0,5},{1,6},{2,7},{3,4},{4,9},{5,10},{6,11},{7,8},{8,13},{9,14},{1... | collective-permute-start | bytes 3538952 | tf_op jit(solution)/shard_map/ppermute | solution.py:378
  47.6 13.5 %copy-start.8 = (s32[1,2]{1,0:T(1,128)S(1)}, s32[1,2]{1,0:T(1,128)}, u32[]{:S(2)}) copy-start(s32[1,2]{1,0:T(1,128)} %param.10) | copy-start | bytes 28
  47.6 20.1 %copy-start.1 = (f32[512,512]{1,0:T(8,128)S(1)}, f32[512,512]{1,0:T(8,128)}, u32[]{:S(2)}) copy-start(f32[512,512]{1,0:T(8,128)} %samp_ref.3) | copy-start | bytes 3145732
  52.5 64.1 %collective-permute-start.8 = (f32[1728,512]{1,0:T(8,128)}, f32[1728,512]{1,0:T(8,128)}, u32[]{:S(2)}, u32[]{:S(2)}) collective-permute-start(f32[1728,512]{1,0:T(8,128)} %constant_dynamic-update-slice_fusion.refs_1_), channel_id=1, source_target_pairs={{0,16},{16,0},{32,48},{48,32},{64,80},{80,64},{96,112},{112,96},{1... | collective-permute-start | bytes 10616840 | tf_op jit(solution)/shard_map/ppermute | solution.py:384
  52.5 64.1 %collective-permute-start.9 = (f32[1728,512]{1,0:T(8,128)}, f32[1728,512]{1,0:T(8,128)}, u32[]{:S(2)}, u32[]{:S(2)}) collective-permute-start(f32[1728,512]{1,0:T(8,128)} %constant_dynamic-update-slice_fusion.refs_1_), channel_id=1, source_target_pairs={{16,32},{32,16},{48,64},{64,48},{80,96},{96,80},{17,33},{33,17},{4... | collective-permute-start | bytes 10616840 | tf_op jit(solution)/shard_map/ppermute | solution.py:385
  57.6 10.2 %all-to-all-start.1 = ((f32[16,16,128]{2,1,0:T(8,128)}), f32[16,16,128]{2,1,0:T(8,128)S(1)}, u32[]{:S(2)}, u32[]{:S(2)}) async-start(f32[16,16,128]{2,1,0:T(8,128)} %broadcast_in_dim.6), calls=%async_computation.1 | async-start | bytes 262144 | tf_op jit(solution)/shard_map/all_to_all | solution.py:360
  67.7 22.8 %copy-start.3 = (f32[512,64]{0,1:T(8,128)S(1)}, f32[512,64]{0,1:T(8,128)}, u32[]{:S(2)}) copy-start(f32[512,64]{0,1:T(8,128)} %param.7) | copy-start | bytes 393220
  86.1 21.7 %all-to-all-start.3 = ((f32[16,16,512]{2,1,0:T(8,128)}), f32[16,16,512]{2,1,0:T(8,128)S(1)}, u32[]{:S(2)}, u32[]{:S(2)}) async-start(f32[16,16,512]{2,1,0:T(8,128)} %broadcast_in_dim.7), calls=%async_computation.3 | async-start | bytes 1048576 | tf_op jit(solution)/shard_map/all_to_all | solution.py:360
  90.6 10.9 %collective-permute-start.5 = (f32[64,512]{1,0:T(8,128)S(1)}, f32[64,512]{1,0:T(8,128)S(1)}, u32[]{:S(2)}, u32[]{:S(2)}) collective-permute-start(f32[64,512]{1,0:T(8,128)S(1)} %bitcast.30), channel_id=1, source_target_pairs={{0,8},{1,9},{2,10},{3,11},{4,12},{5,13},{6,14},{7,15},{8,0},{9,1},... | collective-permute-start | bytes 393224 | tf_op jit(solution)/shard_map/ppermute | solution.py:388
  93.5 11.6 %collective-permute-start.6 = (f32[64,512]{1,0:T(8,128)S(1)}, f32[64,512]{1,0:T(8,128)S(1)}, u32[]{:S(2)}, u32[]{:S(2)}) collective-permute-start(f32[64,512]{1,0:T(8,128)S(1)} %bitcast.31), channel_id=1, source_target_pairs={{0,2},{1,3},{2,0},{3,1},{4,6},{5,7},{6,4},{7,5},{8,10},{9,11},{10,... | collective-permute-start | bytes 393224 | tf_op jit(solution)/shard_map/ppermute | solution.py:388
  96.2 10.2 %collective-permute-start.7 = (f32[64,512]{1,0:T(8,128)S(1)}, f32[64,512]{1,0:T(8,128)S(1)}, u32[]{:S(2)}, u32[]{:S(2)}) collective-permute-start(f32[64,512]{1,0:T(8,128)S(1)} %bitcast.32), channel_id=1, source_target_pairs={{0,10},{1,11},{2,8},{3,9},{4,14},{5,15},{6,12},{7,13},{8,2},{9,3},... | collective-permute-start | bytes 393224 | tf_op jit(solution)/shard_map/ppermute | solution.py:388
  101.4 64.8 %collective-permute-start.12 = (f32[256,128]{1,0:T(8,128)S(1)}, f32[256,128]{1,0:T(8,128)}, u32[]{:S(2)}, u32[]{:S(2)}) collective-permute-start(f32[256,128]{1,0:T(8,128)S(1)} %bitcast.35), channel_id=1, source_target_pairs={{0,16},{16,0},{32,48},{48,32},{64,80},{80,64},{96,112},{112,96},{1... | collective-permute-start | bytes 393224 | tf_op jit(solution)/shard_map/ppermute | solution.py:394
  106.8 1.0 copy-start.4
  107.8 32.6 %copy-start.6 = (bf16[4,512,256]{2,1,0:T(8,128)(2,1)S(1)}, bf16[4,512,256]{2,1,0:T(8,128)(2,1)}, u32[]{:S(2)}) copy-start(bf16[4,512,256]{2,1,0:T(8,128)(2,1)} %copy-done.4) | copy-start | bytes 3145732
  113.8 52.4 %collective-permute-start.11 = (f32[256,512]{1,0:T(8,128)S(1)}, f32[256,512]{1,0:T(8,128)S(1)}, u32[]{:S(2)}, u32[]{:S(2)}) collective-permute-start(f32[256,512]{1,0:T(8,128)S(1)} %bitcast.26), channel_id=1, source_target_pairs={{0,16},{16,0},{32,48},{48,32},{64,80},{80,64},{96,112},{112,96},{1... | collective-permute-start | bytes 1572872 | tf_op jit(solution)/shard_map/ppermute | solution.py:393
  116.6 1.2 copy-start.5
  139.6 26.6 %collective-permute-start.10 = (f32[512,256]{1,0:T(8,128)S(1)}, f32[512,256]{1,0:T(8,128)S(1)}, u32[]{:S(2)}, u32[]{:S(2)}) collective-permute-start(f32[512,256]{1,0:T(8,128)S(1)} %get-tuple-element.42), channel_id=1, source_target_pairs={{0,10},{1,11},{2,8},{3,9},{4,14},{5,15},{6,12},{7,13},{8,2},{9,3},... | collective-permute-start | bytes 1572872 | tf_op jit(solution)/shard_map/ppermute | solution.py:402
  161.2 17.5 %collective-permute-start.13 = (f32[512,256]{1,0:T(8,128)S(1)}, f32[512,256]{1,0:T(8,128)S(1)}, u32[]{:S(2)}, u32[]{:S(2)}) collective-permute-start(f32[512,256]{1,0:T(8,128)S(1)} %get-tuple-element.44), channel_id=1, source_target_pairs={{0,8},{1,9},{2,10},{3,11},{4,12},{5,13},{6,14},{7,15},{8,0},{9,1},... | collective-permute-start | bytes 1572872 | tf_op jit(solution)/shard_map/ppermute | solution.py:407
  163.5 15.2 %collective-permute-start.14 = (f32[512,256]{1,0:T(8,128)S(1)}, f32[512,256]{1,0:T(8,128)S(1)}, u32[]{:S(2)}, u32[]{:S(2)}) collective-permute-start(f32[512,256]{1,0:T(8,128)S(1)} %get-tuple-element.45), channel_id=1, source_target_pairs={{0,2},{1,3},{2,0},{3,1},{4,6},{5,7},{6,4},{7,5},{8,10},{9,11},{10,... | collective-permute-start | bytes 1572872 | tf_op jit(solution)/shard_map/ppermute | solution.py:408
  207.4 5.6 %collective-permute-start.15 = (f32[256,512]{1,0:T(8,128)S(1)}, f32[256,512]{1,0:T(8,128)S(1)}, u32[]{:S(2)}, u32[]{:S(2)}) collective-permute-start(f32[256,512]{1,0:T(8,128)S(1)} %bitcast.37), channel_id=1, source_target_pairs={{0,16},{16,0},{32,48},{48,32},{64,80},{80,64},{96,112},{112,96},{1... | collective-permute-start | bytes 1572872 | tf_op jit(solution)/shard_map/ppermute | solution.py:416
  217.3 12.4 %collective-permute-start.16 = (f32[128,640]{1,0:T(8,128)S(1)}, f32[128,640]{1,0:T(8,128)S(1)}, u32[]{:S(2)}, u32[]{:S(2)}) collective-permute-start(f32[128,640]{1,0:T(8,128)S(1)} %get-tuple-element.55), channel_id=1, source_target_pairs={{0,32},{16,48},{32,0},{48,16},{64,96},{80,112},{96,64},{112,80},{1... | collective-permute-start | bytes 983048 | tf_op jit(solution)/shard_map/ppermute | solution.py:431
  219.3 1.3 copy-start.7
  220.6 17.8 %copy-start.9 = (s32[2,256]{1,0:T(2,128)S(1)}, s32[2,256]{1,0:T(2,128)}, u32[]{:S(2)}) copy-start(s32[2,256]{1,0:T(2,128)} %param.13) | copy-start | bytes 6148
  229.6 7.2 %collective-permute-start.18 = (f32[128,512]{1,0:T(8,128)S(1)}, f32[128,512]{1,0:T(8,128)S(1)}, u32[]{:S(2)}, u32[]{:S(2)}) collective-permute-start(f32[128,512]{1,0:T(8,128)S(1)} %get-tuple-element.56), channel_id=1, source_target_pairs={{0,32},{16,48},{32,0},{48,16},{64,96},{80,112},{96,64},{112,80},{1... | collective-permute-start | bytes 786440 | tf_op jit(solution)/shard_map/ppermute | solution.py:438
  229.6 9.9 %collective-permute-start.17 = (f32[128,640]{1,0:T(8,128)S(1)}, f32[128,640]{1,0:T(8,128)S(1)}, u32[]{:S(2)}, u32[]{:S(2)}) collective-permute-start(f32[128,640]{1,0:T(8,128)S(1)} %collective-permute-done.16.pick_1), channel_id=1, source_target_pairs={{0,16},{16,0},{32,48},{48,32},{64,80},{80,64},{96,112},{112,96},{1... | collective-permute-start | bytes 983048 | tf_op jit(solution)/shard_map/ppermute | solution.py:432
  236.8 2.7 %collective-permute-start.19 = (f32[128,512]{1,0:T(8,128)S(1)}, f32[128,512]{1,0:T(8,128)S(1)}, u32[]{:S(2)}, u32[]{:S(2)}) collective-permute-start(f32[128,512]{1,0:T(8,128)S(1)} %collective-permute-done.18.proj_1), channel_id=1, source_target_pairs={{0,16},{16,0},{32,48},{48,32},{64,80},{80,64},{96,112},{112,96},{1... | collective-permute-start | bytes 786440 | tf_op jit(solution)/shard_map/ppermute | solution.py:439

commit v6 on v4

--- a/solution.py
+++ b/solution.py
@@ -70,7 +70,6 @@
 
 SOURCE = ((-1, 0), (0, -1), (1, 1))
 TARGET = ((2, 0), (0, 2), (2, 2))
-COUNT = 3 * SIDE
 
 
 def norm_rows(xt, first):
@@ -104,21 +103,19 @@
     return jnp.where(piv_ref[...] == column + start, 1.0, 0.0).astype(BF16)
 
 
-def skel_kernel(start_ref, piv_ref, points_ref, skel_ref):
-    one_hot = rows_of(start_ref[0, 0], piv_ref)
-    skel = sum(mm(one_hot, part, NT) for part in split3(points_ref[...]))
+def pivot_kernel(
+    row_ref, weight_ref, piv_ref, all_ref, samp_ref, own_ref, sib_ref, out_ref,
+    feat_ref, part_ref, skel_ref, right_ref
+):
+    row = row_ref[0, 0]
+    x, y = row >> 2, row & 3
+    for i, (dx, dy) in enumerate(((0, 0),) + TARGET):
+        feat_ref[i] = left_features(all_ref[(x + dx & 3) << 2 | (y + dy & 3)])
+    got = jnp.zeros((RANK, 3 * DIM), F32)
+    for r in range(16):
+        got += mm(rows_of(r * BLK, piv_ref), jnp.concatenate(split3(all_ref[r]), axis=0), NT)
+    skel = (got[:, :DIM] + got[:, DIM:2 * DIM]) + got[:, 2 * DIM:]
     skel_ref[...] = jnp.concatenate([skel, jnp.zeros((RANK, DIM), F32)], axis=1)
-
-
-def feature_kernel(p0, p1, p2, p3, feat_ref):
-    for i, ref in enumerate((p0, p1, p2, p3)):
-        feat_ref[i] = left_features(ref[...])
-
-
-def pivot_kernel(
-    start_ref, weight_ref, piv_ref, skel_ref, samp_ref, own_ref, sib_ref, out_ref, part_ref, right_ref
-):
-    skel = skel_ref[:, :DIM]
     scaled = skel * (2.0 * SCALE)
     hi = scaled.astype(BF16).astype(F32)
     lane = lax.broadcasted_iota(jnp.int32, (RANK, DIM), 1)
@@ -127,7 +124,7 @@
     for n, part in enumerate(split3(sq)):
         aux = jnp.where(lane == n, part.astype(F32), aux)
     feat = jnp.concatenate([hi, hi, scaled - hi, aux], axis=1).astype(BF16)
-    total = pick(rows_of(start_ref[0, 0], piv_ref), samp_ref[...])
+    total = pick(rows_of(row * BLK, piv_ref), samp_ref[...])
     for n, ref in enumerate((own_ref, sib_ref, out_ref)):
         right_features(ref[BLK:, :], right_ref)
         kern = jnp.exp2(mm(feat, right_ref[...]))
@@ -137,54 +134,59 @@
     part_ref[...] = total
 
 
-def far_kernel(targets, weight_ref, coeffs_ref, feat_ref, *refs):
-    msgs, refs = refs[:COUNT], refs[COUNT:]
-    outs, (prod_ref, right_ref), scratch = refs[:len(targets)], refs[len(targets):-3], refs[-3:]
+def near_steps(targets, feat_ref, groups, before, outs, acc, buf_a, buf_b):
+    for i in range(len(targets)):
+        acc[i] = before[i][...] if before else jnp.zeros((BLK, RANK), F32)
+    for prod_ref, right_ref in groups:
+        count = prod_ref.shape[0]
+        total = len(targets) * count
+
+        def entries(t, buf):
+            k = jnp.exp2(mm(feat_ref[targets[0] + t // count], right_ref[t % count]))
+            hi = k.astype(BF16)
+            buf[:, BLK:] = hi
+            buf[:, 0:BLK] = (k - hi.astype(F32)).astype(BF16)
+
+        def fold(t, buf):
+            b = t % count
+            acc[t // count] += mm(buf[...], prod_ref[b]) + mm(buf[:, BLK:], prod_ref[b, 0:BLK, :])
+
+        entries(0, buf_a)
+
+        @pl.loop(0, total // 2)
+        def _(u):
+            t = 2 * u
+            entries(t + 1, buf_b)
+            fold(t, buf_a)
+            entries(jnp.minimum(t + 2, total - 1), buf_a)
+            fold(t + 1, buf_b)
+
+    for i in range(len(targets)):
+        outs[i][...] = acc[i]
+
+
+def first_kernel(targets, count, weighted, weight_ref, coeffs_ref, feat_ref, *refs):
+    n = len(targets)
+    msgs, before = refs[:count], refs[count:-5 - n]
+    outs, (prod_ref, right_ref), scratch = refs[-5 - n:-5], refs[-5:-3], refs[-3:]
     ch, cl = split2(coeffs_ref[...])
     for at, ref in enumerate(msgs):
         right_features(ref[BLK:, :], right_ref.at[at])
         test = ref[0:BLK, :]
-        if at >= 2 * SIDE:
+        if weighted:
             test = test * weight_ref[0, 0]
         th, tl = split2(test)
         hi, lo = split2(mm(th, ch, NT) + (mm(th, cl, NT) + mm(tl, ch, NT)))
         prod_ref[at, 0:BLK, :] = hi
         prod_ref[at, BLK:, :] = lo
-    near_kernel(targets, feat_ref, prod_ref, right_ref, *outs, *scratch)
-
-
-def near_kernel(targets, feat_ref, prod_ref, right_ref, *refs):
-    before, outs, (acc, buf_a, buf_b) = refs[:-3 - len(targets)], refs[-3 - len(targets):-3], refs[-3:]
-    acc[...] = jnp.zeros_like(acc)
-    for ref in before:
-        acc[0] += ref[...]
-    total = len(targets) * COUNT
-
-    def left(t):
-        return feat_ref[targets[0] + t // COUNT]
-
-    def entries(t, buf):
-        k = jnp.exp2(mm(left(t), right_ref[t % COUNT]))
-        hi = k.astype(BF16)
-        buf[:, BLK:] = hi
-        buf[:, 0:BLK] = (k - hi.astype(F32)).astype(BF16)
-
-    def fold(t, buf):
-        b = t % COUNT
-        acc[t // COUNT] += mm(buf[...], prod_ref[b]) + mm(buf[:, BLK:], prod_ref[b, 0:BLK, :])
-
-    entries(0, buf_a)
-
-    @pl.loop(0, total // 2)
-    def _(u):
-        t = 2 * u
-        entries(t + 1, buf_b)
-        fold(t, buf_a)
-        entries(jnp.minimum(t + 2, total - 1), buf_a)
-        fold(t + 1, buf_b)
-
-    for i in range(len(targets)):
-        outs[i][...] = acc[i]
+    near_steps(targets, feat_ref, [(prod_ref, right_ref)], before, outs, *scratch)
+
+
+def next_kernel(targets, n_groups, feat_ref, *refs):
+    n = len(targets)
+    groups = [refs[2 * g:2 * g + 2] for g in range(n_groups)]
+    before, outs, scratch = refs[2 * n_groups:-3 - n], refs[-3 - n:-3], refs[-3:]
+    near_steps(targets, feat_ref, groups, before, outs, *scratch)
 
 
 def call(kernel, outs, n_smem, n_vmem, scratch=(), name=None, flops=0, trans=0):
@@ -196,13 +198,34 @@
         out_specs=[pl.BlockSpec(memory_space=VMEM)] * len(outs),
         scratch_shapes=list(scratch),
         compiler_params=pltpu.CompilerParams(vmem_limit_bytes=50 * 2**20),
-        cost_estimate=pl.CostEstimate(flops=flops, bytes_accessed=4 * 2**20, transcendentals=trans),
+        cost_estimate=pl.CostEstimate(flops=flops, bytes_accessed=2**16, transcendentals=trans),
         name=name,
     )
 
 
 def near_scratch(targets):
     return [VMEM((len(targets), BLK, RANK), F32), VMEM((BLK, 2 * BLK), BF16), VMEM((BLK, 2 * BLK), BF16)]
+
+
+BLOCK = ((BLK, RANK), F32)
+
+
+def first_near(name, targets, weight, coeffs, feats, msgs, before=(), weighted=False):
+    count = len(msgs)
+    *sums, prods, rights = call(
+        functools.partial(first_kernel, targets, count, weighted),
+        [BLOCK] * len(targets) + [((count, 2 * BLK, RANK), BF16), ((count, 4 * DIM, BLK), BF16)],
+        1, 2 + count + len(before), near_scratch(targets), name=name, flops=10**10,
+    )(weight, coeffs, feats, *msgs, *before)
+    return sums, (prods, rights)
+
+
+def next_near(name, targets, feats, groups, before):
+    return call(
+        functools.partial(next_kernel, targets, len(groups)),
+        [BLOCK] * len(targets), 0, 1 + 2 * len(groups) + len(before), near_scratch(targets),
+        name=name, flops=10**10,
+    )(feats, *[v for g in groups for v in g], *before)
 
 
 SOLVE_SCRATCH = [VMEM((RANK, RANK), F32), VMEM((RANK, RANK), F32)]
@@ -363,51 +386,41 @@
     leaf = lax.axis_index("leaf")
     row = lax.axis_index("row")
     core = leaf & 1
-    start = (row * BLK).reshape(1, 1)
     xt = points.T
     pivots = leaf_pivots[0].reshape(RANK, 1)
     weight = jnp.where(core == 0, near_mask[0, 0], near_mask[0, 1]).astype(F32).reshape(1, 1)
 
-    (skel,) = call(skel_kernel, [((RANK, 2 * DIM), F32)], 1, 2, name="skel")(start, pivots, xt)
-    skel, message = after(skel, jnp.concatenate([test_matrix, xt], axis=0))
-    own = [message]
+    message = jnp.concatenate([test_matrix, xt], axis=0)
     sib = [lax.ppermute(message, "leaf", SIBLING)]
     outer = [lax.ppermute(message, "leaf", OUTER)]
-    skel, message = sum_row(skel, message)
-    own += [lax.ppermute(message, "row", shift(*by)) for by in SOURCE]
-    (part,) = call(
-        pivot_kernel, [((RANK, SAMP), F32)], 2, 6, [VMEM((4 * DIM, BLK), BF16)], name="pivot", flops=2 * 10**9
-    )(start, weight, pivots, skel, samples, own[0], sib[0], outer[0])
-    part, *own[1:] = after(part, *own[1:])
+    points_all = lax.all_to_all(jnp.broadcast_to(xt[None], (16, DIM, BLK)), "row", 0, 0)
+    points_all, late = after(points_all, message)
+    own = [message] + [lax.ppermute(late, "row", shift(*by)) for by in SOURCE]
+    feats, part, skel = call(
+        pivot_kernel,
+        [((SIDE, BLK, 4 * DIM), BF16), ((RANK, SAMP), F32), ((RANK, 2 * DIM), F32)], 2, 6,
+        [VMEM((4 * DIM, BLK), BF16)], name="pivot",
+    )(row.reshape(1, 1), weight, pivots, points_all, samples, own[0], sib[0], outer[0])
+    picked, *own[1:] = sum_row(part, *own[1:])
+    outer += [lax.ppermute(m, "leaf", OUTER) for m in own[1:]]
     sib += [lax.ppermute(m, "leaf", SIBLING) for m in own[1:]]
-    outer += [lax.ppermute(m, "leaf", OUTER) for m in own[1:]]
-    picked, xt = sum_row(part, xt)
-    (feats,) = call(feature_kernel, [((SIDE, BLK, 4 * DIM), BF16)], 0, 4, name="features")(
-        xt, *[lax.ppermute(xt, "row", shift(*by)) for by in TARGET]
-    )
     (coeffs,) = call(
-        solve_kernel, [((RANK, SAMP), F32)], 0, 1, SOLVE_SCRATCH, name="solve", flops=3 * 10**9
+        solve_kernel, [((RANK, SAMP), F32)], 0, 1, SOLVE_SCRATCH, name="solve"
     )(picked)
     picked_sib = lax.ppermute(picked, "leaf", SIBLING)
     skel_sib = lax.ppermute(skel, "leaf", SIBLING)
 
-    block = ((BLK, RANK), F32)
-    sum_3, prods, rights = call(
-        functools.partial(far_kernel, (3,)),
-        [block] + [((COUNT, 2 * BLK, RANK), BF16), ((COUNT, 4 * DIM, BLK), BF16)], 1, 2 + COUNT,
-        near_scratch((3,)), name="near_3", flops=10**10,
-    )(weight, coeffs, feats, *own, *sib, *outer)
+    (sum_1, sum_2, sum_3), inner = first_near("near_inner", (1, 2, 3), weight, coeffs, feats, own + sib)
+    feats, sum_1, sum_2, sum_3 = after(feats, sum_1, sum_2, sum_3)
+    (sum_3,), outside = first_near("near_3", (3,), weight, coeffs, feats, outer, [sum_3], True)
     got_3 = lax.ppermute(sum_3, "row", shift(*TARGET[2]))
-    sum_1, sum_2 = call(
-        functools.partial(near_kernel, (1, 2)), [block] * 2, 0, 3, near_scratch((1, 2)), name="near_12", flops=2 * 10**10,
-    )(feats, prods, rights)
+    sum_1, sum_2 = next_near("near_12", (1, 2), feats, [outside], [sum_1, sum_2])
+    got_3, picked_sib, skel_sib = after(got_3, picked_sib, skel_sib)
     got_1 = lax.ppermute(sum_1, "row", shift(*TARGET[0]))
     got_2 = lax.ppermute(sum_2, "row", shift(*TARGET[1]))
-    (sum_0,) = call(
-        functools.partial(near_kernel, (0,)), [block], 0, 4, near_scratch((0,)), name="near_0", flops=10**10
-    )(feats, prods, rights, got_3)
+    (sum_0,) = next_near("near_0", (0,), feats, [inner, outside], [got_3])
     leaf_basis, proj = call(
-        basis_kernel, [block, ((RANK, SAMP), F32)], 0, 6, name="basis", flops=10**9
+        basis_kernel, [BLOCK, ((RANK, SAMP), F32)], 0, 6, name="basis", flops=10**9
     )(samples, test_matrix, coeffs, sum_0, got_1, got_2)
     (proj,) = sum_row(proj)
     proj_sib = lax.ppermute(proj, "leaf", SIBLING)

time: 261 us -> 241 us (0.923)
  waiting for transfers between devices: 59.7 us -> 35.2 us
  blocking collectives: 39.1 us -> 55.3 us
  starting transfers between devices: 55.4 us -> 45.2 us
    all_to_all x3 -> x1, waiting for transfers between devices: 40.5 us -> 0.74 us  [sum_row(): lax.all_to_all(jnp.broadcast_to(mine[None], (16, *mine.shape)), 'row', 0, 0)]
    all_to_all x0 -> x1, waiting for transfers between devices: none -> 23.2 us  [body(): lax.all_to_all(jnp.broadcast_to(xt[None], (16, DIM, BLK)), 'row', 0, 0)]
    all_to_all x0 -> x1, blocking collectives: none -> 13.5 us  [sum_row(): lax.all_to_all(jnp.broadcast_to(mine[None], (16, *mine.shape)), 'row', 0, 0)]
    ppermute x3, waiting for transfers between devices: 10.4 us -> 0.01 us  [body(): outer += [lax.ppermute(m, 'leaf', OUTER) for m in own[1:]]]
    all_to_all x3 -> x1, starting transfers between devices: 13.2 us -> 3.85 us  [sum_row(): lax.all_to_all(jnp.broadcast_to(mine[None], (16, *mine.shape)), 'row', 0, 0)]
    all_to_all x0 -> x1, starting transfers between devices: none -> 7.77 us  [body(): lax.all_to_all(jnp.broadcast_to(xt[None], (16, DIM, BLK)), 'row', 0, 0)]
    ppermute x6 -> x3, starting transfers between devices: 8.45 us -> 2.65 us  [body(): own = [message] + [lax.ppermute(late, 'row', shift(*by)) for by in SOURCE]]
    ppermute x1, starting transfers between devices: 6.16 us -> 0.52 us  [body(): pick_1 = lax.ppermute(send, 'leaf', COUSIN)]
  transfers between devices with their start and end apart: 27 -> 23, of which waited for: 7 -> 6; matrix products, arithmetic and copies ran while one was open for 1% -> 1% of each run, Pallas kernels for 21% -> 31%
where the time goes in v6:
time: 241 us; the launch traced here: 240 us
  Pallas kernels  92.9 us (39%)
  blocking collectives  55.3 us (23%)
  starting transfers between devices  45.2 us (19%)
  waiting for transfers between devices  35.2 us (15%)
  local copies, waits for them, and re-layouts  7.75 us (3%)
    all_to_all x2, blocking collectives, sum_row(): parts = lax.all_to_all(part.reshape(16, share, -1), 'row', 0, 0)  41.8 us
    pallas_call x2, Pallas kernels, first_near(): call(functools.partial(first_kernel, targets, count, weighted), [BLOCK] *...  32.7 us
    all_to_all x1, waiting for transfers between devices, body(): lax.all_to_all(jnp.broadcast_to(xt[None], (16, DIM, BLK)), 'row', 0, 0)  23.2 us
    pallas_call x2, Pallas kernels, next_near(): call(functools.partial(next_kernel, targets, len(groups)), [BLOCK] * len(...  20 us
    all_to_all x1, blocking collectives, sum_row(): lax.all_to_all(jnp.broadcast_to(mine[None], (16, *mine.shape)), 'row', 0, 0)  13.5 us
    pallas_call x1, Pallas kernels, body(): call(functools.partial(top_kernel, top_share), [((top_share, RANK), F32)]...  11.1 us
    ppermute x3, starting transfers between devices, body(): outer += [lax.ppermute(m, 'leaf', OUTER) for m in own[1:]]  9.36 us
    pallas_call x1, Pallas kernels, body(): call(functools.partial(mid_kernel, mid_share), [((mid_share, RANK), F32),...  9.05 us
  transfers between devices with their start and end apart: 23, of which 6 were waited for; matrix products, arithmetic and copies ran while one was open for 1% of the time, Pallas kernels for 31%

profile of v6, /device:TPU:1, one launch (start us, length us, event | category | flops | bytes accessed | tf_op | source)
XLA Modules:
  0.0 240.0 jit_solution(16338549785012561474)
XLA Ops:
  0.6 2.5 %broadcast_in_dim.6 = f32[16,64,512]{2,1,0:T(8,128)} broadcast(f32[64,512]{1,0:T(8,128)} %bitcast.30), dimensions={1,2} | broadcast | bytes 2228224 | tf_op jit(solution)/shard_map/broadcast_in_dim | solution.py:396
  3.2 7.8 %all-to-all-start = ((f32[16,64,512]{2,1,0:T(8,128)}), f32[16,64,512]{2,1,0:T(8,128)}, u32[]{:S(2)}, u32[]{:S(2)}) async-start(f32[16,64,512]{2,1,0:T(8,128)} %broadcast_in_dim.6), calls=%async_computation | async-start | bytes 4194304 | tf_op jit(solution)/shard_map/all_to_all | solution.py:396
  11.1 1.0 collective-permute-start
  12.1 3.6 %collective-permute-start.1 = (f32[576,512]{1,0:T(8,128)S(1)}, f32[576,512]{1,0:T(8,128)S(1)}, u32[]{:S(2)}, u32[]{:S(2)}) collective-permute-start(f32[576,512]{1,0:T(8,128)S(1)} %pad_maximum_fusion.own_ref.refs_0_), channel_id=1, source_target_pairs={{16,32},{32,16},{48,64},{64,48},{80,96},{96,80},{17,33},{33,17},{4... | collective-permute-start | bytes 3538952 | tf_op jit(solution)/shard_map/ppermute | solution.py:395
  15.7 23.2 %all-to-all-done.all_ref = f32[16,64,512]{2,1,0:T(8,128)} async-done(((f32[16,64,512]{2,1,0:T(8,128)}), f32[16,64,512]{2,1,0:T(8,128)}, u32[]{:S(2)}, u32[]{:S(2)}) %all-to-all-start) | async-done | bytes 2097184 | tf_op jit(solution)/shard_map/all_to_all | solution.py:396
  38.9 0.4 collective-permute-start.2
  39.2 0.4 collective-permute-start.3
  39.6 1.9 collective-permute-start.4
  41.5 0.6 fusion
  43.6 1.0 copy-done.9
  44.6 6.9 %pivot.1 = (bf16[4,512,256]{2,1,0:T(8,128)(2,1)S(1)}, f32[256,512]{1,0:T(8,128)S(1)}, f32[256,128]{1,0:T(8,128)S(1)}) custom-call(s32[1,1]{1,0:T(1,128)} %bitcast.row_ref, f32[1,1]{1,0:T(1,128)} %bitcast.3.weight_ref, s32[256,1]{1,0:T(8,128)S(1)} %copy.10.piv_ref, f32[16,64,512]{2,1,0:T(8,128)} %all-to-all-done.all_ref, f32[512,512]{1,0:T(8,128)S(1)} %copy-done.2, ...), custom_call_target="tpu_custom_call" | custom-call | bytes 65536 | tf_op jit(solution)/shard_map/pivot/pallas_call | solution.py:399
  51.6 24.6 %all_to_all.25 = f32[16,16,512]{2,1,0:T(8,128)} all-to-all(f32[16,16,512]{2,1,0:T(8,128)S(1)} %bitcast.29), channel_id=1, replica_groups=mesh['leaf'=8,'row'=16] {'row'}, dimensions={0} | all-to-all | bytes 1048576 | tf_op jit(solution)/shard_map/all_to_all | solution.py:379
  76.2 1.1 reduce_sum.18
  77.3 2.0 collective-permute-start.5
  79.4 0.4 collective-permute-start.7
  79.8 0.9 broadcast_in_dim.7
  80.7 3.8 %all-to-all-start.2 = ((f32[16,16,512]{2,1,0:T(8,128)}), f32[16,16,512]{2,1,0:T(8,128)S(1)}, u32[]{:S(2)}, u32[]{:S(2)}) async-start(f32[16,16,512]{2,1,0:T(8,128)} %broadcast_in_dim.7), calls=%async_computation.2 | async-start | bytes 1048576 | tf_op jit(solution)/shard_map/all_to_all | solution.py:381
  84.5 3.8 %collective-permute-start.10 = (f32[576,512]{1,0:T(8,128)}, f32[576,512]{1,0:T(8,128)}, u32[]{:S(2)}, u32[]{:S(2)}) collective-permute-start(f32[576,512]{1,0:T(8,128)} %collective-permute-done.4.refs_3_), channel_id=1, source_target_pairs={{16,32},{32,16},{48,64},{64,48},{80,96},{96,80},{17,33},{33,17},{4... | collective-permute-start | bytes 3538952 | tf_op jit(solution)/shard_map/ppermute | solution.py:405
  88.3 1.9 collective-permute-start.8
  90.3 3.6 %collective-permute-start.9 = (f32[576,512]{1,0:T(8,128)}, f32[576,512]{1,0:T(8,128)}, u32[]{:S(2)}, u32[]{:S(2)}) collective-permute-start(f32[576,512]{1,0:T(8,128)} %collective-permute-done.3.refs_2_), channel_id=1, source_target_pairs={{16,32},{32,16},{48,64},{64,48},{80,96},{96,80},{17,33},{33,17},{4... | collective-permute-start | bytes 3538952 | tf_op jit(solution)/shard_map/ppermute | solution.py:405
  93.9 0.7 all-to-all-done.2
  94.7 6.1 %solve.1.coeffs_ref = f32[256,512]{1,0:T(8,128)S(1)} custom-call(f32[256,512]{1,0:T(8,128)S(1)} %bitcast.22), custom_call_target="tpu_custom_call" | custom-call | bytes 65536 | tf_op jit(solution)/shard_map/solve/pallas_call | solution.py:407
  100.7 2.4 collective-permute-start.13
  103.1 0.3 collective-permute-start.12
  103.4 25.4 %near_inner.1 = (f32[512,256]{1,0:T(8,128)S(1)}, f32[512,256]{1,0:T(8,128)S(1)}, f32[512,256]{1,0:T(8,128)S(1)}, bf16[8,1024,256]{2,1,0:T(8,128)(2,1)}, bf16[8,256,512]{2,1,0:T(8,128)(2,1)}) custom-call(f32[1,1]{1,0:T(1,128)} %bitcast.3.weight_ref, f32[256,512]{1,0:T(8,128)S(1)} %solve.1.coeffs_ref, bf16[4,512,256]{2,1,0:T(8,128)(2,1)S(1)} %get-tuple-element.49.feat_ref, ...), custom_call_target="tpu_custom_call" | custom-call | flops 10000000000 | bytes 65536 | tf_op jit(solution)/shard_map/near_inner/pallas_call | solution.py:215
  128.8 7.4 %near_3.1 = (f32[512,256]{1,0:T(8,128)S(1)}, bf16[4,1024,256]{2,1,0:T(8,128)(2,1)}, bf16[4,256,512]{2,1,0:T(8,128)(2,1)S(1)}) custom-call(f32[1,1]{1,0:T(1,128)} %bitcast.3.weight_ref, f32[256,512]{1,0:T(8,128)S(1)} %solve.1.coeffs_ref, bf16[4,512,256]{2,1,0:T(8,128)(2,1)S(1)} %get-tuple-element.49.feat_ref, f32[576,512]{1,0:T(8,128)} %copy-done.9, ...), custom_call_target="tpu_custom_call" | custom-call | flops 10000000000 | bytes 65536 | tf_op jit(solution)/shard_map/near_3/pallas_call | solution.py:215
  136.2 1.0 copy-done.6
  137.2 4.5 %collective-permute-start.11 = (f32[512,256]{1,0:T(8,128)S(1)}, f32[512,256]{1,0:T(8,128)S(1)}, u32[]{:S(2)}, u32[]{:S(2)}) collective-permute-start(f32[512,256]{1,0:T(8,128)S(1)} %get-tuple-element.55), channel_id=1, source_target_pairs={{0,10},{1,11},{2,8},{3,9},{4,14},{5,15},{6,12},{7,13},{8,2},{9,3},... | collective-permute-start | bytes 1572872 | tf_op jit(solution)/shard_map/ppermute | solution.py:416
  141.7 7.7 %near_12.1 = (f32[512,256]{1,0:T(8,128)S(1)}, f32[512,256]{1,0:T(8,128)S(1)}) custom-call(bf16[4,512,256]{2,1,0:T(8,128)(2,1)S(1)} %get-tuple-element.49.feat_ref, bf16[4,1024,256]{2,1,0:T(8,128)(2,1)} %get-tuple-element.53.refs_2_.refs_0_, bf16[4,256,512]{2,1,0:T(8,128)(2,1)} %copy-done.6, f32[512,256]{1,0:T(8,128)S(1)} %get-tuple-element.58.refs_2_, ...), custom_call_target="tpu_custom_call" | custom-call | flops 10000000000 | bytes 65536 | tf_op jit(solution)/shard_map/near_12/pallas_call | solution.py:224
  149.4 0.3 collective-permute-start.14
  149.8 0.8 collective-permute-start.15
  150.6 3.7 %collective-permute-done.11.refs_4_ = f32[512,256]{1,0:T(8,128)S(1)} collective-permute-done((f32[512,256]{1,0:T(8,128)S(1)}, f32[512,256]{1,0:T(8,128)S(1)}, u32[]{:S(2)}, u32[]{:S(2)}) %collective-permute-start.11) | collective-permute-done | bytes 524320 | tf_op jit(solution)/shard_map/ppermute | solution.py:416
  154.4 12.3 %near_0.1.refs_0_ = f32[512,256]{1,0:T(8,128)S(1)} custom-call(bf16[4,512,256]{2,1,0:T(8,128)(2,1)S(1)} %get-tuple-element.49.feat_ref, bf16[8,1024,256]{2,1,0:T(8,128)(2,1)} %get-tuple-element.50.refs_0_, bf16[8,256,512]{2,1,0:T(8,128)(2,1)} %get-tuple-element.51.refs_1_, bf16[4,1024,256]{2,1,0:T(8,128)(2,1)} %get-tuple-element.53.refs_2_.refs_0_, ...), custom_call_target="tpu_custom_call" | custom-call | flops 10000000000 | bytes 65536 | tf_op jit(solution)/shard_map/near_0/pallas_call | solution.py:224
  166.7 3.1 %basis.1 = (f32[512,256]{1,0:T(8,128)}, f32[256,512]{1,0:T(8,128)S(1)}) custom-call(f32[512,512]{1,0:T(8,128)S(1)} %copy-done.2, f32[512,512]{1,0:T(8,128)} %test_ref.1, f32[256,512]{1,0:T(8,128)S(1)} %solve.1.coeffs_ref, f32[512,256]{1,0:T(8,128)S(1)} %near_0.1.refs_0_, f32[512,256]{1,0:T(8,128)S(1)} %collective-permute-done.14.refs_1_, ...), custom_call_target="tpu_custom_call" | custom-call | flops 1000000000 | bytes 65536 | tf_op jit(solution)/shard_map/basis/pallas_call | solution.py:422
  169.8 17.2 %all_to_all.26 = f32[16,16,512]{2,1,0:T(8,128)S(1)} all-to-all(f32[16,16,512]{2,1,0:T(8,128)S(1)} %bitcast.28), channel_id=1, replica_groups=mesh['leaf'=8,'row'=16] {'row'}, dimensions={0} | all-to-all | bytes 1048576 | tf_op jit(solution)/shard_map/all_to_all | solution.py:379
  187.0 13.5 %all_to_all.27 = f32[16,16,512]{2,1,0:T(8,128)S(1)} all-to-all(f32[16,16,512]{2,1,0:T(8,128)S(1)} %broadcast_in_dim.8), channel_id=1, replica_groups=mesh['leaf'=8,'row'=16] {'row'}, dimensions={0} | all-to-all | bytes 1048576 | tf_op jit(solution)/shard_map/all_to_all | solution.py:381
  200.6 2.1 collective-permute-start.16
  202.9 1.3 collective-permute-done.16.proj_peer
  204.2 3.9 %mid_stack.1 = (f32[512,640]{1,0:T(8,128)}, f32[256,512]{1,0:T(8,128)S(1)}, f32[256,128]{1,0:T(8,128)S(1)}, f32[128,640]{1,0:T(8,128)S(1)}) custom-call(s32[1,3]{1,0:T(1,128)S(1)} %add_bitcast_fusion.info_ref, s32[256,1]{1,0:T(8,128)S(1)} %copy.11.piv_ref, f32[256,512]{1,0:T(8,128)S(1)} %bitcast.24, f32[256,128]{1,0:T(8,128)S(1)} %get-tuple-element.56.skel_own, ...), custom_call_target="tpu_custom_call" | custom-call | flops 1000000000 | bytes 65536 | tf_op jit(solution)/shard_map/mid_stack/pallas_call | solution.py:437
  208.1 0.5 collective-permute-start.17
  208.7 1.3 copy-done.5
  210.0 9.0 %mid_solve.1 = (f32[16,256]{1,0:T(8,128)}, f32[256,512]{1,0:T(8,128)S(1)}, f32[128,512]{1,0:T(8,128)S(1)}) custom-call(s32[1,3]{1,0:T(1,128)S(1)} %add_bitcast_fusion.info_ref, f32[512,640]{1,0:T(8,128)S(1)} %copy-done.5, f32[256,512]{1,0:T(8,128)S(1)} %get-tuple-element.67.picked_ref.pick_own, f32[256,512]{1,0:T(8,128)S(1)} %bitcast.27, ...), custom_call_target="tpu_custom_call" | custom-call | flops 3000000000 | bytes 65536 | tf_op jit(solution)/shard_map/mid_solve/pallas_call | solution.py:443
  219.0 0.9 collective-permute-start.19
  220.0 0.9 collective-permute-start.18
  220.9 5.3 %collective-permute-done.19.proj_1 = f32[128,512]{1,0:T(8,128)S(1)} collective-permute-done((f32[128,512]{1,0:T(8,128)S(1)}, f32[128,512]{1,0:T(8,128)S(1)}, u32[]{:S(2)}, u32[]{:S(2)}) %collective-permute-start.19) | collective-permute-done | bytes 262176 | tf_op jit(solution)/shard_map/ppermute | solution.py:448
  226.2 1.5 collective-permute-start.20
  228.0 0.9 collective-permute-done.20.proj_2
  228.9 11.1 %top.1 = f32[8,256]{1,0:T(8,128)} custom-call(s32[1,3]{1,0:T(1,128)S(1)} %add_bitcast_fusion.1.info_ref, s32[256,1]{1,0:T(8,128)S(1)} %copy.12.piv_ref, f32[256,512]{1,0:T(8,128)S(1)} %get-tuple-element.67.picked_ref.pick_own, f32[256,128]{1,0:T(8,128)S(1)} %get-tuple-element.69.skel_own, f32[256,512]{1,0:T(8,128)S(1)} %get-tuple-element.70.proj_own, ...), custom_call_target="tpu_custom_call" | custom-call | flops 3000000000 | bytes 65536 | tf_op jit(solution)/shard_map/top/pallas_call | solution.py:451
  (53 shorter events, 0.9 us)
Async XLA Ops:
  0.6 202.0 %copy-start = (s32[4,256]{1,0:T(4,128)S(1)}, s32[4,256]{1,0:T(4,128)}, u32[]{:S(2)}) copy-start(s32[4,256]{1,0:T(4,128)} %param.12) | copy-start | bytes 12292
  3.2 7.8 %copy-start.8 = (f32[512,512]{1,0:T(8,128)S(1)}, f32[512,512]{1,0:T(8,128)}, u32[]{:S(2)}) copy-start(f32[512,512]{1,0:T(8,128)} %test_ref.1) | copy-start | bytes 3145732
  3.2 7.8 %copy-start.10 = (f32[512,64]{0,1:T(8,128)S(1)}, f32[512,64]{0,1:T(8,128)}, u32[]{:S(2)}) copy-start(f32[512,64]{0,1:T(8,128)} %param.7) | copy-start | bytes 393220
  3.2 35.7 %all-to-all-start = ((f32[16,64,512]{2,1,0:T(8,128)}), f32[16,64,512]{2,1,0:T(8,128)}, u32[]{:S(2)}, u32[]{:S(2)}) async-start(f32[16,64,512]{2,1,0:T(8,128)} %broadcast_in_dim.6), calls=%async_computation | async-start | bytes 4194304 | tf_op jit(solution)/shard_map/all_to_all | solution.py:396
  11.0 30.6 %copy-start.11 = (s32[1,2]{1,0:T(1,128)S(1)}, s32[1,2]{1,0:T(1,128)}, u32[]{:S(2)}) copy-start(s32[1,2]{1,0:T(1,128)} %param.10) | copy-start | bytes 28
  11.0 32.4 %copy-start.12 = (s32[1,256]{1,0:T(1,128)S(1)}, s32[1,256]{1,0:T(1,128)}, u32[]{:S(2)}) copy-start(s32[1,256]{1,0:T(1,128)} %param.11) | copy-start | bytes 3076
  11.0 33.6 %copy-start.2 = (f32[512,512]{1,0:T(8,128)S(1)}, f32[512,512]{1,0:T(8,128)}, u32[]{:S(2)}) copy-start(f32[512,512]{1,0:T(8,128)} %samp_ref.3) | copy-start | bytes 3145732
  11.1 40.5 %copy-start.1 = (f32[576,512]{1,0:T(8,128)}, f32[576,512]{1,0:T(8,128)S(1)}, u32[]{:S(2)}) copy-start(f32[576,512]{1,0:T(8,128)S(1)} %pad_maximum_fusion.own_ref.refs_0_) | copy-start | bytes 3538948
  11.1 32.5 %collective-permute-start = (f32[576,512]{1,0:T(8,128)S(1)}, f32[576,512]{1,0:T(8,128)}, u32[]{:S(2)}, u32[]{:S(2)}) collective-permute-start(f32[576,512]{1,0:T(8,128)S(1)} %pad_maximum_fusion.own_ref.refs_0_), channel_id=1, source_target_pairs={{0,16},{16,0},{32,48},{48,32},{64,80},{80,64},{96,112},{112,96},{1... | collective-permute-start | bytes 3538952 | tf_op jit(solution)/shard_map/ppermute | solution.py:394
  12.1 31.4 %collective-permute-start.1 = (f32[576,512]{1,0:T(8,128)S(1)}, f32[576,512]{1,0:T(8,128)S(1)}, u32[]{:S(2)}, u32[]{:S(2)}) collective-permute-start(f32[576,512]{1,0:T(8,128)S(1)} %pad_maximum_fusion.own_ref.refs_0_), channel_id=1, source_target_pairs={{16,32},{32,16},{48,64},{64,48},{80,96},{96,80},{17,33},{33,17},{4... | collective-permute-start | bytes 3538952 | tf_op jit(solution)/shard_map/ppermute | solution.py:395
  38.9 38.4 %collective-permute-start.2 = (f32[576,512]{1,0:T(8,128)S(1)}, f32[576,512]{1,0:T(8,128)}, u32[]{:S(2)}, u32[]{:S(2)}) collective-permute-start(f32[576,512]{1,0:T(8,128)S(1)} %pad_maximum_fusion.own_ref.refs_0_), channel_id=1, source_target_pairs={{0,12},{1,13},{2,14},{3,15},{4,0},{5,1},{6,2},{7,3},{8,4},{9,5},{1... | collective-permute-start | bytes 3538952 | tf_op jit(solution)/shard_map/ppermute | solution.py:398
  39.2 38.0 %collective-permute-start.3 = (f32[576,512]{1,0:T(8,128)S(1)}, f32[576,512]{1,0:T(8,128)}, u32[]{:S(2)}, u32[]{:S(2)}) collective-permute-start(f32[576,512]{1,0:T(8,128)S(1)} %pad_maximum_fusion.own_ref.refs_0_), channel_id=1, source_target_pairs={{0,3},{1,0},{2,1},{3,2},{4,7},{5,4},{6,5},{7,6},{8,11},{9,8},{10,9... | collective-permute-start | bytes 3538952 | tf_op jit(solution)/shard_map/ppermute | solution.py:398
  39.6 37.7 %collective-permute-start.4 = (f32[576,512]{1,0:T(8,128)S(1)}, f32[576,512]{1,0:T(8,128)}, u32[]{:S(2)}, u32[]{:S(2)}) collective-permute-start(f32[576,512]{1,0:T(8,128)S(1)} %pad_maximum_fusion.own_ref.refs_0_), channel_id=1, source_target_pairs={{0,5},{1,6},{2,7},{3,4},{4,9},{5,10},{6,11},{7,8},{8,13},{9,14},{1... | collective-permute-start | bytes 3538952 | tf_op jit(solution)/shard_map/ppermute | solution.py:398
  43.6 1.0 copy-start.9
  77.3 13.0 %collective-permute-start.5 = (f32[576,512]{1,0:T(8,128)}, f32[576,512]{1,0:T(8,128)}, u32[]{:S(2)}, u32[]{:S(2)}) collective-permute-start(f32[576,512]{1,0:T(8,128)} %collective-permute-done.2.refs_1_), channel_id=1, source_target_pairs={{0,16},{16,0},{32,48},{48,32},{64,80},{80,64},{96,112},{112,96},{1... | collective-permute-start | bytes 3538952 | tf_op jit(solution)/shard_map/ppermute | solution.py:406
  79.3 21.4 %collective-permute-start.6 = (f32[576,512]{1,0:T(8,128)}, f32[576,512]{1,0:T(8,128)}, u32[]{:S(2)}, u32[]{:S(2)}) collective-permute-start(f32[576,512]{1,0:T(8,128)} %collective-permute-done.3.refs_2_), channel_id=1, source_target_pairs={{0,16},{16,0},{32,48},{48,32},{64,80},{80,64},{96,112},{112,96},{1... | collective-permute-start | bytes 3538952 | tf_op jit(solution)/shard_map/ppermute | solution.py:406
  79.4 23.7 %collective-permute-start.7 = (f32[576,512]{1,0:T(8,128)}, f32[576,512]{1,0:T(8,128)}, u32[]{:S(2)}, u32[]{:S(2)}) collective-permute-start(f32[576,512]{1,0:T(8,128)} %collective-permute-done.4.refs_3_), channel_id=1, source_target_pairs={{0,16},{16,0},{32,48},{48,32},{64,80},{80,64},{96,112},{112,96},{1... | collective-permute-start | bytes 3538952 | tf_op jit(solution)/shard_map/ppermute | solution.py:406
  80.7 14.0 %all-to-all-start.2 = ((f32[16,16,512]{2,1,0:T(8,128)}), f32[16,16,512]{2,1,0:T(8,128)S(1)}, u32[]{:S(2)}, u32[]{:S(2)}) async-start(f32[16,16,512]{2,1,0:T(8,128)} %broadcast_in_dim.7), calls=%async_computation.2 | async-start | bytes 1048576 | tf_op jit(solution)/shard_map/all_to_all | solution.py:381
  84.5 44.2 %collective-permute-start.10 = (f32[576,512]{1,0:T(8,128)}, f32[576,512]{1,0:T(8,128)}, u32[]{:S(2)}, u32[]{:S(2)}) collective-permute-start(f32[576,512]{1,0:T(8,128)} %collective-permute-done.4.refs_3_), channel_id=1, source_target_pairs={{16,32},{32,16},{48,64},{64,48},{80,96},{96,80},{17,33},{33,17},{4... | collective-permute-start | bytes 3538952 | tf_op jit(solution)/shard_map/ppermute | solution.py:405
  88.3 40.4 %collective-permute-start.8 = (f32[576,512]{1,0:T(8,128)}, f32[576,512]{1,0:T(8,128)}, u32[]{:S(2)}, u32[]{:S(2)}) collective-permute-start(f32[576,512]{1,0:T(8,128)} %collective-permute-done.2.refs_1_), channel_id=1, source_target_pairs={{16,32},{32,16},{48,64},{64,48},{80,96},{96,80},{17,33},{33,17},{4... | collective-permute-start | bytes 3538952 | tf_op jit(solution)/shard_map/ppermute | solution.py:405
  90.3 38.5 %collective-permute-start.9 = (f32[576,512]{1,0:T(8,128)}, f32[576,512]{1,0:T(8,128)}, u32[]{:S(2)}, u32[]{:S(2)}) collective-permute-start(f32[576,512]{1,0:T(8,128)} %collective-permute-done.3.refs_2_), channel_id=1, source_target_pairs={{16,32},{32,16},{48,64},{64,48},{80,96},{96,80},{17,33},{33,17},{4... | collective-permute-start | bytes 3538952 | tf_op jit(solution)/shard_map/ppermute | solution.py:405
  100.7 49.9 %collective-permute-start.13 = (f32[256,128]{1,0:T(8,128)S(1)}, f32[256,128]{1,0:T(8,128)S(1)}, u32[]{:S(2)}, u32[]{:S(2)}) collective-permute-start(f32[256,128]{1,0:T(8,128)S(1)} %get-tuple-element.56.skel_own), channel_id=1, source_target_pairs={{0,16},{16,0},{32,48},{48,32},{64,80},{80,64},{96,112},{112,96},{1... | collective-permute-start | bytes 393224 | tf_op jit(solution)/shard_map/ppermute | solution.py:411
  103.1 47.5 %collective-permute-start.12 = (f32[256,512]{1,0:T(8,128)S(1)}, f32[256,512]{1,0:T(8,128)S(1)}, u32[]{:S(2)}, u32[]{:S(2)}) collective-permute-start(f32[256,512]{1,0:T(8,128)S(1)} %bitcast.23), channel_id=1, source_target_pairs={{0,16},{16,0},{32,48},{48,32},{64,80},{80,64},{96,112},{112,96},{1... | collective-permute-start | bytes 1572872 | tf_op jit(solution)/shard_map/ppermute | solution.py:410
  136.2 1.0 copy-start.6
  137.2 17.2 %collective-permute-start.11 = (f32[512,256]{1,0:T(8,128)S(1)}, f32[512,256]{1,0:T(8,128)S(1)}, u32[]{:S(2)}, u32[]{:S(2)}) collective-permute-start(f32[512,256]{1,0:T(8,128)S(1)} %get-tuple-element.55), channel_id=1, source_target_pairs={{0,10},{1,11},{2,8},{3,9},{4,14},{5,15},{6,12},{7,13},{8,2},{9,3},... | collective-permute-start | bytes 1572872 | tf_op jit(solution)/shard_map/ppermute | solution.py:416
  141.7 12.7 %copy-start.7 = (bf16[4,256,512]{2,1,0:T(8,128)(2,1)S(1)}, bf16[4,256,512]{2,1,0:T(8,128)(2,1)}, u32[]{:S(2)}) copy-start(bf16[4,256,512]{2,1,0:T(8,128)(2,1)} %copy-done.6) | copy-start | bytes 3145732
  149.4 17.2 %collective-permute-start.14 = (f32[512,256]{1,0:T(8,128)S(1)}, f32[512,256]{1,0:T(8,128)S(1)}, u32[]{:S(2)}, u32[]{:S(2)}) collective-permute-start(f32[512,256]{1,0:T(8,128)S(1)} %get-tuple-element.60), channel_id=1, source_target_pairs={{0,8},{1,9},{2,10},{3,11},{4,12},{5,13},{6,14},{7,15},{8,0},{9,1},... | collective-permute-start | bytes 1572872 | tf_op jit(solution)/shard_map/ppermute | solution.py:419
  149.8 16.9 %collective-permute-start.15 = (f32[512,256]{1,0:T(8,128)S(1)}, f32[512,256]{1,0:T(8,128)S(1)}, u32[]{:S(2)}, u32[]{:S(2)}) collective-permute-start(f32[512,256]{1,0:T(8,128)S(1)} %get-tuple-element.61), channel_id=1, source_target_pairs={{0,2},{1,3},{2,0},{3,1},{4,6},{5,7},{6,4},{7,5},{8,10},{9,11},{10,... | collective-permute-start | bytes 1572872 | tf_op jit(solution)/shard_map/ppermute | solution.py:420
  150.6 16.0 %copy-start.3 = (f32[256,512]{1,0:T(8,128)}, f32[256,512]{1,0:T(8,128)S(1)}, u32[]{:S(2)}) copy-start(f32[256,512]{1,0:T(8,128)S(1)} %collective-permute-done.12.pick_peer) | copy-start | bytes 1572868
  187.0 17.3 %copy-start.4 = (f32[256,512]{1,0:T(8,128)S(1)}, f32[256,512]{1,0:T(8,128)}, u32[]{:S(2)}) copy-start(f32[256,512]{1,0:T(8,128)} %copy-done.3) | copy-start | bytes 1572868
  200.6 3.6 %collective-permute-start.16 = (f32[256,512]{1,0:T(8,128)S(1)}, f32[256,512]{1,0:T(8,128)S(1)}, u32[]{:S(2)}, u32[]{:S(2)}) collective-permute-start(f32[256,512]{1,0:T(8,128)S(1)} %bitcast.25), channel_id=1, source_target_pairs={{0,16},{16,0},{32,48},{48,32},{64,80},{80,64},{96,112},{112,96},{1... | collective-permute-start | bytes 1572872 | tf_op jit(solution)/shard_map/ppermute | solution.py:426
  208.1 11.8 %collective-permute-start.17 = (f32[128,640]{1,0:T(8,128)S(1)}, f32[128,640]{1,0:T(8,128)S(1)}, u32[]{:S(2)}, u32[]{:S(2)}) collective-permute-start(f32[128,640]{1,0:T(8,128)S(1)} %get-tuple-element.71), channel_id=1, source_target_pairs={{0,32},{16,48},{32,0},{48,16},{64,96},{80,112},{96,64},{112,80},{1... | collective-permute-start | bytes 983048 | tf_op jit(solution)/shard_map/ppermute | solution.py:441
  208.7 1.3 copy-start.5
  210.0 17.8 %copy-start.13 = (s32[2,256]{1,0:T(2,128)S(1)}, s32[2,256]{1,0:T(2,128)}, u32[]{:S(2)}) copy-start(s32[2,256]{1,0:T(2,128)} %param.13) | copy-start | bytes 6148
  219.0 7.2 %collective-permute-start.19 = (f32[128,512]{1,0:T(8,128)S(1)}, f32[128,512]{1,0:T(8,128)S(1)}, u32[]{:S(2)}, u32[]{:S(2)}) collective-permute-start(f32[128,512]{1,0:T(8,128)S(1)} %get-tuple-element.72), channel_id=1, source_target_pairs={{0,32},{16,48},{32,0},{48,16},{64,96},{80,112},{96,64},{112,80},{1... | collective-permute-start | bytes 786440 | tf_op jit(solution)/shard_map/ppermute | solution.py:448
  220.0 8.9 %collective-permute-start.18 = (f32[128,640]{1,0:T(8,128)S(1)}, f32[128,640]{1,0:T(8,128)S(1)}, u32[]{:S(2)}, u32[]{:S(2)}) collective-permute-start(f32[128,640]{1,0:T(8,128)S(1)} %collective-permute-done.17.pick_1), channel_id=1, source_target_pairs={{0,16},{16,0},{32,48},{48,32},{64,80},{80,64},{96,112},{112,96},{1... | collective-permute-start | bytes 983048 | tf_op jit(solution)/shard_map/ppermute | solution.py:442
  226.2 2.7 %collective-permute-start.20 = (f32[128,512]{1,0:T(8,128)S(1)}, f32[128,512]{1,0:T(8,128)S(1)}, u32[]{:S(2)}, u32[]{:S(2)}) collective-permute-start(f32[128,512]{1,0:T(8,128)S(1)} %collective-permute-done.19.proj_1), channel_id=1, source_target_pairs={{0,16},{16,0},{32,48},{48,32},{64,80},{80,64},{96,112},{112,96},{1... | collective-permute-start | bytes 786440 | tf_op jit(solution)/shard_map/ppermute | solution.py:449

commit v7 on v6

--- a/solution.py
+++ b/solution.py
@@ -103,19 +103,21 @@
     return jnp.where(piv_ref[...] == column + start, 1.0, 0.0).astype(BF16)
 
 
+def skel_kernel(start_ref, piv_ref, points_ref, skel_ref):
+    one_hot = rows_of(start_ref[0, 0], piv_ref)
+    skel = sum(mm(one_hot, part, NT) for part in split3(points_ref[...]))
+    skel_ref[...] = jnp.concatenate([skel, jnp.zeros((RANK, DIM), F32)], axis=1)
+
+
+def feature_kernel(p0, p1, p2, p3, feat_ref):
+    for i, ref in enumerate((p0, p1, p2, p3)):
+        feat_ref[i] = left_features(ref[...])
+
+
 def pivot_kernel(
-    row_ref, weight_ref, piv_ref, all_ref, samp_ref, own_ref, sib_ref, out_ref,
-    feat_ref, part_ref, skel_ref, right_ref
+    start_ref, weight_ref, piv_ref, skel_ref, samp_ref, own_ref, sib_ref, out_ref, part_ref, right_ref
 ):
-    row = row_ref[0, 0]
-    x, y = row >> 2, row & 3
-    for i, (dx, dy) in enumerate(((0, 0),) + TARGET):
-        feat_ref[i] = left_features(all_ref[(x + dx & 3) << 2 | (y + dy & 3)])
-    got = jnp.zeros((RANK, 3 * DIM), F32)
-    for r in range(16):
-        got += mm(rows_of(r * BLK, piv_ref), jnp.concatenate(split3(all_ref[r]), axis=0), NT)
-    skel = (got[:, :DIM] + got[:, DIM:2 * DIM]) + got[:, 2 * DIM:]
-    skel_ref[...] = jnp.concatenate([skel, jnp.zeros((RANK, DIM), F32)], axis=1)
+    skel = skel_ref[:, :DIM]
     scaled = skel * (2.0 * SCALE)
     hi = scaled.astype(BF16).astype(F32)
     lane = lax.broadcasted_iota(jnp.int32, (RANK, DIM), 1)
@@ -124,7 +126,7 @@
     for n, part in enumerate(split3(sq)):
         aux = jnp.where(lane == n, part.astype(F32), aux)
     feat = jnp.concatenate([hi, hi, scaled - hi, aux], axis=1).astype(BF16)
-    total = pick(rows_of(row * BLK, piv_ref), samp_ref[...])
+    total = pick(rows_of(start_ref[0, 0], piv_ref), samp_ref[...])
     for n, ref in enumerate((own_ref, sib_ref, out_ref)):
         right_features(ref[BLK:, :], right_ref)
         kern = jnp.exp2(mm(feat, right_ref[...]))
@@ -393,15 +395,19 @@
     message = jnp.concatenate([test_matrix, xt], axis=0)
     sib = [lax.ppermute(message, "leaf", SIBLING)]
     outer = [lax.ppermute(message, "leaf", OUTER)]
-    points_all = lax.all_to_all(jnp.broadcast_to(xt[None], (16, DIM, BLK)), "row", 0, 0)
-    points_all, late = after(points_all, message)
+    start = (row * BLK).reshape(1, 1)
+    (skel,) = call(skel_kernel, [((RANK, 2 * DIM), F32)], 1, 2, name="skel")(start, pivots, xt)
+    (skel,) = sum_row(skel)
+    skel, late = after(skel, message)
     own = [message] + [lax.ppermute(late, "row", shift(*by)) for by in SOURCE]
-    feats, part, skel = call(
-        pivot_kernel,
-        [((SIDE, BLK, 4 * DIM), BF16), ((RANK, SAMP), F32), ((RANK, 2 * DIM), F32)], 2, 6,
-        [VMEM((4 * DIM, BLK), BF16)], name="pivot",
-    )(row.reshape(1, 1), weight, pivots, points_all, samples, own[0], sib[0], outer[0])
-    picked, *own[1:] = sum_row(part, *own[1:])
+    (part,) = call(
+        pivot_kernel, [((RANK, SAMP), F32)], 2, 6, [VMEM((4 * DIM, BLK), BF16)], name="pivot"
+    )(start, weight, pivots, skel, samples, own[0], sib[0], outer[0])
+    part, xt = after(part, xt)
+    targets = [lax.ppermute(xt, "row", shift(*by)) for by in TARGET]
+    picked, *rest = sum_row(part, *own[1:], *targets)
+    own[1:], targets = rest[:3], rest[3:]
+    (feats,) = call(feature_kernel, [((SIDE, BLK, 4 * DIM), BF16)], 0, 4, name="features")(xt, *targets)
     outer += [lax.ppermute(m, "leaf", OUTER) for m in own[1:]]
     sib += [lax.ppermute(m, "leaf", SIBLING) for m in own[1:]]
     (coeffs,) = call(

time: 241 us -> 245 us (1.017)
  starting transfers between devices: 45.2 us -> 57 us
  blocking collectives: 55.3 us -> 51.3 us
  waiting for transfers between devices: 35.2 us -> 32 us
    all_to_all x1, waiting for transfers between devices: 23.2 us -> 0.73 us  [sum_row(): parts = lax.all_to_all(part.reshape(16, share, -1), 'row', 0, 0)]
    ppermute x0 -> x3, waiting for transfers between devices: none -> 19.9 us  [body(): targets = [lax.ppermute(xt, 'row', shift(*by)) for by in TARGET]]
    all_to_all x2, blocking collectives: 41.8 us -> 28.8 us  [sum_row(): parts = lax.all_to_all(part.reshape(16, share, -1), 'row', 0, 0)]
    ppermute x0 -> x3, starting transfers between devices: none -> 9.29 us  [body(): targets = [lax.ppermute(xt, 'row', shift(*by)) for by in TARGET]]
    all_to_all x1 -> x2, blocking collectives: 13.5 us -> 22.5 us  [sum_row(): lax.all_to_all(jnp.broadcast_to(mine[None], (16, *mine.shape)), 'row', 0, 0)]
    all_to_all x1, starting transfers between devices: 7.77 us -> 4.98 us  [sum_row(): parts = lax.all_to_all(part.reshape(16, share, -1), 'row', 0, 0)]
    broadcast_in_dim x1 -> x0, local copies, waits for them, and re-layouts: 2.51 us -> none  [body(): jnp.broadcast_to(xt[None], (16, DIM, BLK))]
    unnamed x28 -> x40, local copies, waits for them, and re-layouts: 3.35 us -> 5.07 us
  transfers between devices with their start and end apart: 23 -> 26, of which waited for: 6 -> 7; matrix products, arithmetic and copies ran while one was open for 1% -> 1% of each run, Pallas kernels for 31% -> 30%
where the time goes in v7:
time: 245 us; the launch traced here: 244 us
  Pallas kernels  92.6 us (38%)
  starting transfers between devices  57 us (23%)
  blocking collectives  51.3 us (21%)
  waiting for transfers between devices  32 us (13%)
  local copies, waits for them, and re-layouts  6.98 us (3%)
    pallas_call x2, Pallas kernels, first_near(): call(functools.partial(first_kernel, targets, count, weighted), [BLOCK] *...  32.7 us
    all_to_all x2, blocking collectives, sum_row(): parts = lax.all_to_all(part.reshape(16, share, -1), 'row', 0, 0)  28.8 us
    all_to_all x2, blocking collectives, sum_row(): lax.all_to_all(jnp.broadcast_to(mine[None], (16, *mine.shape)), 'row', 0, 0)  22.5 us
    pallas_call x2, Pallas kernels, next_near(): call(functools.partial(next_kernel, targets, len(groups)), [BLOCK] * len(...  20 us
    ppermute x3, waiting for transfers between devices, body(): targets = [lax.ppermute(xt, 'row', shift(*by)) for by in TARGET]  19.9 us
    pallas_call x1, Pallas kernels, body(): call(functools.partial(top_kernel, top_share), [((top_share, RANK), F32)]...  11.6 us
    ppermute x3, starting transfers between devices, body(): outer += [lax.ppermute(m, 'leaf', OUTER) for m in own[1:]]  9.32 us
    ppermute x3, starting transfers between devices, body(): targets = [lax.ppermute(xt, 'row', shift(*by)) for by in TARGET]  9.29 us
  transfers between devices with their start and end apart: 26, of which 7 were waited for; matrix products, arithmetic and copies ran while one was open for 1% of the time, Pallas kernels for 30%

profile of v7, /device:TPU:1, one launch (start us, length us, event | category | flops | bytes accessed | tf_op | source)
XLA Modules:
  0.0 243.8 jit_solution(3854709286085002021)
XLA Ops:
  0.7 1.4 pad_maximum_fusion.own_ref.refs_0_
  2.1 1.5 collective-permute-start
  3.6 3.7 %collective-permute-start.1 = (f32[576,512]{1,0:T(8,128)S(1)}, f32[576,512]{1,0:T(8,128)}, u32[]{:S(2)}, u32[]{:S(2)}) collective-permute-start(f32[576,512]{1,0:T(8,128)S(1)} %pad_maximum_fusion.own_ref.refs_0_), channel_id=1, source_target_pairs={{16,32},{32,16},{48,64},{64,48},{80,96},{96,80},{17,33},{33,17},{4... | collective-permute-start | bytes 3538952 | tf_op jit(solution)/shard_map/ppermute | solution.py:397
  7.9 13.3 %all_to_all.30 = f32[16,16,128]{2,1,0:T(8,128)S(1)} all-to-all(f32[16,16,128]{2,1,0:T(8,128)S(1)} %bitcast.40), channel_id=1, replica_groups=mesh['leaf'=8,'row'=16] {'row'}, dimensions={0} | all-to-all | bytes 262144 | tf_op jit(solution)/shard_map/all_to_all | solution.py:381
  21.2 10.2 %all_to_all.31 = f32[16,16,128]{2,1,0:T(8,128)S(1)} all-to-all(f32[16,16,128]{2,1,0:T(8,128)S(1)} %broadcast_in_dim.6), channel_id=1, replica_groups=mesh['leaf'=8,'row'=16] {'row'}, dimensions={0} | all-to-all | bytes 262144 | tf_op jit(solution)/shard_map/all_to_all | solution.py:383
  31.3 0.9 collective-permute-start.2
  32.8 1.2 collective-permute-start.4
  34.0 0.6 fusion
  35.9 4.9 %pivot.1 = f32[256,512]{1,0:T(8,128)} custom-call(s32[1,1]{1,0:T(1,128)} %bitcast.start_ref, f32[1,1]{1,0:T(1,128)} %bitcast.3.weight_ref, s32[256,1]{1,0:T(8,128)S(1)} %copy.11.piv_ref, f32[256,128]{1,0:T(8,128)S(1)} %bitcast.33, f32[512,512]{1,0:T(8,128)S(1)} %copy-done.2, f32[576,512]{1,0:T(8,128)S(1)} %pad_maximum_fusion.own_ref.refs_0_, ...), custom_call_target="tpu_custom_call" | custom-call | bytes 65536 | tf_op jit(solution)/shard_map/pivot/pallas_call | solution.py:403
  40.8 5.0 %all-to-all-start.2 = ((f32[16,16,512]{2,1,0:T(8,128)}), f32[16,16,512]{2,1,0:T(8,128)S(1)}, u32[]{:S(2)}, u32[]{:S(2)}) async-start(f32[16,16,512]{2,1,0:T(8,128)} %bitcast.8), calls=%async_computation.2 | async-start | bytes 1048576 | tf_op jit(solution)/shard_map/all_to_all | solution.py:381
  45.8 2.9 %collective-permute-start.5 = (f32[64,512]{1,0:T(8,128)S(1)}, f32[64,512]{1,0:T(8,128)S(1)}, u32[]{:S(2)}, u32[]{:S(2)}) collective-permute-start(f32[64,512]{1,0:T(8,128)S(1)} %bitcast.29), channel_id=1, source_target_pairs={{0,8},{1,9},{2,10},{3,11},{4,12},{5,13},{6,14},{7,15},{8,0},{9,1},... | collective-permute-start | bytes 393224 | tf_op jit(solution)/shard_map/ppermute | solution.py:407
  48.6 2.7 %collective-permute-start.6 = (f32[64,512]{1,0:T(8,128)S(1)}, f32[64,512]{1,0:T(8,128)S(1)}, u32[]{:S(2)}, u32[]{:S(2)}) collective-permute-start(f32[64,512]{1,0:T(8,128)S(1)} %bitcast.30), channel_id=1, source_target_pairs={{0,2},{1,3},{2,0},{3,1},{4,6},{5,7},{6,4},{7,5},{8,10},{9,11},{10,... | collective-permute-start | bytes 393224 | tf_op jit(solution)/shard_map/ppermute | solution.py:407
  51.3 16.7 %collective-permute-done.5.p1 = f32[64,512]{1,0:T(8,128)S(1)} collective-permute-done((f32[64,512]{1,0:T(8,128)S(1)}, f32[64,512]{1,0:T(8,128)S(1)}, u32[]{:S(2)}, u32[]{:S(2)}) %collective-permute-start.5) | collective-permute-done | bytes 131104 | tf_op jit(solution)/shard_map/ppermute | solution.py:407
  68.0 3.7 %collective-permute-start.7 = (f32[64,512]{1,0:T(8,128)S(1)}, f32[64,512]{1,0:T(8,128)S(1)}, u32[]{:S(2)}, u32[]{:S(2)}) collective-permute-start(f32[64,512]{1,0:T(8,128)S(1)} %bitcast.31), channel_id=1, source_target_pairs={{0,10},{1,11},{2,8},{3,9},{4,14},{5,15},{6,12},{7,13},{8,2},{9,3},... | collective-permute-start | bytes 393224 | tf_op jit(solution)/shard_map/ppermute | solution.py:407
  71.7 0.7 all-to-all-done.2
  72.5 3.2 %collective-permute-done.7.p3 = f32[64,512]{1,0:T(8,128)S(1)} collective-permute-done((f32[64,512]{1,0:T(8,128)S(1)}, f32[64,512]{1,0:T(8,128)S(1)}, u32[]{:S(2)}, u32[]{:S(2)}) %collective-permute-start.7) | collective-permute-done | bytes 131104 | tf_op jit(solution)/shard_map/ppermute | solution.py:407
  75.7 3.7 %collective-permute-start.10 = (f32[576,512]{1,0:T(8,128)}, f32[576,512]{1,0:T(8,128)}, u32[]{:S(2)}, u32[]{:S(2)}) collective-permute-start(f32[576,512]{1,0:T(8,128)} %collective-permute-done.4.refs_3_), channel_id=1, source_target_pairs={{0,16},{16,0},{32,48},{48,32},{64,80},{80,64},{96,112},{112,96},{1... | collective-permute-start | bytes 3538952 | tf_op jit(solution)/shard_map/ppermute | solution.py:412
  80.0 0.9 broadcast_in_dim.7
  80.8 6.1 %all-to-all-start.3 = ((f32[16,16,512]{2,1,0:T(8,128)}), f32[16,16,512]{2,1,0:T(8,128)S(1)}, u32[]{:S(2)}, u32[]{:S(2)}) async-start(f32[16,16,512]{2,1,0:T(8,128)} %broadcast_in_dim.7), calls=%async_computation.3 | async-start | bytes 1048576 | tf_op jit(solution)/shard_map/all_to_all | solution.py:383
  87.0 3.8 %collective-permute-start.11 = (f32[576,512]{1,0:T(8,128)}, f32[576,512]{1,0:T(8,128)}, u32[]{:S(2)}, u32[]{:S(2)}) collective-permute-start(f32[576,512]{1,0:T(8,128)} %collective-permute-done.2.refs_1_), channel_id=1, source_target_pairs={{16,32},{32,16},{48,64},{64,48},{80,96},{96,80},{17,33},{33,17},{4... | collective-permute-start | bytes 3538952 | tf_op jit(solution)/shard_map/ppermute | solution.py:411
  90.7 1.9 collective-permute-start.12
  92.7 3.6 %collective-permute-start.13 = (f32[576,512]{1,0:T(8,128)}, f32[576,512]{1,0:T(8,128)}, u32[]{:S(2)}, u32[]{:S(2)}) collective-permute-start(f32[576,512]{1,0:T(8,128)} %collective-permute-done.4.refs_3_), channel_id=1, source_target_pairs={{16,32},{32,16},{48,64},{64,48},{80,96},{96,80},{17,33},{33,17},{4... | collective-permute-start | bytes 3538952 | tf_op jit(solution)/shard_map/ppermute | solution.py:411
  96.4 0.9 copy-done.5
  97.3 0.9 copy-done.7
  98.2 0.9 copy-done.9
  99.5 6.5 %solve.1.coeffs_ref = f32[256,512]{1,0:T(8,128)S(1)} custom-call(f32[256,512]{1,0:T(8,128)S(1)} %bitcast.24), custom_call_target="tpu_custom_call" | custom-call | bytes 65536 | tf_op jit(solution)/shard_map/solve/pallas_call | solution.py:413
  106.7 25.4 %near_inner.1 = (f32[512,256]{1,0:T(8,128)S(1)}, f32[512,256]{1,0:T(8,128)S(1)}, f32[512,256]{1,0:T(8,128)S(1)}, bf16[8,1024,256]{2,1,0:T(8,128)(2,1)}, bf16[8,256,512]{2,1,0:T(8,128)(2,1)}) custom-call(f32[1,1]{1,0:T(1,128)} %bitcast.3.weight_ref, f32[256,512]{1,0:T(8,128)S(1)} %solve.1.coeffs_ref, bf16[4,512,256]{2,1,0:T(8,128)(2,1)S(1)} %features.1.feat_ref, ...), custom_call_target="tpu_custom_call" | custom-call | flops 10000000000 | bytes 65536 | tf_op jit(solution)/shard_map/near_inner/pallas_call | solution.py:217
  132.1 7.3 %near_3.1 = (f32[512,256]{1,0:T(8,128)S(1)}, bf16[4,1024,256]{2,1,0:T(8,128)(2,1)}, bf16[4,256,512]{2,1,0:T(8,128)(2,1)S(1)}) custom-call(f32[1,1]{1,0:T(1,128)} %bitcast.3.weight_ref, f32[256,512]{1,0:T(8,128)S(1)} %solve.1.coeffs_ref, bf16[4,512,256]{2,1,0:T(8,128)(2,1)S(1)} %features.1.feat_ref, f32[576,512]{1,0:T(8,128)} %collective-permute-done.1.out_ref.refs_0_, ...), custom_call_target="tpu_custom_call" | custom-call | flops 10000000000 | bytes 65536 | tf_op jit(solution)/shard_map/near_3/pallas_call | solution.py:217
  139.4 1.0 copy-done.15
  140.3 5.6 %collective-permute-start.14 = (f32[512,256]{1,0:T(8,128)S(1)}, f32[512,256]{1,0:T(8,128)S(1)}, u32[]{:S(2)}, u32[]{:S(2)}) collective-permute-start(f32[512,256]{1,0:T(8,128)S(1)} %get-tuple-element.60), channel_id=1, source_target_pairs={{0,10},{1,11},{2,8},{3,9},{4,14},{5,15},{6,12},{7,13},{8,2},{9,3},... | collective-permute-start | bytes 1572872 | tf_op jit(solution)/shard_map/ppermute | solution.py:422
  145.9 7.7 %near_12.1 = (f32[512,256]{1,0:T(8,128)S(1)}, f32[512,256]{1,0:T(8,128)S(1)}) custom-call(bf16[4,512,256]{2,1,0:T(8,128)(2,1)S(1)} %features.1.feat_ref, bf16[4,1024,256]{2,1,0:T(8,128)(2,1)} %get-tuple-element.58.refs_2_.refs_0_, bf16[4,256,512]{2,1,0:T(8,128)(2,1)} %copy-done.15, f32[512,256]{1,0:T(8,128)S(1)} %get-tuple-element.62.refs_2_, ...), custom_call_target="tpu_custom_call" | custom-call | flops 10000000000 | bytes 65536 | tf_op jit(solution)/shard_map/near_12/pallas_call | solution.py:226
  154.3 3.6 %collective-permute-done.14.refs_4_ = f32[512,256]{1,0:T(8,128)S(1)} collective-permute-done((f32[512,256]{1,0:T(8,128)S(1)}, f32[512,256]{1,0:T(8,128)S(1)}, u32[]{:S(2)}, u32[]{:S(2)}) %collective-permute-start.14) | collective-permute-done | bytes 524320 | tf_op jit(solution)/shard_map/ppermute | solution.py:422
  157.9 12.3 %near_0.1.refs_0_ = f32[512,256]{1,0:T(8,128)S(1)} custom-call(bf16[4,512,256]{2,1,0:T(8,128)(2,1)S(1)} %features.1.feat_ref, bf16[8,1024,256]{2,1,0:T(8,128)(2,1)} %get-tuple-element.55.refs_0_, bf16[8,256,512]{2,1,0:T(8,128)(2,1)} %get-tuple-element.56.refs_1_, bf16[4,1024,256]{2,1,0:T(8,128)(2,1)} %get-tuple-element.58.refs_2_.refs_0_, ...), custom_call_target="tpu_custom_call" | custom-call | flops 10000000000 | bytes 65536 | tf_op jit(solution)/shard_map/near_0/pallas_call | solution.py:226
  170.2 3.1 %basis.1 = (f32[512,256]{1,0:T(8,128)}, f32[256,512]{1,0:T(8,128)S(1)}) custom-call(f32[512,512]{1,0:T(8,128)S(1)} %copy-done.2, f32[512,512]{1,0:T(8,128)} %test_ref.1, f32[256,512]{1,0:T(8,128)S(1)} %solve.1.coeffs_ref, f32[512,256]{1,0:T(8,128)S(1)} %near_0.1.refs_0_, f32[512,256]{1,0:T(8,128)S(1)} %collective-permute-done.17.refs_1_, ...), custom_call_target="tpu_custom_call" | custom-call | flops 1000000000 | bytes 65536 | tf_op jit(solution)/shard_map/basis/pallas_call | solution.py:428
  173.4 15.6 %all_to_all.32 = f32[16,16,512]{2,1,0:T(8,128)S(1)} all-to-all(f32[16,16,512]{2,1,0:T(8,128)S(1)} %bitcast.39), channel_id=1, replica_groups=mesh['leaf'=8,'row'=16] {'row'}, dimensions={0} | all-to-all | bytes 1048576 | tf_op jit(solution)/shard_map/all_to_all | solution.py:381
  189.0 12.3 %all_to_all.33 = f32[16,16,512]{2,1,0:T(8,128)S(1)} all-to-all(f32[16,16,512]{2,1,0:T(8,128)S(1)} %broadcast_in_dim.8), channel_id=1, replica_groups=mesh['leaf'=8,'row'=16] {'row'}, dimensions={0} | all-to-all | bytes 1048576 | tf_op jit(solution)/shard_map/all_to_all | solution.py:383
  201.3 4.4 %collective-permute-start.19 = (f32[256,512]{1,0:T(8,128)S(1)}, f32[256,512]{1,0:T(8,128)S(1)}, u32[]{:S(2)}, u32[]{:S(2)}) collective-permute-start(f32[256,512]{1,0:T(8,128)S(1)} %bitcast.36), channel_id=1, source_target_pairs={{0,16},{16,0},{32,48},{48,32},{64,80},{80,64},{96,112},{112,96},{1... | collective-permute-start | bytes 1572872 | tf_op jit(solution)/shard_map/ppermute | solution.py:432
  206.0 1.3 collective-permute-done.19.proj_peer
  207.3 4.0 %mid_stack.1 = (f32[512,640]{1,0:T(8,128)}, f32[256,512]{1,0:T(8,128)S(1)}, f32[256,128]{1,0:T(8,128)S(1)}, f32[128,640]{1,0:T(8,128)S(1)}) custom-call(s32[1,3]{1,0:T(1,128)S(1)} %add_bitcast_fusion.info_ref, s32[256,1]{1,0:T(8,128)S(1)} %copy.12.piv_ref, f32[256,512]{1,0:T(8,128)S(1)} %bitcast.26, f32[256,128]{1,0:T(8,128)S(1)} %bitcast.35, ...), custom_call_target="tpu_custom_call" | custom-call | flops 1000000000 | bytes 65536 | tf_op jit(solution)/shard_map/mid_stack/pallas_call | solution.py:443
  211.2 0.8 collective-permute-start.20
  212.0 1.3 copy-done.14
  213.3 9.0 %mid_solve.1 = (f32[16,256]{1,0:T(8,128)}, f32[256,512]{1,0:T(8,128)S(1)}, f32[128,512]{1,0:T(8,128)S(1)}) custom-call(s32[1,3]{1,0:T(1,128)S(1)} %add_bitcast_fusion.info_ref, f32[512,640]{1,0:T(8,128)S(1)} %copy-done.14, f32[256,512]{1,0:T(8,128)S(1)} %get-tuple-element.71.picked_ref.pick_own, f32[256,512]{1,0:T(8,128)S(1)} %bitcast.38, ...), custom_call_target="tpu_custom_call" | custom-call | flops 3000000000 | bytes 65536 | tf_op jit(solution)/shard_map/mid_solve/pallas_call | solution.py:449
  222.4 0.7 collective-permute-start.22
  223.1 0.9 collective-permute-start.21
  224.0 5.5 %collective-permute-done.22.proj_1 = f32[128,512]{1,0:T(8,128)S(1)} collective-permute-done((f32[128,512]{1,0:T(8,128)S(1)}, f32[128,512]{1,0:T(8,128)S(1)}, u32[]{:S(2)}, u32[]{:S(2)}) %collective-permute-start.22) | collective-permute-done | bytes 262176 | tf_op jit(solution)/shard_map/ppermute | solution.py:454
  229.5 1.5 collective-permute-start.23
  231.3 0.9 collective-permute-done.23.proj_2
  232.2 11.6 %top.1 = f32[8,256]{1,0:T(8,128)} custom-call(s32[1,3]{1,0:T(1,128)S(1)} %add_bitcast_fusion.1.info_ref, s32[256,1]{1,0:T(8,128)S(1)} %copy.13.piv_ref, f32[256,512]{1,0:T(8,128)S(1)} %get-tuple-element.71.picked_ref.pick_own, f32[256,128]{1,0:T(8,128)S(1)} %get-tuple-element.73.skel_own, f32[256,512]{1,0:T(8,128)S(1)} %get-tuple-element.74.proj_own, ...), custom_call_target="tpu_custom_call" | custom-call | flops 3000000000 | bytes 65536 | tf_op jit(solution)/shard_map/top/pallas_call | solution.py:457
  (75 shorter events, 3.9 us)
Async XLA Ops:
  0.6 205.1 %copy-start = (s32[4,256]{1,0:T(4,128)S(1)}, s32[4,256]{1,0:T(4,128)}, u32[]{:S(2)}) copy-start(s32[4,256]{1,0:T(4,128)} %param.12) | copy-start | bytes 12292
  0.6 6.6 %copy-start.18 = (s32[1,256]{1,0:T(1,128)S(1)}, s32[1,256]{1,0:T(1,128)}, u32[]{:S(2)}) copy-start(s32[1,256]{1,0:T(1,128)} %param.11) | copy-start | bytes 3076
  0.7 6.8 %copy-start.3 = (f32[512,64]{0,1:T(8,128)S(1)}, f32[512,64]{0,1:T(8,128)}, u32[]{:S(2)}) copy-start(f32[512,64]{0,1:T(8,128)} %param.7) | copy-start | bytes 393220
  2.1 38.7 %copy-start.1 = (f32[576,512]{1,0:T(8,128)}, f32[576,512]{1,0:T(8,128)S(1)}, u32[]{:S(2)}) copy-start(f32[576,512]{1,0:T(8,128)S(1)} %pad_maximum_fusion.own_ref.refs_0_) | copy-start | bytes 3538948
  2.1 31.9 %copy-start.17 = (s32[1,2]{1,0:T(1,128)S(1)}, s32[1,2]{1,0:T(1,128)}, u32[]{:S(2)}) copy-start(s32[1,2]{1,0:T(1,128)} %param.10) | copy-start | bytes 28
  2.1 33.8 %copy-start.2 = (f32[512,512]{1,0:T(8,128)S(1)}, f32[512,512]{1,0:T(8,128)}, u32[]{:S(2)}) copy-start(f32[512,512]{1,0:T(8,128)} %samp_ref.3) | copy-start | bytes 3145732
  2.1 33.8 %collective-permute-start = (f32[576,512]{1,0:T(8,128)S(1)}, f32[576,512]{1,0:T(8,128)}, u32[]{:S(2)}, u32[]{:S(2)}) collective-permute-start(f32[576,512]{1,0:T(8,128)S(1)} %pad_maximum_fusion.own_ref.refs_0_), channel_id=1, source_target_pairs={{0,16},{16,0},{32,48},{48,32},{64,80},{80,64},{96,112},{112,96},{1... | collective-permute-start | bytes 3538952 | tf_op jit(solution)/shard_map/ppermute | solution.py:396
  3.6 32.3 %collective-permute-start.1 = (f32[576,512]{1,0:T(8,128)S(1)}, f32[576,512]{1,0:T(8,128)}, u32[]{:S(2)}, u32[]{:S(2)}) collective-permute-start(f32[576,512]{1,0:T(8,128)S(1)} %pad_maximum_fusion.own_ref.refs_0_), channel_id=1, source_target_pairs={{16,32},{32,16},{48,64},{64,48},{80,96},{96,80},{17,33},{33,17},{4... | collective-permute-start | bytes 3538952 | tf_op jit(solution)/shard_map/ppermute | solution.py:397
  31.3 44.4 %collective-permute-start.2 = (f32[576,512]{1,0:T(8,128)S(1)}, f32[576,512]{1,0:T(8,128)}, u32[]{:S(2)}, u32[]{:S(2)}) collective-permute-start(f32[576,512]{1,0:T(8,128)S(1)} %pad_maximum_fusion.own_ref.refs_0_), channel_id=1, source_target_pairs={{0,12},{1,13},{2,14},{3,15},{4,0},{5,1},{6,2},{7,3},{8,4},{9,5},{1... | collective-permute-start | bytes 3538952 | tf_op jit(solution)/shard_map/ppermute | solution.py:402
  32.3 43.4 %collective-permute-start.3 = (f32[576,512]{1,0:T(8,128)S(1)}, f32[576,512]{1,0:T(8,128)}, u32[]{:S(2)}, u32[]{:S(2)}) collective-permute-start(f32[576,512]{1,0:T(8,128)S(1)} %pad_maximum_fusion.own_ref.refs_0_), channel_id=1, source_target_pairs={{0,3},{1,0},{2,1},{3,2},{4,7},{5,4},{6,5},{7,6},{8,11},{9,8},{10,9... | collective-permute-start | bytes 3538952 | tf_op jit(solution)/shard_map/ppermute | solution.py:402
  32.8 42.9 %collective-permute-start.4 = (f32[576,512]{1,0:T(8,128)S(1)}, f32[576,512]{1,0:T(8,128)}, u32[]{:S(2)}, u32[]{:S(2)}) collective-permute-start(f32[576,512]{1,0:T(8,128)S(1)} %pad_maximum_fusion.own_ref.refs_0_), channel_id=1, source_target_pairs={{0,5},{1,6},{2,7},{3,4},{4,9},{5,10},{6,11},{7,8},{8,13},{9,14},{1... | collective-permute-start | bytes 3538952 | tf_op jit(solution)/shard_map/ppermute | solution.py:402
  40.8 31.7 %all-to-all-start.2 = ((f32[16,16,512]{2,1,0:T(8,128)}), f32[16,16,512]{2,1,0:T(8,128)S(1)}, u32[]{:S(2)}, u32[]{:S(2)}) async-start(f32[16,16,512]{2,1,0:T(8,128)} %bitcast.8), calls=%async_computation.2 | async-start | bytes 1048576 | tf_op jit(solution)/shard_map/all_to_all | solution.py:381
  45.8 22.2 %collective-permute-start.5 = (f32[64,512]{1,0:T(8,128)S(1)}, f32[64,512]{1,0:T(8,128)S(1)}, u32[]{:S(2)}, u32[]{:S(2)}) collective-permute-start(f32[64,512]{1,0:T(8,128)S(1)} %bitcast.29), channel_id=1, source_target_pairs={{0,8},{1,9},{2,10},{3,11},{4,12},{5,13},{6,14},{7,15},{8,0},{9,1},... | collective-permute-start | bytes 393224 | tf_op jit(solution)/shard_map/ppermute | solution.py:407
  48.6 23.9 %collective-permute-start.6 = (f32[64,512]{1,0:T(8,128)S(1)}, f32[64,512]{1,0:T(8,128)S(1)}, u32[]{:S(2)}, u32[]{:S(2)}) collective-permute-start(f32[64,512]{1,0:T(8,128)S(1)} %bitcast.30), channel_id=1, source_target_pairs={{0,2},{1,3},{2,0},{3,1},{4,6},{5,7},{6,4},{7,5},{8,10},{9,11},{10,... | collective-permute-start | bytes 393224 | tf_op jit(solution)/shard_map/ppermute | solution.py:407
  68.0 24.7 %copy-start.4 = (f32[64,512]{1,0:T(8,128)}, f32[64,512]{1,0:T(8,128)S(1)}, u32[]{:S(2)}) copy-start(f32[64,512]{1,0:T(8,128)S(1)} %collective-permute-done.5.p1) | copy-start | bytes 393220
  68.0 7.7 %collective-permute-start.7 = (f32[64,512]{1,0:T(8,128)S(1)}, f32[64,512]{1,0:T(8,128)S(1)}, u32[]{:S(2)}, u32[]{:S(2)}) collective-permute-start(f32[64,512]{1,0:T(8,128)S(1)} %bitcast.31), channel_id=1, source_target_pairs={{0,10},{1,11},{2,8},{3,9},{4,14},{5,15},{6,12},{7,13},{8,2},{9,3},... | collective-permute-start | bytes 393224 | tf_op jit(solution)/shard_map/ppermute | solution.py:407
  72.5 20.2 %copy-start.6 = (f32[64,512]{1,0:T(8,128)}, f32[64,512]{1,0:T(8,128)S(1)}, u32[]{:S(2)}) copy-start(f32[64,512]{1,0:T(8,128)S(1)} %collective-permute-done.6.p2) | copy-start | bytes 393220
  75.7 17.0 %copy-start.8 = (f32[64,512]{1,0:T(8,128)}, f32[64,512]{1,0:T(8,128)S(1)}, u32[]{:S(2)}) copy-start(f32[64,512]{1,0:T(8,128)S(1)} %collective-permute-done.7.p3) | copy-start | bytes 393220
  75.7 16.9 %collective-permute-start.10 = (f32[576,512]{1,0:T(8,128)}, f32[576,512]{1,0:T(8,128)}, u32[]{:S(2)}, u32[]{:S(2)}) collective-permute-start(f32[576,512]{1,0:T(8,128)} %collective-permute-done.4.refs_3_), channel_id=1, source_target_pairs={{0,16},{16,0},{32,48},{48,32},{64,80},{80,64},{96,112},{112,96},{1... | collective-permute-start | bytes 3538952 | tf_op jit(solution)/shard_map/ppermute | solution.py:412
  79.5 26.6 %collective-permute-start.8 = (f32[576,512]{1,0:T(8,128)}, f32[576,512]{1,0:T(8,128)}, u32[]{:S(2)}, u32[]{:S(2)}) collective-permute-start(f32[576,512]{1,0:T(8,128)} %collective-permute-done.2.refs_1_), channel_id=1, source_target_pairs={{0,16},{16,0},{32,48},{48,32},{64,80},{80,64},{96,112},{112,96},{1... | collective-permute-start | bytes 3538952 | tf_op jit(solution)/shard_map/ppermute | solution.py:412
  79.6 26.6 %collective-permute-start.9 = (f32[576,512]{1,0:T(8,128)}, f32[576,512]{1,0:T(8,128)}, u32[]{:S(2)}, u32[]{:S(2)}) collective-permute-start(f32[576,512]{1,0:T(8,128)} %collective-permute-done.3.refs_2_), channel_id=1, source_target_pairs={{0,16},{16,0},{32,48},{48,32},{64,80},{80,64},{96,112},{112,96},{1... | collective-permute-start | bytes 3538952 | tf_op jit(solution)/shard_map/ppermute | solution.py:412
  80.8 18.6 %all-to-all-start.3 = ((f32[16,16,512]{2,1,0:T(8,128)}), f32[16,16,512]{2,1,0:T(8,128)S(1)}, u32[]{:S(2)}, u32[]{:S(2)}) async-start(f32[16,16,512]{2,1,0:T(8,128)} %broadcast_in_dim.7), calls=%async_computation.3 | async-start | bytes 1048576 | tf_op jit(solution)/shard_map/all_to_all | solution.py:383
  87.0 45.1 %collective-permute-start.11 = (f32[576,512]{1,0:T(8,128)}, f32[576,512]{1,0:T(8,128)}, u32[]{:S(2)}, u32[]{:S(2)}) collective-permute-start(f32[576,512]{1,0:T(8,128)} %collective-permute-done.2.refs_1_), channel_id=1, source_target_pairs={{16,32},{32,16},{48,64},{64,48},{80,96},{96,80},{17,33},{33,17},{4... | collective-permute-start | bytes 3538952 | tf_op jit(solution)/shard_map/ppermute | solution.py:411
  90.7 41.3 %collective-permute-start.12 = (f32[576,512]{1,0:T(8,128)}, f32[576,512]{1,0:T(8,128)}, u32[]{:S(2)}, u32[]{:S(2)}) collective-permute-start(f32[576,512]{1,0:T(8,128)} %collective-permute-done.3.refs_2_), channel_id=1, source_target_pairs={{16,32},{32,16},{48,64},{64,48},{80,96},{96,80},{17,33},{33,17},{4... | collective-permute-start | bytes 3538952 | tf_op jit(solution)/shard_map/ppermute | solution.py:411
  92.7 39.4 %collective-permute-start.13 = (f32[576,512]{1,0:T(8,128)}, f32[576,512]{1,0:T(8,128)}, u32[]{:S(2)}, u32[]{:S(2)}) collective-permute-start(f32[576,512]{1,0:T(8,128)} %collective-permute-done.4.refs_3_), channel_id=1, source_target_pairs={{16,32},{32,16},{48,64},{64,48},{80,96},{96,80},{17,33},{33,17},{4... | collective-permute-start | bytes 3538952 | tf_op jit(solution)/shard_map/ppermute | solution.py:411
  96.4 0.9 copy-start.5
  97.3 0.9 copy-start.7
  98.2 0.9 copy-start.9
  106.1 48.3 %collective-permute-start.16 = (f32[256,128]{1,0:T(8,128)S(1)}, f32[256,128]{1,0:T(8,128)S(1)}, u32[]{:S(2)}, u32[]{:S(2)}) collective-permute-start(f32[256,128]{1,0:T(8,128)S(1)} %bitcast.34), channel_id=1, source_target_pairs={{0,16},{16,0},{32,48},{48,32},{64,80},{80,64},{96,112},{112,96},{1... | collective-permute-start | bytes 393224 | tf_op jit(solution)/shard_map/ppermute | solution.py:417
  106.2 48.2 %collective-permute-start.15 = (f32[256,512]{1,0:T(8,128)S(1)}, f32[256,512]{1,0:T(8,128)S(1)}, u32[]{:S(2)}, u32[]{:S(2)}) collective-permute-start(f32[256,512]{1,0:T(8,128)S(1)} %bitcast.25), channel_id=1, source_target_pairs={{0,16},{16,0},{32,48},{48,32},{64,80},{80,64},{96,112},{112,96},{1... | collective-permute-start | bytes 1572872 | tf_op jit(solution)/shard_map/ppermute | solution.py:416
  139.4 1.0 copy-start.15
  140.3 17.6 %collective-permute-start.14 = (f32[512,256]{1,0:T(8,128)S(1)}, f32[512,256]{1,0:T(8,128)S(1)}, u32[]{:S(2)}, u32[]{:S(2)}) collective-permute-start(f32[512,256]{1,0:T(8,128)S(1)} %get-tuple-element.60), channel_id=1, source_target_pairs={{0,10},{1,11},{2,8},{3,9},{4,14},{5,15},{6,12},{7,13},{8,2},{9,3},... | collective-permute-start | bytes 1572872 | tf_op jit(solution)/shard_map/ppermute | solution.py:422
  145.9 12.0 %copy-start.16 = (bf16[4,256,512]{2,1,0:T(8,128)(2,1)S(1)}, bf16[4,256,512]{2,1,0:T(8,128)(2,1)}, u32[]{:S(2)}) copy-start(bf16[4,256,512]{2,1,0:T(8,128)(2,1)} %copy-done.15) | copy-start | bytes 3145732
  153.7 16.6 %collective-permute-start.17 = (f32[512,256]{1,0:T(8,128)S(1)}, f32[512,256]{1,0:T(8,128)S(1)}, u32[]{:S(2)}, u32[]{:S(2)}) collective-permute-start(f32[512,256]{1,0:T(8,128)S(1)} %get-tuple-element.64), channel_id=1, source_target_pairs={{0,8},{1,9},{2,10},{3,11},{4,12},{5,13},{6,14},{7,15},{8,0},{9,1},... | collective-permute-start | bytes 1572872 | tf_op jit(solution)/shard_map/ppermute | solution.py:425
  154.0 16.2 %collective-permute-start.18 = (f32[512,256]{1,0:T(8,128)S(1)}, f32[512,256]{1,0:T(8,128)S(1)}, u32[]{:S(2)}, u32[]{:S(2)}) collective-permute-start(f32[512,256]{1,0:T(8,128)S(1)} %get-tuple-element.65), channel_id=1, source_target_pairs={{0,2},{1,3},{2,0},{3,1},{4,6},{5,7},{6,4},{7,5},{8,10},{9,11},{10,... | collective-permute-start | bytes 1572872 | tf_op jit(solution)/shard_map/ppermute | solution.py:426
  154.3 15.9 %copy-start.12 = (f32[256,128]{1,0:T(8,128)}, f32[256,128]{1,0:T(8,128)S(1)}, u32[]{:S(2)}) copy-start(f32[256,128]{1,0:T(8,128)S(1)} %collective-permute-done.16.skel_peer) | copy-start | bytes 393220
  154.3 15.9 %copy-start.10 = (f32[256,512]{1,0:T(8,128)}, f32[256,512]{1,0:T(8,128)S(1)}, u32[]{:S(2)}) copy-start(f32[256,512]{1,0:T(8,128)S(1)} %collective-permute-done.15.pick_peer) | copy-start | bytes 1572868
  188.9 18.3 %copy-start.11 = (f32[256,512]{1,0:T(8,128)S(1)}, f32[256,512]{1,0:T(8,128)}, u32[]{:S(2)}) copy-start(f32[256,512]{1,0:T(8,128)} %copy-done.10) | copy-start | bytes 1572868
  188.9 18.3 %copy-start.13 = (f32[256,128]{1,0:T(8,128)S(1)}, f32[256,128]{1,0:T(8,128)}, u32[]{:S(2)}) copy-start(f32[256,128]{1,0:T(8,128)} %copy-done.12) | copy-start | bytes 393220
  201.3 6.0 %collective-permute-start.19 = (f32[256,512]{1,0:T(8,128)S(1)}, f32[256,512]{1,0:T(8,128)S(1)}, u32[]{:S(2)}, u32[]{:S(2)}) collective-permute-start(f32[256,512]{1,0:T(8,128)S(1)} %bitcast.36), channel_id=1, source_target_pairs={{0,16},{16,0},{32,48},{48,32},{64,80},{80,64},{96,112},{112,96},{1... | collective-permute-start | bytes 1572872 | tf_op jit(solution)/shard_map/ppermute | solution.py:432
  211.2 11.8 %collective-permute-start.20 = (f32[128,640]{1,0:T(8,128)S(1)}, f32[128,640]{1,0:T(8,128)S(1)}, u32[]{:S(2)}, u32[]{:S(2)}) collective-permute-start(f32[128,640]{1,0:T(8,128)S(1)} %get-tuple-element.75), channel_id=1, source_target_pairs={{0,32},{16,48},{32,0},{48,16},{64,96},{80,112},{96,64},{112,80},{1... | collective-permute-start | bytes 983048 | tf_op jit(solution)/shard_map/ppermute | solution.py:447
  212.0 1.3 copy-start.14
  213.3 17.8 %copy-start.19 = (s32[2,256]{1,0:T(2,128)S(1)}, s32[2,256]{1,0:T(2,128)}, u32[]{:S(2)}) copy-start(s32[2,256]{1,0:T(2,128)} %param.13) | copy-start | bytes 6148
  222.4 7.2 %collective-permute-start.22 = (f32[128,512]{1,0:T(8,128)S(1)}, f32[128,512]{1,0:T(8,128)S(1)}, u32[]{:S(2)}, u32[]{:S(2)}) collective-permute-start(f32[128,512]{1,0:T(8,128)S(1)} %get-tuple-element.76), channel_id=1, source_target_pairs={{0,32},{16,48},{32,0},{48,16},{64,96},{80,112},{96,64},{112,80},{1... | collective-permute-start | bytes 786440 | tf_op jit(solution)/shard_map/ppermute | solution.py:454
  223.1 9.2 %collective-permute-start.21 = (f32[128,640]{1,0:T(8,128)S(1)}, f32[128,640]{1,0:T(8,128)S(1)}, u32[]{:S(2)}, u32[]{:S(2)}) collective-permute-start(f32[128,640]{1,0:T(8,128)S(1)} %collective-permute-done.20.pick_1), channel_id=1, source_target_pairs={{0,16},{16,0},{32,48},{48,32},{64,80},{80,64},{96,112},{112,96},{1... | collective-permute-start | bytes 983048 | tf_op jit(solution)/shard_map/ppermute | solution.py:448
  229.5 2.7 %collective-permute-start.23 = (f32[128,512]{1,0:T(8,128)S(1)}, f32[128,512]{1,0:T(8,128)S(1)}, u32[]{:S(2)}, u32[]{:S(2)}) collective-permute-start(f32[128,512]{1,0:T(8,128)S(1)} %collective-permute-done.22.proj_1), channel_id=1, source_target_pairs={{0,16},{16,0},{32,48},{48,32},{64,80},{80,64},{96,112},{112,96},{1... | collective-permute-start | bytes 786440 | tf_op jit(solution)/shard_map/ppermute | solution.py:455

commit v8 on v7

--- a/solution.py
+++ b/solution.py
@@ -397,16 +397,14 @@
     outer = [lax.ppermute(message, "leaf", OUTER)]
     start = (row * BLK).reshape(1, 1)
     (skel,) = call(skel_kernel, [((RANK, 2 * DIM), F32)], 1, 2, name="skel")(start, pivots, xt)
-    (skel,) = sum_row(skel)
+    targets = [lax.ppermute(xt, "row", shift(*by)) for by in TARGET]
+    skel, *targets = sum_row(skel, *targets)
     skel, late = after(skel, message)
     own = [message] + [lax.ppermute(late, "row", shift(*by)) for by in SOURCE]
     (part,) = call(
         pivot_kernel, [((RANK, SAMP), F32)], 2, 6, [VMEM((4 * DIM, BLK), BF16)], name="pivot"
     )(start, weight, pivots, skel, samples, own[0], sib[0], outer[0])
-    part, xt = after(part, xt)
-    targets = [lax.ppermute(xt, "row", shift(*by)) for by in TARGET]
-    picked, *rest = sum_row(part, *own[1:], *targets)
-    own[1:], targets = rest[:3], rest[3:]
+    picked, *own[1:] = sum_row(part, *own[1:])
     (feats,) = call(feature_kernel, [((SIDE, BLK, 4 * DIM), BF16)], 0, 4, name="features")(xt, *targets)
     outer += [lax.ppermute(m, "leaf", OUTER) for m in own[1:]]
     sib += [lax.ppermute(m, "leaf", SIBLING) for m in own[1:]]

time: 245 us -> 239 us (0.976)
  blocking collectives: 51.3 us -> 81.3 us
  waiting for transfers between devices: 32 us -> 12.3 us
  starting transfers between devices: 57 us -> 43.4 us
    all_to_all x2 -> x3, blocking collectives: 28.8 us -> 59.2 us  [sum_row(): parts = lax.all_to_all(part.reshape(16, share, -1), 'row', 0, 0)]
    ppermute x3, waiting for transfers between devices: 19.9 us -> 0.01 us  [body(): targets = [lax.ppermute(xt, 'row', shift(*by)) for by in TARGET]]
    all_to_all x1 -> x0, starting transfers between devices: 4.98 us -> none  [sum_row(): parts = lax.all_to_all(part.reshape(16, share, -1), 'row', 0, 0)]
    ppermute x3, starting transfers between devices: 9.29 us -> 5.74 us  [body(): targets = [lax.ppermute(xt, 'row', shift(*by)) for by in TARGET]]
    ppermute x3, starting transfers between devices: 4.26 us -> 1.08 us  [body(): sib += [lax.ppermute(m, 'leaf', SIBLING) for m in own[1:]]]
  transfers between devices with their start and end apart: 26 -> 25, of which waited for: 7 -> 4; matrix products, arithmetic and copies ran while one was open for 1% -> 1% of each run, Pallas kernels for 30% -> 30%
where the time goes in v8:
time: 239 us
  Pallas kernels  90.8 us (38%)
  blocking collectives  81.3 us (34%)
  starting transfers between devices  43.4 us (18%)
  waiting for transfers between devices  12.3 us (5%)
  local copies, waits for them, and re-layouts  6.99 us (3%)
  between operations  2.41 us (1%)
    all_to_all x3, blocking collectives, sum_row(): parts = lax.all_to_all(part.reshape(16, share, -1), 'row', 0, 0)  59.2 us
    pallas_call x2, Pallas kernels, first_near(): call(functools.partial(first_kernel, targets, count, weighted), [BLOCK] *...  32.7 us
    all_to_all x2, blocking collectives, sum_row(): lax.all_to_all(jnp.broadcast_to(mine[None], (16, *mine.shape)), 'row', 0, 0)  22.1 us
    pallas_call x2, Pallas kernels, next_near(): call(functools.partial(next_kernel, targets, len(groups)), [BLOCK] * len(...  20 us
    pallas_call x1, Pallas kernels, body(): call(functools.partial(top_kernel, top_share), [((top_share, RANK), F32)]...  11.1 us
    ppermute x3, starting transfers between devices, body(): outer += [lax.ppermute(m, 'leaf', OUTER) for m in own[1:]]  9.53 us
    pallas_call x1, Pallas kernels, body(): call(functools.partial(mid_kernel, mid_share), [((mid_share, RANK), F32),...  9.05 us
    ppermute x1, waiting for transfers between devices, body(): proj_1 = lax.ppermute(send, 'leaf', COUSIN)  6.51 us
  transfers between devices with their start and end apart: 25, of which 4 were waited for; matrix products, arithmetic and copies ran while one was open for 1% of the time, Pallas kernels for 30%

profile of v8, /device:TPU:1, one launch (start us, length us, event | category | flops | bytes accessed | tf_op | source)
XLA Modules:
  0.0 238.9 jit_solution(18238518813295449746)
XLA Ops:
  0.7 1.4 pad_maximum_fusion.own_ref.refs_0_
  2.1 1.5 collective-permute-start.3
  3.6 3.7 %collective-permute-start.4 = (f32[576,512]{1,0:T(8,128)S(1)}, f32[576,512]{1,0:T(8,128)}, u32[]{:S(2)}, u32[]{:S(2)}) collective-permute-start(f32[576,512]{1,0:T(8,128)S(1)} %pad_maximum_fusion.own_ref.refs_0_), channel_id=1, source_target_pairs={{16,32},{32,16},{48,64},{64,48},{80,96},{96,80},{17,33},{33,17},{4... | collective-permute-start | bytes 3538952 | tf_op jit(solution)/shard_map/ppermute | solution.py:397
  7.3 2.8 %collective-permute-start = (f32[64,512]{1,0:T(8,128)S(1)}, f32[64,512]{1,0:T(8,128)S(1)}, u32[]{:S(2)}, u32[]{:S(2)}) collective-permute-start(f32[64,512]{1,0:T(8,128)S(1)} %bitcast.29), channel_id=1, source_target_pairs={{0,8},{1,9},{2,10},{3,11},{4,12},{5,13},{6,14},{7,15},{8,0},{9,1},... | collective-permute-start | bytes 393224 | tf_op jit(solution)/shard_map/ppermute | solution.py:400
  10.1 2.9 %collective-permute-start.1 = (f32[64,512]{1,0:T(8,128)S(1)}, f32[64,512]{1,0:T(8,128)S(1)}, u32[]{:S(2)}, u32[]{:S(2)}) collective-permute-start(f32[64,512]{1,0:T(8,128)S(1)} %bitcast.30), channel_id=1, source_target_pairs={{0,2},{1,3},{2,0},{3,1},{4,6},{5,7},{6,4},{7,5},{8,10},{9,11},{10,... | collective-permute-start | bytes 393224 | tf_op jit(solution)/shard_map/ppermute | solution.py:400
  13.2 0.4 skel.1
  13.6 13.7 %all_to_all.30 = f32[16,16,128]{2,1,0:T(8,128)S(1)} all-to-all(f32[16,16,128]{2,1,0:T(8,128)S(1)} %bitcast.41), channel_id=1, replica_groups=mesh['leaf'=8,'row'=16] {'row'}, dimensions={0} | all-to-all | bytes 262144 | tf_op jit(solution)/shard_map/all_to_all | solution.py:381
  27.4 9.9 %all_to_all.31 = f32[16,16,128]{2,1,0:T(8,128)S(1)} all-to-all(f32[16,16,128]{2,1,0:T(8,128)S(1)} %broadcast_in_dim.6), channel_id=1, replica_groups=mesh['leaf'=8,'row'=16] {'row'}, dimensions={0} | all-to-all | bytes 262144 | tf_op jit(solution)/shard_map/all_to_all | solution.py:383
  37.3 1.0 collective-permute-start.5
  38.3 0.7 collective-permute-start.6
  39.0 0.9 collective-permute-start.7
  39.9 0.6 fusion
  41.9 4.1 %pivot.1 = f32[256,512]{1,0:T(8,128)S(1)} custom-call(s32[1,1]{1,0:T(1,128)} %bitcast.start_ref, f32[1,1]{1,0:T(1,128)} %bitcast.3.weight_ref, s32[256,1]{1,0:T(8,128)S(1)} %copy.11.piv_ref, f32[256,128]{1,0:T(8,128)S(1)} %bitcast.34, f32[512,512]{1,0:T(8,128)S(1)} %copy-done.2, f32[576,512]{1,0:T(8,128)S(1)} %pad_maximum_fusion.own_ref.refs_0_, ...), custom_call_target="tpu_custom_call" | custom-call | bytes 65536 | tf_op jit(solution)/shard_map/pivot/pallas_call | solution.py:404
  46.0 29.9 %all_to_all.32 = f32[16,16,512]{2,1,0:T(8,128)S(1)} all-to-all(f32[16,16,512]{2,1,0:T(8,128)S(1)} %bitcast.24), channel_id=1, replica_groups=mesh['leaf'=8,'row'=16] {'row'}, dimensions={0} | all-to-all | bytes 1048576 | tf_op jit(solution)/shard_map/all_to_all | solution.py:381
  75.9 0.6 collective-permute-start.10
  76.6 0.4 collective-permute-start.9
  77.0 0.9 broadcast_in_dim.7
  77.9 4.0 %all-to-all-start.3 = ((f32[16,16,512]{2,1,0:T(8,128)}), f32[16,16,512]{2,1,0:T(8,128)S(1)}, u32[]{:S(2)}, u32[]{:S(2)}) async-start(f32[16,16,512]{2,1,0:T(8,128)} %broadcast_in_dim.7), calls=%async_computation.3 | async-start | bytes 1048576 | tf_op jit(solution)/shard_map/all_to_all | solution.py:383
  81.9 4.0 %collective-permute-start.11 = (f32[576,512]{1,0:T(8,128)}, f32[576,512]{1,0:T(8,128)}, u32[]{:S(2)}, u32[]{:S(2)}) collective-permute-start(f32[576,512]{1,0:T(8,128)} %collective-permute-done.5.refs_1_), channel_id=1, source_target_pairs={{16,32},{32,16},{48,64},{64,48},{80,96},{96,80},{17,33},{33,17},{4... | collective-permute-start | bytes 3538952 | tf_op jit(solution)/shard_map/ppermute | solution.py:409
  85.9 1.9 collective-permute-start.12
  87.8 3.6 %collective-permute-start.13 = (f32[576,512]{1,0:T(8,128)}, f32[576,512]{1,0:T(8,128)}, u32[]{:S(2)}, u32[]{:S(2)}) collective-permute-start(f32[576,512]{1,0:T(8,128)} %collective-permute-done.7.refs_3_), channel_id=1, source_target_pairs={{16,32},{32,16},{48,64},{64,48},{80,96},{96,80},{17,33},{33,17},{4... | collective-permute-start | bytes 3538952 | tf_op jit(solution)/shard_map/ppermute | solution.py:409
  91.5 0.9 copy-done.5
  92.4 0.9 copy-done.7
  93.3 0.9 copy-done.9
  94.2 0.4 features.1.feat_ref
  94.6 6.1 %solve.1.coeffs_ref = f32[256,512]{1,0:T(8,128)S(1)} custom-call(f32[256,512]{1,0:T(8,128)S(1)} %bitcast.25), custom_call_target="tpu_custom_call" | custom-call | bytes 65536 | tf_op jit(solution)/shard_map/solve/pallas_call | solution.py:411
  100.8 0.5 collective-permute-start.15
  101.3 25.4 %near_inner.1 = (f32[512,256]{1,0:T(8,128)S(1)}, f32[512,256]{1,0:T(8,128)S(1)}, f32[512,256]{1,0:T(8,128)S(1)}, bf16[8,1024,256]{2,1,0:T(8,128)(2,1)}, bf16[8,256,512]{2,1,0:T(8,128)(2,1)}) custom-call(f32[1,1]{1,0:T(1,128)} %bitcast.3.weight_ref, f32[256,512]{1,0:T(8,128)S(1)} %solve.1.coeffs_ref, bf16[4,512,256]{2,1,0:T(8,128)(2,1)S(1)} %features.1.feat_ref, ...), custom_call_target="tpu_custom_call" | custom-call | flops 10000000000 | bytes 65536 | tf_op jit(solution)/shard_map/near_inner/pallas_call | solution.py:217
  126.7 7.3 %near_3.1 = (f32[512,256]{1,0:T(8,128)S(1)}, bf16[4,1024,256]{2,1,0:T(8,128)(2,1)}, bf16[4,256,512]{2,1,0:T(8,128)(2,1)S(1)}) custom-call(f32[1,1]{1,0:T(1,128)} %bitcast.3.weight_ref, f32[256,512]{1,0:T(8,128)S(1)} %solve.1.coeffs_ref, bf16[4,512,256]{2,1,0:T(8,128)(2,1)S(1)} %features.1.feat_ref, f32[576,512]{1,0:T(8,128)} %collective-permute-done.4.out_ref.refs_0_, ...), custom_call_target="tpu_custom_call" | custom-call | flops 10000000000 | bytes 65536 | tf_op jit(solution)/shard_map/near_3/pallas_call | solution.py:217
  134.0 1.0 copy-done.15
  135.0 5.5 %collective-permute-start.14 = (f32[512,256]{1,0:T(8,128)S(1)}, f32[512,256]{1,0:T(8,128)S(1)}, u32[]{:S(2)}, u32[]{:S(2)}) collective-permute-start(f32[512,256]{1,0:T(8,128)S(1)} %get-tuple-element.58), channel_id=1, source_target_pairs={{0,10},{1,11},{2,8},{3,9},{4,14},{5,15},{6,12},{7,13},{8,2},{9,3},... | collective-permute-start | bytes 1572872 | tf_op jit(solution)/shard_map/ppermute | solution.py:420
  140.5 7.7 %near_12.1 = (f32[512,256]{1,0:T(8,128)S(1)}, f32[512,256]{1,0:T(8,128)S(1)}) custom-call(bf16[4,512,256]{2,1,0:T(8,128)(2,1)S(1)} %features.1.feat_ref, bf16[4,1024,256]{2,1,0:T(8,128)(2,1)} %get-tuple-element.56.refs_2_.refs_0_, bf16[4,256,512]{2,1,0:T(8,128)(2,1)} %copy-done.15, f32[512,256]{1,0:T(8,128)S(1)} %get-tuple-element.60.refs_2_, ...), custom_call_target="tpu_custom_call" | custom-call | flops 10000000000 | bytes 65536 | tf_op jit(solution)/shard_map/near_12/pallas_call | solution.py:226
  149.0 3.5 %collective-permute-done.14.refs_4_ = f32[512,256]{1,0:T(8,128)S(1)} collective-permute-done((f32[512,256]{1,0:T(8,128)S(1)}, f32[512,256]{1,0:T(8,128)S(1)}, u32[]{:S(2)}, u32[]{:S(2)}) %collective-permute-start.14) | collective-permute-done | bytes 524320 | tf_op jit(solution)/shard_map/ppermute | solution.py:420
  152.5 12.3 %near_0.1.refs_0_ = f32[512,256]{1,0:T(8,128)S(1)} custom-call(bf16[4,512,256]{2,1,0:T(8,128)(2,1)S(1)} %features.1.feat_ref, bf16[8,1024,256]{2,1,0:T(8,128)(2,1)} %get-tuple-element.53.refs_0_, bf16[8,256,512]{2,1,0:T(8,128)(2,1)} %get-tuple-element.54.refs_1_, bf16[4,1024,256]{2,1,0:T(8,128)(2,1)} %get-tuple-element.56.refs_2_.refs_0_, ...), custom_call_target="tpu_custom_call" | custom-call | flops 10000000000 | bytes 65536 | tf_op jit(solution)/shard_map/near_0/pallas_call | solution.py:226
  164.8 3.1 %basis.1 = (f32[512,256]{1,0:T(8,128)}, f32[256,512]{1,0:T(8,128)S(1)}) custom-call(f32[512,512]{1,0:T(8,128)S(1)} %copy-done.2, f32[512,512]{1,0:T(8,128)} %test_ref.1, f32[256,512]{1,0:T(8,128)S(1)} %solve.1.coeffs_ref, f32[512,256]{1,0:T(8,128)S(1)} %near_0.1.refs_0_, f32[512,256]{1,0:T(8,128)S(1)} %collective-permute-done.17.refs_1_, ...), custom_call_target="tpu_custom_call" | custom-call | flops 1000000000 | bytes 65536 | tf_op jit(solution)/shard_map/basis/pallas_call | solution.py:426
  167.9 15.6 %all_to_all.33 = f32[16,16,512]{2,1,0:T(8,128)S(1)} all-to-all(f32[16,16,512]{2,1,0:T(8,128)S(1)} %bitcast.40), channel_id=1, replica_groups=mesh['leaf'=8,'row'=16] {'row'}, dimensions={0} | all-to-all | bytes 1048576 | tf_op jit(solution)/shard_map/all_to_all | solution.py:381
  183.6 12.2 %all_to_all.34 = f32[16,16,512]{2,1,0:T(8,128)S(1)} all-to-all(f32[16,16,512]{2,1,0:T(8,128)S(1)} %broadcast_in_dim.8), channel_id=1, replica_groups=mesh['leaf'=8,'row'=16] {'row'}, dimensions={0} | all-to-all | bytes 1048576 | tf_op jit(solution)/shard_map/all_to_all | solution.py:383
  195.9 4.5 %collective-permute-start.19 = (f32[256,512]{1,0:T(8,128)S(1)}, f32[256,512]{1,0:T(8,128)S(1)}, u32[]{:S(2)}, u32[]{:S(2)}) collective-permute-start(f32[256,512]{1,0:T(8,128)S(1)} %bitcast.37), channel_id=1, source_target_pairs={{0,16},{16,0},{32,48},{48,32},{64,80},{80,64},{96,112},{112,96},{1... | collective-permute-start | bytes 1572872 | tf_op jit(solution)/shard_map/ppermute | solution.py:430
  200.6 1.3 collective-permute-done.19.proj_peer
  201.9 3.9 %mid_stack.1 = (f32[512,640]{1,0:T(8,128)}, f32[256,512]{1,0:T(8,128)S(1)}, f32[256,128]{1,0:T(8,128)S(1)}, f32[128,640]{1,0:T(8,128)S(1)}) custom-call(s32[1,3]{1,0:T(1,128)S(1)} %add_bitcast_fusion.info_ref, s32[256,1]{1,0:T(8,128)S(1)} %copy.12.piv_ref, f32[256,512]{1,0:T(8,128)S(1)} %bitcast.27, f32[256,128]{1,0:T(8,128)S(1)} %bitcast.36, ...), custom_call_target="tpu_custom_call" | custom-call | flops 1000000000 | bytes 65536 | tf_op jit(solution)/shard_map/mid_stack/pallas_call | solution.py:441
  205.8 1.7 collective-permute-start.20
  207.5 1.3 copy-done.14
  208.8 9.0 %mid_solve.1 = (f32[16,256]{1,0:T(8,128)}, f32[256,512]{1,0:T(8,128)S(1)}, f32[128,512]{1,0:T(8,128)S(1)}) custom-call(s32[1,3]{1,0:T(1,128)S(1)} %add_bitcast_fusion.info_ref, f32[512,640]{1,0:T(8,128)S(1)} %copy-done.14, f32[256,512]{1,0:T(8,128)S(1)} %get-tuple-element.69.picked_ref.pick_own, f32[256,512]{1,0:T(8,128)S(1)} %bitcast.39, ...), custom_call_target="tpu_custom_call" | custom-call | flops 3000000000 | bytes 65536 | tf_op jit(solution)/shard_map/mid_solve/pallas_call | solution.py:447
  217.9 0.7 collective-permute-start.21
  218.6 6.5 %collective-permute-done.22.proj_1 = f32[128,512]{1,0:T(8,128)S(1)} collective-permute-done((f32[128,512]{1,0:T(8,128)S(1)}, f32[128,512]{1,0:T(8,128)S(1)}, u32[]{:S(2)}, u32[]{:S(2)}) %collective-permute-start.22) | collective-permute-done | bytes 262176 | tf_op jit(solution)/shard_map/ppermute | solution.py:452
  225.1 1.5 collective-permute-start.23
  226.9 0.9 collective-permute-done.23.proj_2
  227.8 11.1 %top.1 = f32[8,256]{1,0:T(8,128)} custom-call(s32[1,3]{1,0:T(1,128)S(1)} %add_bitcast_fusion.1.info_ref, s32[256,1]{1,0:T(8,128)S(1)} %copy.13.piv_ref, f32[256,512]{1,0:T(8,128)S(1)} %get-tuple-element.69.picked_ref.pick_own, f32[256,128]{1,0:T(8,128)S(1)} %get-tuple-element.71.skel_own, f32[256,512]{1,0:T(8,128)S(1)} %get-tuple-element.72.proj_own, ...), custom_call_target="tpu_custom_call" | custom-call | flops 3000000000 | bytes 65536 | tf_op jit(solution)/shard_map/top/pallas_call | solution.py:455
  (74 shorter events, 1.7 us)
Async XLA Ops:
  0.6 199.7 %copy-start = (s32[4,256]{1,0:T(4,128)S(1)}, s32[4,256]{1,0:T(4,128)}, u32[]{:S(2)}) copy-start(s32[4,256]{1,0:T(4,128)} %param.12) | copy-start | bytes 12292
  0.6 6.6 %copy-start.3 = (f32[512,64]{0,1:T(8,128)S(1)}, f32[512,64]{0,1:T(8,128)}, u32[]{:S(2)}) copy-start(f32[512,64]{0,1:T(8,128)} %param.7) | copy-start | bytes 393220
  0.7 12.4 %copy-start.18 = (s32[1,256]{1,0:T(1,128)S(1)}, s32[1,256]{1,0:T(1,128)}, u32[]{:S(2)}) copy-start(s32[1,256]{1,0:T(1,128)} %param.11) | copy-start | bytes 3076
  2.1 43.8 %copy-start.1 = (f32[576,512]{1,0:T(8,128)}, f32[576,512]{1,0:T(8,128)S(1)}, u32[]{:S(2)}) copy-start(f32[576,512]{1,0:T(8,128)S(1)} %pad_maximum_fusion.own_ref.refs_0_) | copy-start | bytes 3538948
  2.1 37.8 %copy-start.17 = (s32[1,2]{1,0:T(1,128)S(1)}, s32[1,2]{1,0:T(1,128)}, u32[]{:S(2)}) copy-start(s32[1,2]{1,0:T(1,128)} %param.10) | copy-start | bytes 28
  2.1 39.7 %copy-start.2 = (f32[512,512]{1,0:T(8,128)S(1)}, f32[512,512]{1,0:T(8,128)}, u32[]{:S(2)}) copy-start(f32[512,512]{1,0:T(8,128)} %samp_ref.3) | copy-start | bytes 3145732
  2.1 39.7 %collective-permute-start.3 = (f32[576,512]{1,0:T(8,128)S(1)}, f32[576,512]{1,0:T(8,128)}, u32[]{:S(2)}, u32[]{:S(2)}) collective-permute-start(f32[576,512]{1,0:T(8,128)S(1)} %pad_maximum_fusion.own_ref.refs_0_), channel_id=1, source_target_pairs={{0,16},{16,0},{32,48},{48,32},{64,80},{80,64},{96,112},{112,96},{1... | collective-permute-start | bytes 3538952 | tf_op jit(solution)/shard_map/ppermute | solution.py:396
  3.6 38.2 %collective-permute-start.4 = (f32[576,512]{1,0:T(8,128)S(1)}, f32[576,512]{1,0:T(8,128)}, u32[]{:S(2)}, u32[]{:S(2)}) collective-permute-start(f32[576,512]{1,0:T(8,128)S(1)} %pad_maximum_fusion.own_ref.refs_0_), channel_id=1, source_target_pairs={{16,32},{32,16},{48,64},{64,48},{80,96},{96,80},{17,33},{33,17},{4... | collective-permute-start | bytes 3538952 | tf_op jit(solution)/shard_map/ppermute | solution.py:397
  7.3 20.0 %collective-permute-start = (f32[64,512]{1,0:T(8,128)S(1)}, f32[64,512]{1,0:T(8,128)S(1)}, u32[]{:S(2)}, u32[]{:S(2)}) collective-permute-start(f32[64,512]{1,0:T(8,128)S(1)} %bitcast.29), channel_id=1, source_target_pairs={{0,8},{1,9},{2,10},{3,11},{4,12},{5,13},{6,14},{7,15},{8,0},{9,1},... | collective-permute-start | bytes 393224 | tf_op jit(solution)/shard_map/ppermute | solution.py:400
  10.1 17.2 %collective-permute-start.1 = (f32[64,512]{1,0:T(8,128)S(1)}, f32[64,512]{1,0:T(8,128)S(1)}, u32[]{:S(2)}, u32[]{:S(2)}) collective-permute-start(f32[64,512]{1,0:T(8,128)S(1)} %bitcast.30), channel_id=1, source_target_pairs={{0,2},{1,3},{2,0},{3,1},{4,6},{5,7},{6,4},{7,5},{8,10},{9,11},{10,... | collective-permute-start | bytes 393224 | tf_op jit(solution)/shard_map/ppermute | solution.py:400
  13.0 14.3 %collective-permute-start.2 = (f32[64,512]{1,0:T(8,128)S(1)}, f32[64,512]{1,0:T(8,128)S(1)}, u32[]{:S(2)}, u32[]{:S(2)}) collective-permute-start(f32[64,512]{1,0:T(8,128)S(1)} %bitcast.31), channel_id=1, source_target_pairs={{0,10},{1,11},{2,8},{3,9},{4,14},{5,15},{6,12},{7,13},{8,2},{9,3},... | collective-permute-start | bytes 393224 | tf_op jit(solution)/shard_map/ppermute | solution.py:400
  27.3 18.6 %copy-start.4 = (f32[64,512]{1,0:T(8,128)}, f32[64,512]{1,0:T(8,128)S(1)}, u32[]{:S(2)}) copy-start(f32[64,512]{1,0:T(8,128)S(1)} %collective-permute-done.p1) | copy-start | bytes 393220
  27.3 18.6 %copy-start.6 = (f32[64,512]{1,0:T(8,128)}, f32[64,512]{1,0:T(8,128)S(1)}, u32[]{:S(2)}) copy-start(f32[64,512]{1,0:T(8,128)S(1)} %collective-permute-done.1.p2) | copy-start | bytes 393220
  27.4 18.6 %copy-start.8 = (f32[64,512]{1,0:T(8,128)}, f32[64,512]{1,0:T(8,128)S(1)}, u32[]{:S(2)}) copy-start(f32[64,512]{1,0:T(8,128)S(1)} %collective-permute-done.2.p3) | copy-start | bytes 393220
  37.3 38.6 %collective-permute-start.5 = (f32[576,512]{1,0:T(8,128)S(1)}, f32[576,512]{1,0:T(8,128)}, u32[]{:S(2)}, u32[]{:S(2)}) collective-permute-start(f32[576,512]{1,0:T(8,128)S(1)} %pad_maximum_fusion.own_ref.refs_0_), channel_id=1, source_target_pairs={{0,12},{1,13},{2,14},{3,15},{4,0},{5,1},{6,2},{7,3},{8,4},{9,5},{1... | collective-permute-start | bytes 3538952 | tf_op jit(solution)/shard_map/ppermute | solution.py:403
  38.3 37.6 %collective-permute-start.6 = (f32[576,512]{1,0:T(8,128)S(1)}, f32[576,512]{1,0:T(8,128)}, u32[]{:S(2)}, u32[]{:S(2)}) collective-permute-start(f32[576,512]{1,0:T(8,128)S(1)} %pad_maximum_fusion.own_ref.refs_0_), channel_id=1, source_target_pairs={{0,3},{1,0},{2,1},{3,2},{4,7},{5,4},{6,5},{7,6},{8,11},{9,8},{10,9... | collective-permute-start | bytes 3538952 | tf_op jit(solution)/shard_map/ppermute | solution.py:403
  39.0 36.9 %collective-permute-start.7 = (f32[576,512]{1,0:T(8,128)S(1)}, f32[576,512]{1,0:T(8,128)}, u32[]{:S(2)}, u32[]{:S(2)}) collective-permute-start(f32[576,512]{1,0:T(8,128)S(1)} %pad_maximum_fusion.own_ref.refs_0_), channel_id=1, source_target_pairs={{0,5},{1,6},{2,7},{3,4},{4,9},{5,10},{6,11},{7,8},{8,13},{9,14},{1... | collective-permute-start | bytes 3538952 | tf_op jit(solution)/shard_map/ppermute | solution.py:403
  75.9 11.9 %collective-permute-start.10 = (f32[576,512]{1,0:T(8,128)}, f32[576,512]{1,0:T(8,128)}, u32[]{:S(2)}, u32[]{:S(2)}) collective-permute-start(f32[576,512]{1,0:T(8,128)} %collective-permute-done.7.refs_3_), channel_id=1, source_target_pairs={{0,16},{16,0},{32,48},{48,32},{64,80},{80,64},{96,112},{112,96},{1... | collective-permute-start | bytes 3538952 | tf_op jit(solution)/shard_map/ppermute | solution.py:410
  76.5 24.2 %collective-permute-start.8 = (f32[576,512]{1,0:T(8,128)}, f32[576,512]{1,0:T(8,128)}, u32[]{:S(2)}, u32[]{:S(2)}) collective-permute-start(f32[576,512]{1,0:T(8,128)} %collective-permute-done.5.refs_1_), channel_id=1, source_target_pairs={{0,16},{16,0},{32,48},{48,32},{64,80},{80,64},{96,112},{112,96},{1... | collective-permute-start | bytes 3538952 | tf_op jit(solution)/shard_map/ppermute | solution.py:410
  76.6 24.2 %collective-permute-start.9 = (f32[576,512]{1,0:T(8,128)}, f32[576,512]{1,0:T(8,128)}, u32[]{:S(2)}, u32[]{:S(2)}) collective-permute-start(f32[576,512]{1,0:T(8,128)} %collective-permute-done.6.refs_2_), channel_id=1, source_target_pairs={{0,16},{16,0},{32,48},{48,32},{64,80},{80,64},{96,112},{112,96},{1... | collective-permute-start | bytes 3538952 | tf_op jit(solution)/shard_map/ppermute | solution.py:410
  77.9 16.7 %all-to-all-start.3 = ((f32[16,16,512]{2,1,0:T(8,128)}), f32[16,16,512]{2,1,0:T(8,128)S(1)}, u32[]{:S(2)}, u32[]{:S(2)}) async-start(f32[16,16,512]{2,1,0:T(8,128)} %broadcast_in_dim.7), calls=%async_computation.3 | async-start | bytes 1048576 | tf_op jit(solution)/shard_map/all_to_all | solution.py:383
  81.9 44.8 %collective-permute-start.11 = (f32[576,512]{1,0:T(8,128)}, f32[576,512]{1,0:T(8,128)}, u32[]{:S(2)}, u32[]{:S(2)}) collective-permute-start(f32[576,512]{1,0:T(8,128)} %collective-permute-done.5.refs_1_), channel_id=1, source_target_pairs={{16,32},{32,16},{48,64},{64,48},{80,96},{96,80},{17,33},{33,17},{4... | collective-permute-start | bytes 3538952 | tf_op jit(solution)/shard_map/ppermute | solution.py:409
  85.9 40.8 %collective-permute-start.12 = (f32[576,512]{1,0:T(8,128)}, f32[576,512]{1,0:T(8,128)}, u32[]{:S(2)}, u32[]{:S(2)}) collective-permute-start(f32[576,512]{1,0:T(8,128)} %collective-permute-done.6.refs_2_), channel_id=1, source_target_pairs={{16,32},{32,16},{48,64},{64,48},{80,96},{96,80},{17,33},{33,17},{4... | collective-permute-start | bytes 3538952 | tf_op jit(solution)/shard_map/ppermute | solution.py:409
  87.8 38.9 %collective-permute-start.13 = (f32[576,512]{1,0:T(8,128)}, f32[576,512]{1,0:T(8,128)}, u32[]{:S(2)}, u32[]{:S(2)}) collective-permute-start(f32[576,512]{1,0:T(8,128)} %collective-permute-done.7.refs_3_), channel_id=1, source_target_pairs={{16,32},{32,16},{48,64},{64,48},{80,96},{96,80},{17,33},{33,17},{4... | collective-permute-start | bytes 3538952 | tf_op jit(solution)/shard_map/ppermute | solution.py:409
  91.5 0.9 copy-start.5
  92.4 0.9 copy-start.7
  93.3 0.9 copy-start.9
  100.7 48.2 %collective-permute-start.16 = (f32[256,128]{1,0:T(8,128)S(1)}, f32[256,128]{1,0:T(8,128)S(1)}, u32[]{:S(2)}, u32[]{:S(2)}) collective-permute-start(f32[256,128]{1,0:T(8,128)S(1)} %bitcast.35), channel_id=1, source_target_pairs={{0,16},{16,0},{32,48},{48,32},{64,80},{80,64},{96,112},{112,96},{1... | collective-permute-start | bytes 393224 | tf_op jit(solution)/shard_map/ppermute | solution.py:415
  100.8 48.1 %collective-permute-start.15 = (f32[256,512]{1,0:T(8,128)S(1)}, f32[256,512]{1,0:T(8,128)S(1)}, u32[]{:S(2)}, u32[]{:S(2)}) collective-permute-start(f32[256,512]{1,0:T(8,128)S(1)} %bitcast.26), channel_id=1, source_target_pairs={{0,16},{16,0},{32,48},{48,32},{64,80},{80,64},{96,112},{112,96},{1... | collective-permute-start | bytes 1572872 | tf_op jit(solution)/shard_map/ppermute | solution.py:414
  134.0 1.0 copy-start.15
  135.0 17.5 %collective-permute-start.14 = (f32[512,256]{1,0:T(8,128)S(1)}, f32[512,256]{1,0:T(8,128)S(1)}, u32[]{:S(2)}, u32[]{:S(2)}) collective-permute-start(f32[512,256]{1,0:T(8,128)S(1)} %get-tuple-element.58), channel_id=1, source_target_pairs={{0,10},{1,11},{2,8},{3,9},{4,14},{5,15},{6,12},{7,13},{8,2},{9,3},... | collective-permute-start | bytes 1572872 | tf_op jit(solution)/shard_map/ppermute | solution.py:420
  140.5 12.0 %copy-start.16 = (bf16[4,256,512]{2,1,0:T(8,128)(2,1)S(1)}, bf16[4,256,512]{2,1,0:T(8,128)(2,1)}, u32[]{:S(2)}) copy-start(bf16[4,256,512]{2,1,0:T(8,128)(2,1)} %copy-done.15) | copy-start | bytes 3145732
  148.2 16.5 %collective-permute-start.17 = (f32[512,256]{1,0:T(8,128)S(1)}, f32[512,256]{1,0:T(8,128)S(1)}, u32[]{:S(2)}, u32[]{:S(2)}) collective-permute-start(f32[512,256]{1,0:T(8,128)S(1)} %get-tuple-element.62), channel_id=1, source_target_pairs={{0,8},{1,9},{2,10},{3,11},{4,12},{5,13},{6,14},{7,15},{8,0},{9,1},... | collective-permute-start | bytes 1572872 | tf_op jit(solution)/shard_map/ppermute | solution.py:423
  148.6 16.2 %collective-permute-start.18 = (f32[512,256]{1,0:T(8,128)S(1)}, f32[512,256]{1,0:T(8,128)S(1)}, u32[]{:S(2)}, u32[]{:S(2)}) collective-permute-start(f32[512,256]{1,0:T(8,128)S(1)} %get-tuple-element.63), channel_id=1, source_target_pairs={{0,2},{1,3},{2,0},{3,1},{4,6},{5,7},{6,4},{7,5},{8,10},{9,11},{10,... | collective-permute-start | bytes 1572872 | tf_op jit(solution)/shard_map/ppermute | solution.py:424
  148.9 15.8 %copy-start.12 = (f32[256,128]{1,0:T(8,128)}, f32[256,128]{1,0:T(8,128)S(1)}, u32[]{:S(2)}) copy-start(f32[256,128]{1,0:T(8,128)S(1)} %collective-permute-done.16.skel_peer) | copy-start | bytes 393220
  148.9 15.8 %copy-start.10 = (f32[256,512]{1,0:T(8,128)}, f32[256,512]{1,0:T(8,128)S(1)}, u32[]{:S(2)}) copy-start(f32[256,512]{1,0:T(8,128)S(1)} %collective-permute-done.15.pick_peer) | copy-start | bytes 1572868
  183.5 18.3 %copy-start.11 = (f32[256,512]{1,0:T(8,128)S(1)}, f32[256,512]{1,0:T(8,128)}, u32[]{:S(2)}) copy-start(f32[256,512]{1,0:T(8,128)} %copy-done.10) | copy-start | bytes 1572868
  183.5 18.3 %copy-start.13 = (f32[256,128]{1,0:T(8,128)S(1)}, f32[256,128]{1,0:T(8,128)}, u32[]{:S(2)}) copy-start(f32[256,128]{1,0:T(8,128)} %copy-done.12) | copy-start | bytes 393220
  195.9 6.0 %collective-permute-start.19 = (f32[256,512]{1,0:T(8,128)S(1)}, f32[256,512]{1,0:T(8,128)S(1)}, u32[]{:S(2)}, u32[]{:S(2)}) collective-permute-start(f32[256,512]{1,0:T(8,128)S(1)} %bitcast.37), channel_id=1, source_target_pairs={{0,16},{16,0},{32,48},{48,32},{64,80},{80,64},{96,112},{112,96},{1... | collective-permute-start | bytes 1572872 | tf_op jit(solution)/shard_map/ppermute | solution.py:430
  205.8 12.1 %collective-permute-start.20 = (f32[128,640]{1,0:T(8,128)S(1)}, f32[128,640]{1,0:T(8,128)S(1)}, u32[]{:S(2)}, u32[]{:S(2)}) collective-permute-start(f32[128,640]{1,0:T(8,128)S(1)} %get-tuple-element.73), channel_id=1, source_target_pairs={{0,32},{16,48},{32,0},{48,16},{64,96},{80,112},{96,64},{112,80},{1... | collective-permute-start | bytes 983048 | tf_op jit(solution)/shard_map/ppermute | solution.py:445
  207.5 1.3 copy-start.14
  208.8 17.8 %copy-start.19 = (s32[2,256]{1,0:T(2,128)S(1)}, s32[2,256]{1,0:T(2,128)}, u32[]{:S(2)}) copy-start(s32[2,256]{1,0:T(2,128)} %param.13) | copy-start | bytes 6148
  217.9 7.2 %collective-permute-start.22 = (f32[128,512]{1,0:T(8,128)S(1)}, f32[128,512]{1,0:T(8,128)S(1)}, u32[]{:S(2)}, u32[]{:S(2)}) collective-permute-start(f32[128,512]{1,0:T(8,128)S(1)} %get-tuple-element.74), channel_id=1, source_target_pairs={{0,32},{16,48},{32,0},{48,16},{64,96},{80,112},{96,64},{112,80},{1... | collective-permute-start | bytes 786440 | tf_op jit(solution)/shard_map/ppermute | solution.py:452
  217.9 9.9 %collective-permute-start.21 = (f32[128,640]{1,0:T(8,128)S(1)}, f32[128,640]{1,0:T(8,128)S(1)}, u32[]{:S(2)}, u32[]{:S(2)}) collective-permute-start(f32[128,640]{1,0:T(8,128)S(1)} %collective-permute-done.20.pick_1), channel_id=1, source_target_pairs={{0,16},{16,0},{32,48},{48,32},{64,80},{80,64},{96,112},{112,96},{1... | collective-permute-start | bytes 983048 | tf_op jit(solution)/shard_map/ppermute | solution.py:446
  225.1 2.7 %collective-permute-start.23 = (f32[128,512]{1,0:T(8,128)S(1)}, f32[128,512]{1,0:T(8,128)S(1)}, u32[]{:S(2)}, u32[]{:S(2)}) collective-permute-start(f32[128,512]{1,0:T(8,128)S(1)} %collective-permute-done.22.proj_1), channel_id=1, source_target_pairs={{0,16},{16,0},{32,48},{48,32},{64,80},{80,64},{96,112},{112,96},{1... | collective-permute-start | bytes 786440 | tf_op jit(solution)/shard_map/ppermute | solution.py:453
